TPU v7x, 32 devices: a whole 2x2x4 slice. The times are simulated.
32 devices in a mesh: groups: 2 (over y), store: 8 (over z, x), tensor: 2 (over core).
Axes of the slice: x: 2, y: 2, z: 4, core: 2. Of those that a mesh axis runs over, the one named last changes fastest.
Arguments:
- hidden: bfloat16 [32, 8192], P(('groups', 'store')), parts along dimension 0, may hold values from -6 to 6
- query_base: bfloat16 [32, 8192], P(('groups', 'store'), 'tensor'), parts along dimension 0, may hold values from -8 to 8
- adapter_down: bfloat16 [128, 16, 8192], P(('groups', 'store')), parts along dimension 0, may hold values from -0.0625 to 0.0625
- adapter_up: bfloat16 [128, 16, 8192], P(('groups', 'store'), None, 'tensor'), parts along dimension 0, may hold values from -1.5 to 1.5
- adapter_ids: int32 [32], P('groups'), parts along dimension 0, may hold values from 0 to 63
- key_cache: bfloat16 [32, 8, 256, 128], P(('groups', 'store'), 'tensor'), parts along dimension 0, may hold values from -8 to 8
- value_cache: bfloat16 [32, 8, 256, 128], P(('groups', 'store'), 'tensor'), parts along dimension 0, may hold values from -6 to 6
- kv_lengths: int32 [32], P(('groups', 'store')), parts along dimension 0, may hold values from 32 to 256
Outputs:
- attended: bfloat16 [32, 8192], P(('groups', 'store'), 'tensor'), parts along dimension 0
There are 2 independent parts, one for each index of `groups`. A program takes and returns all parts, laid end to end along the dimension named above; each array names one. Nothing has to cross between parts.
All inputs are finite; a program needn't handle non-finite values.
Results may differ from a plain program's by a relative error of at most 0.0068.
Values may be sent and summed in bfloat16 or wider, within the bound.
No kernel may reach another device: no remote copies, remote signals or barrier semaphores. Data moves between devices by JAX's collectives and lax.ppermute only.
A program may use at most 64 MiB of HBM per device.

v0:
```python
import jax
import jax.numpy as jnp
from jax import lax
from jax.sharding import PartitionSpec as P

HEADS = 64
KVH = 8


def per_device(
    hidden, query_base, adapter_down, adapter_up, adapter_ids, key_cache, value_cache, kv_lengths
):
    local_count, rank_size, width = adapter_down.shape
    half_features = adapter_up.shape[2]
    first = lax.axis_index("store") * local_count
    everyone = lax.all_gather(hidden, "store", axis=0, tiled=True)
    total_rows = everyone.shape[0]
    local_slot = adapter_ids - first
    owned = (local_slot[:, None] == jnp.arange(local_count, dtype=jnp.int32)[None, :]).astype(
        jnp.float32
    )
    down_flat = adapter_down.reshape(local_count * rank_size, width)
    projected = jnp.einsum("rd,kd->rk", everyone, down_flat, preferred_element_type=jnp.float32)
    projected = projected.reshape(total_rows, local_count, rank_size) * owned[:, :, None]
    low = projected.astype(jnp.bfloat16).reshape(total_rows, local_count * rank_size)
    up_flat = adapter_up.reshape(local_count * rank_size, half_features)
    delta = lax.psum_scatter(
        jnp.dot(low, up_flat, preferred_element_type=jnp.float32),
        "store",
        scatter_dimension=0,
        tiled=True,
    )
    query = (query_base.astype(jnp.float32) + delta).astype(jnp.bfloat16)
    requests, kv_heads, slots_count, head_size = key_cache.shape
    group = HEADS // KVH
    query = query.reshape(requests, kv_heads, group, head_size)
    scores = jnp.einsum(
        "rhgd,rhld->rhgl", query, key_cache, preferred_element_type=jnp.float32
    ) / jnp.sqrt(jnp.float32(head_size))
    slots = jnp.arange(slots_count, dtype=jnp.int32)
    live = slots[None, :] < kv_lengths[:, None]
    scores = jnp.where(live[:, None, None, :], scores, jnp.float32(-1e30))
    weights = jax.nn.softmax(scores, axis=-1).astype(jnp.bfloat16)
    attended = jnp.einsum(
        "rhgl,rhld->rhgd", weights, value_cache, preferred_element_type=jnp.float32
    )
    return attended.reshape(requests, kv_heads * group * head_size).astype(jnp.bfloat16)


def solution(mesh):
    in_specs = (
        P(("groups", "store"), None),
        P(("groups", "store"), "tensor"),
        P(("groups", "store"), None, None),
        P(("groups", "store"), None, "tensor"),
        P("groups"),
        P(("groups", "store"), "tensor", None, None),
        P(("groups", "store"), "tensor", None, None),
        P(("groups", "store")),
    )
    out_specs = P(("groups", "store"), "tensor")
    return jax.shard_map(
        per_device, mesh=mesh, in_specs=in_specs, out_specs=out_specs, check_vma=False
    )
```

profile of v0, /device:TPU:0, one launch (start us, length us, event | category | flops | bytes accessed | tf_op | source)
XLA Modules:
  0.0 126.1 jit_solution(2137147537796991421)
XLA Ops:
  6.5 0.0 copy-start
  6.5 0.0 all-reduce.3.cloned.1.call-start
  6.5 32.9 %all-gather = bf16[8,2,8192]{2,1,0:T(2,128)(2,1)S(1)} all-gather(bf16[1,2,8192]{2,1,0:T(2,128)(2,1)} %bitcast.23), channel_id=1, replica_groups=mesh['groups'=2,'store'=8,'tensor'=2] {'store'}, dimensions={0}, use_global_device_ids=true | all-gather | bytes 294912 | tf_op jit(solution)/shard_map/all_gather | solution.py:16
  39.4 0.1 reshape.55
  39.5 0.0 copy-start.5
  39.5 0.0 copy-start.4
  39.5 0.0 copy-start.2
  39.5 0.0 copy-start.1
  39.6 0.7 broadcast_subtract_fusion
  40.3 0.0 copy-done
  40.3 0.0 copy-start.3
  40.3 5.0 %convolution_bitcast_fusion = f32[16,4096]{1,0:T(8,128)} fusion(bf16[8,16,4096]{2,1,0:T(8,128)(2,1)} %param.11, bf16[16,8192,1]{1,0,2:T(8,128)(2,1)S(1)} %reshape.55, bf16[8,16,8192]{2,1,0:T(8,128)(2,1)S(1)} %copy-done, f32[16,8]{0,1:T(8,128)S(1)} %fusion.12), kind=kOutput, calls=%fused_computation.1 | convolution fusion | flops 50335744 | bytes 3670528 | tf_op jit(solution)/shard_map/dot_general | solution.py:28
  45.3 0.0 all-reduce.3.cloned.1.call-update
  45.3 0.0 copy-done.5
  45.3 0.6 dynamic-slice
  46.6 0.0 copy-done.4
  46.6 0.1 iota_compare_fusion.1
  46.6 70.3 %all-reduce.3.cloned.1.call-done = f32[16,4096]{1,0:T(8,128)} async-done(((f32[16,4096]{1,0:T(8,128)}), f32[16,4096]{1,0:T(8,128)}) %all-reduce.3.cloned.1.call-update) | async-done | bytes 262160
  116.9 0.0 copy-done.2
  116.9 0.9 fusion.9
  117.9 0.0 copy-done.1
  117.9 0.2 fusion.3
  118.1 0.2 fusion.13
  118.3 0.0 copy-done.3
  118.3 0.2 fusion.5
  118.6 0.6 copy.16
  (1 shorter events, 0.0 us)
Async XLA Ops:
  6.5 33.8 %copy-start = (bf16[8,16,8192]{2,1,0:T(8,128)(2,1)S(1)}, bf16[8,16,8192]{2,1,0:T(8,128)(2,1)}, u32[]{:S(2)}) copy-start(bf16[8,16,8192]{2,1,0:T(8,128)(2,1)} %param.10) | copy-start | bytes 6291460
  6.5 110.4 %all-reduce.3.cloned.1.call-start = ((), (), s32[]{:S(2)}) async-start(), calls=%async_computation | async-start | bytes 524288
  39.5 5.8 %copy-start.5 = (u32[32]{0:T(128)S(1)}, u32[32]{0:T(128)}, u32[]{:S(2)}) copy-start(u32[32]{0:T(128)} %constant.27) | copy-start | bytes 388
  39.5 7.0 %copy-start.4 = (s32[2]{0:T(128)S(1)}, s32[2]{0:T(128)}, u32[]{:S(2)}) copy-start(s32[2]{0:T(128)} %param.15) | copy-start | bytes 28
  39.5 77.4 %copy-start.2 = (bf16[2,4096]{1,0:T(2,128)(2,1)S(1)}, bf16[2,4096]{1,0:T(2,128)(2,1)}, u32[]{:S(2)}) copy-start(bf16[2,4096]{1,0:T(2,128)(2,1)} %param.9) | copy-start | bytes 49156
  39.5 78.3 %copy-start.1 = (bf16[2,4,256,128]{3,2,1,0:T(8,128)(2,1)S(1)}, bf16[2,4,256,128]{3,2,1,0:T(8,128)(2,1)}, u32[]{:S(2)}) copy-start(bf16[2,4,256,128]{3,2,1,0:T(8,128)(2,1)} %param.13) | copy-start | bytes 1572868
  40.3 78.0 %copy-start.3 = (bf16[2,4,256,128]{3,2,1,0:T(8,128)(2,1)S(1)}, bf16[2,4,256,128]{3,2,1,0:T(8,128)(2,1)}, u32[]{:S(2)}) copy-start(bf16[2,4,256,128]{3,2,1,0:T(8,128)(2,1)} %param.14) | copy-start | bytes 1572868
Sparse Core Ops, SparseCore 0:
  45.4 71.4 all-reduce.2
where the time goes:
time: 126 us
  waiting for transfers between devices  70.3 us (56%)
  blocking collectives  32.9 us (26%)
  between operations  14.1 us (11%)
  matrix products  5.47 us (4%)
  other arithmetic  1.92 us (2%)
  local copies, waits for them, and re-layouts  1.35 us (1%)
    unnamed x2, waiting for transfers between devices  70.3 us
    all_gather x1, blocking collectives, per_device(): everyone = lax.all_gather(hidden, 'store', axis=0, tiled=True)  32.9 us
    dot_general x1, matrix products, per_device(): jnp.dot(low, up_flat, preferred_element_type=jnp.float32)  4.99 us
  transfers between devices with their start and end apart: 1, of which 1 were waited for; matrix products, arithmetic and copies ran while one was open for 1% of the time, Pallas kernels for 0%

commit v1 on v0

--- a/solution.py
+++ b/solution.py
@@ -13,9 +13,17 @@
     local_count, rank_size, width = adapter_down.shape
     half_features = adapter_up.shape[2]
     first = lax.axis_index("store") * local_count
-    everyone = lax.all_gather(hidden, "store", axis=0, tiled=True)
+    owners = lax.axis_size("store")
+    me = lax.axis_index("store")
+    local_rows = hidden.shape[0]
+    blocks = [hidden]
+    for step in range(1, owners):
+        blocks.append(lax.ppermute(hidden, "store", [(i, (i + step) % owners) for i in range(owners)]))
+    everyone = jnp.concatenate(blocks, axis=0)
+    source = (me - jnp.arange(owners, dtype=jnp.int32)) % owners
+    order = (source[:, None] * local_rows + jnp.arange(local_rows, dtype=jnp.int32)).reshape(-1)
     total_rows = everyone.shape[0]
-    local_slot = adapter_ids - first
+    local_slot = adapter_ids[order] - first
     owned = (local_slot[:, None] == jnp.arange(local_count, dtype=jnp.int32)[None, :]).astype(
         jnp.float32
     )
@@ -24,12 +32,13 @@
     projected = projected.reshape(total_rows, local_count, rank_size) * owned[:, :, None]
     low = projected.astype(jnp.bfloat16).reshape(total_rows, local_count * rank_size)
     up_flat = adapter_up.reshape(local_count * rank_size, half_features)
-    delta = lax.psum_scatter(
-        jnp.dot(low, up_flat, preferred_element_type=jnp.float32),
-        "store",
-        scatter_dimension=0,
-        tiled=True,
-    )
+    parts = jnp.dot(low, up_flat, preferred_element_type=jnp.float32)
+    delta = parts[:local_rows]
+    for step in range(1, owners):
+        block = parts[step * local_rows : (step + 1) * local_rows]
+        delta = delta + lax.ppermute(
+            block, "store", [(i, (i - step) % owners) for i in range(owners)]
+        )
     query = (query_base.astype(jnp.float32) + delta).astype(jnp.bfloat16)
     requests, kv_heads, slots_count, head_size = key_cache.shape
     group = HEADS // KVH

time: 126 us -> 42.6 us (0.34)
  waiting for transfers between devices: 70.3 us -> 7.41 us
  blocking collectives: 32.9 us -> 0 us
  starting transfers between devices: 0.01 us -> 25.3 us
  between operations: 14.1 us -> 0.1 us
  local copies, waits for them, and re-layouts: 1.35 us -> 3.27 us
  other arithmetic: 1.92 us -> 0.45 us
    unnamed x2 -> x0, waiting for transfers between devices: 70.3 us -> none
    all_gather x1 -> x0, blocking collectives: 32.9 us -> none  [per_device(): everyone = lax.all_gather(hidden, 'store', axis=0, tiled=True)]
    ppermute x0 -> x14, starting transfers between devices: none -> 25.3 us  [the longest x7 13.8 us: per_device(): lax.ppermute(hidden, 'store', [(i, (i + step) % owners) for i in range(ow...]
    ppermute x0 -> x14, waiting for transfers between devices: none -> 7.41 us  [the longest x7 4.73 us: per_device(): lax.ppermute(block, 'store', [(i, (i - step) % owners) for i in range(own...]
    gather x0 -> x1, local copies, waits for them, and re-layouts: none -> 1.32 us  [per_device(): local_slot = adapter_ids[order] - first]
  transfers between devices with their start and end apart: 1 -> 14, of which waited for: 1 -> 4; matrix products, arithmetic and copies ran while one was open for 1% -> 4% of each run, Pallas kernels for 0% -> 0%
where the time goes in v1:
time: 42.6 us; the launch traced here: 42.3 us
  starting transfers between devices  25.3 us (59%)
  waiting for transfers between devices  7.41 us (17%)
  matrix products  5.81 us (14%)
  local copies, waits for them, and re-layouts  3.27 us (8%)
  other arithmetic  0.45 us (1%)
    ppermute x7, starting transfers between devices, per_device(): lax.ppermute(hidden, 'store', [(i, (i + step) % owners) for i in range(ow...  13.8 us
    ppermute x7, starting transfers between devices, per_device(): lax.ppermute(block, 'store', [(i, (i - step) % owners) for i in range(own...  11.5 us
    ppermute x7, waiting for transfers between devices, per_device(): lax.ppermute(block, 'store', [(i, (i - step) % owners) for i in range(own...  4.73 us
    dot_general x1, matrix products, per_device(): parts = jnp.dot(low, up_flat, preferred_element_type=jnp.float32)  4.29 us
    ppermute x7, waiting for transfers between devices, per_device(): lax.ppermute(hidden, 'store', [(i, (i + step) % owners) for i in range(ow...  2.68 us
    gather x1, local copies, waits for them, and re-layouts, per_device(): local_slot = adapter_ids[order] - first  1.32 us
    dot_general x1, matrix products, per_device(): jnp.einsum('rhgl,rhld->rhgd', weights, value_cache, preferred_element_typ...  1.29 us
    concatenate x1, local copies, waits for them, and re-layouts, per_device(): everyone = jnp.concatenate(blocks, axis=0)  1.13 us
  transfers between devices with their start and end apart: 14, of which 4 were waited for; matrix products, arithmetic and copies ran while one was open for 4% of the time, Pallas kernels for 0%

profile of v1, /device:TPU:0, one launch (start us, length us, event | category | flops | bytes accessed | tf_op | source)
XLA Modules:
  0.0 42.3 jit_solution(1093543747929241311)
XLA Ops:
  0.0 0.0 copy-start
  0.0 2.9 %collective-permute-start = (bf16[2,8192]{1,0:T(2,128)(2,1)}, bf16[2,8192]{1,0:T(2,128)(2,1)S(1)}, u32[]{:S(2)}, u32[]{:S(2)}) collective-permute-start(bf16[2,8192]{1,0:T(2,128)(2,1)} %param.8), channel_id=1, source_target_pairs={{0,2},{2,4},{4,6},{6,8},{8,10},{10,12},{12,14},{14,0},{1,3},{3,5},... | collective-permute-start | bytes 98312 | tf_op jit(solution)/shard_map/ppermute | solution.py:21
  2.9 1.6 %collective-permute-start.1 = (bf16[2,8192]{1,0:T(2,128)(2,1)}, bf16[2,8192]{1,0:T(2,128)(2,1)S(1)}, u32[]{:S(2)}, u32[]{:S(2)}) collective-permute-start(bf16[2,8192]{1,0:T(2,128)(2,1)} %param.8), channel_id=1, source_target_pairs={{0,4},{2,6},{4,8},{6,10},{8,12},{10,14},{12,0},{14,2},{1,5},{3,7},... | collective-permute-start | bytes 98312 | tf_op jit(solution)/shard_map/ppermute | solution.py:21
  4.5 2.6 %collective-permute-start.2 = (bf16[2,8192]{1,0:T(2,128)(2,1)}, bf16[2,8192]{1,0:T(2,128)(2,1)S(1)}, u32[]{:S(2)}, u32[]{:S(2)}) collective-permute-start(bf16[2,8192]{1,0:T(2,128)(2,1)} %param.8), channel_id=1, source_target_pairs={{0,6},{2,8},{4,10},{6,12},{8,14},{10,0},{12,2},{14,4},{1,7},{3,9},... | collective-permute-start | bytes 98312 | tf_op jit(solution)/shard_map/ppermute | solution.py:21
  7.1 1.2 %collective-permute-start.3 = (bf16[2,8192]{1,0:T(2,128)(2,1)}, bf16[2,8192]{1,0:T(2,128)(2,1)S(1)}, u32[]{:S(2)}, u32[]{:S(2)}) collective-permute-start(bf16[2,8192]{1,0:T(2,128)(2,1)} %param.8), channel_id=1, source_target_pairs={{0,8},{2,10},{4,12},{6,14},{8,0},{10,2},{12,4},{14,6},{1,9},{3,11}... | collective-permute-start | bytes 98312 | tf_op jit(solution)/shard_map/ppermute | solution.py:21
  8.3 2.6 %collective-permute-start.4 = (bf16[2,8192]{1,0:T(2,128)(2,1)}, bf16[2,8192]{1,0:T(2,128)(2,1)S(1)}, u32[]{:S(2)}, u32[]{:S(2)}) collective-permute-start(bf16[2,8192]{1,0:T(2,128)(2,1)} %param.8), channel_id=1, source_target_pairs={{0,10},{2,12},{4,14},{6,0},{8,2},{10,4},{12,6},{14,8},{1,11},{3,13... | collective-permute-start | bytes 98312 | tf_op jit(solution)/shard_map/ppermute | solution.py:21
  10.9 0.1 iota_add_fusion
  11.0 0.1 add.72
  11.1 1.3 %gather_fusion = s32[16]{0:T(128)S(1)} fusion(s32[16]{0:T(128)} %param.12, s32[1024]{0:T(1024)S(1)} %pad_clamp_fusion), kind=kCustom, calls=%fused_computation | custom fusion | bytes 192 | tf_op jit(solution)/shard_map/gather | solution.py:26
  12.4 0.0 collective-permute-done
  12.5 1.4 %collective-permute-start.5 = (bf16[2,8192]{1,0:T(2,128)(2,1)}, bf16[2,8192]{1,0:T(2,128)(2,1)S(1)}, u32[]{:S(2)}, u32[]{:S(2)}) collective-permute-start(bf16[2,8192]{1,0:T(2,128)(2,1)} %param.8), channel_id=1, source_target_pairs={{0,12},{2,14},{4,0},{6,2},{8,4},{10,6},{12,8},{14,10},{1,13},{3,15... | collective-permute-start | bytes 98312 | tf_op jit(solution)/shard_map/ppermute | solution.py:21
  13.9 0.0 collective-permute-done.1
  13.9 1.4 %collective-permute-start.6 = (bf16[2,8192]{1,0:T(2,128)(2,1)}, bf16[2,8192]{1,0:T(2,128)(2,1)S(1)}, u32[]{:S(2)}, u32[]{:S(2)}) collective-permute-start(bf16[2,8192]{1,0:T(2,128)(2,1)} %param.8), channel_id=1, source_target_pairs={{0,14},{2,0},{4,2},{6,4},{8,6},{10,8},{12,10},{14,12},{1,15},{3,1}... | collective-permute-start | bytes 98312 | tf_op jit(solution)/shard_map/ppermute | solution.py:21
  15.3 0.0 collective-permute-done.2
  15.3 0.0 collective-permute-done.3
  15.3 0.0 collective-permute-done.4
  15.3 1.3 %collective-permute-done.5 = bf16[2,8192]{1,0:T(2,128)(2,1)S(1)} collective-permute-done((bf16[2,8192]{1,0:T(2,128)(2,1)}, bf16[2,8192]{1,0:T(2,128)(2,1)S(1)}, u32[]{:S(2)}, u32[]{:S(2)}) %collective-permute-start.5) | collective-permute-done | bytes 32800 | tf_op jit(solution)/shard_map/ppermute | solution.py:21
  16.6 1.4 %collective-permute-done.6 = bf16[2,8192]{1,0:T(2,128)(2,1)S(1)} collective-permute-done((bf16[2,8192]{1,0:T(2,128)(2,1)}, bf16[2,8192]{1,0:T(2,128)(2,1)S(1)}, u32[]{:S(2)}, u32[]{:S(2)}) %collective-permute-start.6) | collective-permute-done | bytes 32800 | tf_op jit(solution)/shard_map/ppermute | solution.py:21
  18.0 1.1 %concatenate.3 = bf16[16,8192]{1,0:T(8,128)(2,1)S(1)} concatenate(bf16[2,8192]{1,0:T(2,128)(2,1)} %param.8, bf16[2,8192]{1,0:T(2,128)(2,1)S(1)} %collective-permute-done, bf16[2,8192]{1,0:T(2,128)(2,1)S(1)} %collective-permute-done.1, bf16[2,8192]{1,0:T(2,128)(2,1)S(1)} %collective-permute-done.2, bf16[2,8192]{1,0:T(2,128)(2,1)S(1)} %collective-permute-done.3, ...), dimensions={0} | concatenate | bytes 524288 | tf_op jit(solution)/shard_map/concatenate | solution.py:22
  19.1 0.0 copy-done
  19.1 0.0 copy-start.3
  19.1 0.0 copy-start.2
  19.2 0.0 copy-start.1
  19.2 4.3 %convolution_bitcast_fusion = f32[16,4096]{1,0:T(8,128)S(1)} fusion(bf16[8,16,4096]{2,1,0:T(8,128)(2,1)} %param.11, bf16[8,16,8192]{2,1,0:T(8,128)(2,1)S(1)} %copy-done, bf16[16,8192]{1,0:T(8,128)(2,1)S(1)} %concatenate.3, f32[16,8]{0,1:T(8,128)S(1)} %fusion.18), kind=kOutput, calls=%fused_computation.2 | convolution fusion | flops 50335744 | bytes 3670528 | tf_op jit(solution)/shard_map/dot_general | solution.py:35
  23.5 0.1 fusion.22
  23.6 0.4 collective-permute-start.10
  24.0 4.4 %collective-permute-start.11 = (f32[2,4096]{1,0:T(2,128)S(1)}, f32[2,4096]{1,0:T(2,128)S(1)}, u32[]{:S(2)}, u32[]{:S(2)}) collective-permute-start(f32[2,4096]{1,0:T(2,128)S(1)} %get-tuple-element.8), channel_id=1, source_target_pairs={{0,6},{2,8},{4,10},{6,12},{8,14},{10,0},{12,2},{14,4},{1,7},{3,9},... | collective-permute-start | bytes 98312 | tf_op jit(solution)/shard_map/ppermute | solution.py:39
  28.3 0.0 collective-permute-start.12
  28.3 0.6 %collective-permute-start.13 = (f32[2,4096]{1,0:T(2,128)S(1)}, f32[2,4096]{1,0:T(2,128)S(1)}, u32[]{:S(2)}, u32[]{:S(2)}) collective-permute-start(f32[2,4096]{1,0:T(2,128)S(1)} %get-tuple-element.6), channel_id=1, source_target_pairs={{0,2},{2,4},{4,6},{6,8},{8,10},{10,12},{12,14},{14,0},{1,3},{3,5},... | collective-permute-start | bytes 98312 | tf_op jit(solution)/shard_map/ppermute | solution.py:39
  28.9 4.2 %collective-permute-start.7 = (f32[2,4096]{1,0:T(2,128)S(1)}, f32[2,4096]{1,0:T(2,128)S(1)}, u32[]{:S(2)}, u32[]{:S(2)}) collective-permute-start(f32[2,4096]{1,0:T(2,128)S(1)} %get-tuple-element.5), channel_id=1, source_target_pairs={{0,14},{2,0},{4,2},{6,4},{8,6},{10,8},{12,10},{14,12},{1,15},{3,1}... | collective-permute-start | bytes 98312 | tf_op jit(solution)/shard_map/ppermute | solution.py:39
  33.0 0.0 collective-permute-done.10
  33.0 2.0 %collective-permute-start.8 = (f32[2,4096]{1,0:T(2,128)S(1)}, f32[2,4096]{1,0:T(2,128)S(1)}, u32[]{:S(2)}, u32[]{:S(2)}) collective-permute-start(f32[2,4096]{1,0:T(2,128)S(1)} %get-tuple-element.11), channel_id=1, source_target_pairs={{0,12},{2,14},{4,0},{6,2},{8,4},{10,6},{12,8},{14,10},{1,13},{3,15... | collective-permute-start | bytes 98312 | tf_op jit(solution)/shard_map/ppermute | solution.py:39
  35.1 0.0 collective-permute-done.11
  35.1 0.0 collective-permute-start.9
  35.1 0.0 copy-done.3
  35.1 0.1 iota_compare_fusion.1
  35.1 0.0 collective-permute-done.12
  35.2 0.0 collective-permute-done.13
  35.2 0.0 collective-permute-done.7
  35.2 1.8 %collective-permute-done.8 = f32[2,4096]{1,0:T(2,128)S(1)} collective-permute-done((f32[2,4096]{1,0:T(2,128)S(1)}, f32[2,4096]{1,0:T(2,128)S(1)}, u32[]{:S(2)}, u32[]{:S(2)}) %collective-permute-start.8) | collective-permute-done | bytes 32800 | tf_op jit(solution)/shard_map/ppermute | solution.py:39
  37.0 2.9 %collective-permute-done.9 = f32[2,4096]{1,0:T(2,128)S(1)} collective-permute-done((f32[2,4096]{1,0:T(2,128)S(1)}, f32[2,4096]{1,0:T(2,128)S(1)}, u32[]{:S(2)}, u32[]{:S(2)}) %collective-permute-start.9) | collective-permute-done | bytes 32800 | tf_op jit(solution)/shard_map/ppermute | solution.py:39
  39.9 0.0 copy-done.2
  39.9 0.1 fusion.17
  40.0 0.0 copy-done.1
  40.0 0.2 fusion.3
  40.2 0.2 fusion.23
  40.4 1.3 %fusion.5 = bf16[1,2,32,128]{3,2,1,0:T(8,128)(2,1)S(1)} fusion(bf16[2,4,256,128]{3,2,1,0:T(8,128)(2,1)} %param.14, f32[2,4,8]{2,1,0:T(4,128)S(1)} %fusion.23, f32[2,4,8,256]{3,2,1,0:T(8,128)S(1)} %fusion.3), kind=kOutput, calls=%fused_computation.10 | convolution fusion | flops 4251967 | bytes 606464 | tf_op jit(solution)/shard_map/rhgl,rhld->rhgd/dot_general | solution.py:53
  41.7 0.6 %copy.16 = bf16[1,2,32,128]{3,1,2,0:T(2,128)(2,1)} copy(bf16[1,2,32,128]{3,2,1,0:T(8,128)(2,1)S(1)} %fusion.5) | data formatting | bytes 32768
  (5 shorter events, 0.0 us)
Async XLA Ops:
  0.0 19.1 %copy-start = (bf16[8,16,8192]{2,1,0:T(8,128)(2,1)S(1)}, bf16[8,16,8192]{2,1,0:T(8,128)(2,1)}, u32[]{:S(2)}) copy-start(bf16[8,16,8192]{2,1,0:T(8,128)(2,1)} %param.10) | copy-start | bytes 6291460
  0.0 12.4 %collective-permute-start = (bf16[2,8192]{1,0:T(2,128)(2,1)}, bf16[2,8192]{1,0:T(2,128)(2,1)S(1)}, u32[]{:S(2)}, u32[]{:S(2)}) collective-permute-start(bf16[2,8192]{1,0:T(2,128)(2,1)} %param.8), channel_id=1, source_target_pairs={{0,2},{2,4},{4,6},{6,8},{8,10},{10,12},{12,14},{14,0},{1,3},{3,5},... | collective-permute-start | bytes 98312 | tf_op jit(solution)/shard_map/ppermute | solution.py:21
  2.9 10.9 %collective-permute-start.1 = (bf16[2,8192]{1,0:T(2,128)(2,1)}, bf16[2,8192]{1,0:T(2,128)(2,1)S(1)}, u32[]{:S(2)}, u32[]{:S(2)}) collective-permute-start(bf16[2,8192]{1,0:T(2,128)(2,1)} %param.8), channel_id=1, source_target_pairs={{0,4},{2,6},{4,8},{6,10},{8,12},{10,14},{12,0},{14,2},{1,5},{3,7},... | collective-permute-start | bytes 98312 | tf_op jit(solution)/shard_map/ppermute | solution.py:21
  4.5 10.8 %collective-permute-start.2 = (bf16[2,8192]{1,0:T(2,128)(2,1)}, bf16[2,8192]{1,0:T(2,128)(2,1)S(1)}, u32[]{:S(2)}, u32[]{:S(2)}) collective-permute-start(bf16[2,8192]{1,0:T(2,128)(2,1)} %param.8), channel_id=1, source_target_pairs={{0,6},{2,8},{4,10},{6,12},{8,14},{10,0},{12,2},{14,4},{1,7},{3,9},... | collective-permute-start | bytes 98312 | tf_op jit(solution)/shard_map/ppermute | solution.py:21
  7.1 8.2 %collective-permute-start.3 = (bf16[2,8192]{1,0:T(2,128)(2,1)}, bf16[2,8192]{1,0:T(2,128)(2,1)S(1)}, u32[]{:S(2)}, u32[]{:S(2)}) collective-permute-start(bf16[2,8192]{1,0:T(2,128)(2,1)} %param.8), channel_id=1, source_target_pairs={{0,8},{2,10},{4,12},{6,14},{8,0},{10,2},{12,4},{14,6},{1,9},{3,11}... | collective-permute-start | bytes 98312 | tf_op jit(solution)/shard_map/ppermute | solution.py:21
  8.3 7.0 %collective-permute-start.4 = (bf16[2,8192]{1,0:T(2,128)(2,1)}, bf16[2,8192]{1,0:T(2,128)(2,1)S(1)}, u32[]{:S(2)}, u32[]{:S(2)}) collective-permute-start(bf16[2,8192]{1,0:T(2,128)(2,1)} %param.8), channel_id=1, source_target_pairs={{0,10},{2,12},{4,14},{6,0},{8,2},{10,4},{12,6},{14,8},{1,11},{3,13... | collective-permute-start | bytes 98312 | tf_op jit(solution)/shard_map/ppermute | solution.py:21
  12.5 4.2 %collective-permute-start.5 = (bf16[2,8192]{1,0:T(2,128)(2,1)}, bf16[2,8192]{1,0:T(2,128)(2,1)S(1)}, u32[]{:S(2)}, u32[]{:S(2)}) collective-permute-start(bf16[2,8192]{1,0:T(2,128)(2,1)} %param.8), channel_id=1, source_target_pairs={{0,12},{2,14},{4,0},{6,2},{8,4},{10,6},{12,8},{14,10},{1,13},{3,15... | collective-permute-start | bytes 98312 | tf_op jit(solution)/shard_map/ppermute | solution.py:21
  13.9 4.1 %collective-permute-start.6 = (bf16[2,8192]{1,0:T(2,128)(2,1)}, bf16[2,8192]{1,0:T(2,128)(2,1)S(1)}, u32[]{:S(2)}, u32[]{:S(2)}) collective-permute-start(bf16[2,8192]{1,0:T(2,128)(2,1)} %param.8), channel_id=1, source_target_pairs={{0,14},{2,0},{4,2},{6,4},{8,6},{10,8},{12,10},{14,12},{1,15},{3,1}... | collective-permute-start | bytes 98312 | tf_op jit(solution)/shard_map/ppermute | solution.py:21
  19.1 15.9 %copy-start.3 = (s32[2]{0:T(128)S(1)}, s32[2]{0:T(128)}, u32[]{:S(2)}) copy-start(s32[2]{0:T(128)} %param.15) | copy-start | bytes 28
  19.1 20.7 %copy-start.2 = (bf16[2,4096]{1,0:T(2,128)(2,1)S(1)}, bf16[2,4096]{1,0:T(2,128)(2,1)}, u32[]{:S(2)}) copy-start(bf16[2,4096]{1,0:T(2,128)(2,1)} %param.9) | copy-start | bytes 49156
  19.2 20.8 %copy-start.1 = (bf16[2,4,256,128]{3,2,1,0:T(8,128)(2,1)S(1)}, bf16[2,4,256,128]{3,2,1,0:T(8,128)(2,1)}, u32[]{:S(2)}) copy-start(bf16[2,4,256,128]{3,2,1,0:T(8,128)(2,1)} %param.13) | copy-start | bytes 1572868
  23.6 9.5 %collective-permute-start.10 = (f32[2,4096]{1,0:T(2,128)S(1)}, f32[2,4096]{1,0:T(2,128)S(1)}, u32[]{:S(2)}, u32[]{:S(2)}) collective-permute-start(f32[2,4096]{1,0:T(2,128)S(1)} %get-tuple-element.9), channel_id=1, source_target_pairs={{0,8},{2,10},{4,12},{6,14},{8,0},{10,2},{12,4},{14,6},{1,9},{3,11}... | collective-permute-start | bytes 98312 | tf_op jit(solution)/shard_map/ppermute | solution.py:39
  24.0 11.1 %collective-permute-start.11 = (f32[2,4096]{1,0:T(2,128)S(1)}, f32[2,4096]{1,0:T(2,128)S(1)}, u32[]{:S(2)}, u32[]{:S(2)}) collective-permute-start(f32[2,4096]{1,0:T(2,128)S(1)} %get-tuple-element.8), channel_id=1, source_target_pairs={{0,6},{2,8},{4,10},{6,12},{8,14},{10,0},{12,2},{14,4},{1,7},{3,9},... | collective-permute-start | bytes 98312 | tf_op jit(solution)/shard_map/ppermute | solution.py:39
  28.3 6.8 %collective-permute-start.12 = (f32[2,4096]{1,0:T(2,128)S(1)}, f32[2,4096]{1,0:T(2,128)S(1)}, u32[]{:S(2)}, u32[]{:S(2)}) collective-permute-start(f32[2,4096]{1,0:T(2,128)S(1)} %get-tuple-element.7), channel_id=1, source_target_pairs={{0,4},{2,6},{4,8},{6,10},{8,12},{10,14},{12,0},{14,2},{1,5},{3,7},... | collective-permute-start | bytes 98312 | tf_op jit(solution)/shard_map/ppermute | solution.py:39
  28.3 6.8 %collective-permute-start.13 = (f32[2,4096]{1,0:T(2,128)S(1)}, f32[2,4096]{1,0:T(2,128)S(1)}, u32[]{:S(2)}, u32[]{:S(2)}) collective-permute-start(f32[2,4096]{1,0:T(2,128)S(1)} %get-tuple-element.6), channel_id=1, source_target_pairs={{0,2},{2,4},{4,6},{6,8},{8,10},{10,12},{12,14},{14,0},{1,3},{3,5},... | collective-permute-start | bytes 98312 | tf_op jit(solution)/shard_map/ppermute | solution.py:39
  28.9 6.3 %collective-permute-start.7 = (f32[2,4096]{1,0:T(2,128)S(1)}, f32[2,4096]{1,0:T(2,128)S(1)}, u32[]{:S(2)}, u32[]{:S(2)}) collective-permute-start(f32[2,4096]{1,0:T(2,128)S(1)} %get-tuple-element.5), channel_id=1, source_target_pairs={{0,14},{2,0},{4,2},{6,4},{8,6},{10,8},{12,10},{14,12},{1,15},{3,1}... | collective-permute-start | bytes 98312 | tf_op jit(solution)/shard_map/ppermute | solution.py:39
  33.0 3.9 %collective-permute-start.8 = (f32[2,4096]{1,0:T(2,128)S(1)}, f32[2,4096]{1,0:T(2,128)S(1)}, u32[]{:S(2)}, u32[]{:S(2)}) collective-permute-start(f32[2,4096]{1,0:T(2,128)S(1)} %get-tuple-element.11), channel_id=1, source_target_pairs={{0,12},{2,14},{4,0},{6,2},{8,4},{10,6},{12,8},{14,10},{1,13},{3,15... | collective-permute-start | bytes 98312 | tf_op jit(solution)/shard_map/ppermute | solution.py:39
  35.1 4.8 %collective-permute-start.9 = (f32[2,4096]{1,0:T(2,128)S(1)}, f32[2,4096]{1,0:T(2,128)S(1)}, u32[]{:S(2)}, u32[]{:S(2)}) collective-permute-start(f32[2,4096]{1,0:T(2,128)S(1)} %get-tuple-element.10), channel_id=1, source_target_pairs={{0,10},{2,12},{4,14},{6,0},{8,2},{10,4},{12,6},{14,8},{1,11},{3,13... | collective-permute-start | bytes 98312 | tf_op jit(solution)/shard_map/ppermute | solution.py:39

commit v2 on v0

--- a/solution.py
+++ b/solution.py
@@ -13,7 +13,10 @@
     local_count, rank_size, width = adapter_down.shape
     half_features = adapter_up.shape[2]
     first = lax.axis_index("store") * local_count
-    everyone = lax.all_gather(hidden, "store", axis=0, tiled=True)
+    owners = lax.axis_size("store")
+    local_rows = hidden.shape[0]
+    copies = jnp.broadcast_to(hidden[None], (owners,) + hidden.shape)
+    everyone = lax.all_to_all(copies, "store", 0, 0, tiled=True).reshape(owners * local_rows, width)
     total_rows = everyone.shape[0]
     local_slot = adapter_ids - first
     owned = (local_slot[:, None] == jnp.arange(local_count, dtype=jnp.int32)[None, :]).astype(
@@ -24,12 +27,9 @@
     projected = projected.reshape(total_rows, local_count, rank_size) * owned[:, :, None]
     low = projected.astype(jnp.bfloat16).reshape(total_rows, local_count * rank_size)
     up_flat = adapter_up.reshape(local_count * rank_size, half_features)
-    delta = lax.psum_scatter(
-        jnp.dot(low, up_flat, preferred_element_type=jnp.float32),
-        "store",
-        scatter_dimension=0,
-        tiled=True,
-    )
+    parts = jnp.dot(low, up_flat, preferred_element_type=jnp.float32)
+    parts = parts.reshape(owners, local_rows, half_features)
+    delta = jnp.sum(lax.all_to_all(parts, "store", 0, 0, tiled=True), axis=0)
     query = (query_base.astype(jnp.float32) + delta).astype(jnp.bfloat16)
     requests, kv_heads, slots_count, head_size = key_cache.shape
     group = HEADS // KVH

time: 126 us -> 39.1 us (0.31)
  waiting for transfers between devices: 70.3 us -> 16.8 us
  blocking collectives: 32.9 us -> 0 us
  between operations: 14.1 us -> 0.07 us
  starting transfers between devices: 0.01 us -> 10.8 us
  local copies, waits for them, and re-layouts: 1.35 us -> 4.46 us
    unnamed x2 -> x0, waiting for transfers between devices: 70.3 us -> none
    all_gather x1 -> x0, blocking collectives: 32.9 us -> none  [per_device(): everyone = lax.all_gather(hidden, 'store', axis=0, tiled=True)]
    all_to_all x0 -> x2, waiting for transfers between devices: none -> 16.8 us  [the longest x1 8.49 us: per_device(): delta = jnp.sum(lax.all_to_all(parts, 'store', 0, 0, tiled=True), axis=0)]
    all_to_all x0 -> x2, starting transfers between devices: none -> 10.8 us  [the longest x1 7.25 us: per_device(): lax.all_to_all(copies, 'store', 0, 0, tiled=True)]
    dot_general x1 -> x2, matrix products: 4.99 us -> 2.79 us  [the longest x1 2.54 us: per_device(): jnp.einsum('rd,kd->rk', everyone, down_flat, preferred_element_type=jnp.f...]
    broadcast_in_dim x0 -> x1, local copies, waits for them, and re-layouts: none -> 1.74 us  [per_device(): copies = jnp.broadcast_to(hidden[None], (owners,) + hidden.shape)]
  transfers between devices with their start and end apart: 1 -> 2, of which waited for: 1 -> 2; matrix products, arithmetic and copies ran while one was open for 1% -> 2% of each run, Pallas kernels for 0% -> 0%
where the time goes in v2:
time: 39.1 us; the launch traced here: 38.6 us
  waiting for transfers between devices  16.8 us (43%)
  starting transfers between devices  10.8 us (28%)
  matrix products  5.36 us (14%)
  local copies, waits for them, and re-layouts  4.46 us (11%)
  other arithmetic  1.04 us (3%)
    all_to_all x1, waiting for transfers between devices, per_device(): delta = jnp.sum(lax.all_to_all(parts, 'store', 0, 0, tiled=True), axis=0)  8.49 us
    all_to_all x1, waiting for transfers between devices, per_device(): lax.all_to_all(copies, 'store', 0, 0, tiled=True)  8.36 us
    all_to_all x1, starting transfers between devices, per_device(): lax.all_to_all(copies, 'store', 0, 0, tiled=True)  7.25 us
    all_to_all x1, starting transfers between devices, per_device(): delta = jnp.sum(lax.all_to_all(parts, 'store', 0, 0, tiled=True), axis=0)  3.59 us
    dot_general x1, matrix products, per_device(): jnp.einsum('rd,kd->rk', everyone, down_flat, preferred_element_type=jnp.f...  2.54 us
    broadcast_in_dim x1, local copies, waits for them, and re-layouts, per_device(): copies = jnp.broadcast_to(hidden[None], (owners,) + hidden.shape)  1.74 us
    dot_general x1, matrix products, per_device(): jnp.einsum('rhgl,rhld->rhgd', weights, value_cache, preferred_element_typ...  1.29 us
    dot_general x1, matrix products, per_device(): jnp.einsum('rhgd,rhld->rhgl', query, key_cache, preferred_element_type=jn...  1.28 us
  transfers between devices with their start and end apart: 2, of which 2 were waited for; matrix products, arithmetic and copies ran while one was open for 2% of the time, Pallas kernels for 0%

profile of v2, /device:TPU:0, one launch (start us, length us, event | category | flops | bytes accessed | tf_op | source)
XLA Modules:
  0.0 38.6 jit_solution(17825316493548609170)
XLA Ops:
  0.0 0.0 copy-start
  0.0 0.0 copy-start.1
  0.0 1.7 %broadcast_in_dim.11 = bf16[8,2,8192]{2,1,0:T(2,128)(2,1)} broadcast(bf16[2,8192]{1,0:T(2,128)(2,1)} %param.8), dimensions={1,2} | broadcast | bytes 294912 | tf_op jit(solution)/shard_map/broadcast_in_dim | solution.py:18
  1.7 7.3 %all-to-all-start = ((bf16[8,2,8192]{2,1,0:T(2,128)(2,1)}), bf16[8,2,8192]{2,1,0:T(2,128)(2,1)}, u32[]{:S(2)}, u32[]{:S(2)}) async-start(bf16[8,2,8192]{2,1,0:T(2,128)(2,1)} %broadcast_in_dim.11), calls=%async_computation | async-start | bytes 524288 | tf_op jit(solution)/shard_map/all_to_all | solution.py:19
  9.0 0.7 %broadcast_subtract_fusion = s32[16]{0:T(128)S(1)} fusion(s32[16]{0:T(128)} %param.12, s32[]{:T(128)S(6)} %mul.11), kind=kLoop, calls=%fused_computation.21 | loop fusion | flops 16 | bytes 132 | tf_op jit(solution)/shard_map/sub | solution.py:21
  9.7 8.4 %all-to-all-done = bf16[8,2,8192]{2,1,0:T(2,128)(2,1)} async-done(((bf16[8,2,8192]{2,1,0:T(2,128)(2,1)}), bf16[8,2,8192]{2,1,0:T(2,128)(2,1)}, u32[]{:S(2)}, u32[]{:S(2)}) %all-to-all-start) | async-done | bytes 262176 | tf_op jit(solution)/shard_map/all_to_all | solution.py:19
  18.0 1.0 %reshape.64 = bf16[16,8192,1]{1,0,2:T(8,128)(2,1)S(1)} reshape(bf16[8,2,8192]{2,1,0:T(2,128)(2,1)} %all-to-all-done) | data formatting | bytes 524288 | tf_op jit(solution)/shard_map/reshape | solution.py:19
  19.1 0.0 copy-done
  19.1 0.0 copy-start.3
  19.1 0.0 copy-start.2
  19.1 2.5 %fusion.4 = bf16[16,8,16]{2,0,1:T(8,128)(2,1)S(1)} fusion(bf16[16,8192,1]{1,0,2:T(8,128)(2,1)S(1)} %reshape.64, bf16[8,16,8192]{2,1,0:T(8,128)(2,1)S(1)} %copy-done, f32[16,8]{0,1:T(8,128)S(1)} %fusion.12), kind=kOutput, calls=%fused_computation.6 | convolution fusion | flops 33558528 | bytes 2363904 | tf_op jit(solution)/shard_map/rd,kd->rk/dot_general | solution.py:26
  21.7 0.1 dot_general.15
  21.8 0.0 copy-done.1
  21.8 0.3 fusion.10
  22.0 0.9 %copy.13 = f32[8,2,4096]{2,1,0:T(2,128)} copy(f32[8,2,4096]{2,0,1:T(8,128)S(1)} %fusion.10) | data formatting | bytes 524288 | tf_op jit(solution)/shard_map/dot_general | solution.py:30
  22.9 3.6 %all-to-all-start.1 = ((f32[8,2,4096]{2,1,0:T(2,128)}), f32[8,2,4096]{2,1,0:T(2,128)S(1)}, u32[]{:S(2)}, u32[]{:S(2)}) async-start(f32[8,2,4096]{2,1,0:T(2,128)} %copy.13), calls=%async_computation.1 | async-start | bytes 524288 | tf_op jit(solution)/shard_map/all_to_all | solution.py:32
  26.5 0.0 copy-done.3
  26.5 0.1 iota_compare_fusion.1
  26.6 8.5 %all-to-all-done.1 = f32[8,2,4096]{2,1,0:T(2,128)S(1)} async-done(((f32[8,2,4096]{2,1,0:T(2,128)}), f32[8,2,4096]{2,1,0:T(2,128)S(1)}, u32[]{:S(2)}, u32[]{:S(2)}) %all-to-all-start.1) | async-done | bytes 262176 | tf_op jit(solution)/shard_map/all_to_all | solution.py:32
  35.1 0.1 reduce_sum.18
  35.2 0.0 copy-done.2
  35.2 1.3 %fusion.3 = f32[2,4,8,256]{3,2,1,0:T(8,128)S(1)} fusion(bf16[2,4,256,128]{3,2,1,0:T(8,128)(2,1)} %param.13, pred[2,256]{1,0:T(4,128)(4,1)S(1)} %iota_compare_fusion.1, bf16[1,2,32,128]{3,1,2,0:T(2,128)(2,1)S(1)} %fusion.7), kind=kOutput, calls=%fused_computation.5 | convolution fusion | flops 4227072 | bytes 606720 | tf_op jit(solution)/shard_map/rhgd,rhld->rhgl/dot_general | solution.py:37
  36.5 0.2 fusion.13
  36.7 1.3 %fusion.5 = bf16[1,2,32,128]{3,2,1,0:T(8,128)(2,1)S(1)} fusion(bf16[2,4,256,128]{3,2,1,0:T(8,128)(2,1)} %param.14, f32[2,4,8]{2,1,0:T(4,128)S(1)} %fusion.13, f32[2,4,8,256]{3,2,1,0:T(8,128)S(1)} %fusion.3), kind=kOutput, calls=%fused_computation.8 | convolution fusion | flops 4251967 | bytes 606464 | tf_op jit(solution)/shard_map/rhgl,rhld->rhgd/dot_general | solution.py:44
  38.0 0.6 %copy.23 = bf16[1,2,32,128]{3,1,2,0:T(2,128)(2,1)} copy(bf16[1,2,32,128]{3,2,1,0:T(8,128)(2,1)S(1)} %fusion.5) | data formatting | bytes 32768
  (3 shorter events, 0.0 us)
Async XLA Ops:
  0.0 19.1 %copy-start = (bf16[8,16,8192]{2,1,0:T(8,128)(2,1)S(1)}, bf16[8,16,8192]{2,1,0:T(8,128)(2,1)}, u32[]{:S(2)}) copy-start(bf16[8,16,8192]{2,1,0:T(8,128)(2,1)} %param.10) | copy-start | bytes 6291460
  0.0 21.8 %copy-start.1 = (bf16[8,16,4096]{2,1,0:T(8,128)(2,1)S(1)}, bf16[8,16,4096]{2,1,0:T(8,128)(2,1)}, u32[]{:S(2)}) copy-start(bf16[8,16,4096]{2,1,0:T(8,128)(2,1)} %param.11) | copy-start | bytes 3145732
  1.7 16.3 %all-to-all-start = ((bf16[8,2,8192]{2,1,0:T(2,128)(2,1)}), bf16[8,2,8192]{2,1,0:T(2,128)(2,1)}, u32[]{:S(2)}, u32[]{:S(2)}) async-start(bf16[8,2,8192]{2,1,0:T(2,128)(2,1)} %broadcast_in_dim.11), calls=%async_computation | async-start | bytes 524288 | tf_op jit(solution)/shard_map/all_to_all | solution.py:19
  19.1 7.4 %copy-start.3 = (s32[2]{0:T(128)S(1)}, s32[2]{0:T(128)}, u32[]{:S(2)}) copy-start(s32[2]{0:T(128)} %param.15) | copy-start | bytes 28
  19.1 16.1 %copy-start.2 = (bf16[2,4096]{1,0:T(2,128)(2,1)S(1)}, bf16[2,4096]{1,0:T(2,128)(2,1)}, u32[]{:S(2)}) copy-start(bf16[2,4096]{1,0:T(2,128)(2,1)} %param.9) | copy-start | bytes 49156
  22.9 12.2 %all-to-all-start.1 = ((f32[8,2,4096]{2,1,0:T(2,128)}), f32[8,2,4096]{2,1,0:T(2,128)S(1)}, u32[]{:S(2)}, u32[]{:S(2)}) async-start(f32[8,2,4096]{2,1,0:T(2,128)} %copy.13), calls=%async_computation.1 | async-start | bytes 524288 | tf_op jit(solution)/shard_map/all_to_all | solution.py:32

commit v3 on v2

v3 whole, which is shorter than its diff:
```python
import functools

import jax
import jax.numpy as jnp
from jax import lax
from jax.experimental import pallas as pl
from jax.experimental.pallas import tpu as pltpu
from jax.sharding import PartitionSpec as P

HEADS = 64
KVH = 8
LANES = 128
CHUNK = 1024


def spread_kernel(hidden_ref, copies_ref):
    value = hidden_ref[...]
    for owner in range(copies_ref.shape[0]):
        copies_ref[owner] = value


def owner_kernel(ids_ref, hidden_ref, down_ref, up_ref, delta_ref, row_ref):
    count, rank, width = down_ref.shape
    owners, rows = hidden_ref.shape[:2]
    heads = delta_ref.shape[2]
    first = lax.axis_index("store") * count

    def one_source(source, carry):
        for row in range(rows):
            slot = ids_ref[source * rows + row] - first

            @pl.when((slot >= 0) & (slot < count))
            def _():
                total = jnp.zeros((rank, CHUNK), jnp.float32)
                for start in range(0, width, CHUNK):
                    down = down_ref[slot, :, start : start + CHUNK].astype(jnp.float32)
                    state = hidden_ref[source, :, start : start + CHUNK].astype(jnp.float32)
                    total = total + down * state[row : row + 1]
                low = jnp.sum(total, axis=1, keepdims=True)
                low = low.astype(jnp.bfloat16).astype(jnp.float32)
                for head in range(heads):
                    up = up_ref[slot, :, head * LANES : (head + 1) * LANES].astype(jnp.float32)
                    row_ref[head : head + 1, :] = jnp.sum(up * low, axis=0, keepdims=True)
                delta_ref[source, row] = row_ref[...].astype(delta_ref.dtype)

        return carry

    lax.fori_loop(0, owners, one_source, 0)


def attend_kernel(
    count, ids_ref, lengths_ref, base_ref, delta_ref, key_ref, value_ref, out_ref, rows_ref
):
    rows, kv_heads, slots, head_size = key_ref.shape
    heads = base_ref.shape[1]
    group = heads // kv_heads
    me = lax.axis_index("store")
    scale = 1.0 / (float(head_size) ** 0.5)
    position = lax.broadcasted_iota(jnp.int32, (group, slots), 1)
    for row in range(rows):
        owner = ids_ref[me * rows + row] // count
        query = base_ref[row].astype(jnp.float32) + delta_ref[owner, row].astype(jnp.float32)
        live = position < lengths_ref[row]
        for kv in range(kv_heads):
            mine = query[kv * group : (kv + 1) * group].astype(jnp.bfloat16)
            scores = lax.dot_general(
                mine,
                key_ref[row, kv],
                (((1,), (1,)), ((), ())),
                preferred_element_type=jnp.float32,
            )
            scores = jnp.where(live, scores * scale, jnp.float32(-1e30))
            top = jnp.max(scores, axis=1, keepdims=True)
            grown = jnp.exp(scores - top)
            weights = grown / jnp.sum(grown, axis=1, keepdims=True)
            rows_ref[row, kv * group : (kv + 1) * group, :] = jnp.dot(
                weights.astype(jnp.bfloat16),
                value_ref[row, kv],
                preferred_element_type=jnp.float32,
            )
    for head in range(heads):
        out_ref[:, head * LANES : (head + 1) * LANES] = rows_ref[:, head, :].astype(out_ref.dtype)


def per_device(
    hidden, query_base, adapter_down, adapter_up, adapter_ids, key_cache, value_cache, kv_lengths
):
    owners = lax.axis_size("store")
    count, rank, width = adapter_down.shape
    features = adapter_up.shape[2]
    rows, kv_heads, slots, head_size = key_cache.shape
    heads = features // head_size
    vmem = pl.BlockSpec(memory_space=pltpu.VMEM)
    smem = pl.BlockSpec(memory_space=pltpu.SMEM)
    near = lambda array: pltpu.with_memory_space_constraint(array, pltpu.VMEM)

    copies = pl.pallas_call(
        spread_kernel,
        out_shape=jax.ShapeDtypeStruct((owners, rows, width), hidden.dtype),
        in_specs=[vmem],
        out_specs=vmem,
        name="spread",
    )(hidden)
    everyone = lax.all_to_all(copies, "store", 0, 0, tiled=True)
    parts = pl.pallas_call(
        owner_kernel,
        out_shape=jax.ShapeDtypeStruct((owners, rows, heads, head_size), jnp.bfloat16),
        in_specs=[smem, vmem, vmem, vmem],
        out_specs=vmem,
        scratch_shapes=[pltpu.VMEM((heads, head_size), jnp.float32)],
        compiler_params=pltpu.CompilerParams(vmem_limit_bytes=VMEM_LIMIT),
        name="owner",
    )(adapter_ids, everyone, near(adapter_down), near(adapter_up))
    delta = lax.all_to_all(parts, "store", 0, 0, tiled=True)
    return pl.pallas_call(
        functools.partial(attend_kernel, count),
        out_shape=jax.ShapeDtypeStruct((rows, features), jnp.bfloat16),
        in_specs=[smem, smem, vmem, vmem, vmem, vmem],
        out_specs=vmem,
        scratch_shapes=[pltpu.VMEM((rows, heads, head_size), jnp.float32)],
        compiler_params=pltpu.CompilerParams(vmem_limit_bytes=VMEM_LIMIT),
        name="attend",
    )(
        adapter_ids,
        kv_lengths,
        near(query_base.reshape(rows, heads, head_size)),
        delta,
        near(key_cache),
        near(value_cache),
    )


VMEM_LIMIT = 32 * 1024 * 1024


def solution(mesh):
    in_specs = (
        P(("groups", "store"), None),
        P(("groups", "store"), "tensor"),
        P(("groups", "store"), None, None),
        P(("groups", "store"), None, "tensor"),
        P("groups"),
        P(("groups", "store"), "tensor", None, None),
        P(("groups", "store"), "tensor", None, None),
        P(("groups", "store")),
    )
    out_specs = P(("groups", "store"), "tensor")
    return jax.shard_map(
        per_device, mesh=mesh, in_specs=in_specs, out_specs=out_specs, check_vma=False
    )
```

time: 39.1 us -> 38.7 us (0.990)
  blocking collectives: 0 us -> 16.3 us
  waiting for transfers between devices: 16.8 us -> 7.33 us
  Pallas kernels: 0 us -> 6.88 us
  starting transfers between devices: 10.8 us -> 4.18 us
  matrix products: 5.36 us -> 0 us
  other arithmetic: 1.04 us -> 0 us
  local copies, waits for them, and re-layouts: 4.46 us -> 3.49 us
    all_to_all x0 -> x1, blocking collectives: none -> 16.3 us  [per_device(): everyone = lax.all_to_all(copies, 'store', 0, 0, tiled=True)]
    all_to_all x2 -> x1, waiting for transfers between devices: 16.8 us -> 7.33 us  [per_device(): delta = lax.all_to_all(parts, 'store', 0, 0, tiled=True)]
    pallas_call x0 -> x3, Pallas kernels: none -> 6.88 us  [the longest x1 3.82 us: per_device(): pl.pallas_call(functools.partial(attend_kernel, count), out_shape=jax.Sha...]
    all_to_all x2 -> x1, starting transfers between devices: 10.8 us -> 4.18 us  [per_device(): delta = lax.all_to_all(parts, 'store', 0, 0, tiled=True)]
    dot_general x4 -> x0, matrix products: 5.36 us -> none  [the longest x1 2.54 us: per_device(): jnp.einsum('rd,kd->rk', everyone, down_flat, preferred_element_type=jnp.f...]
    unnamed x9 -> x17, local copies, waits for them, and re-layouts: 0.65 us -> 3.49 us
    broadcast_in_dim x1 -> x0, local copies, waits for them, and re-layouts: 1.74 us -> none  [per_device(): copies = jnp.broadcast_to(hidden[None], (owners,) + hidden.shape)]
    reshape x1 -> x0, local copies, waits for them, and re-layouts: 1.05 us -> none  [per_device(): lax.all_to_all(copies, 'store', 0, 0, tiled=True)]
  transfers between devices with their start and end apart: 2 -> 1, of which waited for: 2 -> 1; matrix products, arithmetic and copies ran while one was open for 2% -> 0% of each run, Pallas kernels for 0% -> 0%
where the time goes in v3:
time: 38.7 us; the launch traced here: 38.2 us
  blocking collectives  16.3 us (42%)
  waiting for transfers between devices  7.33 us (19%)
  Pallas kernels  6.88 us (18%)
  starting transfers between devices  4.18 us (11%)
  local copies, waits for them, and re-layouts  3.49 us (9%)
    all_to_all x1, blocking collectives, per_device(): everyone = lax.all_to_all(copies, 'store', 0, 0, tiled=True)  16.3 us
    all_to_all x1, waiting for transfers between devices, per_device(): delta = lax.all_to_all(parts, 'store', 0, 0, tiled=True)  7.33 us
    all_to_all x1, starting transfers between devices, per_device(): delta = lax.all_to_all(parts, 'store', 0, 0, tiled=True)  4.18 us
    pallas_call x1, Pallas kernels, per_device(): pl.pallas_call(functools.partial(attend_kernel, count), out_shape=jax.Sha...  3.82 us
    unnamed x17, local copies, waits for them, and re-layouts  3.49 us
    pallas_call x1, Pallas kernels, per_device(): pl.pallas_call(owner_kernel, out_shape=jax.ShapeDtypeStruct((owners, rows...  1.59 us
    pallas_call x1, Pallas kernels, per_device(): pl.pallas_call(spread_kernel, out_shape=jax.ShapeDtypeStruct((owners, row...  1.47 us
  transfers between devices with their start and end apart: 1, of which 1 were waited for; matrix products, arithmetic and copies ran while one was open for 0% of the time, Pallas kernels for 0%

profile of v3, /device:TPU:0, one launch (start us, length us, event | category | flops | bytes accessed | tf_op | source)
XLA Modules:
  0.0 38.2 jit_solution(1807919939956867664)
XLA Ops:
  0.0 1.5 %spread.1 = bf16[8,2,8192]{2,1,0:T(2,128)(2,1)} custom-call(bf16[2,8192]{1,0:T(2,128)(2,1)} %hidden_ref.1), custom_call_target="tpu_custom_call" | custom-call | tf_op jit(solution)/shard_map/spread/pallas_call | solution.py:97
  1.5 0.0 copy-start.2
  1.5 16.3 %all_to_all.10.hidden_ref = bf16[8,2,8192]{2,1,0:T(2,128)(2,1)S(1)} all-to-all(bf16[8,2,8192]{2,1,0:T(2,128)(2,1)} %spread.1), channel_id=1, replica_groups=mesh['groups'=2,'store'=8,'tensor'=2] {'store'}, dimensions={0} | all-to-all | bytes 524288 | tf_op jit(solution)/shard_map/all_to_all | solution.py:104
  17.8 0.0 copy-start
  17.8 1.6 %copy-done = bf16[8,16,8192]{2,1,0:T(8,128)(2,1)S(1)} copy-done((bf16[8,16,8192]{2,1,0:T(8,128)(2,1)S(1)}, bf16[8,16,8192]{2,1,0:T(8,128)(2,1)}, u32[]{:S(2)}) %copy-start) | copy-done | bytes 2097176
  19.4 0.0 copy-start.1
  19.4 1.2 %copy-done.1 = bf16[8,16,4096]{2,1,0:T(8,128)(2,1)S(1)} copy-done((bf16[8,16,4096]{2,1,0:T(8,128)(2,1)S(1)}, bf16[8,16,4096]{2,1,0:T(8,128)(2,1)}, u32[]{:S(2)}) %copy-start.1) | copy-done | bytes 1048600
  20.6 0.0 copy-start.4
  20.6 0.7 %copy-done.4 = s32[16]{0:T(128)S(1)} copy-done((s32[16]{0:T(128)S(1)}, s32[16]{0:T(128)}, u32[]{:S(2)}) %copy-start.4) | copy-done | bytes 88
  21.2 0.0 copy-start.7
  21.2 0.0 copy-start.3
  21.3 0.0 copy-start.5
  21.3 0.0 copy-start.6
  21.3 1.6 %owner.1 = bf16[8,2,32,128]{3,2,1,0:T(8,128)(2,1)} custom-call(s32[16]{0:T(128)S(1)} %copy-done.4, bf16[8,2,8192]{2,1,0:T(2,128)(2,1)S(1)} %all_to_all.10.hidden_ref, bf16[8,16,8192]{2,1,0:T(8,128)(2,1)S(1)} %copy-done, bf16[8,16,4096]{2,1,0:T(8,128)(2,1)S(1)} %copy-done.1), custom_call_target="tpu_custom_call" | custom-call | tf_op jit(solution)/shard_map/owner/pallas_call | solution.py:105
  22.8 4.2 %all-to-all-start.1 = ((bf16[8,2,32,128]{3,2,1,0:T(8,128)(2,1)}), bf16[8,2,32,128]{3,2,1,0:T(8,128)(2,1)S(1)}, u32[]{:S(2)}, u32[]{:S(2)}) async-start(bf16[8,2,32,128]{3,2,1,0:T(8,128)(2,1)} %owner.1), calls=%async_computation.1 | async-start | bytes 262144 | tf_op jit(solution)/shard_map/all_to_all | solution.py:114
  27.0 0.0 copy-done.7
  27.0 7.3 %all-to-all-done.1.delta_ref = bf16[8,2,32,128]{3,2,1,0:T(8,128)(2,1)S(1)} async-done(((bf16[8,2,32,128]{3,2,1,0:T(8,128)(2,1)}), bf16[8,2,32,128]{3,2,1,0:T(8,128)(2,1)S(1)}, u32[]{:S(2)}, u32[]{:S(2)}) %all-to-all-start.1) | async-done | bytes 131104 | tf_op jit(solution)/shard_map/all_to_all | solution.py:114
  34.4 0.0 copy-done.2
  34.4 0.0 copy-done.3
  34.4 0.0 copy-done.5
  34.4 0.0 copy-done.6
  34.4 3.8 %attend.1 = bf16[2,4096]{1,0:T(2,128)(2,1)} custom-call(s32[16]{0:T(128)S(1)} %copy-done.5, s32[2]{0:T(128)S(1)} %copy-done.6, bf16[2,32,128]{2,1,0:T(8,128)(2,1)S(1)} %bitcast.4, bf16[8,2,32,128]{3,2,1,0:T(8,128)(2,1)S(1)} %all-to-all-done.1.delta_ref, bf16[2,4,256,128]{3,2,1,0:T(8,128)(2,1)S(1)} %copy-done.2, bf16[2,4,256,128]{3,2,1,0:T(8,128)(2,1)S(1)} %copy-done.3), custom_call_target="tpu_custom_call" | custom-call | tf_op jit(solution)/shard_map/attend/pallas_call | solution.py:115
  (1 shorter events, 0.0 us)
Async XLA Ops:
  1.5 32.9 %copy-start.2 = (bf16[2,4,256,128]{3,2,1,0:T(8,128)(2,1)S(1)}, bf16[2,4,256,128]{3,2,1,0:T(8,128)(2,1)}, u32[]{:S(2)}) copy-start(bf16[2,4,256,128]{3,2,1,0:T(8,128)(2,1)} %key_ref.1) | copy-start | bytes 1572868
  17.8 1.6 %copy-start = (bf16[8,16,8192]{2,1,0:T(8,128)(2,1)S(1)}, bf16[8,16,8192]{2,1,0:T(8,128)(2,1)}, u32[]{:S(2)}) copy-start(bf16[8,16,8192]{2,1,0:T(8,128)(2,1)} %down_ref.1) | copy-start | bytes 6291460
  19.4 1.2 %copy-start.1 = (bf16[8,16,4096]{2,1,0:T(8,128)(2,1)S(1)}, bf16[8,16,4096]{2,1,0:T(8,128)(2,1)}, u32[]{:S(2)}) copy-start(bf16[8,16,4096]{2,1,0:T(8,128)(2,1)} %up_ref.1) | copy-start | bytes 3145732
  20.6 0.7 %copy-start.4 = (s32[16]{0:T(128)S(1)}, s32[16]{0:T(128)}, u32[]{:S(2)}) copy-start(s32[16]{0:T(128)} %ids_ref.3) | copy-start | bytes 196
  21.2 5.8 %copy-start.7 = (bf16[2,4096]{1,0:T(2,128)(2,1)S(1)}, bf16[2,4096]{1,0:T(2,128)(2,1)}, u32[]{:S(2)}) copy-start(bf16[2,4096]{1,0:T(2,128)(2,1)} %param.9) | copy-start | bytes 49156
  21.2 13.1 %copy-start.3 = (bf16[2,4,256,128]{3,2,1,0:T(8,128)(2,1)S(1)}, bf16[2,4,256,128]{3,2,1,0:T(8,128)(2,1)}, u32[]{:S(2)}) copy-start(bf16[2,4,256,128]{3,2,1,0:T(8,128)(2,1)} %value_ref.1) | copy-start | bytes 1572868
  21.3 13.1 %copy-start.5 = (s32[16]{0:T(128)S(1)}, s32[16]{0:T(128)}, u32[]{:S(2)}) copy-start(s32[16]{0:T(128)} %ids_ref.3) | copy-start | bytes 196
  21.3 13.1 %copy-start.6 = (s32[2]{0:T(128)S(1)}, s32[2]{0:T(128)}, u32[]{:S(2)}) copy-start(s32[2]{0:T(128)} %lengths_ref.1) | copy-start | bytes 28
  22.8 11.5 %all-to-all-start.1 = ((bf16[8,2,32,128]{3,2,1,0:T(8,128)(2,1)}), bf16[8,2,32,128]{3,2,1,0:T(8,128)(2,1)S(1)}, u32[]{:S(2)}, u32[]{:S(2)}) async-start(bf16[8,2,32,128]{3,2,1,0:T(8,128)(2,1)} %owner.1), calls=%async_computation.1 | async-start | bytes 262144 | tf_op jit(solution)/shard_map/all_to_all | solution.py:114

commit v4 on v3

v4 whole, which is shorter than its diff:
```python
import functools

import jax
import jax.numpy as jnp
from jax import lax
from jax.experimental import pallas as pl
from jax.experimental.pallas import tpu as pltpu
from jax.sharding import PartitionSpec as P

HEADS = 64
KVH = 8
LANES = 128
CHUNK = 1024
VMEM_LIMIT = 32 * 1024 * 1024
VMEM = pl.BlockSpec(memory_space=pltpu.VMEM)
SMEM = pl.BlockSpec(memory_space=pltpu.SMEM)
PARAMS = pltpu.CompilerParams(vmem_limit_bytes=VMEM_LIMIT)
TURNS = ((1, 2, 3, 0), (4, 5, 6, 7))


def fetch_kernel(*refs):
    *pairs, arrived = refs
    half = len(pairs) // 2
    copies = [
        pltpu.make_async_copy(source, target, arrived.at[i])
        for i, (source, target) in enumerate(zip(pairs[:half], pairs[half:]))
    ]
    for copy in copies:
        copy.start()
    for copy in copies:
        copy.wait()


def fetch(name, *arrays):
    size = sum(array.size * array.dtype.itemsize for array in arrays)
    return pl.pallas_call(
        fetch_kernel,
        out_shape=[pltpu.VMEM(array.shape, array.dtype) for array in arrays],
        in_specs=[pl.BlockSpec(memory_space=pl.ANY)] * len(arrays),
        out_specs=[VMEM] * len(arrays),
        scratch_shapes=[pltpu.SemaphoreType.DMA((len(arrays),))],
        compiler_params=PARAMS,
        cost_estimate=pl.CostEstimate(flops=0, transcendentals=0, bytes_accessed=2 * size),
        name=name,
    )(*[pltpu.with_memory_space_constraint(array, pltpu.HBM) for array in arrays])


def near(array):
    return pltpu.with_memory_space_constraint(array, pltpu.VMEM)


def owner_kernel(ids_ref, *refs):
    turns = len(TURNS[0])
    hidden_refs, refs = refs[:turns], refs[turns:]
    down_ref, mine_ref, other_ref = refs[:3]
    delta_refs, (state_ref, sum_ref, row_ref) = refs[3 : 3 + turns], refs[3 + turns :]
    count, rank, width = down_ref.shape
    rows = state_ref.shape[1]
    heads = row_ref.shape[0]
    me, core = lax.axis_index("store"), lax.axis_index("tensor")
    first = me * count
    for turn, hidden_ref in enumerate(hidden_refs):
        state_ref[turn] = hidden_ref[...]

    def one_turn(turn, carry):
        source = me ^ jnp.where(core == 0, lax.rem(turn + 1, turns), turns + turn)
        for row in range(rows):
            slot = ids_ref[source * rows + row] - first
            owned = (slot >= 0) & (slot < count)

            @pl.when(owned)
            def _():
                total = jnp.zeros((rank, CHUNK), jnp.float32)
                for start in range(0, width, CHUNK):
                    down = down_ref[slot, :, start : start + CHUNK].astype(jnp.float32)
                    state = state_ref[turn, :, start : start + CHUNK].astype(jnp.float32)
                    total = total + down * state[row : row + 1]
                low = jnp.sum(total, axis=1, keepdims=True)
                low = low.astype(jnp.bfloat16).astype(jnp.float32)
                for half, up_ref in ((core, mine_ref), (1 - core, other_ref)):
                    for head in range(heads):
                        up = up_ref[slot, :, head * LANES : (head + 1) * LANES]
                        row_ref[head : head + 1, :] = jnp.sum(
                            up.astype(jnp.float32) * low, axis=0, keepdims=True
                        )
                    sum_ref[turn, row, half] = row_ref[...].astype(sum_ref.dtype)

            @pl.when(jnp.logical_not(owned))
            def _():
                sum_ref[turn, row] = jnp.zeros(sum_ref.shape[2:], sum_ref.dtype)

        return carry

    lax.fori_loop(0, turns, one_turn, 0)
    for turn, delta_ref in enumerate(delta_refs):
        delta_ref[...] = sum_ref[turn]


def merge_kernel(*refs):
    came_refs, (kept_ref, sent_ref) = refs[:-2], refs[-2:]
    core = lax.axis_index("tensor")
    for half, out_ref in ((core, kept_ref), (1 - core, sent_ref)):
        total = came_refs[0][:, half].astype(jnp.float32)
        for came_ref in came_refs[1:]:
            total = total + came_ref[:, half].astype(jnp.float32)
        out_ref[...] = total.astype(out_ref.dtype)


def attend_kernel(parts, live_ref, base_ref, *refs):
    delta_refs, (key_ref, value_ref, out_ref, rows_ref) = refs[:parts], refs[parts:]
    rows, kv_heads, slots, head_size = key_ref.shape
    heads = base_ref.shape[1]
    group = heads // kv_heads
    scale = 1.0 / (float(head_size) ** 0.5)
    scores = []
    for row in range(rows):
        query = base_ref[row].astype(jnp.float32)
        delta = delta_refs[0][row].astype(jnp.float32)
        for ref in delta_refs[1:]:
            delta = delta + ref[row].astype(jnp.float32)
        query = query + delta
        live = live_ref[row] > 0
        for kv in range(kv_heads):
            mine = query[kv * group : (kv + 1) * group].astype(jnp.bfloat16)
            score = lax.dot_general(
                mine,
                key_ref[row, kv],
                (((1,), (1,)), ((), ())),
                preferred_element_type=jnp.float32,
            )
            scores.append(jnp.where(live, score * scale, jnp.float32(-1e30)))
    scores = jnp.concatenate(scores, axis=0)
    grown = jnp.exp(scores - jnp.max(scores, axis=1, keepdims=True))
    weights = grown / jnp.sum(grown, axis=1, keepdims=True)
    for row in range(rows):
        for kv in range(kv_heads):
            at = (row * kv_heads + kv) * group
            rows_ref[row, kv * group : (kv + 1) * group, :] = jnp.dot(
                weights[at : at + group].astype(jnp.bfloat16),
                value_ref[row, kv],
                preferred_element_type=jnp.float32,
            )
    for head in range(heads):
        out_ref[:, head * LANES : (head + 1) * LANES] = rows_ref[:, head, :].astype(out_ref.dtype)


def shared_deltas(hidden, adapter_down, adapter_up, adapter_ids, block):
    rows, heads, head_size = block
    owners, cores, turns = lax.axis_size("store"), len(TURNS), len(TURNS[0])

    def turn_pairs(turn):
        return [
            (i * cores + core, (i ^ TURNS[core][turn]) * cores + core)
            for i in range(owners)
            for core in range(cores)
        ]

    def visit(array, turn):
        return lax.ppermute(array, ("store", "tensor"), turn_pairs(turn))

    def swap(array):
        return lax.ppermute(array, "tensor", [(0, 1), (1, 0)])

    states = [visit(hidden, turn) for turn in range(turns)]
    other = swap(adapter_up)
    ids, down, up = fetch("fetch_adapters", adapter_ids, adapter_down, adapter_up)
    wide = (rows, cores, heads, head_size)
    deltas = pl.pallas_call(
        owner_kernel,
        out_shape=[jax.ShapeDtypeStruct(wide, jnp.bfloat16)] * turns,
        in_specs=[SMEM] + [VMEM] * (turns + 3),
        out_specs=[VMEM] * turns,
        scratch_shapes=[
            pltpu.VMEM((turns,) + hidden.shape, hidden.dtype),
            pltpu.VMEM((turns,) + wide, jnp.bfloat16),
            pltpu.VMEM((heads, head_size), jnp.float32),
        ],
        compiler_params=PARAMS,
        name="owner",
    )(ids, *states, down, up, near(other))
    came = [visit(delta, turn) for turn, delta in enumerate(deltas)]
    kept, sent = pl.pallas_call(
        merge_kernel,
        out_shape=[jax.ShapeDtypeStruct(block, jnp.bfloat16)] * 2,
        in_specs=[VMEM] * turns,
        out_specs=[VMEM] * 2,
        compiler_params=PARAMS,
        name="merge",
    )(*came)
    return [kept, swap(sent)]


def exchanged_deltas(hidden, adapter_down, adapter_up, adapter_ids, block):
    count, rank, width = adapter_down.shape
    owners, rows = lax.axis_size("store"), hidden.shape[0]
    copies = jnp.broadcast_to(hidden[None], (owners,) + hidden.shape)
    everyone = lax.all_to_all(copies, "store", 0, 0, tiled=True).reshape(owners * rows, width)
    slot = adapter_ids - lax.axis_index("store") * count
    owned = slot[:, None] == jnp.arange(count, dtype=jnp.int32)[None, :]
    low = jnp.einsum(
        "rd,kd->rk",
        everyone,
        adapter_down.reshape(count * rank, width),
        preferred_element_type=jnp.float32,
    ).reshape(owners * rows, count, rank)
    low = (low * owned[:, :, None].astype(jnp.float32)).astype(jnp.bfloat16)
    parts = jnp.dot(
        low.reshape(owners * rows, count * rank),
        adapter_up.reshape(count * rank, -1),
        preferred_element_type=jnp.float32,
    )
    came = lax.all_to_all(parts.reshape((owners,) + block), "store", 0, 0, tiled=True)
    return [jnp.sum(came, axis=0)]


def per_device(
    hidden, query_base, adapter_down, adapter_up, adapter_ids, key_cache, value_cache, kv_lengths
):
    features = adapter_up.shape[2]
    rows, kv_heads, slots, head_size = key_cache.shape
    block = (rows, features // head_size, head_size)
    shared = lax.axis_size("tensor") == len(TURNS) and lax.axis_size("store") == sum(
        len(turns) for turns in TURNS
    )
    deltas = (shared_deltas if shared else exchanged_deltas)(
        hidden, adapter_down, adapter_up, adapter_ids, block
    )
    live = jnp.arange(slots, dtype=jnp.int32)[None, None, :] < kv_lengths[:, None, None]
    return pl.pallas_call(
        functools.partial(attend_kernel, len(deltas)),
        out_shape=jax.ShapeDtypeStruct((rows, features), jnp.bfloat16),
        in_specs=[VMEM] * (len(deltas) + 4),
        out_specs=VMEM,
        scratch_shapes=[pltpu.VMEM(block, jnp.float32)],
        compiler_params=PARAMS,
        name="attend",
    )(
        near(live.astype(jnp.float32)),
        near(query_base.reshape(block)),
        *deltas,
        near(key_cache),
        near(value_cache),
    )


def solution(mesh):
    in_specs = (
        P(("groups", "store"), None),
        P(("groups", "store"), "tensor"),
        P(("groups", "store"), None, None),
        P(("groups", "store"), None, "tensor"),
        P("groups"),
        P(("groups", "store"), "tensor", None, None),
        P(("groups", "store"), "tensor", None, None),
        P(("groups", "store")),
    )
    out_specs = P(("groups", "store"), "tensor")
    return jax.shard_map(
        per_device, mesh=mesh, in_specs=in_specs, out_specs=out_specs, check_vma=False
    )
```

time: 38.7 us -> 29.7 us (0.77); the launches traced: 38.2 us -> 29.7 us
  starting transfers between devices: 4.18 us -> 20.8 us
  blocking collectives: 16.3 us -> 0 us
  local copies, waits for them, and re-layouts: 3.49 us -> 0.03 us
  waiting for transfers between devices: 7.33 us -> 4.44 us
  Pallas kernels: 6.88 us -> 4.29 us
    ppermute x0 -> x10, starting transfers between devices: none -> 20.8 us  [the longest x2 11.1 us: swap(): return lax.ppermute(array, 'tensor', [(0, 1), (1, 0)])]
    all_to_all x1 -> x0, blocking collectives: 16.3 us -> none  [per_device(): everyone = lax.all_to_all(copies, 'store', 0, 0, tiled=True)]
    all_to_all x1 -> x0, waiting for transfers between devices: 7.33 us -> none  [per_device(): delta = lax.all_to_all(parts, 'store', 0, 0, tiled=True)]
    ppermute x0 -> x10, waiting for transfers between devices: none -> 4.44 us  [the longest x8 3.68 us: visit(): return lax.ppermute(array, ('store', 'tensor'), turn_pairs(turn))]
    all_to_all x1 -> x0, starting transfers between devices: 4.18 us -> none  [per_device(): delta = lax.all_to_all(parts, 'store', 0, 0, tiled=True)]
    unnamed x17 -> x9, local copies, waits for them, and re-layouts: 3.49 us -> 0.03 us
    pallas_call x3 -> x4, Pallas kernels: 6.88 us -> 4.29 us  [the longest x1 1.9 us: fetch(): pl.pallas_call(fetch_kernel, out_shape=[pltpu.VMEM(array.shape, array.dty...]
  transfers between devices with their start and end apart: 1 -> 10, of which waited for: 1 -> 3; matrix products, arithmetic and copies ran while one was open for 0% -> 0% of each run, Pallas kernels for 0% -> 6%
where the time goes in v4:
time: 29.7 us
  starting transfers between devices  20.8 us (70%)
  waiting for transfers between devices  4.44 us (15%)
  Pallas kernels  4.29 us (14%)
    ppermute x2, starting transfers between devices, swap(): return lax.ppermute(array, 'tensor', [(0, 1), (1, 0)])  11.1 us
    ppermute x8, starting transfers between devices, visit(): return lax.ppermute(array, ('store', 'tensor'), turn_pairs(turn))  9.68 us
    ppermute x8, waiting for transfers between devices, visit(): return lax.ppermute(array, ('store', 'tensor'), turn_pairs(turn))  3.68 us
    pallas_call x1, Pallas kernels, fetch(): pl.pallas_call(fetch_kernel, out_shape=[pltpu.VMEM(array.shape, array.dty...  1.9 us
    pallas_call x1, Pallas kernels, shared_deltas(): pl.pallas_call(owner_kernel, out_shape=[jax.ShapeDtypeStruct(wide, jnp.bf...  1.21 us
    pallas_call x1, Pallas kernels, per_device(): pl.pallas_call(functools.partial(attend_kernel, len(deltas)), out_shape=j...  1.17 us
    ppermute x2, waiting for transfers between devices, swap(): return lax.ppermute(array, 'tensor', [(0, 1), (1, 0)])  0.75 us
  transfers between devices with their start and end apart: 10, of which 3 were waited for; matrix products, arithmetic and copies ran while one was open for 0% of the time, Pallas kernels for 6%

profile of v4, /device:TPU:0, one launch (start us, length us, event | category | flops | bytes accessed | tf_op | source)
XLA Modules:
  0.0 29.7 jit_solution(17675472525104248608)
XLA Ops:
  0.0 0.5 %collective-permute-start.4 = (bf16[8,16,4096]{2,1,0:T(8,128)(2,1)}, bf16[8,16,4096]{2,1,0:T(8,128)(2,1)S(1)}, u32[]{:S(2)}, u32[]{:S(2)}) collective-permute-start(bf16[8,16,4096]{2,1,0:T(8,128)(2,1)} %refs_2_.2), channel_id=1, source_target_pairs={{0,1},{1,0},{2,3},{3,2},{4,5},{5,4},{6,7},{7,6},{8,9},{9,8},{10,11... | collective-permute-start | bytes 3145736 | tf_op jit(solution)/shard_map/ppermute | solution.py:162
  0.5 2.5 %collective-permute-start = (bf16[2,8192]{1,0:T(2,128)(2,1)}, bf16[2,8192]{1,0:T(2,128)(2,1)S(1)}, u32[]{:S(2)}, u32[]{:S(2)}) collective-permute-start(bf16[2,8192]{1,0:T(2,128)(2,1)} %param.8), channel_id=1, source_target_pairs={{0,2},{1,9},{2,0},{3,11},{4,6},{5,13},{6,4},{7,15},{8,10},{9,1},{1... | collective-permute-start | bytes 98312 | tf_op jit(solution)/shard_map/ppermute | solution.py:159
  2.9 1.6 %collective-permute-start.1 = (bf16[2,8192]{1,0:T(2,128)(2,1)}, bf16[2,8192]{1,0:T(2,128)(2,1)S(1)}, u32[]{:S(2)}, u32[]{:S(2)}) collective-permute-start(bf16[2,8192]{1,0:T(2,128)(2,1)} %param.8), channel_id=1, source_target_pairs={{0,4},{1,11},{2,6},{3,9},{4,0},{5,15},{6,2},{7,13},{8,12},{9,3},{1... | collective-permute-start | bytes 98312 | tf_op jit(solution)/shard_map/ppermute | solution.py:159
  4.5 0.0 collective-permute-start.2
  4.5 1.4 %collective-permute-start.3 = (bf16[2,8192]{1,0:T(2,128)(2,1)}, bf16[2,8192]{1,0:T(2,128)(2,1)S(1)}, u32[]{:S(2)}, u32[]{:S(2)}) collective-permute-start(bf16[2,8192]{1,0:T(2,128)(2,1)} %param.8), channel_id=1, source_target_pairs={{0,0},{1,15},{2,2},{3,13},{4,4},{5,11},{6,6},{7,9},{8,8},{9,7},{10... | collective-permute-start | bytes 98312 | tf_op jit(solution)/shard_map/ppermute | solution.py:159
  5.9 1.9 %fetch_adapters.1 = (s32[16]{0:T(128)S(1)}, bf16[8,16,8192]{2,1,0:T(8,128)(2,1)S(1)}, bf16[8,16,4096]{2,1,0:T(8,128)(2,1)S(1)}) custom-call(s32[16]{0:T(128)} %refs_0_.1, bf16[8,16,8192]{2,1,0:T(8,128)(2,1)} %refs_1_.1, bf16[8,16,4096]{2,1,0:T(8,128)(2,1)} %refs_2_.2), custom_call_target="tpu_custom_call" | custom-call | bytes 6291584 | tf_op jit(solution)/shard_map/fetch_adapters/pallas_call | solution.py:36
  7.8 0.0 collective-permute-done.refs_0_
  7.8 0.0 collective-permute-done.1.refs_1_
  7.9 1.7 %collective-permute-done.2.refs_2_ = bf16[2,8192]{1,0:T(2,128)(2,1)S(1)} collective-permute-done((bf16[2,8192]{1,0:T(2,128)(2,1)}, bf16[2,8192]{1,0:T(2,128)(2,1)S(1)}, u32[]{:S(2)}, u32[]{:S(2)}) %collective-permute-start.2) | collective-permute-done | bytes 32800 | tf_op jit(solution)/shard_map/ppermute | solution.py:159
  9.6 0.0 collective-permute-done.3.refs_3_
  9.6 0.0 collective-permute-done.4.refs_6_
  9.6 0.0 copy-start.3
  9.6 0.0 copy-start.2
  9.6 0.0 copy-start
  9.6 0.0 copy-start.1
  9.6 1.2 %owner.1 = (bf16[2,2,32,128]{3,2,1,0:T(8,128)(2,1)S(1)}, bf16[2,2,32,128]{3,2,1,0:T(8,128)(2,1)S(1)}, bf16[2,2,32,128]{3,2,1,0:T(8,128)(2,1)S(1)}, bf16[2,2,32,128]{3,2,1,0:T(8,128)(2,1)S(1)}) custom-call(s32[16]{0:T(128)S(1)} %get-tuple-element.14.ids_ref, bf16[2,8192]{1,0:T(2,128)(2,1)S(1)} %collective-permute-done.refs_0_, ...), custom_call_target="tpu_custom_call" | custom-call | tf_op jit(solution)/shard_map/owner/pallas_call | solution.py:168
  10.8 0.3 %collective-permute-start.5 = (bf16[2,2,32,128]{3,2,1,0:T(8,128)(2,1)S(1)}, bf16[2,2,32,128]{3,2,1,0:T(8,128)(2,1)S(1)}, u32[]{:S(2)}, u32[]{:S(2)}) collective-permute-start(bf16[2,2,32,128]{3,2,1,0:T(8,128)(2,1)S(1)} %get-tuple-element.17), channel_id=1, source_target_pairs={{0,2},{1,9},{2,0},{3,11},{4,6},{5,13},{6,4},{7,15},{8,10},{9,1},{1... | collective-permute-start | bytes 98312 | tf_op jit(solution)/shard_map/ppermute | solution.py:159
  11.2 1.0 %collective-permute-start.6 = (bf16[2,2,32,128]{3,2,1,0:T(8,128)(2,1)S(1)}, bf16[2,2,32,128]{3,2,1,0:T(8,128)(2,1)S(1)}, u32[]{:S(2)}, u32[]{:S(2)}) collective-permute-start(bf16[2,2,32,128]{3,2,1,0:T(8,128)(2,1)S(1)} %get-tuple-element.18), channel_id=1, source_target_pairs={{0,4},{1,11},{2,6},{3,9},{4,0},{5,15},{6,2},{7,13},{8,12},{9,3},{1... | collective-permute-start | bytes 98312 | tf_op jit(solution)/shard_map/ppermute | solution.py:159
  12.2 2.2 %collective-permute-start.7 = (bf16[2,2,32,128]{3,2,1,0:T(8,128)(2,1)S(1)}, bf16[2,2,32,128]{3,2,1,0:T(8,128)(2,1)S(1)}, u32[]{:S(2)}, u32[]{:S(2)}) collective-permute-start(bf16[2,2,32,128]{3,2,1,0:T(8,128)(2,1)S(1)} %get-tuple-element.19), channel_id=1, source_target_pairs={{0,6},{1,13},{2,4},{3,15},{4,2},{5,9},{6,0},{7,11},{8,14},{9,5},{1... | collective-permute-start | bytes 98312 | tf_op jit(solution)/shard_map/ppermute | solution.py:159
  14.4 0.7 %collective-permute-start.8 = (bf16[2,2,32,128]{3,2,1,0:T(8,128)(2,1)S(1)}, bf16[2,2,32,128]{3,2,1,0:T(8,128)(2,1)S(1)}, u32[]{:S(2)}, u32[]{:S(2)}) collective-permute-start(bf16[2,2,32,128]{3,2,1,0:T(8,128)(2,1)S(1)} %get-tuple-element.20), channel_id=1, source_target_pairs={{0,0},{1,15},{2,2},{3,13},{4,4},{5,11},{6,6},{7,9},{8,8},{9,7},{10... | collective-permute-start | bytes 98312 | tf_op jit(solution)/shard_map/ppermute | solution.py:159
  15.0 0.0 collective-permute-done.5.refs_0_
  15.1 0.0 collective-permute-done.6.refs_1_
  15.1 1.9 %collective-permute-done.7.refs_2_ = bf16[2,2,32,128]{3,2,1,0:T(8,128)(2,1)S(1)} collective-permute-done((bf16[2,2,32,128]{3,2,1,0:T(8,128)(2,1)S(1)}, bf16[2,2,32,128]{3,2,1,0:T(8,128)(2,1)S(1)}, u32[]{:S(2)}, u32[]{:S(2)}) %collective-permute-start.7) | collective-permute-done | bytes 32800 | tf_op jit(solution)/shard_map/ppermute | solution.py:159
  17.0 0.0 collective-permute-done.8.refs_3_
  17.0 10.7 %collective-permute-start.9 = (bf16[2,32,128]{2,1,0:T(8,128)(2,1)S(1)}, bf16[2,32,128]{2,1,0:T(8,128)(2,1)S(1)}, u32[]{:S(2)}, u32[]{:S(2)}) collective-permute-start(bf16[2,32,128]{2,1,0:T(8,128)(2,1)S(1)} %get-tuple-element.22), channel_id=1, source_target_pairs={{0,1},{1,0},{2,3},{3,2},{4,5},{5,4},{6,7},{7,6},{8,9},{9,8},{10,11... | collective-permute-start | bytes 49160 | tf_op jit(solution)/shard_map/ppermute | solution.py:162
  27.7 0.0 copy-done.3
  27.7 0.1 compare_convert_fusion.live_ref
  27.8 0.0 copy-done.2
  27.8 0.8 %collective-permute-done.9.refs_1_ = bf16[2,32,128]{2,1,0:T(8,128)(2,1)S(1)} collective-permute-done((bf16[2,32,128]{2,1,0:T(8,128)(2,1)S(1)}, bf16[2,32,128]{2,1,0:T(8,128)(2,1)S(1)}, u32[]{:S(2)}, u32[]{:S(2)}) %collective-permute-start.9) | collective-permute-done | bytes 16416 | tf_op jit(solution)/shard_map/ppermute | solution.py:162
  28.6 0.0 copy-done
  28.6 0.0 copy-done.1
  28.6 1.2 %attend.1 = bf16[2,4096]{1,0:T(2,128)(2,1)} custom-call(f32[2,1,256]{2,1,0:T(1,128)S(1)} %compare_convert_fusion.live_ref, bf16[2,32,128]{2,1,0:T(8,128)(2,1)S(1)} %bitcast.4, bf16[2,32,128]{2,1,0:T(8,128)(2,1)S(1)} %get-tuple-element.21.refs_0_, bf16[2,32,128]{2,1,0:T(8,128)(2,1)S(1)} %collective-permute-done.9.refs_1_, ...), custom_call_target="tpu_custom_call" | custom-call | tf_op jit(solution)/shard_map/attend/pallas_call | solution.py:229
  (2 shorter events, 0.0 us)
Async XLA Ops:
  0.0 9.6 %collective-permute-start.4 = (bf16[8,16,4096]{2,1,0:T(8,128)(2,1)}, bf16[8,16,4096]{2,1,0:T(8,128)(2,1)S(1)}, u32[]{:S(2)}, u32[]{:S(2)}) collective-permute-start(bf16[8,16,4096]{2,1,0:T(8,128)(2,1)} %refs_2_.2), channel_id=1, source_target_pairs={{0,1},{1,0},{2,3},{3,2},{4,5},{5,4},{6,7},{7,6},{8,9},{9,8},{10,11... | collective-permute-start | bytes 3145736 | tf_op jit(solution)/shard_map/ppermute | solution.py:162
  0.5 7.4 %collective-permute-start = (bf16[2,8192]{1,0:T(2,128)(2,1)}, bf16[2,8192]{1,0:T(2,128)(2,1)S(1)}, u32[]{:S(2)}, u32[]{:S(2)}) collective-permute-start(bf16[2,8192]{1,0:T(2,128)(2,1)} %param.8), channel_id=1, source_target_pairs={{0,2},{1,9},{2,0},{3,11},{4,6},{5,13},{6,4},{7,15},{8,10},{9,1},{1... | collective-permute-start | bytes 98312 | tf_op jit(solution)/shard_map/ppermute | solution.py:159
  2.9 4.9 %collective-permute-start.1 = (bf16[2,8192]{1,0:T(2,128)(2,1)}, bf16[2,8192]{1,0:T(2,128)(2,1)S(1)}, u32[]{:S(2)}, u32[]{:S(2)}) collective-permute-start(bf16[2,8192]{1,0:T(2,128)(2,1)} %param.8), channel_id=1, source_target_pairs={{0,4},{1,11},{2,6},{3,9},{4,0},{5,15},{6,2},{7,13},{8,12},{9,3},{1... | collective-permute-start | bytes 98312 | tf_op jit(solution)/shard_map/ppermute | solution.py:159
  4.5 5.1 %collective-permute-start.2 = (bf16[2,8192]{1,0:T(2,128)(2,1)}, bf16[2,8192]{1,0:T(2,128)(2,1)S(1)}, u32[]{:S(2)}, u32[]{:S(2)}) collective-permute-start(bf16[2,8192]{1,0:T(2,128)(2,1)} %param.8), channel_id=1, source_target_pairs={{0,6},{1,13},{2,4},{3,15},{4,2},{5,9},{6,0},{7,11},{8,14},{9,5},{1... | collective-permute-start | bytes 98312 | tf_op jit(solution)/shard_map/ppermute | solution.py:159
  4.5 5.1 %collective-permute-start.3 = (bf16[2,8192]{1,0:T(2,128)(2,1)}, bf16[2,8192]{1,0:T(2,128)(2,1)S(1)}, u32[]{:S(2)}, u32[]{:S(2)}) collective-permute-start(bf16[2,8192]{1,0:T(2,128)(2,1)} %param.8), channel_id=1, source_target_pairs={{0,0},{1,15},{2,2},{3,13},{4,4},{5,11},{6,6},{7,9},{8,8},{9,7},{10... | collective-permute-start | bytes 98312 | tf_op jit(solution)/shard_map/ppermute | solution.py:159
  9.6 18.1 %copy-start.3 = (s32[2]{0:T(128)S(1)}, s32[2]{0:T(128)}, u32[]{:S(2)}) copy-start(s32[2]{0:T(128)} %param.15) | copy-start | bytes 28
  9.6 18.2 %copy-start.2 = (bf16[2,4096]{1,0:T(2,128)(2,1)S(1)}, bf16[2,4096]{1,0:T(2,128)(2,1)}, u32[]{:S(2)}) copy-start(bf16[2,4096]{1,0:T(2,128)(2,1)} %param.9) | copy-start | bytes 49156
  9.6 19.0 %copy-start = (bf16[2,4,256,128]{3,2,1,0:T(8,128)(2,1)S(1)}, bf16[2,4,256,128]{3,2,1,0:T(8,128)(2,1)}, u32[]{:S(2)}) copy-start(bf16[2,4,256,128]{3,2,1,0:T(8,128)(2,1)} %refs_2_.3) | copy-start | bytes 1572868
  9.6 19.0 %copy-start.1 = (bf16[2,4,256,128]{3,2,1,0:T(8,128)(2,1)S(1)}, bf16[2,4,256,128]{3,2,1,0:T(8,128)(2,1)}, u32[]{:S(2)}) copy-start(bf16[2,4,256,128]{3,2,1,0:T(8,128)(2,1)} %refs_3_.1) | copy-start | bytes 1572868
  10.8 4.2 %collective-permute-start.5 = (bf16[2,2,32,128]{3,2,1,0:T(8,128)(2,1)S(1)}, bf16[2,2,32,128]{3,2,1,0:T(8,128)(2,1)S(1)}, u32[]{:S(2)}, u32[]{:S(2)}) collective-permute-start(bf16[2,2,32,128]{3,2,1,0:T(8,128)(2,1)S(1)} %get-tuple-element.17), channel_id=1, source_target_pairs={{0,2},{1,9},{2,0},{3,11},{4,6},{5,13},{6,4},{7,15},{8,10},{9,1},{1... | collective-permute-start | bytes 98312 | tf_op jit(solution)/shard_map/ppermute | solution.py:159
  11.2 3.9 %collective-permute-start.6 = (bf16[2,2,32,128]{3,2,1,0:T(8,128)(2,1)S(1)}, bf16[2,2,32,128]{3,2,1,0:T(8,128)(2,1)S(1)}, u32[]{:S(2)}, u32[]{:S(2)}) collective-permute-start(bf16[2,2,32,128]{3,2,1,0:T(8,128)(2,1)S(1)} %get-tuple-element.18), channel_id=1, source_target_pairs={{0,4},{1,11},{2,6},{3,9},{4,0},{5,15},{6,2},{7,13},{8,12},{9,3},{1... | collective-permute-start | bytes 98312 | tf_op jit(solution)/shard_map/ppermute | solution.py:159
  12.2 4.8 %collective-permute-start.7 = (bf16[2,2,32,128]{3,2,1,0:T(8,128)(2,1)S(1)}, bf16[2,2,32,128]{3,2,1,0:T(8,128)(2,1)S(1)}, u32[]{:S(2)}, u32[]{:S(2)}) collective-permute-start(bf16[2,2,32,128]{3,2,1,0:T(8,128)(2,1)S(1)} %get-tuple-element.19), channel_id=1, source_target_pairs={{0,6},{1,13},{2,4},{3,15},{4,2},{5,9},{6,0},{7,11},{8,14},{9,5},{1... | collective-permute-start | bytes 98312 | tf_op jit(solution)/shard_map/ppermute | solution.py:159
  14.4 2.6 %collective-permute-start.8 = (bf16[2,2,32,128]{3,2,1,0:T(8,128)(2,1)S(1)}, bf16[2,2,32,128]{3,2,1,0:T(8,128)(2,1)S(1)}, u32[]{:S(2)}, u32[]{:S(2)}) collective-permute-start(bf16[2,2,32,128]{3,2,1,0:T(8,128)(2,1)S(1)} %get-tuple-element.20), channel_id=1, source_target_pairs={{0,0},{1,15},{2,2},{3,13},{4,4},{5,11},{6,6},{7,9},{8,8},{9,7},{10... | collective-permute-start | bytes 98312 | tf_op jit(solution)/shard_map/ppermute | solution.py:159
  17.0 11.5 %collective-permute-start.9 = (bf16[2,32,128]{2,1,0:T(8,128)(2,1)S(1)}, bf16[2,32,128]{2,1,0:T(8,128)(2,1)S(1)}, u32[]{:S(2)}, u32[]{:S(2)}) collective-permute-start(bf16[2,32,128]{2,1,0:T(8,128)(2,1)S(1)} %get-tuple-element.22), channel_id=1, source_target_pairs={{0,1},{1,0},{2,3},{3,2},{4,5},{5,4},{6,7},{7,6},{8,9},{9,8},{10,11... | collective-permute-start | bytes 49160 | tf_op jit(solution)/shard_map/ppermute | solution.py:162

commit v5 on v4

--- a/solution.py
+++ b/solution.py
@@ -15,7 +15,7 @@
 VMEM = pl.BlockSpec(memory_space=pltpu.VMEM)
 SMEM = pl.BlockSpec(memory_space=pltpu.SMEM)
 PARAMS = pltpu.CompilerParams(vmem_limit_bytes=VMEM_LIMIT)
-TURNS = ((1, 2, 3, 0), (4, 5, 6, 7))
+TURNS = ((7, 5, 1, 0), (6, 4, 3, 2))
 
 
 def fetch_kernel(*refs):
@@ -49,7 +49,12 @@
     return pltpu.with_memory_space_constraint(array, pltpu.VMEM)
 
 
-def owner_kernel(ids_ref, *refs):
+def partner(core, turn):
+    packed = [sum(value << (4 * i) for i, value in enumerate(turns)) for turns in TURNS]
+    return (jnp.where(core == 0, packed[0], packed[1]) >> (4 * turn)) & 15
+
+
+def owner_kernel(ids_ref, own_ref, *refs):
     turns = len(TURNS[0])
     hidden_refs, refs = refs[:turns], refs[turns:]
     down_ref, mine_ref, other_ref = refs[:3]
@@ -59,11 +64,19 @@
     heads = row_ref.shape[0]
     me, core = lax.axis_index("store"), lax.axis_index("tensor")
     first = me * count
-    for turn, hidden_ref in enumerate(hidden_refs):
+    for turn, hidden_ref in enumerate(hidden_refs[:-1]):
         state_ref[turn] = hidden_ref[...]
 
+    @pl.when(core == 0)
+    def _():
+        state_ref[turns - 1] = own_ref[...]
+
+    @pl.when(core != 0)
+    def _():
+        state_ref[turns - 1] = hidden_refs[-1][...]
+
     def one_turn(turn, carry):
-        source = me ^ jnp.where(core == 0, lax.rem(turn + 1, turns), turns + turn)
+        source = me ^ partner(core, turn)
         for row in range(rows):
             slot = ids_ref[source * rows + row] - first
             owned = (slot >= 0) & (slot < count)
@@ -96,12 +109,13 @@
         delta_ref[...] = sum_ref[turn]
 
 
-def merge_kernel(*refs):
+def merge_kernel(own_ref, *refs):
     came_refs, (kept_ref, sent_ref) = refs[:-2], refs[-2:]
     core = lax.axis_index("tensor")
     for half, out_ref in ((core, kept_ref), (1 - core, sent_ref)):
-        total = came_refs[0][:, half].astype(jnp.float32)
-        for came_ref in came_refs[1:]:
+        total = jnp.where(core == 0, own_ref[:, half], came_refs[-1][:, half])
+        total = total.astype(jnp.float32)
+        for came_ref in came_refs[:-1]:
             total = total + came_ref[:, half].astype(jnp.float32)
         out_ref[...] = total.astype(out_ref.dtype)
 
@@ -153,6 +167,7 @@
             (i * cores + core, (i ^ TURNS[core][turn]) * cores + core)
             for i in range(owners)
             for core in range(cores)
+            if TURNS[core][turn]
         ]
 
     def visit(array, turn):
@@ -163,12 +178,12 @@
 
     states = [visit(hidden, turn) for turn in range(turns)]
     other = swap(adapter_up)
-    ids, down, up = fetch("fetch_adapters", adapter_ids, adapter_down, adapter_up)
+    ids, own, down, up = fetch("fetch", adapter_ids, hidden, adapter_down, adapter_up)
     wide = (rows, cores, heads, head_size)
     deltas = pl.pallas_call(
         owner_kernel,
         out_shape=[jax.ShapeDtypeStruct(wide, jnp.bfloat16)] * turns,
-        in_specs=[SMEM] + [VMEM] * (turns + 3),
+        in_specs=[SMEM] + [VMEM] * (turns + 4),
         out_specs=[VMEM] * turns,
         scratch_shapes=[
             pltpu.VMEM((turns,) + hidden.shape, hidden.dtype),
@@ -177,16 +192,16 @@
         ],
         compiler_params=PARAMS,
         name="owner",
-    )(ids, *states, down, up, near(other))
+    )(ids, own, *states, down, up, near(other))
     came = [visit(delta, turn) for turn, delta in enumerate(deltas)]
     kept, sent = pl.pallas_call(
         merge_kernel,
         out_shape=[jax.ShapeDtypeStruct(block, jnp.bfloat16)] * 2,
-        in_specs=[VMEM] * turns,
+        in_specs=[VMEM] * (turns + 1),
         out_specs=[VMEM] * 2,
         compiler_params=PARAMS,
         name="merge",
-    )(*came)
+    )(deltas[-1], *came)
     return [kept, swap(sent)]
 
 

time: 29.7 us -> 24.7 us (0.83)
  starting transfers between devices: 20.8 us -> 12.1 us
  waiting for transfers between devices: 4.44 us -> 8.09 us
    ppermute x2, starting transfers between devices: 11.1 us -> 1.39 us  [swap(): return lax.ppermute(array, 'tensor', [(0, 1), (1, 0)])]
    ppermute x8, waiting for transfers between devices: 3.68 us -> 7.34 us  [visit(): return lax.ppermute(array, ('store', 'tensor'), turn_pairs(turn))]
    ppermute x8, starting transfers between devices: 9.68 us -> 10.7 us  [visit(): return lax.ppermute(array, ('store', 'tensor'), turn_pairs(turn))]
  transfers between devices with their start and end apart: 10 -> 10, of which waited for: 3 -> 4; matrix products, arithmetic and copies ran while one was open for 0% -> 0% of each run, Pallas kernels for 6% -> 8%
where the time goes in v5:
time: 24.7 us; the launch traced here: 24.5 us
  starting transfers between devices  12.1 us (49%)
  waiting for transfers between devices  8.09 us (33%)
  Pallas kernels  4.07 us (16%)
    ppermute x8, starting transfers between devices, visit(): return lax.ppermute(array, ('store', 'tensor'), turn_pairs(turn))  10.7 us
    ppermute x8, waiting for transfers between devices, visit(): return lax.ppermute(array, ('store', 'tensor'), turn_pairs(turn))  7.34 us
    pallas_call x1, Pallas kernels, fetch(): pl.pallas_call(fetch_kernel, out_shape=[pltpu.VMEM(array.shape, array.dty...  1.93 us
    ppermute x2, starting transfers between devices, swap(): return lax.ppermute(array, 'tensor', [(0, 1), (1, 0)])  1.39 us
    pallas_call x1, Pallas kernels, per_device(): pl.pallas_call(functools.partial(attend_kernel, len(deltas)), out_shape=j...  1.17 us
    pallas_call x1, Pallas kernels, shared_deltas(): pl.pallas_call(owner_kernel, out_shape=[jax.ShapeDtypeStruct(wide, jnp.bf...  0.95 us
    ppermute x2, waiting for transfers between devices, swap(): return lax.ppermute(array, 'tensor', [(0, 1), (1, 0)])  0.75 us
  transfers between devices with their start and end apart: 10, of which 4 were waited for; matrix products, arithmetic and copies ran while one was open for 0% of the time, Pallas kernels for 8%

profile of v5, /device:TPU:0, one launch (start us, length us, event | category | flops | bytes accessed | tf_op | source)
XLA Modules:
  0.0 24.5 jit_solution(17880090383781654052)
XLA Ops:
  0.0 0.5 %collective-permute-start.4 = (bf16[8,16,4096]{2,1,0:T(8,128)(2,1)}, bf16[8,16,4096]{2,1,0:T(8,128)(2,1)S(1)}, u32[]{:S(2)}, u32[]{:S(2)}) collective-permute-start(bf16[8,16,4096]{2,1,0:T(8,128)(2,1)} %refs_3_.2), channel_id=1, source_target_pairs={{0,1},{1,0},{2,3},{3,2},{4,5},{5,4},{6,7},{7,6},{8,9},{9,8},{10,11... | collective-permute-start | bytes 3145736 | tf_op jit(solution)/shard_map/ppermute | solution.py:177
  0.5 5.5 %collective-permute-start = (bf16[2,8192]{1,0:T(2,128)(2,1)}, bf16[2,8192]{1,0:T(2,128)(2,1)S(1)}, u32[]{:S(2)}, u32[]{:S(2)}) collective-permute-start(bf16[2,8192]{1,0:T(2,128)(2,1)} %refs_1_.1), channel_id=1, source_target_pairs={{0,14},{1,13},{2,12},{3,15},{4,10},{5,9},{6,8},{7,11},{8,6},{9,5},... | collective-permute-start | bytes 98312 | tf_op jit(solution)/shard_map/ppermute | solution.py:174
  6.0 0.0 collective-permute-start.1
  6.0 0.9 %collective-permute-start.2 = (bf16[2,8192]{1,0:T(2,128)(2,1)}, bf16[2,8192]{1,0:T(2,128)(2,1)S(1)}, u32[]{:S(2)}, u32[]{:S(2)}) collective-permute-start(bf16[2,8192]{1,0:T(2,128)(2,1)} %refs_1_.1), channel_id=1, source_target_pairs={{0,2},{1,7},{2,0},{3,5},{4,6},{5,3},{6,4},{7,1},{8,10},{9,15},{10,... | collective-permute-start | bytes 98312 | tf_op jit(solution)/shard_map/ppermute | solution.py:174
  6.9 0.7 %collective-permute-start.3 = (bf16[2,8192]{1,0:T(2,128)(2,1)}, bf16[2,8192]{1,0:T(2,128)(2,1)S(1)}, u32[]{:S(2)}, u32[]{:S(2)}) collective-permute-start(bf16[2,8192]{1,0:T(2,128)(2,1)} %refs_1_.1), channel_id=1, source_target_pairs={{1,5},{3,7},{5,1},{7,3},{9,13},{11,15},{13,9},{15,11},{17,21},{19,... | collective-permute-start | bytes 98312 | tf_op jit(solution)/shard_map/ppermute | solution.py:174
  7.5 1.9 %fetch.1 = (s32[16]{0:T(128)S(1)}, bf16[2,8192]{1,0:T(2,128)(2,1)S(1)}, bf16[8,16,8192]{2,1,0:T(8,128)(2,1)S(1)}, bf16[8,16,4096]{2,1,0:T(8,128)(2,1)S(1)}) custom-call(s32[16]{0:T(128)} %refs_0_.1, bf16[2,8192]{1,0:T(2,128)(2,1)} %refs_1_.1, bf16[8,16,8192]{2,1,0:T(8,128)(2,1)} %refs_2_.2, bf16[8,16,4096]{2,1,0:T(8,128)(2,1)} %refs_3_.2), custom_call_target="tpu_custom_call" | custom-call | bytes 6357120 | tf_op jit(solution)/shard_map/fetch/pallas_call | solution.py:36
  9.5 0.0 collective-permute-done.refs_0_
  9.5 2.4 %collective-permute-done.1.refs_1_ = bf16[2,8192]{1,0:T(2,128)(2,1)S(1)} collective-permute-done((bf16[2,8192]{1,0:T(2,128)(2,1)}, bf16[2,8192]{1,0:T(2,128)(2,1)S(1)}, u32[]{:S(2)}, u32[]{:S(2)}) %collective-permute-start.1) | collective-permute-done | bytes 32800 | tf_op jit(solution)/shard_map/ppermute | solution.py:174
  11.9 0.0 collective-permute-done.2.refs_2_
  11.9 0.0 collective-permute-done.3.refs_3_
  11.9 0.0 collective-permute-done.4.refs_6_
  11.9 0.0 copy-start.3
  11.9 0.0 copy-start.2
  11.9 0.0 copy-start
  12.0 0.0 copy-start.1
  12.0 1.0 %owner.1 = (bf16[2,2,32,128]{3,2,1,0:T(8,128)(2,1)S(1)}, bf16[2,2,32,128]{3,2,1,0:T(8,128)(2,1)S(1)}, bf16[2,2,32,128]{3,2,1,0:T(8,128)(2,1)S(1)}, bf16[2,2,32,128]{3,2,1,0:T(8,128)(2,1)S(1)}) custom-call(s32[16]{0:T(128)S(1)} %get-tuple-element.15.ids_ref, bf16[2,8192]{1,0:T(2,128)(2,1)S(1)} %get-tuple-element.16.own_ref, ...), custom_call_target="tpu_custom_call" | custom-call | tf_op jit(solution)/shard_map/owner/pallas_call | solution.py:183
  12.9 0.7 %collective-permute-start.8 = (bf16[2,2,32,128]{3,2,1,0:T(8,128)(2,1)S(1)}, bf16[2,2,32,128]{3,2,1,0:T(8,128)(2,1)S(1)}, u32[]{:S(2)}, u32[]{:S(2)}) collective-permute-start(bf16[2,2,32,128]{3,2,1,0:T(8,128)(2,1)S(1)} %get-tuple-element.19.own_ref), channel_id=1, source_target_pairs={{1,5},{3,7},{5,1},{7,3},{9,13},{11,15},{13,9},{15,11},{17,21},{19,... | collective-permute-start | bytes 98312 | tf_op jit(solution)/shard_map/ppermute | solution.py:174
  13.6 1.4 %collective-permute-start.5 = (bf16[2,2,32,128]{3,2,1,0:T(8,128)(2,1)S(1)}, bf16[2,2,32,128]{3,2,1,0:T(8,128)(2,1)S(1)}, u32[]{:S(2)}, u32[]{:S(2)}) collective-permute-start(bf16[2,2,32,128]{3,2,1,0:T(8,128)(2,1)S(1)} %get-tuple-element.20), channel_id=1, source_target_pairs={{0,14},{1,13},{2,12},{3,15},{4,10},{5,9},{6,8},{7,11},{8,6},{9,5},... | collective-permute-start | bytes 98312 | tf_op jit(solution)/shard_map/ppermute | solution.py:174
  15.0 0.5 %collective-permute-start.6 = (bf16[2,2,32,128]{3,2,1,0:T(8,128)(2,1)S(1)}, bf16[2,2,32,128]{3,2,1,0:T(8,128)(2,1)S(1)}, u32[]{:S(2)}, u32[]{:S(2)}) collective-permute-start(bf16[2,2,32,128]{3,2,1,0:T(8,128)(2,1)S(1)} %get-tuple-element.21), channel_id=1, source_target_pairs={{0,10},{1,9},{2,8},{3,11},{4,14},{5,13},{6,12},{7,15},{8,2},{9,1},... | collective-permute-start | bytes 98312 | tf_op jit(solution)/shard_map/ppermute | solution.py:174
  15.5 1.1 %collective-permute-start.7 = (bf16[2,2,32,128]{3,2,1,0:T(8,128)(2,1)S(1)}, bf16[2,2,32,128]{3,2,1,0:T(8,128)(2,1)S(1)}, u32[]{:S(2)}, u32[]{:S(2)}) collective-permute-start(bf16[2,2,32,128]{3,2,1,0:T(8,128)(2,1)S(1)} %get-tuple-element.22), channel_id=1, source_target_pairs={{0,2},{1,7},{2,0},{3,5},{4,6},{5,3},{6,4},{7,1},{8,10},{9,15},{10,... | collective-permute-start | bytes 98312 | tf_op jit(solution)/shard_map/ppermute | solution.py:174
  16.6 0.0 collective-permute-done.8.refs_3_
  16.6 3.9 %collective-permute-done.5.refs_0_ = bf16[2,2,32,128]{3,2,1,0:T(8,128)(2,1)S(1)} collective-permute-done((bf16[2,2,32,128]{3,2,1,0:T(8,128)(2,1)S(1)}, bf16[2,2,32,128]{3,2,1,0:T(8,128)(2,1)S(1)}, u32[]{:S(2)}, u32[]{:S(2)}) %collective-permute-start.5) | collective-permute-done | bytes 32800 | tf_op jit(solution)/shard_map/ppermute | solution.py:174
  20.5 1.0 %collective-permute-done.6.refs_1_ = bf16[2,2,32,128]{3,2,1,0:T(8,128)(2,1)S(1)} collective-permute-done((bf16[2,2,32,128]{3,2,1,0:T(8,128)(2,1)S(1)}, bf16[2,2,32,128]{3,2,1,0:T(8,128)(2,1)S(1)}, u32[]{:S(2)}, u32[]{:S(2)}) %collective-permute-start.6) | collective-permute-done | bytes 32800 | tf_op jit(solution)/shard_map/ppermute | solution.py:174
  21.5 0.0 collective-permute-done.7.refs_2_
  21.5 0.9 %collective-permute-start.9 = (bf16[2,32,128]{2,1,0:T(8,128)(2,1)S(1)}, bf16[2,32,128]{2,1,0:T(8,128)(2,1)S(1)}, u32[]{:S(2)}, u32[]{:S(2)}) collective-permute-start(bf16[2,32,128]{2,1,0:T(8,128)(2,1)S(1)} %get-tuple-element.24), channel_id=1, source_target_pairs={{0,1},{1,0},{2,3},{3,2},{4,5},{5,4},{6,7},{7,6},{8,9},{9,8},{10,11... | collective-permute-start | bytes 49160 | tf_op jit(solution)/shard_map/ppermute | solution.py:177
  22.4 0.0 copy-done.3
  22.4 0.1 compare_convert_fusion.live_ref
  22.5 0.0 copy-done.2
  22.5 0.8 %collective-permute-done.9.refs_1_ = bf16[2,32,128]{2,1,0:T(8,128)(2,1)S(1)} collective-permute-done((bf16[2,32,128]{2,1,0:T(8,128)(2,1)S(1)}, bf16[2,32,128]{2,1,0:T(8,128)(2,1)S(1)}, u32[]{:S(2)}, u32[]{:S(2)}) %collective-permute-start.9) | collective-permute-done | bytes 16416 | tf_op jit(solution)/shard_map/ppermute | solution.py:177
  23.3 0.0 copy-done
  23.3 0.0 copy-done.1
  23.3 1.2 %attend.1 = bf16[2,4096]{1,0:T(2,128)(2,1)} custom-call(f32[2,1,256]{2,1,0:T(1,128)S(1)} %compare_convert_fusion.live_ref, bf16[2,32,128]{2,1,0:T(8,128)(2,1)S(1)} %bitcast.4, bf16[2,32,128]{2,1,0:T(8,128)(2,1)S(1)} %get-tuple-element.23.refs_0_, bf16[2,32,128]{2,1,0:T(8,128)(2,1)S(1)} %collective-permute-done.9.refs_1_, ...), custom_call_target="tpu_custom_call" | custom-call | tf_op jit(solution)/shard_map/attend/pallas_call | solution.py:244
  (2 shorter events, 0.0 us)
Async XLA Ops:
  0.0 11.9 %collective-permute-start.4 = (bf16[8,16,4096]{2,1,0:T(8,128)(2,1)}, bf16[8,16,4096]{2,1,0:T(8,128)(2,1)S(1)}, u32[]{:S(2)}, u32[]{:S(2)}) collective-permute-start(bf16[8,16,4096]{2,1,0:T(8,128)(2,1)} %refs_3_.2), channel_id=1, source_target_pairs={{0,1},{1,0},{2,3},{3,2},{4,5},{5,4},{6,7},{7,6},{8,9},{9,8},{10,11... | collective-permute-start | bytes 3145736 | tf_op jit(solution)/shard_map/ppermute | solution.py:177
  0.5 9.0 %collective-permute-start = (bf16[2,8192]{1,0:T(2,128)(2,1)}, bf16[2,8192]{1,0:T(2,128)(2,1)S(1)}, u32[]{:S(2)}, u32[]{:S(2)}) collective-permute-start(bf16[2,8192]{1,0:T(2,128)(2,1)} %refs_1_.1), channel_id=1, source_target_pairs={{0,14},{1,13},{2,12},{3,15},{4,10},{5,9},{6,8},{7,11},{8,6},{9,5},... | collective-permute-start | bytes 98312 | tf_op jit(solution)/shard_map/ppermute | solution.py:174
  6.0 5.9 %collective-permute-start.1 = (bf16[2,8192]{1,0:T(2,128)(2,1)}, bf16[2,8192]{1,0:T(2,128)(2,1)S(1)}, u32[]{:S(2)}, u32[]{:S(2)}) collective-permute-start(bf16[2,8192]{1,0:T(2,128)(2,1)} %refs_1_.1), channel_id=1, source_target_pairs={{0,10},{1,9},{2,8},{3,11},{4,14},{5,13},{6,12},{7,15},{8,2},{9,1},... | collective-permute-start | bytes 98312 | tf_op jit(solution)/shard_map/ppermute | solution.py:174
  6.0 5.9 %collective-permute-start.2 = (bf16[2,8192]{1,0:T(2,128)(2,1)}, bf16[2,8192]{1,0:T(2,128)(2,1)S(1)}, u32[]{:S(2)}, u32[]{:S(2)}) collective-permute-start(bf16[2,8192]{1,0:T(2,128)(2,1)} %refs_1_.1), channel_id=1, source_target_pairs={{0,2},{1,7},{2,0},{3,5},{4,6},{5,3},{6,4},{7,1},{8,10},{9,15},{10,... | collective-permute-start | bytes 98312 | tf_op jit(solution)/shard_map/ppermute | solution.py:174
  6.9 5.0 %collective-permute-start.3 = (bf16[2,8192]{1,0:T(2,128)(2,1)}, bf16[2,8192]{1,0:T(2,128)(2,1)S(1)}, u32[]{:S(2)}, u32[]{:S(2)}) collective-permute-start(bf16[2,8192]{1,0:T(2,128)(2,1)} %refs_1_.1), channel_id=1, source_target_pairs={{1,5},{3,7},{5,1},{7,3},{9,13},{11,15},{13,9},{15,11},{17,21},{19,... | collective-permute-start | bytes 98312 | tf_op jit(solution)/shard_map/ppermute | solution.py:174
  11.9 10.5 %copy-start.3 = (s32[2]{0:T(128)S(1)}, s32[2]{0:T(128)}, u32[]{:S(2)}) copy-start(s32[2]{0:T(128)} %param.15) | copy-start | bytes 28
  11.9 10.6 %copy-start.2 = (bf16[2,4096]{1,0:T(2,128)(2,1)S(1)}, bf16[2,4096]{1,0:T(2,128)(2,1)}, u32[]{:S(2)}) copy-start(bf16[2,4096]{1,0:T(2,128)(2,1)} %param.9) | copy-start | bytes 49156
  11.9 11.3 %copy-start = (bf16[2,4,256,128]{3,2,1,0:T(8,128)(2,1)S(1)}, bf16[2,4,256,128]{3,2,1,0:T(8,128)(2,1)}, u32[]{:S(2)}) copy-start(bf16[2,4,256,128]{3,2,1,0:T(8,128)(2,1)} %refs_2_.3) | copy-start | bytes 1572868
  12.0 11.3 %copy-start.1 = (bf16[2,4,256,128]{3,2,1,0:T(8,128)(2,1)S(1)}, bf16[2,4,256,128]{3,2,1,0:T(8,128)(2,1)}, u32[]{:S(2)}) copy-start(bf16[2,4,256,128]{3,2,1,0:T(8,128)(2,1)} %refs_3_.3) | copy-start | bytes 1572868
  12.9 3.6 %collective-permute-start.8 = (bf16[2,2,32,128]{3,2,1,0:T(8,128)(2,1)S(1)}, bf16[2,2,32,128]{3,2,1,0:T(8,128)(2,1)S(1)}, u32[]{:S(2)}, u32[]{:S(2)}) collective-permute-start(bf16[2,2,32,128]{3,2,1,0:T(8,128)(2,1)S(1)} %get-tuple-element.19.own_ref), channel_id=1, source_target_pairs={{1,5},{3,7},{5,1},{7,3},{9,13},{11,15},{13,9},{15,11},{17,21},{19,... | collective-permute-start | bytes 98312 | tf_op jit(solution)/shard_map/ppermute | solution.py:174
  13.6 6.9 %collective-permute-start.5 = (bf16[2,2,32,128]{3,2,1,0:T(8,128)(2,1)S(1)}, bf16[2,2,32,128]{3,2,1,0:T(8,128)(2,1)S(1)}, u32[]{:S(2)}, u32[]{:S(2)}) collective-permute-start(bf16[2,2,32,128]{3,2,1,0:T(8,128)(2,1)S(1)} %get-tuple-element.20), channel_id=1, source_target_pairs={{0,14},{1,13},{2,12},{3,15},{4,10},{5,9},{6,8},{7,11},{8,6},{9,5},... | collective-permute-start | bytes 98312 | tf_op jit(solution)/shard_map/ppermute | solution.py:174
  15.0 6.5 %collective-permute-start.6 = (bf16[2,2,32,128]{3,2,1,0:T(8,128)(2,1)S(1)}, bf16[2,2,32,128]{3,2,1,0:T(8,128)(2,1)S(1)}, u32[]{:S(2)}, u32[]{:S(2)}) collective-permute-start(bf16[2,2,32,128]{3,2,1,0:T(8,128)(2,1)S(1)} %get-tuple-element.21), channel_id=1, source_target_pairs={{0,10},{1,9},{2,8},{3,11},{4,14},{5,13},{6,12},{7,15},{8,2},{9,1},... | collective-permute-start | bytes 98312 | tf_op jit(solution)/shard_map/ppermute | solution.py:174
  15.5 6.0 %collective-permute-start.7 = (bf16[2,2,32,128]{3,2,1,0:T(8,128)(2,1)S(1)}, bf16[2,2,32,128]{3,2,1,0:T(8,128)(2,1)S(1)}, u32[]{:S(2)}, u32[]{:S(2)}) collective-permute-start(bf16[2,2,32,128]{3,2,1,0:T(8,128)(2,1)S(1)} %get-tuple-element.22), channel_id=1, source_target_pairs={{0,2},{1,7},{2,0},{3,5},{4,6},{5,3},{6,4},{7,1},{8,10},{9,15},{10,... | collective-permute-start | bytes 98312 | tf_op jit(solution)/shard_map/ppermute | solution.py:174
  21.5 1.8 %collective-permute-start.9 = (bf16[2,32,128]{2,1,0:T(8,128)(2,1)S(1)}, bf16[2,32,128]{2,1,0:T(8,128)(2,1)S(1)}, u32[]{:S(2)}, u32[]{:S(2)}) collective-permute-start(bf16[2,32,128]{2,1,0:T(8,128)(2,1)S(1)} %get-tuple-element.24), channel_id=1, source_target_pairs={{0,1},{1,0},{2,3},{3,2},{4,5},{5,4},{6,7},{7,6},{8,9},{9,8},{10,11... | collective-permute-start | bytes 49160 | tf_op jit(solution)/shard_map/ppermute | solution.py:177

commit v6 on v4

--- a/solution.py
+++ b/solution.py
@@ -15,7 +15,9 @@
 VMEM = pl.BlockSpec(memory_space=pltpu.VMEM)
 SMEM = pl.BlockSpec(memory_space=pltpu.SMEM)
 PARAMS = pltpu.CompilerParams(vmem_limit_bytes=VMEM_LIMIT)
-TURNS = ((1, 2, 3, 0), (4, 5, 6, 7))
+COLUMN = ((3, 0), (2, 1))
+SIDES = 2
+SLOTS = len(COLUMN[0])
 
 
 def fetch_kernel(*refs):
@@ -49,21 +51,37 @@
     return pltpu.with_memory_space_constraint(array, pltpu.VMEM)
 
 
-def owner_kernel(ids_ref, *refs):
-    turns = len(TURNS[0])
-    hidden_refs, refs = refs[:turns], refs[turns:]
-    down_ref, mine_ref, other_ref = refs[:3]
-    delta_refs, (state_ref, sum_ref, row_ref) = refs[3 : 3 + turns], refs[3 + turns :]
+def stack_kernel(own_ref, *refs):
+    *came_refs, out_ref = refs
+    core = lax.axis_index("tensor")
+    for slot, came_ref in enumerate(came_refs):
+        for value in range(len(COLUMN)):
+            ref = came_ref if COLUMN[value][slot] else own_ref
+
+            @pl.when(core == value)
+            def _():
+                out_ref[slot] = ref[...]
+
+
+def home(side, slot):
+    packed = [sum(value << (4 * i) for i, value in enumerate(steps)) for steps in COLUMN]
+    packed = jnp.where(lax.axis_index("tensor") == 0, packed[0], packed[1])
+    return lax.axis_index("store") ^ (((packed >> (4 * slot)) & 15) * SIDES + side)
+
+
+def owner_kernel(ids_ref, near_ref, far_ref, down_ref, mine_ref, other_ref, *refs):
+    delta_refs, (state_ref, sum_ref, row_ref) = refs[:SIDES], refs[SIDES:]
     count, rank, width = down_ref.shape
     rows = state_ref.shape[1]
     heads = row_ref.shape[0]
-    me, core = lax.axis_index("store"), lax.axis_index("tensor")
-    first = me * count
-    for turn, hidden_ref in enumerate(hidden_refs):
-        state_ref[turn] = hidden_ref[...]
-
-    def one_turn(turn, carry):
-        source = me ^ jnp.where(core == 0, lax.rem(turn + 1, turns), turns + turn)
+    core = lax.axis_index("tensor")
+    first = lax.axis_index("store") * count
+    for side, hidden_ref in enumerate((near_ref, far_ref)):
+        for slot in range(SLOTS):
+            state_ref[side * SLOTS + slot] = hidden_ref[slot]
+
+    def one_home(turn, carry):
+        source = home(turn // SLOTS, turn % SLOTS)
         for row in range(rows):
             slot = ids_ref[source * rows + row] - first
             owned = (slot >= 0) & (slot < count)
@@ -91,18 +109,29 @@
 
         return carry
 
-    lax.fori_loop(0, turns, one_turn, 0)
-    for turn, delta_ref in enumerate(delta_refs):
-        delta_ref[...] = sum_ref[turn]
+    lax.fori_loop(0, SIDES * SLOTS, one_home, 0)
+    for side, delta_ref in enumerate(delta_refs):
+        for slot in range(SLOTS):
+            delta_ref[slot] = sum_ref[side * SLOTS + slot]
+
+
+def side_kernel(near_ref, came_ref, *out_refs):
+    for slot, out_ref in enumerate(out_refs):
+        total = near_ref[slot].astype(jnp.float32) + came_ref[slot].astype(jnp.float32)
+        out_ref[...] = total.astype(out_ref.dtype)
 
 
 def merge_kernel(*refs):
-    came_refs, (kept_ref, sent_ref) = refs[:-2], refs[-2:]
+    own_refs, came_refs, (kept_ref, sent_ref) = refs[:SLOTS], refs[SLOTS:-2], refs[-2:]
     core = lax.axis_index("tensor")
     for half, out_ref in ((core, kept_ref), (1 - core, sent_ref)):
-        total = came_refs[0][:, half].astype(jnp.float32)
-        for came_ref in came_refs[1:]:
-            total = total + came_ref[:, half].astype(jnp.float32)
+        total = jnp.zeros(out_ref.shape, jnp.float32)
+        for slot in range(SLOTS):
+            part = came_refs[slot][:, half]
+            for value in range(len(COLUMN)):
+                if not COLUMN[value][slot]:
+                    part = jnp.where(core == value, own_refs[slot][:, half], part)
+            total = total + part.astype(jnp.float32)
         out_ref[...] = total.astype(out_ref.dtype)
 
 
@@ -146,47 +175,59 @@
 
 def shared_deltas(hidden, adapter_down, adapter_up, adapter_ids, block):
     rows, heads, head_size = block
-    owners, cores, turns = lax.axis_size("store"), len(TURNS), len(TURNS[0])
-
-    def turn_pairs(turn):
-        return [
-            (i * cores + core, (i ^ TURNS[core][turn]) * cores + core)
+    owners, cores = lax.axis_size("store"), len(COLUMN)
+
+    def along(array, slot):
+        pairs = [
+            (i * cores + core, (i ^ (COLUMN[core][slot] * SIDES)) * cores + core)
             for i in range(owners)
             for core in range(cores)
+            if COLUMN[core][slot]
         ]
-
-    def visit(array, turn):
-        return lax.ppermute(array, ("store", "tensor"), turn_pairs(turn))
+        return lax.ppermute(array, ("store", "tensor"), pairs)
+
+    def across(array):
+        return lax.ppermute(array, "store", [(i, i ^ 1) for i in range(owners)])
 
     def swap(array):
         return lax.ppermute(array, "tensor", [(0, 1), (1, 0)])
 
-    states = [visit(hidden, turn) for turn in range(turns)]
+    def call(kernel, shapes, name, *operands, **options):
+        return pl.pallas_call(
+            kernel,
+            out_shape=[jax.ShapeDtypeStruct(shape, jnp.bfloat16) for shape in shapes],
+            out_specs=[VMEM] * len(shapes),
+            compiler_params=PARAMS,
+            name=name,
+            **{"in_specs": [VMEM] * len(operands), **options},
+        )(*operands)
+
+    wide = (rows, cores, heads, head_size)
+    came = [along(hidden, slot) for slot in range(SLOTS)]
     other = swap(adapter_up)
+    (own,) = fetch("fetch_hidden", hidden)
+    (near_side,) = call(stack_kernel, [(SLOTS,) + hidden.shape], "stack", own, *came)
     ids, down, up = fetch("fetch_adapters", adapter_ids, adapter_down, adapter_up)
-    wide = (rows, cores, heads, head_size)
-    deltas = pl.pallas_call(
+    near_deltas, far_deltas = call(
         owner_kernel,
-        out_shape=[jax.ShapeDtypeStruct(wide, jnp.bfloat16)] * turns,
-        in_specs=[SMEM] + [VMEM] * (turns + 3),
-        out_specs=[VMEM] * turns,
+        [(SLOTS,) + wide] * SIDES,
+        "owner",
+        ids,
+        near_side,
+        across(near_side),
+        down,
+        up,
+        near(other),
+        in_specs=[SMEM] + [VMEM] * 5,
         scratch_shapes=[
-            pltpu.VMEM((turns,) + hidden.shape, hidden.dtype),
-            pltpu.VMEM((turns,) + wide, jnp.bfloat16),
+            pltpu.VMEM((SIDES * SLOTS,) + hidden.shape, hidden.dtype),
+            pltpu.VMEM((SIDES * SLOTS,) + wide, jnp.bfloat16),
             pltpu.VMEM((heads, head_size), jnp.float32),
         ],
-        compiler_params=PARAMS,
-        name="owner",
-    )(ids, *states, down, up, near(other))
-    came = [visit(delta, turn) for turn, delta in enumerate(deltas)]
-    kept, sent = pl.pallas_call(
-        merge_kernel,
-        out_shape=[jax.ShapeDtypeStruct(block, jnp.bfloat16)] * 2,
-        in_specs=[VMEM] * turns,
-        out_specs=[VMEM] * 2,
-        compiler_params=PARAMS,
-        name="merge",
-    )(*came)
+    )
+    sums = call(side_kernel, [wide] * SLOTS, "side", near_deltas, across(far_deltas))
+    came = [along(part, slot) for slot, part in enumerate(sums)]
+    kept, sent = call(merge_kernel, [block] * 2, "merge", *sums, *came)
     return [kept, swap(sent)]
 
 
@@ -219,9 +260,7 @@
     features = adapter_up.shape[2]
     rows, kv_heads, slots, head_size = key_cache.shape
     block = (rows, features // head_size, head_size)
-    shared = lax.axis_size("tensor") == len(TURNS) and lax.axis_size("store") == sum(
-        len(turns) for turns in TURNS
-    )
+    shared = (lax.axis_size("store"), lax.axis_size("tensor")) == (8, len(COLUMN))
     deltas = (shared_deltas if shared else exchanged_deltas)(
         hidden, adapter_down, adapter_up, adapter_ids, block
     )

time: 29.7 us -> 25.9 us (0.87); the launches traced: 29.7 us -> 25.6 us
  starting transfers between devices: 20.8 us -> 13.4 us
  waiting for transfers between devices: 4.44 us -> 7.15 us
  Pallas kernels: 4.29 us -> 4.84 us
    ppermute x2, starting transfers between devices: 11.1 us -> 0.52 us  [swap(): return lax.ppermute(array, 'tensor', [(0, 1), (1, 0)])]
    ppermute x8 -> x6, starting transfers between devices: 9.68 us -> 12.9 us  [the longest x4 9.8 us: along(): return lax.ppermute(array, ('store', 'tensor'), pairs)]
    ppermute x8 -> x6, waiting for transfers between devices: 3.68 us -> 6.07 us  [the longest x2 3.94 us: across(): return lax.ppermute(array, 'store', [(i, i ^ 1) for i in range(owners)])]
    pallas_call x1 -> x2, Pallas kernels: 1.9 us -> 2.66 us  [fetch(): pl.pallas_call(fetch_kernel, out_shape=[pltpu.VMEM(array.shape, array.dty...]
    ppermute x2, waiting for transfers between devices: 0.75 us -> 1.08 us  [swap(): return lax.ppermute(array, 'tensor', [(0, 1), (1, 0)])]
    pallas_call x2 -> x4, Pallas kernels: 1.23 us -> 1.01 us  [call(): pl.pallas_call(kernel, out_shape=[jax.ShapeDtypeStruct(shape, jnp.bfloat1...]
  transfers between devices with their start and end apart: 10 -> 8, of which waited for: 3 -> 5; matrix products, arithmetic and copies ran while one was open for 0% -> 0% of each run, Pallas kernels for 6% -> 10%
where the time goes in v6:
time: 25.9 us; the launch traced here: 25.6 us
  starting transfers between devices  13.4 us (52%)
  waiting for transfers between devices  7.15 us (28%)
  Pallas kernels  4.84 us (19%)
    ppermute x4, starting transfers between devices, along(): return lax.ppermute(array, ('store', 'tensor'), pairs)  9.8 us
    ppermute x2, waiting for transfers between devices, across(): return lax.ppermute(array, 'store', [(i, i ^ 1) for i in range(owners)])  3.94 us
    ppermute x2, starting transfers between devices, across(): return lax.ppermute(array, 'store', [(i, i ^ 1) for i in range(owners)])  3.11 us
    pallas_call x2, Pallas kernels, fetch(): pl.pallas_call(fetch_kernel, out_shape=[pltpu.VMEM(array.shape, array.dty...  2.66 us
    ppermute x4, waiting for transfers between devices, along(): return lax.ppermute(array, ('store', 'tensor'), pairs)  2.13 us
    pallas_call x1, Pallas kernels, per_device(): pl.pallas_call(functools.partial(attend_kernel, len(deltas)), out_shape=j...  1.17 us
    ppermute x2, waiting for transfers between devices, swap(): return lax.ppermute(array, 'tensor', [(0, 1), (1, 0)])  1.08 us
    pallas_call x4, Pallas kernels, call(): pl.pallas_call(kernel, out_shape=[jax.ShapeDtypeStruct(shape, jnp.bfloat1...  1.01 us
  transfers between devices with their start and end apart: 8, of which 5 were waited for; matrix products, arithmetic and copies ran while one was open for 0% of the time, Pallas kernels for 10%

profile of v6, /device:TPU:0, one launch (start us, length us, event | category | flops | bytes accessed | tf_op | source)
XLA Modules:
  0.0 25.6 jit_solution(18440965820374697418)
XLA Ops:
  0.0 0.5 %collective-permute-start.3 = (bf16[8,16,4096]{2,1,0:T(8,128)(2,1)}, bf16[8,16,4096]{2,1,0:T(8,128)(2,1)S(1)}, u32[]{:S(2)}, u32[]{:S(2)}) collective-permute-start(bf16[8,16,4096]{2,1,0:T(8,128)(2,1)} %refs_2_.2), channel_id=1, source_target_pairs={{0,1},{1,0},{2,3},{3,2},{4,5},{5,4},{6,7},{7,6},{8,9},{9,8},{10,11... | collective-permute-start | bytes 3145736 | tf_op jit(solution)/shard_map/ppermute | solution.py:193
  0.5 4.6 %collective-permute-start = (bf16[2,8192]{1,0:T(2,128)(2,1)}, bf16[2,8192]{1,0:T(2,128)(2,1)S(1)}, u32[]{:S(2)}, u32[]{:S(2)}) collective-permute-start(bf16[2,8192]{1,0:T(2,128)(2,1)} %refs_0_.3), channel_id=1, source_target_pairs={{0,12},{1,9},{2,14},{3,11},{4,8},{5,13},{6,10},{7,15},{8,4},{9,1},... | collective-permute-start | bytes 98312 | tf_op jit(solution)/shard_map/ppermute | solution.py:187
  5.1 0.7 %collective-permute-start.1 = (bf16[2,8192]{1,0:T(2,128)(2,1)}, bf16[2,8192]{1,0:T(2,128)(2,1)S(1)}, u32[]{:S(2)}, u32[]{:S(2)}) collective-permute-start(bf16[2,8192]{1,0:T(2,128)(2,1)} %refs_0_.3), channel_id=1, source_target_pairs={{1,5},{3,7},{5,1},{7,3},{9,13},{11,15},{13,9},{15,11},{17,21},{19,... | collective-permute-start | bytes 98312 | tf_op jit(solution)/shard_map/ppermute | solution.py:187
  5.7 0.8 %fetch_hidden.1.own_ref = bf16[2,8192]{1,0:T(2,128)(2,1)S(1)} custom-call(bf16[2,8192]{1,0:T(2,128)(2,1)} %refs_0_.3), custom_call_target="tpu_custom_call" | custom-call | bytes 65536 | tf_op jit(solution)/shard_map/fetch_hidden/pallas_call | solution.py:38
  6.5 0.9 %collective-permute-done.refs_0_ = bf16[2,8192]{1,0:T(2,128)(2,1)S(1)} collective-permute-done((bf16[2,8192]{1,0:T(2,128)(2,1)}, bf16[2,8192]{1,0:T(2,128)(2,1)S(1)}, u32[]{:S(2)}, u32[]{:S(2)}) %collective-permute-start) | collective-permute-done | bytes 32800 | tf_op jit(solution)/shard_map/ppermute | solution.py:187
  7.4 0.0 collective-permute-done.1.refs_1_
  7.4 1.6 %collective-permute-start.2 = (bf16[2,2,8192]{2,1,0:T(2,128)(2,1)S(1)}, bf16[2,2,8192]{2,1,0:T(2,128)(2,1)S(1)}, u32[]{:S(2)}, u32[]{:S(2)}) collective-permute-start(bf16[2,2,8192]{2,1,0:T(2,128)(2,1)S(1)} %stack.1.near_ref), channel_id=1, source_target_pairs={{0,2},{2,0},{4,6},{6,4},{8,10},{10,8},{12,14},{14,12},{1,3},{3,1},... | collective-permute-start | bytes 196616 | tf_op jit(solution)/shard_map/ppermute | solution.py:190
  9.0 1.9 %fetch_adapters.1 = (s32[16]{0:T(128)S(1)}, bf16[8,16,8192]{2,1,0:T(8,128)(2,1)S(1)}, bf16[8,16,4096]{2,1,0:T(8,128)(2,1)S(1)}) custom-call(s32[16]{0:T(128)} %refs_0_.2, bf16[8,16,8192]{2,1,0:T(8,128)(2,1)} %refs_1_.1, bf16[8,16,4096]{2,1,0:T(8,128)(2,1)} %refs_2_.2), custom_call_target="tpu_custom_call" | custom-call | bytes 6291584 | tf_op jit(solution)/shard_map/fetch_adapters/pallas_call | solution.py:38
  10.9 0.9 %collective-permute-done.2.far_ref = bf16[2,2,8192]{2,1,0:T(2,128)(2,1)S(1)} collective-permute-done((bf16[2,2,8192]{2,1,0:T(2,128)(2,1)S(1)}, bf16[2,2,8192]{2,1,0:T(2,128)(2,1)S(1)}, u32[]{:S(2)}, u32[]{:S(2)}) %collective-permute-start.2) | collective-permute-done | bytes 65568 | tf_op jit(solution)/shard_map/ppermute | solution.py:190
  11.7 0.0 collective-permute-done.3.other_ref
  11.7 0.0 copy-start.3
  11.7 0.0 copy-start.2
  11.7 0.0 copy-start
  11.7 0.0 copy-start.1
  11.8 1.0 %owner.1 = (bf16[2,2,2,32,128]{4,3,2,1,0:T(8,128)(2,1)S(1)}, bf16[2,2,2,32,128]{4,3,2,1,0:T(8,128)(2,1)S(1)}) custom-call(s32[16]{0:T(128)S(1)} %get-tuple-element.14.ids_ref, bf16[2,2,8192]{2,1,0:T(2,128)(2,1)S(1)} %stack.1.near_ref, bf16[2,2,8192]{2,1,0:T(2,128)(2,1)S(1)} %collective-permute-done.2.far_ref, ...), custom_call_target="tpu_custom_call" | custom-call | tf_op jit(solution)/shard_map/owner/pallas_call | solution.py:196
  12.7 1.6 %collective-permute-start.4 = (bf16[2,2,2,32,128]{4,3,2,1,0:T(8,128)(2,1)S(1)}, bf16[2,2,2,32,128]{4,3,2,1,0:T(8,128)(2,1)S(1)}, u32[]{:S(2)}, u32[]{:S(2)}) collective-permute-start(bf16[2,2,2,32,128]{4,3,2,1,0:T(8,128)(2,1)S(1)} %get-tuple-element.18), channel_id=1, source_target_pairs={{0,2},{2,0},{4,6},{6,4},{8,10},{10,8},{12,14},{14,12},{1,3},{3,1},... | collective-permute-start | bytes 196616 | tf_op jit(solution)/shard_map/ppermute | solution.py:190
  14.3 3.1 %collective-permute-done.4.came_ref = bf16[2,2,2,32,128]{4,3,2,1,0:T(8,128)(2,1)S(1)} collective-permute-done((bf16[2,2,2,32,128]{4,3,2,1,0:T(8,128)(2,1)S(1)}, bf16[2,2,2,32,128]{4,3,2,1,0:T(8,128)(2,1)S(1)}, u32[]{:S(2)}, u32[]{:S(2)}) %collective-permute-start.4) | collective-permute-done | bytes 65568 | tf_op jit(solution)/shard_map/ppermute | solution.py:190
  17.4 3.9 %collective-permute-start.5 = (bf16[2,2,32,128]{3,2,1,0:T(8,128)(2,1)S(1)}, bf16[2,2,32,128]{3,2,1,0:T(8,128)(2,1)S(1)}, u32[]{:S(2)}, u32[]{:S(2)}) collective-permute-start(bf16[2,2,32,128]{3,2,1,0:T(8,128)(2,1)S(1)} %get-tuple-element.19.refs_0_), channel_id=1, source_target_pairs={{0,12},{1,9},{2,14},{3,11},{4,8},{5,13},{6,10},{7,15},{8,4},{9,1},... | collective-permute-start | bytes 98312 | tf_op jit(solution)/shard_map/ppermute | solution.py:187
  21.3 0.7 %collective-permute-start.6 = (bf16[2,2,32,128]{3,2,1,0:T(8,128)(2,1)S(1)}, bf16[2,2,32,128]{3,2,1,0:T(8,128)(2,1)S(1)}, u32[]{:S(2)}, u32[]{:S(2)}) collective-permute-start(bf16[2,2,32,128]{3,2,1,0:T(8,128)(2,1)S(1)} %get-tuple-element.20.refs_1_), channel_id=1, source_target_pairs={{1,5},{3,7},{5,1},{7,3},{9,13},{11,15},{13,9},{15,11},{17,21},{19,... | collective-permute-start | bytes 98312 | tf_op jit(solution)/shard_map/ppermute | solution.py:187
  21.9 1.2 %collective-permute-done.5.refs_2_ = bf16[2,2,32,128]{3,2,1,0:T(8,128)(2,1)S(1)} collective-permute-done((bf16[2,2,32,128]{3,2,1,0:T(8,128)(2,1)S(1)}, bf16[2,2,32,128]{3,2,1,0:T(8,128)(2,1)S(1)}, u32[]{:S(2)}, u32[]{:S(2)}) %collective-permute-start.5) | collective-permute-done | bytes 32800 | tf_op jit(solution)/shard_map/ppermute | solution.py:187
  23.2 0.0 collective-permute-done.6.refs_3_
  23.2 0.1 collective-permute-start.7
  23.3 0.0 copy-done.3
  23.3 0.1 compare_convert_fusion.live_ref
  23.4 0.0 copy-done.2
  23.4 1.1 %collective-permute-done.7.refs_1_ = bf16[2,32,128]{2,1,0:T(8,128)(2,1)S(1)} collective-permute-done((bf16[2,32,128]{2,1,0:T(8,128)(2,1)S(1)}, bf16[2,32,128]{2,1,0:T(8,128)(2,1)S(1)}, u32[]{:S(2)}, u32[]{:S(2)}) %collective-permute-start.7) | collective-permute-done | bytes 16416 | tf_op jit(solution)/shard_map/ppermute | solution.py:193
  24.4 0.0 copy-done
  24.5 0.0 copy-done.1
  24.5 1.2 %attend.1 = bf16[2,4096]{1,0:T(2,128)(2,1)} custom-call(f32[2,1,256]{2,1,0:T(1,128)S(1)} %compare_convert_fusion.live_ref, bf16[2,32,128]{2,1,0:T(8,128)(2,1)S(1)} %bitcast.4, bf16[2,32,128]{2,1,0:T(8,128)(2,1)S(1)} %get-tuple-element.21.refs_0_, bf16[2,32,128]{2,1,0:T(8,128)(2,1)S(1)} %collective-permute-done.7.refs_1_, ...), custom_call_target="tpu_custom_call" | custom-call | tf_op jit(solution)/shard_map/attend/pallas_call | solution.py:268
  (4 shorter events, 0.0 us)
Async XLA Ops:
  0.0 11.7 %collective-permute-start.3 = (bf16[8,16,4096]{2,1,0:T(8,128)(2,1)}, bf16[8,16,4096]{2,1,0:T(8,128)(2,1)S(1)}, u32[]{:S(2)}, u32[]{:S(2)}) collective-permute-start(bf16[8,16,4096]{2,1,0:T(8,128)(2,1)} %refs_2_.2), channel_id=1, source_target_pairs={{0,1},{1,0},{2,3},{3,2},{4,5},{5,4},{6,7},{7,6},{8,9},{9,8},{10,11... | collective-permute-start | bytes 3145736 | tf_op jit(solution)/shard_map/ppermute | solution.py:193
  0.5 6.9 %collective-permute-start = (bf16[2,8192]{1,0:T(2,128)(2,1)}, bf16[2,8192]{1,0:T(2,128)(2,1)S(1)}, u32[]{:S(2)}, u32[]{:S(2)}) collective-permute-start(bf16[2,8192]{1,0:T(2,128)(2,1)} %refs_0_.3), channel_id=1, source_target_pairs={{0,12},{1,9},{2,14},{3,11},{4,8},{5,13},{6,10},{7,15},{8,4},{9,1},... | collective-permute-start | bytes 98312 | tf_op jit(solution)/shard_map/ppermute | solution.py:187
  5.1 2.3 %collective-permute-start.1 = (bf16[2,8192]{1,0:T(2,128)(2,1)}, bf16[2,8192]{1,0:T(2,128)(2,1)S(1)}, u32[]{:S(2)}, u32[]{:S(2)}) collective-permute-start(bf16[2,8192]{1,0:T(2,128)(2,1)} %refs_0_.3), channel_id=1, source_target_pairs={{1,5},{3,7},{5,1},{7,3},{9,13},{11,15},{13,9},{15,11},{17,21},{19,... | collective-permute-start | bytes 98312 | tf_op jit(solution)/shard_map/ppermute | solution.py:187
  7.4 4.3 %collective-permute-start.2 = (bf16[2,2,8192]{2,1,0:T(2,128)(2,1)S(1)}, bf16[2,2,8192]{2,1,0:T(2,128)(2,1)S(1)}, u32[]{:S(2)}, u32[]{:S(2)}) collective-permute-start(bf16[2,2,8192]{2,1,0:T(2,128)(2,1)S(1)} %stack.1.near_ref), channel_id=1, source_target_pairs={{0,2},{2,0},{4,6},{6,4},{8,10},{10,8},{12,14},{14,12},{1,3},{3,1},... | collective-permute-start | bytes 196616 | tf_op jit(solution)/shard_map/ppermute | solution.py:190
  11.7 11.6 %copy-start.3 = (s32[2]{0:T(128)S(1)}, s32[2]{0:T(128)}, u32[]{:S(2)}) copy-start(s32[2]{0:T(128)} %param.15) | copy-start | bytes 28
  11.7 11.6 %copy-start.2 = (bf16[2,4096]{1,0:T(2,128)(2,1)S(1)}, bf16[2,4096]{1,0:T(2,128)(2,1)}, u32[]{:S(2)}) copy-start(bf16[2,4096]{1,0:T(2,128)(2,1)} %param.9) | copy-start | bytes 49156
  11.7 12.7 %copy-start = (bf16[2,4,256,128]{3,2,1,0:T(8,128)(2,1)S(1)}, bf16[2,4,256,128]{3,2,1,0:T(8,128)(2,1)}, u32[]{:S(2)}) copy-start(bf16[2,4,256,128]{3,2,1,0:T(8,128)(2,1)} %refs_2_.3) | copy-start | bytes 1572868
  11.7 12.7 %copy-start.1 = (bf16[2,4,256,128]{3,2,1,0:T(8,128)(2,1)S(1)}, bf16[2,4,256,128]{3,2,1,0:T(8,128)(2,1)}, u32[]{:S(2)}) copy-start(bf16[2,4,256,128]{3,2,1,0:T(8,128)(2,1)} %refs_3_.1) | copy-start | bytes 1572868
  12.7 4.6 %collective-permute-start.4 = (bf16[2,2,2,32,128]{4,3,2,1,0:T(8,128)(2,1)S(1)}, bf16[2,2,2,32,128]{4,3,2,1,0:T(8,128)(2,1)S(1)}, u32[]{:S(2)}, u32[]{:S(2)}) collective-permute-start(bf16[2,2,2,32,128]{4,3,2,1,0:T(8,128)(2,1)S(1)} %get-tuple-element.18), channel_id=1, source_target_pairs={{0,2},{2,0},{4,6},{6,4},{8,10},{10,8},{12,14},{14,12},{1,3},{3,1},... | collective-permute-start | bytes 196616 | tf_op jit(solution)/shard_map/ppermute | solution.py:190
  17.4 5.8 %collective-permute-start.5 = (bf16[2,2,32,128]{3,2,1,0:T(8,128)(2,1)S(1)}, bf16[2,2,32,128]{3,2,1,0:T(8,128)(2,1)S(1)}, u32[]{:S(2)}, u32[]{:S(2)}) collective-permute-start(bf16[2,2,32,128]{3,2,1,0:T(8,128)(2,1)S(1)} %get-tuple-element.19.refs_0_), channel_id=1, source_target_pairs={{0,12},{1,9},{2,14},{3,11},{4,8},{5,13},{6,10},{7,15},{8,4},{9,1},... | collective-permute-start | bytes 98312 | tf_op jit(solution)/shard_map/ppermute | solution.py:187
  21.3 1.9 %collective-permute-start.6 = (bf16[2,2,32,128]{3,2,1,0:T(8,128)(2,1)S(1)}, bf16[2,2,32,128]{3,2,1,0:T(8,128)(2,1)S(1)}, u32[]{:S(2)}, u32[]{:S(2)}) collective-permute-start(bf16[2,2,32,128]{3,2,1,0:T(8,128)(2,1)S(1)} %get-tuple-element.20.refs_1_), channel_id=1, source_target_pairs={{1,5},{3,7},{5,1},{7,3},{9,13},{11,15},{13,9},{15,11},{17,21},{19,... | collective-permute-start | bytes 98312 | tf_op jit(solution)/shard_map/ppermute | solution.py:187
  23.2 1.2 %collective-permute-start.7 = (bf16[2,32,128]{2,1,0:T(8,128)(2,1)S(1)}, bf16[2,32,128]{2,1,0:T(8,128)(2,1)S(1)}, u32[]{:S(2)}, u32[]{:S(2)}) collective-permute-start(bf16[2,32,128]{2,1,0:T(8,128)(2,1)S(1)} %get-tuple-element.22), channel_id=1, source_target_pairs={{0,1},{1,0},{2,3},{3,2},{4,5},{5,4},{6,7},{7,6},{8,9},{9,8},{10,11... | collective-permute-start | bytes 49160 | tf_op jit(solution)/shard_map/ppermute | solution.py:193

commit v7 on v5

--- a/solution.py
+++ b/solution.py
@@ -15,7 +15,9 @@
 VMEM = pl.BlockSpec(memory_space=pltpu.VMEM)
 SMEM = pl.BlockSpec(memory_space=pltpu.SMEM)
 PARAMS = pltpu.CompilerParams(vmem_limit_bytes=VMEM_LIMIT)
-TURNS = ((7, 5, 1, 0), (6, 4, 3, 2))
+TURNS = ((7, 4, 1, 2, 0), (6, 5, 3, 2, 0))
+SENT = len(TURNS[0]) - 1
+SHARED = [turn for turn in range(SENT + 1) if TURNS[0][turn] == TURNS[1][turn]][0]
 
 
 def fetch_kernel(*refs):
@@ -55,31 +57,23 @@
 
 
 def owner_kernel(ids_ref, own_ref, *refs):
-    turns = len(TURNS[0])
-    hidden_refs, refs = refs[:turns], refs[turns:]
+    hidden_refs, refs = refs[:SENT] + (own_ref,), refs[SENT:]
     down_ref, mine_ref, other_ref = refs[:3]
-    delta_refs, (state_ref, sum_ref, row_ref) = refs[3 : 3 + turns], refs[3 + turns :]
+    delta_refs, (state_ref, sum_ref, row_ref) = refs[3:-3], refs[-3:]
     count, rank, width = down_ref.shape
     rows = state_ref.shape[1]
     heads = row_ref.shape[0]
     me, core = lax.axis_index("store"), lax.axis_index("tensor")
     first = me * count
-    for turn, hidden_ref in enumerate(hidden_refs[:-1]):
+    for turn, hidden_ref in enumerate(hidden_refs):
         state_ref[turn] = hidden_ref[...]
-
-    @pl.when(core == 0)
-    def _():
-        state_ref[turns - 1] = own_ref[...]
-
-    @pl.when(core != 0)
-    def _():
-        state_ref[turns - 1] = hidden_refs[-1][...]
 
     def one_turn(turn, carry):
         source = me ^ partner(core, turn)
         for row in range(rows):
             slot = ids_ref[source * rows + row] - first
-            owned = (slot >= 0) & (slot < count)
+            mine = (turn < SHARED) | (core == row % len(TURNS))
+            owned = mine & (slot >= 0) & (slot < count)
 
             @pl.when(owned)
             def _():
@@ -104,7 +98,7 @@
 
         return carry
 
-    lax.fori_loop(0, turns, one_turn, 0)
+    lax.fori_loop(0, SENT + 1, one_turn, 0)
     for turn, delta_ref in enumerate(delta_refs):
         delta_ref[...] = sum_ref[turn]
 
@@ -113,9 +107,8 @@
     came_refs, (kept_ref, sent_ref) = refs[:-2], refs[-2:]
     core = lax.axis_index("tensor")
     for half, out_ref in ((core, kept_ref), (1 - core, sent_ref)):
-        total = jnp.where(core == 0, own_ref[:, half], came_refs[-1][:, half])
-        total = total.astype(jnp.float32)
-        for came_ref in came_refs[:-1]:
+        total = own_ref[:, half].astype(jnp.float32)
+        for came_ref in came_refs:
             total = total + came_ref[:, half].astype(jnp.float32)
         out_ref[...] = total.astype(out_ref.dtype)
 
@@ -160,14 +153,13 @@
 
 def shared_deltas(hidden, adapter_down, adapter_up, adapter_ids, block):
     rows, heads, head_size = block
-    owners, cores, turns = lax.axis_size("store"), len(TURNS), len(TURNS[0])
+    owners, cores = lax.axis_size("store"), len(TURNS)
 
     def turn_pairs(turn):
         return [
             (i * cores + core, (i ^ TURNS[core][turn]) * cores + core)
             for i in range(owners)
             for core in range(cores)
-            if TURNS[core][turn]
         ]
 
     def visit(array, turn):
@@ -176,28 +168,28 @@
     def swap(array):
         return lax.ppermute(array, "tensor", [(0, 1), (1, 0)])
 
-    states = [visit(hidden, turn) for turn in range(turns)]
+    states = [visit(hidden, turn) for turn in range(SENT)]
     other = swap(adapter_up)
     ids, own, down, up = fetch("fetch", adapter_ids, hidden, adapter_down, adapter_up)
     wide = (rows, cores, heads, head_size)
     deltas = pl.pallas_call(
         owner_kernel,
-        out_shape=[jax.ShapeDtypeStruct(wide, jnp.bfloat16)] * turns,
-        in_specs=[SMEM] + [VMEM] * (turns + 4),
-        out_specs=[VMEM] * turns,
+        out_shape=[jax.ShapeDtypeStruct(wide, jnp.bfloat16)] * (SENT + 1),
+        in_specs=[SMEM] + [VMEM] * (SENT + 4),
+        out_specs=[VMEM] * (SENT + 1),
         scratch_shapes=[
-            pltpu.VMEM((turns,) + hidden.shape, hidden.dtype),
-            pltpu.VMEM((turns,) + wide, jnp.bfloat16),
+            pltpu.VMEM((SENT + 1,) + hidden.shape, hidden.dtype),
+            pltpu.VMEM((SENT + 1,) + wide, jnp.bfloat16),
             pltpu.VMEM((heads, head_size), jnp.float32),
         ],
         compiler_params=PARAMS,
         name="owner",
     )(ids, own, *states, down, up, near(other))
-    came = [visit(delta, turn) for turn, delta in enumerate(deltas)]
+    came = [visit(delta, turn) for turn, delta in enumerate(deltas[:SENT])]
     kept, sent = pl.pallas_call(
         merge_kernel,
         out_shape=[jax.ShapeDtypeStruct(block, jnp.bfloat16)] * 2,
-        in_specs=[VMEM] * (turns + 1),
+        in_specs=[VMEM] * (SENT + 1),
         out_specs=[VMEM] * 2,
         compiler_params=PARAMS,
         name="merge",
@@ -234,9 +226,7 @@
     features = adapter_up.shape[2]
     rows, kv_heads, slots, head_size = key_cache.shape
     block = (rows, features // head_size, head_size)
-    shared = lax.axis_size("tensor") == len(TURNS) and lax.axis_size("store") == sum(
-        len(turns) for turns in TURNS
-    )
+    shared = (lax.axis_size("store"), lax.axis_size("tensor")) == (8, len(TURNS))
     deltas = (shared_deltas if shared else exchanged_deltas)(
         hidden, adapter_down, adapter_up, adapter_ids, block
     )

time: 24.7 us -> 23.2 us (0.939)
  waiting for transfers between devices: 8.09 us -> 5.06 us
  starting transfers between devices: 12.1 us -> 13.2 us
  Pallas kernels: 4.07 us -> 4.62 us
    ppermute x8, waiting for transfers between devices: 7.34 us -> 3.98 us  [visit(): return lax.ppermute(array, ('store', 'tensor'), turn_pairs(turn))]
    ppermute x8, starting transfers between devices: 10.7 us -> 12.6 us  [visit(): return lax.ppermute(array, ('store', 'tensor'), turn_pairs(turn))]
    ppermute x2, starting transfers between devices: 1.39 us -> 0.52 us  [swap(): return lax.ppermute(array, 'tensor', [(0, 1), (1, 0)])]
    pallas_call x1, Pallas kernels: 0.95 us -> 1.5 us  [shared_deltas(): pl.pallas_call(owner_kernel, out_shape=[jax.ShapeDtypeStruct(wide, jnp.bf...]
    ppermute x2, waiting for transfers between devices: 0.75 us -> 1.08 us  [swap(): return lax.ppermute(array, 'tensor', [(0, 1), (1, 0)])]
  transfers between devices with their start and end apart: 10 -> 10, of which waited for: 4 -> 5; matrix products, arithmetic and copies ran while one was open for 0% -> 0% of each run, Pallas kernels for 8% -> 8%
where the time goes in v7:
time: 23.2 us; the launch traced here: 23 us
  starting transfers between devices  13.2 us (57%)
  waiting for transfers between devices  5.06 us (22%)
  Pallas kernels  4.62 us (20%)
    ppermute x8, starting transfers between devices, visit(): return lax.ppermute(array, ('store', 'tensor'), turn_pairs(turn))  12.6 us
    ppermute x8, waiting for transfers between devices, visit(): return lax.ppermute(array, ('store', 'tensor'), turn_pairs(turn))  3.98 us
    pallas_call x1, Pallas kernels, fetch(): pl.pallas_call(fetch_kernel, out_shape=[pltpu.VMEM(array.shape, array.dty...  1.92 us
    pallas_call x1, Pallas kernels, shared_deltas(): pl.pallas_call(owner_kernel, out_shape=[jax.ShapeDtypeStruct(wide, jnp.bf...  1.5 us
    pallas_call x1, Pallas kernels, per_device(): pl.pallas_call(functools.partial(attend_kernel, len(deltas)), out_shape=j...  1.17 us
    ppermute x2, waiting for transfers between devices, swap(): return lax.ppermute(array, 'tensor', [(0, 1), (1, 0)])  1.08 us
    ppermute x2, starting transfers between devices, swap(): return lax.ppermute(array, 'tensor', [(0, 1), (1, 0)])  0.52 us
  transfers between devices with their start and end apart: 10, of which 5 were waited for; matrix products, arithmetic and copies ran while one was open for 0% of the time, Pallas kernels for 8%

profile of v7, /device:TPU:0, one launch (start us, length us, event | category | flops | bytes accessed | tf_op | source)
XLA Modules:
  0.0 23.0 jit_solution(3301814331725189970)
XLA Ops:
  0.0 0.5 %collective-permute-start.4 = (bf16[8,16,4096]{2,1,0:T(8,128)(2,1)}, bf16[8,16,4096]{2,1,0:T(8,128)(2,1)S(1)}, u32[]{:S(2)}, u32[]{:S(2)}) collective-permute-start(bf16[8,16,4096]{2,1,0:T(8,128)(2,1)} %refs_3_.2), channel_id=1, source_target_pairs={{0,1},{1,0},{2,3},{3,2},{4,5},{5,4},{6,7},{7,6},{8,9},{9,8},{10,11... | collective-permute-start | bytes 3145736 | tf_op jit(solution)/shard_map/ppermute | solution.py:169
  0.5 5.5 %collective-permute-start = (bf16[2,8192]{1,0:T(2,128)(2,1)}, bf16[2,8192]{1,0:T(2,128)(2,1)S(1)}, u32[]{:S(2)}, u32[]{:S(2)}) collective-permute-start(bf16[2,8192]{1,0:T(2,128)(2,1)} %refs_1_.1), channel_id=1, source_target_pairs={{0,14},{1,13},{2,12},{3,15},{4,10},{5,9},{6,8},{7,11},{8,6},{9,5},... | collective-permute-start | bytes 98312 | tf_op jit(solution)/shard_map/ppermute | solution.py:166
  6.0 0.0 collective-permute-start.1
  6.0 0.5 %collective-permute-start.2 = (bf16[2,8192]{1,0:T(2,128)(2,1)}, bf16[2,8192]{1,0:T(2,128)(2,1)S(1)}, u32[]{:S(2)}, u32[]{:S(2)}) collective-permute-start(bf16[2,8192]{1,0:T(2,128)(2,1)} %refs_1_.1), channel_id=1, source_target_pairs={{0,2},{1,7},{2,0},{3,5},{4,6},{5,3},{6,4},{7,1},{8,10},{9,15},{10,... | collective-permute-start | bytes 98312 | tf_op jit(solution)/shard_map/ppermute | solution.py:166
  6.5 0.7 %collective-permute-start.3 = (bf16[2,8192]{1,0:T(2,128)(2,1)}, bf16[2,8192]{1,0:T(2,128)(2,1)S(1)}, u32[]{:S(2)}, u32[]{:S(2)}) collective-permute-start(bf16[2,8192]{1,0:T(2,128)(2,1)} %refs_1_.1), channel_id=1, source_target_pairs={{0,4},{1,5},{2,6},{3,7},{4,0},{5,1},{6,2},{7,3},{8,12},{9,13},{10,... | collective-permute-start | bytes 98312 | tf_op jit(solution)/shard_map/ppermute | solution.py:166
  7.2 1.9 %fetch.1 = (s32[16]{0:T(128)S(1)}, bf16[2,8192]{1,0:T(2,128)(2,1)S(1)}, bf16[8,16,8192]{2,1,0:T(8,128)(2,1)S(1)}, bf16[8,16,4096]{2,1,0:T(8,128)(2,1)S(1)}) custom-call(s32[16]{0:T(128)} %refs_0_.1, bf16[2,8192]{1,0:T(2,128)(2,1)} %refs_1_.1, bf16[8,16,8192]{2,1,0:T(8,128)(2,1)} %refs_2_.2, bf16[8,16,4096]{2,1,0:T(8,128)(2,1)} %refs_3_.2), custom_call_target="tpu_custom_call" | custom-call | bytes 6357120 | tf_op jit(solution)/shard_map/fetch/pallas_call | solution.py:38
  9.1 0.0 collective-permute-done.refs_0_
  9.1 1.9 %collective-permute-done.1.refs_1_ = bf16[2,8192]{1,0:T(2,128)(2,1)S(1)} collective-permute-done((bf16[2,8192]{1,0:T(2,128)(2,1)}, bf16[2,8192]{1,0:T(2,128)(2,1)S(1)}, u32[]{:S(2)}, u32[]{:S(2)}) %collective-permute-start.1) | collective-permute-done | bytes 32800 | tf_op jit(solution)/shard_map/ppermute | solution.py:166
  11.0 0.0 collective-permute-done.2.refs_2_
  11.0 0.0 collective-permute-done.3.refs_3_
  11.1 0.0 collective-permute-done.4.refs_6_
  11.1 0.0 copy-start.3
  11.1 0.0 copy-start.2
  11.1 0.0 copy-start
  11.1 0.0 copy-start.1
  11.1 1.5 %owner.1 = (bf16[2,2,32,128]{3,2,1,0:T(8,128)(2,1)S(1)}, bf16[2,2,32,128]{3,2,1,0:T(8,128)(2,1)S(1)}, bf16[2,2,32,128]{3,2,1,0:T(8,128)(2,1)S(1)}, bf16[2,2,32,1...) custom-call(s32[16]{0:T(128)S(1)} %get-tuple-element.16.ids_ref, bf16[2,8192]{1,0:T(2,128)(2,1)S(1)} %get-tuple-element.17.own_ref, ...), custom_call_target="tpu_custom_call" | custom-call | tf_op jit(solution)/shard_map/owner/pallas_call | solution.py:175
  12.6 2.7 %collective-permute-start.5 = (bf16[2,2,32,128]{3,2,1,0:T(8,128)(2,1)S(1)}, bf16[2,2,32,128]{3,2,1,0:T(8,128)(2,1)S(1)}, u32[]{:S(2)}, u32[]{:S(2)}) collective-permute-start(bf16[2,2,32,128]{3,2,1,0:T(8,128)(2,1)S(1)} %get-tuple-element.21), channel_id=1, source_target_pairs={{0,14},{1,13},{2,12},{3,15},{4,10},{5,9},{6,8},{7,11},{8,6},{9,5},... | collective-permute-start | bytes 98312 | tf_op jit(solution)/shard_map/ppermute | solution.py:166
  15.3 0.0 collective-permute-start.6
  15.3 0.7 %collective-permute-start.7 = (bf16[2,2,32,128]{3,2,1,0:T(8,128)(2,1)S(1)}, bf16[2,2,32,128]{3,2,1,0:T(8,128)(2,1)S(1)}, u32[]{:S(2)}, u32[]{:S(2)}) collective-permute-start(bf16[2,2,32,128]{3,2,1,0:T(8,128)(2,1)S(1)} %get-tuple-element.23), channel_id=1, source_target_pairs={{0,2},{1,7},{2,0},{3,5},{4,6},{5,3},{6,4},{7,1},{8,10},{9,15},{10,... | collective-permute-start | bytes 98312 | tf_op jit(solution)/shard_map/ppermute | solution.py:166
  16.0 2.5 %collective-permute-start.8 = (bf16[2,2,32,128]{3,2,1,0:T(8,128)(2,1)S(1)}, bf16[2,2,32,128]{3,2,1,0:T(8,128)(2,1)S(1)}, u32[]{:S(2)}, u32[]{:S(2)}) collective-permute-start(bf16[2,2,32,128]{3,2,1,0:T(8,128)(2,1)S(1)} %get-tuple-element.24), channel_id=1, source_target_pairs={{0,4},{1,5},{2,6},{3,7},{4,0},{5,1},{6,2},{7,3},{8,12},{9,13},{10,... | collective-permute-start | bytes 98312 | tf_op jit(solution)/shard_map/ppermute | solution.py:166
  18.5 0.9 %collective-permute-done.5.refs_0_ = bf16[2,2,32,128]{3,2,1,0:T(8,128)(2,1)S(1)} collective-permute-done((bf16[2,2,32,128]{3,2,1,0:T(8,128)(2,1)S(1)}, bf16[2,2,32,128]{3,2,1,0:T(8,128)(2,1)S(1)}, u32[]{:S(2)}, u32[]{:S(2)}) %collective-permute-start.5) | collective-permute-done | bytes 32800 | tf_op jit(solution)/shard_map/ppermute | solution.py:166
  19.4 1.0 %collective-permute-done.6.refs_1_ = bf16[2,2,32,128]{3,2,1,0:T(8,128)(2,1)S(1)} collective-permute-done((bf16[2,2,32,128]{3,2,1,0:T(8,128)(2,1)S(1)}, bf16[2,2,32,128]{3,2,1,0:T(8,128)(2,1)S(1)}, u32[]{:S(2)}, u32[]{:S(2)}) %collective-permute-start.6) | collective-permute-done | bytes 32800 | tf_op jit(solution)/shard_map/ppermute | solution.py:166
  20.4 0.0 collective-permute-done.7.refs_2_
  20.4 0.2 collective-permute-done.8.refs_3_
  20.6 0.1 collective-permute-start.9
  20.7 0.0 copy-done.3
  20.7 0.1 compare_convert_fusion.live_ref
  20.8 0.0 copy-done.2
  20.8 1.1 %collective-permute-done.9.refs_1_ = bf16[2,32,128]{2,1,0:T(8,128)(2,1)S(1)} collective-permute-done((bf16[2,32,128]{2,1,0:T(8,128)(2,1)S(1)}, bf16[2,32,128]{2,1,0:T(8,128)(2,1)S(1)}, u32[]{:S(2)}, u32[]{:S(2)}) %collective-permute-start.9) | collective-permute-done | bytes 16416 | tf_op jit(solution)/shard_map/ppermute | solution.py:169
  21.9 0.0 copy-done
  21.9 0.0 copy-done.1
  21.9 1.2 %attend.1 = bf16[2,4096]{1,0:T(2,128)(2,1)} custom-call(f32[2,1,256]{2,1,0:T(1,128)S(1)} %compare_convert_fusion.live_ref, bf16[2,32,128]{2,1,0:T(8,128)(2,1)S(1)} %bitcast.4, bf16[2,32,128]{2,1,0:T(8,128)(2,1)S(1)} %get-tuple-element.25.refs_0_, bf16[2,32,128]{2,1,0:T(8,128)(2,1)S(1)} %collective-permute-done.9.refs_1_, ...), custom_call_target="tpu_custom_call" | custom-call | tf_op jit(solution)/shard_map/attend/pallas_call | solution.py:234
  (2 shorter events, 0.0 us)
Async XLA Ops:
  0.0 11.1 %collective-permute-start.4 = (bf16[8,16,4096]{2,1,0:T(8,128)(2,1)}, bf16[8,16,4096]{2,1,0:T(8,128)(2,1)S(1)}, u32[]{:S(2)}, u32[]{:S(2)}) collective-permute-start(bf16[8,16,4096]{2,1,0:T(8,128)(2,1)} %refs_3_.2), channel_id=1, source_target_pairs={{0,1},{1,0},{2,3},{3,2},{4,5},{5,4},{6,7},{7,6},{8,9},{9,8},{10,11... | collective-permute-start | bytes 3145736 | tf_op jit(solution)/shard_map/ppermute | solution.py:169
  0.5 8.7 %collective-permute-start = (bf16[2,8192]{1,0:T(2,128)(2,1)}, bf16[2,8192]{1,0:T(2,128)(2,1)S(1)}, u32[]{:S(2)}, u32[]{:S(2)}) collective-permute-start(bf16[2,8192]{1,0:T(2,128)(2,1)} %refs_1_.1), channel_id=1, source_target_pairs={{0,14},{1,13},{2,12},{3,15},{4,10},{5,9},{6,8},{7,11},{8,6},{9,5},... | collective-permute-start | bytes 98312 | tf_op jit(solution)/shard_map/ppermute | solution.py:166
  6.0 5.1 %collective-permute-start.1 = (bf16[2,8192]{1,0:T(2,128)(2,1)}, bf16[2,8192]{1,0:T(2,128)(2,1)S(1)}, u32[]{:S(2)}, u32[]{:S(2)}) collective-permute-start(bf16[2,8192]{1,0:T(2,128)(2,1)} %refs_1_.1), channel_id=1, source_target_pairs={{0,8},{1,11},{2,10},{3,9},{4,12},{5,15},{6,14},{7,13},{8,0},{9,3},... | collective-permute-start | bytes 98312 | tf_op jit(solution)/shard_map/ppermute | solution.py:166
  6.0 5.1 %collective-permute-start.2 = (bf16[2,8192]{1,0:T(2,128)(2,1)}, bf16[2,8192]{1,0:T(2,128)(2,1)S(1)}, u32[]{:S(2)}, u32[]{:S(2)}) collective-permute-start(bf16[2,8192]{1,0:T(2,128)(2,1)} %refs_1_.1), channel_id=1, source_target_pairs={{0,2},{1,7},{2,0},{3,5},{4,6},{5,3},{6,4},{7,1},{8,10},{9,15},{10,... | collective-permute-start | bytes 98312 | tf_op jit(solution)/shard_map/ppermute | solution.py:166
  6.5 4.5 %collective-permute-start.3 = (bf16[2,8192]{1,0:T(2,128)(2,1)}, bf16[2,8192]{1,0:T(2,128)(2,1)S(1)}, u32[]{:S(2)}, u32[]{:S(2)}) collective-permute-start(bf16[2,8192]{1,0:T(2,128)(2,1)} %refs_1_.1), channel_id=1, source_target_pairs={{0,4},{1,5},{2,6},{3,7},{4,0},{5,1},{6,2},{7,3},{8,12},{9,13},{10,... | collective-permute-start | bytes 98312 | tf_op jit(solution)/shard_map/ppermute | solution.py:166
  11.1 9.6 %copy-start.3 = (s32[2]{0:T(128)S(1)}, s32[2]{0:T(128)}, u32[]{:S(2)}) copy-start(s32[2]{0:T(128)} %param.15) | copy-start | bytes 28
  11.1 9.7 %copy-start.2 = (bf16[2,4096]{1,0:T(2,128)(2,1)S(1)}, bf16[2,4096]{1,0:T(2,128)(2,1)}, u32[]{:S(2)}) copy-start(bf16[2,4096]{1,0:T(2,128)(2,1)} %param.9) | copy-start | bytes 49156
  11.1 10.8 %copy-start = (bf16[2,4,256,128]{3,2,1,0:T(8,128)(2,1)S(1)}, bf16[2,4,256,128]{3,2,1,0:T(8,128)(2,1)}, u32[]{:S(2)}) copy-start(bf16[2,4,256,128]{3,2,1,0:T(8,128)(2,1)} %refs_2_.3) | copy-start | bytes 1572868
  11.1 10.8 %copy-start.1 = (bf16[2,4,256,128]{3,2,1,0:T(8,128)(2,1)S(1)}, bf16[2,4,256,128]{3,2,1,0:T(8,128)(2,1)}, u32[]{:S(2)}) copy-start(bf16[2,4,256,128]{3,2,1,0:T(8,128)(2,1)} %refs_3_.3) | copy-start | bytes 1572868
  12.6 6.8 %collective-permute-start.5 = (bf16[2,2,32,128]{3,2,1,0:T(8,128)(2,1)S(1)}, bf16[2,2,32,128]{3,2,1,0:T(8,128)(2,1)S(1)}, u32[]{:S(2)}, u32[]{:S(2)}) collective-permute-start(bf16[2,2,32,128]{3,2,1,0:T(8,128)(2,1)S(1)} %get-tuple-element.21), channel_id=1, source_target_pairs={{0,14},{1,13},{2,12},{3,15},{4,10},{5,9},{6,8},{7,11},{8,6},{9,5},... | collective-permute-start | bytes 98312 | tf_op jit(solution)/shard_map/ppermute | solution.py:166
  15.3 5.1 %collective-permute-start.6 = (bf16[2,2,32,128]{3,2,1,0:T(8,128)(2,1)S(1)}, bf16[2,2,32,128]{3,2,1,0:T(8,128)(2,1)S(1)}, u32[]{:S(2)}, u32[]{:S(2)}) collective-permute-start(bf16[2,2,32,128]{3,2,1,0:T(8,128)(2,1)S(1)} %get-tuple-element.22), channel_id=1, source_target_pairs={{0,8},{1,11},{2,10},{3,9},{4,12},{5,15},{6,14},{7,13},{8,0},{9,3},... | collective-permute-start | bytes 98312 | tf_op jit(solution)/shard_map/ppermute | solution.py:166
  15.3 5.1 %collective-permute-start.7 = (bf16[2,2,32,128]{3,2,1,0:T(8,128)(2,1)S(1)}, bf16[2,2,32,128]{3,2,1,0:T(8,128)(2,1)S(1)}, u32[]{:S(2)}, u32[]{:S(2)}) collective-permute-start(bf16[2,2,32,128]{3,2,1,0:T(8,128)(2,1)S(1)} %get-tuple-element.23), channel_id=1, source_target_pairs={{0,2},{1,7},{2,0},{3,5},{4,6},{5,3},{6,4},{7,1},{8,10},{9,15},{10,... | collective-permute-start | bytes 98312 | tf_op jit(solution)/shard_map/ppermute | solution.py:166
  16.0 4.6 %collective-permute-start.8 = (bf16[2,2,32,128]{3,2,1,0:T(8,128)(2,1)S(1)}, bf16[2,2,32,128]{3,2,1,0:T(8,128)(2,1)S(1)}, u32[]{:S(2)}, u32[]{:S(2)}) collective-permute-start(bf16[2,2,32,128]{3,2,1,0:T(8,128)(2,1)S(1)} %get-tuple-element.24), channel_id=1, source_target_pairs={{0,4},{1,5},{2,6},{3,7},{4,0},{5,1},{6,2},{7,3},{8,12},{9,13},{10,... | collective-permute-start | bytes 98312 | tf_op jit(solution)/shard_map/ppermute | solution.py:166
  20.6 1.2 %collective-permute-start.9 = (bf16[2,32,128]{2,1,0:T(8,128)(2,1)S(1)}, bf16[2,32,128]{2,1,0:T(8,128)(2,1)S(1)}, u32[]{:S(2)}, u32[]{:S(2)}) collective-permute-start(bf16[2,32,128]{2,1,0:T(8,128)(2,1)S(1)} %get-tuple-element.26), channel_id=1, source_target_pairs={{0,1},{1,0},{2,3},{3,2},{4,5},{5,4},{6,7},{7,6},{8,9},{9,8},{10,11... | collective-permute-start | bytes 49160 | tf_op jit(solution)/shard_map/ppermute | solution.py:169

commit v8 on v7

--- a/solution.py
+++ b/solution.py
@@ -15,8 +15,9 @@
 VMEM = pl.BlockSpec(memory_space=pltpu.VMEM)
 SMEM = pl.BlockSpec(memory_space=pltpu.SMEM)
 PARAMS = pltpu.CompilerParams(vmem_limit_bytes=VMEM_LIMIT)
-TURNS = ((7, 4, 1, 2, 0), (6, 5, 3, 2, 0))
+TURNS = ((7, 1, 4, 2, 0), (6, 3, 5, 2, 0))
 SENT = len(TURNS[0]) - 1
+FAR = 2
 SHARED = [turn for turn in range(SENT + 1) if TURNS[0][turn] == TURNS[1][turn]][0]
 
 
@@ -51,56 +52,64 @@
     return pltpu.with_memory_space_constraint(array, pltpu.VMEM)
 
 
-def partner(core, turn):
-    packed = [sum(value << (4 * i) for i, value in enumerate(turns)) for turns in TURNS]
-    return (jnp.where(core == 0, packed[0], packed[1]) >> (4 * turn)) & 15
-
-
-def owner_kernel(ids_ref, own_ref, *refs):
-    hidden_refs, refs = refs[:SENT] + (own_ref,), refs[SENT:]
-    down_ref, mine_ref, other_ref = refs[:3]
-    delta_refs, (state_ref, sum_ref, row_ref) = refs[3:-3], refs[-3:]
+def owner_kernel(turns, ids_ref, down_ref, mine_ref, other_ref, *refs):
+    amount = len(turns)
+    hidden_refs, (delta_refs, scratch) = refs[:amount], (refs[-3 - amount : -3], refs[-3:])
+    state_ref, sum_ref, row_ref = scratch
     count, rank, width = down_ref.shape
     rows = state_ref.shape[1]
     heads = row_ref.shape[0]
     me, core = lax.axis_index("store"), lax.axis_index("tensor")
-    first = me * count
-    for turn, hidden_ref in enumerate(hidden_refs):
-        state_ref[turn] = hidden_ref[...]
-
-    def one_turn(turn, carry):
-        source = me ^ partner(core, turn)
+
+    def slot_of(partners, row, shared):
+        source = me ^ jnp.where(core == 0, partners[0], partners[1])
+        slot = ids_ref[source * rows + row] - me * count
+        mine = jnp.logical_not(shared) | (core == lax.rem(row, len(TURNS)))
+        return slot, mine & (slot >= 0) & (slot < count)
+
+    owned = {}
+    for i, turn in enumerate(turns):
         for row in range(rows):
-            slot = ids_ref[source * rows + row] - first
-            mine = (turn < SHARED) | (core == row % len(TURNS))
-            owned = mine & (slot >= 0) & (slot < count)
-
-            @pl.when(owned)
+            owned[i, row] = slot_of([steps[turn] for steps in TURNS], row, turn >= SHARED)[1]
+
+            @pl.when(owned[i, row])
             def _():
-                total = jnp.zeros((rank, CHUNK), jnp.float32)
-                for start in range(0, width, CHUNK):
-                    down = down_ref[slot, :, start : start + CHUNK].astype(jnp.float32)
-                    state = state_ref[turn, :, start : start + CHUNK].astype(jnp.float32)
-                    total = total + down * state[row : row + 1]
-                low = jnp.sum(total, axis=1, keepdims=True)
-                low = low.astype(jnp.bfloat16).astype(jnp.float32)
-                for half, up_ref in ((core, mine_ref), (1 - core, other_ref)):
-                    for head in range(heads):
-                        up = up_ref[slot, :, head * LANES : (head + 1) * LANES]
-                        row_ref[head : head + 1, :] = jnp.sum(
-                            up.astype(jnp.float32) * low, axis=0, keepdims=True
-                        )
-                    sum_ref[turn, row, half] = row_ref[...].astype(sum_ref.dtype)
-
-            @pl.when(jnp.logical_not(owned))
-            def _():
-                sum_ref[turn, row] = jnp.zeros(sum_ref.shape[2:], sum_ref.dtype)
+                state_ref[i, row : row + 1] = hidden_refs[i][row : row + 1, :].astype(jnp.float32)
+
+        delta_refs[i][...] = jnp.zeros(delta_refs[i].shape, delta_refs[i].dtype)
+
+    packed = [sum(steps[turn] << (4 * i) for i, turn in enumerate(turns)) for steps in TURNS]
+    late = sum((turn >= SHARED) << i for i, turn in enumerate(turns))
+
+    def one_request(index, carry):
+        i, row = lax.div(index, rows), lax.rem(index, rows)
+        partners = [(jnp.int32(value) >> (4 * i)) & 15 for value in packed]
+        slot, here = slot_of(partners, row, ((jnp.int32(late) >> i) & 1) == 1)
+
+        @pl.when(here)
+        def _():
+            total = jnp.zeros((rank, CHUNK), jnp.float32)
+            for start in range(0, width, CHUNK):
+                down = down_ref[slot, :, start : start + CHUNK].astype(jnp.float32)
+                total = total + down * state_ref[i, pl.ds(row, 1), start : start + CHUNK]
+            low = jnp.sum(total, axis=1, keepdims=True)
+            low = low.astype(jnp.bfloat16).astype(jnp.float32)
+            for half, up_ref in ((core, mine_ref), (1 - core, other_ref)):
+                for head in range(heads):
+                    up = up_ref[slot, :, head * LANES : (head + 1) * LANES]
+                    row_ref[head : head + 1, :] = jnp.sum(
+                        up.astype(jnp.float32) * low, axis=0, keepdims=True
+                    )
+                sum_ref[i, row, half] = row_ref[...].astype(sum_ref.dtype)
 
         return carry
 
-    lax.fori_loop(0, SENT + 1, one_turn, 0)
-    for turn, delta_ref in enumerate(delta_refs):
-        delta_ref[...] = sum_ref[turn]
+    lax.fori_loop(0, amount * rows, one_request, 0)
+    for (i, row), here in owned.items():
+
+        @pl.when(here)
+        def _():
+            delta_refs[i][row] = sum_ref[i, row]
 
 
 def merge_kernel(own_ref, *refs):
@@ -171,20 +180,28 @@
     states = [visit(hidden, turn) for turn in range(SENT)]
     other = swap(adapter_up)
     ids, own, down, up = fetch("fetch", adapter_ids, hidden, adapter_down, adapter_up)
+    other = near(other)
     wide = (rows, cores, heads, head_size)
-    deltas = pl.pallas_call(
-        owner_kernel,
-        out_shape=[jax.ShapeDtypeStruct(wide, jnp.bfloat16)] * (SENT + 1),
-        in_specs=[SMEM] + [VMEM] * (SENT + 4),
-        out_specs=[VMEM] * (SENT + 1),
-        scratch_shapes=[
-            pltpu.VMEM((SENT + 1,) + hidden.shape, hidden.dtype),
-            pltpu.VMEM((SENT + 1,) + wide, jnp.bfloat16),
-            pltpu.VMEM((heads, head_size), jnp.float32),
-        ],
-        compiler_params=PARAMS,
-        name="owner",
-    )(ids, own, *states, down, up, near(other))
+
+    def work(name, after, *turns):
+        amount = len(turns)
+        return pl.pallas_call(
+            functools.partial(owner_kernel, turns),
+            out_shape=[jax.ShapeDtypeStruct(wide, jnp.bfloat16)] * amount,
+            in_specs=[SMEM] + [VMEM] * (amount + 3) + [pl.BlockSpec(memory_space=pl.ANY)] * len(after),
+            out_specs=[VMEM] * amount,
+            scratch_shapes=[
+                pltpu.VMEM((amount,) + hidden.shape, jnp.float32),
+                pltpu.VMEM((amount,) + wide, jnp.bfloat16),
+                pltpu.VMEM((heads, head_size), jnp.float32),
+            ],
+            compiler_params=PARAMS,
+            name=name,
+        )(ids, down, up, other, *[states[turn] for turn in turns], *after)
+
+    states.append(own)
+    deltas = work("owner_far", (), *range(FAR))
+    deltas += work("owner_near", deltas[:1], *range(FAR, SENT + 1))
     came = [visit(delta, turn) for turn, delta in enumerate(deltas[:SENT])]
     kept, sent = pl.pallas_call(
         merge_kernel,

time: 23.2 us -> 23.2 us (level)
    pallas_call x1 -> x2, Pallas kernels: 1.5 us -> 1.47 us  [work(): pl.pallas_call(functools.partial(owner_kernel, turns), out_shape=[jax.Sha...]
  transfers between devices with their start and end apart: 10 -> 10, of which waited for: 5 -> 4; matrix products, arithmetic and copies ran while one was open for 0% -> 0% of each run, Pallas kernels for 8% -> 15%
where the time goes in v8:
time: 23.2 us; the launch traced here: 23.1 us
  starting transfers between devices  13.2 us (57%)
  waiting for transfers between devices  5.07 us (22%)
  Pallas kernels  4.59 us (20%)
    ppermute x8, starting transfers between devices, visit(): return lax.ppermute(array, ('store', 'tensor'), turn_pairs(turn))  12.7 us
    ppermute x8, waiting for transfers between devices, visit(): return lax.ppermute(array, ('store', 'tensor'), turn_pairs(turn))  3.99 us
    pallas_call x1, Pallas kernels, fetch(): pl.pallas_call(fetch_kernel, out_shape=[pltpu.VMEM(array.shape, array.dty...  1.92 us
    pallas_call x2, Pallas kernels, work(): pl.pallas_call(functools.partial(owner_kernel, turns), out_shape=[jax.Sha...  1.47 us
    pallas_call x1, Pallas kernels, per_device(): pl.pallas_call(functools.partial(attend_kernel, len(deltas)), out_shape=j...  1.17 us
    ppermute x2, waiting for transfers between devices, swap(): return lax.ppermute(array, 'tensor', [(0, 1), (1, 0)])  1.08 us
    ppermute x2, starting transfers between devices, swap(): return lax.ppermute(array, 'tensor', [(0, 1), (1, 0)])  0.52 us
  transfers between devices with their start and end apart: 10, of which 4 were waited for; matrix products, arithmetic and copies ran while one was open for 0% of the time, Pallas kernels for 15%

profile of v8, /device:TPU:0, one launch (start us, length us, event | category | flops | bytes accessed | tf_op | source)
XLA Modules:
  0.0 23.1 jit_solution(17152521101271603364)
XLA Ops:
  0.0 0.5 %collective-permute-start = (bf16[8,16,4096]{2,1,0:T(8,128)(2,1)}, bf16[8,16,4096]{2,1,0:T(8,128)(2,1)S(1)}, u32[]{:S(2)}, u32[]{:S(2)}) collective-permute-start(bf16[8,16,4096]{2,1,0:T(8,128)(2,1)} %refs_3_.2), channel_id=1, source_target_pairs={{0,1},{1,0},{2,3},{3,2},{4,5},{5,4},{6,7},{7,6},{8,9},{9,8},{10,11... | collective-permute-start | bytes 3145736 | tf_op jit(solution)/shard_map/ppermute | solution.py:178
  0.5 5.5 %collective-permute-start.3 = (bf16[2,8192]{1,0:T(2,128)(2,1)}, bf16[2,8192]{1,0:T(2,128)(2,1)S(1)}, u32[]{:S(2)}, u32[]{:S(2)}) collective-permute-start(bf16[2,8192]{1,0:T(2,128)(2,1)} %refs_1_.1), channel_id=1, source_target_pairs={{0,14},{1,13},{2,12},{3,15},{4,10},{5,9},{6,8},{7,11},{8,6},{9,5},... | collective-permute-start | bytes 98312 | tf_op jit(solution)/shard_map/ppermute | solution.py:175
  6.0 0.5 %collective-permute-start.4 = (bf16[2,8192]{1,0:T(2,128)(2,1)}, bf16[2,8192]{1,0:T(2,128)(2,1)S(1)}, u32[]{:S(2)}, u32[]{:S(2)}) collective-permute-start(bf16[2,8192]{1,0:T(2,128)(2,1)} %refs_1_.1), channel_id=1, source_target_pairs={{0,2},{1,7},{2,0},{3,5},{4,6},{5,3},{6,4},{7,1},{8,10},{9,15},{10,... | collective-permute-start | bytes 98312 | tf_op jit(solution)/shard_map/ppermute | solution.py:175
  6.5 0.0 collective-permute-start.1
  6.5 0.7 %collective-permute-start.2 = (bf16[2,8192]{1,0:T(2,128)(2,1)}, bf16[2,8192]{1,0:T(2,128)(2,1)S(1)}, u32[]{:S(2)}, u32[]{:S(2)}) collective-permute-start(bf16[2,8192]{1,0:T(2,128)(2,1)} %refs_1_.1), channel_id=1, source_target_pairs={{0,4},{1,5},{2,6},{3,7},{4,0},{5,1},{6,2},{7,3},{8,12},{9,13},{10,... | collective-permute-start | bytes 98312 | tf_op jit(solution)/shard_map/ppermute | solution.py:175
  7.2 1.9 %fetch.1 = (s32[16]{0:T(128)S(1)}, bf16[2,8192]{1,0:T(2,128)(2,1)S(1)}, bf16[8,16,8192]{2,1,0:T(8,128)(2,1)S(1)}, bf16[8,16,4096]{2,1,0:T(8,128)(2,1)S(1)}) custom-call(s32[16]{0:T(128)} %refs_0_.1, bf16[2,8192]{1,0:T(2,128)(2,1)} %refs_1_.1, bf16[8,16,8192]{2,1,0:T(8,128)(2,1)} %refs_2_.2, bf16[8,16,4096]{2,1,0:T(8,128)(2,1)} %refs_3_.2), custom_call_target="tpu_custom_call" | custom-call | bytes 6357120 | tf_op jit(solution)/shard_map/fetch/pallas_call | solution.py:39
  9.1 0.0 collective-permute-done.3.refs_0_
  9.1 1.0 %collective-permute-done.4.refs_1_ = bf16[2,8192]{1,0:T(2,128)(2,1)S(1)} collective-permute-done((bf16[2,8192]{1,0:T(2,128)(2,1)}, bf16[2,8192]{1,0:T(2,128)(2,1)S(1)}, u32[]{:S(2)}, u32[]{:S(2)}) %collective-permute-start.4) | collective-permute-done | bytes 32800 | tf_op jit(solution)/shard_map/ppermute | solution.py:175
  10.1 0.0 collective-permute-done.other_ref
  10.1 0.7 %owner_far.1 = (bf16[2,2,32,128]{3,2,1,0:T(8,128)(2,1)S(1)}, bf16[2,2,32,128]{3,2,1,0:T(8,128)(2,1)S(1)}) custom-call(s32[16]{0:T(128)S(1)} %get-tuple-element.16.ids_ref, bf16[8,16,8192]{2,1,0:T(8,128)(2,1)S(1)} %get-tuple-element.17.down_ref, bf16[8,16,4096]{2,1,0:T(8,128)(2,1)S(1)} %get-tuple-element.18.mine_ref, ...), custom_call_target="tpu_custom_call" | custom-call | tf_op jit(solution)/shard_map/owner_far/pallas_call | solution.py:188
  10.8 4.0 %collective-permute-start.5 = (bf16[2,2,32,128]{3,2,1,0:T(8,128)(2,1)S(1)}, bf16[2,2,32,128]{3,2,1,0:T(8,128)(2,1)S(1)}, u32[]{:S(2)}, u32[]{:S(2)}) collective-permute-start(bf16[2,2,32,128]{3,2,1,0:T(8,128)(2,1)S(1)} %get-tuple-element.20.refs_3_), channel_id=1, source_target_pairs={{0,14},{1,13},{2,12},{3,15},{4,10},{5,9},{6,8},{7,11},{8,6},{9,5},... | collective-permute-start | bytes 98312 | tf_op jit(solution)/shard_map/ppermute | solution.py:175
  14.8 0.0 collective-permute-done.1.refs_0_
  14.8 0.0 collective-permute-done.2.refs_1_
  14.8 0.0 copy-start.3
  14.8 0.0 copy-start.2
  14.8 0.0 copy-start
  14.8 0.0 copy-start.1
  14.8 0.8 %owner_near.1 = (bf16[2,2,32,128]{3,2,1,0:T(8,128)(2,1)S(1)}, bf16[2,2,32,128]{3,2,1,0:T(8,128)(2,1)S(1)}, bf16[2,2,32,128]{3,2,1,0:T(8,128)(2,1)S(1)}) custom-call(s32[16]{0:T(128)S(1)} %get-tuple-element.16.ids_ref, bf16[8,16,8192]{2,1,0:T(8,128)(2,1)S(1)} %get-tuple-element.17.down_ref, bf16[8,16,4096]{2,1,0:T(8,128)(2,1)S(1)} %get-tuple-element.18.mine_ref, ...), custom_call_target="tpu_custom_call" | custom-call | tf_op jit(solution)/shard_map/owner_near/pallas_call | solution.py:188
  15.6 0.1 collective-permute-start.7
  15.7 1.0 %collective-permute-start.8 = (bf16[2,2,32,128]{3,2,1,0:T(8,128)(2,1)S(1)}, bf16[2,2,32,128]{3,2,1,0:T(8,128)(2,1)S(1)}, u32[]{:S(2)}, u32[]{:S(2)}) collective-permute-start(bf16[2,2,32,128]{3,2,1,0:T(8,128)(2,1)S(1)} %get-tuple-element.24), channel_id=1, source_target_pairs={{0,4},{1,5},{2,6},{3,7},{4,0},{5,1},{6,2},{7,3},{8,12},{9,13},{10,... | collective-permute-start | bytes 98312 | tf_op jit(solution)/shard_map/ppermute | solution.py:175
  16.7 0.9 %collective-permute-start.6 = (bf16[2,2,32,128]{3,2,1,0:T(8,128)(2,1)S(1)}, bf16[2,2,32,128]{3,2,1,0:T(8,128)(2,1)S(1)}, u32[]{:S(2)}, u32[]{:S(2)}) collective-permute-start(bf16[2,2,32,128]{3,2,1,0:T(8,128)(2,1)S(1)} %get-tuple-element.22), channel_id=1, source_target_pairs={{0,2},{1,7},{2,0},{3,5},{4,6},{5,3},{6,4},{7,1},{8,10},{9,15},{10,... | collective-permute-start | bytes 98312 | tf_op jit(solution)/shard_map/ppermute | solution.py:175
  17.6 2.9 %collective-permute-done.7.refs_2_ = bf16[2,2,32,128]{3,2,1,0:T(8,128)(2,1)S(1)} collective-permute-done((bf16[2,2,32,128]{3,2,1,0:T(8,128)(2,1)S(1)}, bf16[2,2,32,128]{3,2,1,0:T(8,128)(2,1)S(1)}, u32[]{:S(2)}, u32[]{:S(2)}) %collective-permute-start.7) | collective-permute-done | bytes 32800 | tf_op jit(solution)/shard_map/ppermute | solution.py:175
  20.5 0.0 collective-permute-done.8.refs_3_
  20.5 0.0 collective-permute-done.5.refs_0_
  20.5 0.1 collective-permute-done.6.refs_1_
  20.7 0.1 collective-permute-start.9
  20.7 0.0 copy-done.3
  20.8 0.1 compare_convert_fusion.live_ref
  20.8 0.0 copy-done.2
  20.8 1.1 %collective-permute-done.9.refs_1_ = bf16[2,32,128]{2,1,0:T(8,128)(2,1)S(1)} collective-permute-done((bf16[2,32,128]{2,1,0:T(8,128)(2,1)S(1)}, bf16[2,32,128]{2,1,0:T(8,128)(2,1)S(1)}, u32[]{:S(2)}, u32[]{:S(2)}) %collective-permute-start.9) | collective-permute-done | bytes 16416 | tf_op jit(solution)/shard_map/ppermute | solution.py:178
  21.9 0.0 copy-done
  21.9 0.0 copy-done.1
  21.9 1.2 %attend.1 = bf16[2,4096]{1,0:T(2,128)(2,1)} custom-call(f32[2,1,256]{2,1,0:T(1,128)S(1)} %compare_convert_fusion.live_ref, bf16[2,32,128]{2,1,0:T(8,128)(2,1)S(1)} %bitcast.4, bf16[2,32,128]{2,1,0:T(8,128)(2,1)S(1)} %get-tuple-element.25.refs_0_, bf16[2,32,128]{2,1,0:T(8,128)(2,1)S(1)} %collective-permute-done.9.refs_1_, ...), custom_call_target="tpu_custom_call" | custom-call | tf_op jit(solution)/shard_map/attend/pallas_call | solution.py:251
  (2 shorter events, 0.0 us)
Async XLA Ops:
  0.0 10.1 %collective-permute-start = (bf16[8,16,4096]{2,1,0:T(8,128)(2,1)}, bf16[8,16,4096]{2,1,0:T(8,128)(2,1)S(1)}, u32[]{:S(2)}, u32[]{:S(2)}) collective-permute-start(bf16[8,16,4096]{2,1,0:T(8,128)(2,1)} %refs_3_.2), channel_id=1, source_target_pairs={{0,1},{1,0},{2,3},{3,2},{4,5},{5,4},{6,7},{7,6},{8,9},{9,8},{10,11... | collective-permute-start | bytes 3145736 | tf_op jit(solution)/shard_map/ppermute | solution.py:178
  0.5 8.7 %collective-permute-start.3 = (bf16[2,8192]{1,0:T(2,128)(2,1)}, bf16[2,8192]{1,0:T(2,128)(2,1)S(1)}, u32[]{:S(2)}, u32[]{:S(2)}) collective-permute-start(bf16[2,8192]{1,0:T(2,128)(2,1)} %refs_1_.1), channel_id=1, source_target_pairs={{0,14},{1,13},{2,12},{3,15},{4,10},{5,9},{6,8},{7,11},{8,6},{9,5},... | collective-permute-start | bytes 98312 | tf_op jit(solution)/shard_map/ppermute | solution.py:175
  6.0 4.1 %collective-permute-start.4 = (bf16[2,8192]{1,0:T(2,128)(2,1)}, bf16[2,8192]{1,0:T(2,128)(2,1)S(1)}, u32[]{:S(2)}, u32[]{:S(2)}) collective-permute-start(bf16[2,8192]{1,0:T(2,128)(2,1)} %refs_1_.1), channel_id=1, source_target_pairs={{0,2},{1,7},{2,0},{3,5},{4,6},{5,3},{6,4},{7,1},{8,10},{9,15},{10,... | collective-permute-start | bytes 98312 | tf_op jit(solution)/shard_map/ppermute | solution.py:175
  6.5 8.3 %collective-permute-start.1 = (bf16[2,8192]{1,0:T(2,128)(2,1)}, bf16[2,8192]{1,0:T(2,128)(2,1)S(1)}, u32[]{:S(2)}, u32[]{:S(2)}) collective-permute-start(bf16[2,8192]{1,0:T(2,128)(2,1)} %refs_1_.1), channel_id=1, source_target_pairs={{0,8},{1,11},{2,10},{3,9},{4,12},{5,15},{6,14},{7,13},{8,0},{9,3},... | collective-permute-start | bytes 98312 | tf_op jit(solution)/shard_map/ppermute | solution.py:175
  6.5 8.3 %collective-permute-start.2 = (bf16[2,8192]{1,0:T(2,128)(2,1)}, bf16[2,8192]{1,0:T(2,128)(2,1)S(1)}, u32[]{:S(2)}, u32[]{:S(2)}) collective-permute-start(bf16[2,8192]{1,0:T(2,128)(2,1)} %refs_1_.1), channel_id=1, source_target_pairs={{0,4},{1,5},{2,6},{3,7},{4,0},{5,1},{6,2},{7,3},{8,12},{9,13},{10,... | collective-permute-start | bytes 98312 | tf_op jit(solution)/shard_map/ppermute | solution.py:175
  10.8 9.7 %collective-permute-start.5 = (bf16[2,2,32,128]{3,2,1,0:T(8,128)(2,1)S(1)}, bf16[2,2,32,128]{3,2,1,0:T(8,128)(2,1)S(1)}, u32[]{:S(2)}, u32[]{:S(2)}) collective-permute-start(bf16[2,2,32,128]{3,2,1,0:T(8,128)(2,1)S(1)} %get-tuple-element.20.refs_3_), channel_id=1, source_target_pairs={{0,14},{1,13},{2,12},{3,15},{4,10},{5,9},{6,8},{7,11},{8,6},{9,5},... | collective-permute-start | bytes 98312 | tf_op jit(solution)/shard_map/ppermute | solution.py:175
  14.8 5.9 %copy-start.3 = (s32[2]{0:T(128)S(1)}, s32[2]{0:T(128)}, u32[]{:S(2)}) copy-start(s32[2]{0:T(128)} %param.15) | copy-start | bytes 28
  14.8 6.0 %copy-start.2 = (bf16[2,4096]{1,0:T(2,128)(2,1)S(1)}, bf16[2,4096]{1,0:T(2,128)(2,1)}, u32[]{:S(2)}) copy-start(bf16[2,4096]{1,0:T(2,128)(2,1)} %param.9) | copy-start | bytes 49156
  14.8 7.1 %copy-start = (bf16[2,4,256,128]{3,2,1,0:T(8,128)(2,1)S(1)}, bf16[2,4,256,128]{3,2,1,0:T(8,128)(2,1)}, u32[]{:S(2)}) copy-start(bf16[2,4,256,128]{3,2,1,0:T(8,128)(2,1)} %refs_2_.3) | copy-start | bytes 1572868
  14.8 7.1 %copy-start.1 = (bf16[2,4,256,128]{3,2,1,0:T(8,128)(2,1)S(1)}, bf16[2,4,256,128]{3,2,1,0:T(8,128)(2,1)}, u32[]{:S(2)}) copy-start(bf16[2,4,256,128]{3,2,1,0:T(8,128)(2,1)} %refs_3_.3) | copy-start | bytes 1572868
  15.6 4.9 %collective-permute-start.7 = (bf16[2,2,32,128]{3,2,1,0:T(8,128)(2,1)S(1)}, bf16[2,2,32,128]{3,2,1,0:T(8,128)(2,1)S(1)}, u32[]{:S(2)}, u32[]{:S(2)}) collective-permute-start(bf16[2,2,32,128]{3,2,1,0:T(8,128)(2,1)S(1)} %get-tuple-element.23), channel_id=1, source_target_pairs={{0,8},{1,11},{2,10},{3,9},{4,12},{5,15},{6,14},{7,13},{8,0},{9,3},... | collective-permute-start | bytes 98312 | tf_op jit(solution)/shard_map/ppermute | solution.py:175
  15.7 4.8 %collective-permute-start.8 = (bf16[2,2,32,128]{3,2,1,0:T(8,128)(2,1)S(1)}, bf16[2,2,32,128]{3,2,1,0:T(8,128)(2,1)S(1)}, u32[]{:S(2)}, u32[]{:S(2)}) collective-permute-start(bf16[2,2,32,128]{3,2,1,0:T(8,128)(2,1)S(1)} %get-tuple-element.24), channel_id=1, source_target_pairs={{0,4},{1,5},{2,6},{3,7},{4,0},{5,1},{6,2},{7,3},{8,12},{9,13},{10,... | collective-permute-start | bytes 98312 | tf_op jit(solution)/shard_map/ppermute | solution.py:175
  16.7 3.9 %collective-permute-start.6 = (bf16[2,2,32,128]{3,2,1,0:T(8,128)(2,1)S(1)}, bf16[2,2,32,128]{3,2,1,0:T(8,128)(2,1)S(1)}, u32[]{:S(2)}, u32[]{:S(2)}) collective-permute-start(bf16[2,2,32,128]{3,2,1,0:T(8,128)(2,1)S(1)} %get-tuple-element.22), channel_id=1, source_target_pairs={{0,2},{1,7},{2,0},{3,5},{4,6},{5,3},{6,4},{7,1},{8,10},{9,15},{10,... | collective-permute-start | bytes 98312 | tf_op jit(solution)/shard_map/ppermute | solution.py:175
  20.7 1.2 %collective-permute-start.9 = (bf16[2,32,128]{2,1,0:T(8,128)(2,1)S(1)}, bf16[2,32,128]{2,1,0:T(8,128)(2,1)S(1)}, u32[]{:S(2)}, u32[]{:S(2)}) collective-permute-start(bf16[2,32,128]{2,1,0:T(8,128)(2,1)S(1)} %get-tuple-element.26), channel_id=1, source_target_pairs={{0,1},{1,0},{2,3},{3,2},{4,5},{5,4},{6,7},{7,6},{8,9},{9,8},{10,11... | collective-permute-start | bytes 49160 | tf_op jit(solution)/shard_map/ppermute | solution.py:178

commit v9 on v8

--- a/solution.py
+++ b/solution.py
@@ -21,30 +21,65 @@
 SHARED = [turn for turn in range(SENT + 1) if TURNS[0][turn] == TURNS[1][turn]][0]
 
 
-def fetch_kernel(*refs):
-    *pairs, arrived = refs
-    half = len(pairs) // 2
-    copies = [
-        pltpu.make_async_copy(source, target, arrived.at[i])
-        for i, (source, target) in enumerate(zip(pairs[:half], pairs[half:]))
-    ]
-    for copy in copies:
-        copy.start()
-    for copy in copies:
-        copy.wait()
-
-
-def fetch(name, *arrays):
+def fetch_kernel(
+    ids_hbm, own_hbm, down_hbm, up_hbm, ids_ref, own_ref, down_ref, up_ref, used_ref, arrived
+):
+    count = down_ref.shape[0]
+    first = lax.axis_index("store") * count
+    own = pltpu.make_async_copy(own_hbm, own_ref, arrived.at[2 * count])
+    own.start()
+    ids = pltpu.make_async_copy(ids_hbm, ids_ref, arrived.at[2 * count + 1])
+    ids.start()
+
+    def adapter(slot):
+        return (
+            pltpu.make_async_copy(down_hbm.at[slot], down_ref.at[slot], arrived.at[slot]),
+            pltpu.make_async_copy(up_hbm.at[slot], up_ref.at[slot], arrived.at[count + slot]),
+        )
+
+    for slot in range(count):
+        used_ref[slot] = 0
+    ids.wait()
+    for request in range(ids_ref.shape[0]):
+        slot = ids_ref[request] - first
+
+        @pl.when((slot >= 0) & (slot < count))
+        def _():
+            used_ref[slot] = 1
+
+    for slot in range(count):
+
+        @pl.when(used_ref[slot] == 1)
+        def _():
+            for copy in adapter(slot):
+                copy.start()
+
+    for slot in range(count):
+
+        @pl.when(used_ref[slot] == 1)
+        def _():
+            for copy in adapter(slot):
+                copy.wait()
+
+    own.wait()
+
+
+def fetch(ids, own, down, up):
+    arrays = (ids, own, down, up)
     size = sum(array.size * array.dtype.itemsize for array in arrays)
     return pl.pallas_call(
         fetch_kernel,
-        out_shape=[pltpu.VMEM(array.shape, array.dtype) for array in arrays],
+        out_shape=[pltpu.SMEM(ids.shape, ids.dtype)]
+        + [pltpu.VMEM(array.shape, array.dtype) for array in arrays[1:]],
         in_specs=[pl.BlockSpec(memory_space=pl.ANY)] * len(arrays),
-        out_specs=[VMEM] * len(arrays),
-        scratch_shapes=[pltpu.SemaphoreType.DMA((len(arrays),))],
+        out_specs=[SMEM, VMEM, VMEM, VMEM],
+        scratch_shapes=[
+            pltpu.SMEM((down.shape[0],), jnp.int32),
+            pltpu.SemaphoreType.DMA((2 * down.shape[0] + 2,)),
+        ],
         compiler_params=PARAMS,
         cost_estimate=pl.CostEstimate(flops=0, transcendentals=0, bytes_accessed=2 * size),
-        name=name,
+        name="fetch",
     )(*[pltpu.with_memory_space_constraint(array, pltpu.HBM) for array in arrays])
 
 
@@ -179,7 +214,7 @@
 
     states = [visit(hidden, turn) for turn in range(SENT)]
     other = swap(adapter_up)
-    ids, own, down, up = fetch("fetch", adapter_ids, hidden, adapter_down, adapter_up)
+    ids, own, down, up = fetch(adapter_ids, hidden, adapter_down, adapter_up)
     other = near(other)
     wide = (rows, cores, heads, head_size)
 

time: 23.2 us -> 22.5 us (0.970)
  waiting for transfers between devices: 5.07 us -> 4.63 us
  Pallas kernels: 4.59 us -> 4.27 us
    pallas_call x2, Pallas kernels: 1.47 us -> 0.82 us  [work(): pl.pallas_call(functools.partial(owner_kernel, turns), out_shape=[jax.Sha...]
    ppermute x8, waiting for transfers between devices: 3.99 us -> 3.55 us  [visit(): return lax.ppermute(array, ('store', 'tensor'), turn_pairs(turn))]
    pallas_call x1, Pallas kernels: 1.92 us -> 2.25 us  [fetch(): pl.pallas_call(fetch_kernel, out_shape=[pltpu.SMEM(ids.shape, ids.dtype)]...]
  transfers between devices with their start and end apart: 10 -> 10, of which waited for: 4 -> 3; matrix products, arithmetic and copies ran while one was open for 0% -> 0% of each run, Pallas kernels for 15% -> 14%
where the time goes in v9:
time: 22.5 us; the launch traced here: 22.3 us
  starting transfers between devices  13.2 us (59%)
  waiting for transfers between devices  4.63 us (21%)
  Pallas kernels  4.27 us (19%)
    ppermute x8, starting transfers between devices, visit(): return lax.ppermute(array, ('store', 'tensor'), turn_pairs(turn))  12.7 us
    ppermute x8, waiting for transfers between devices, visit(): return lax.ppermute(array, ('store', 'tensor'), turn_pairs(turn))  3.55 us
    pallas_call x1, Pallas kernels, fetch(): pl.pallas_call(fetch_kernel, out_shape=[pltpu.SMEM(ids.shape, ids.dtype)]...  2.25 us
    pallas_call x1, Pallas kernels, per_device(): pl.pallas_call(functools.partial(attend_kernel, len(deltas)), out_shape=j...  1.16 us
    ppermute x2, waiting for transfers between devices, swap(): return lax.ppermute(array, 'tensor', [(0, 1), (1, 0)])  1.08 us
    pallas_call x2, Pallas kernels, work(): pl.pallas_call(functools.partial(owner_kernel, turns), out_shape=[jax.Sha...  0.82 us
    ppermute x2, starting transfers between devices, swap(): return lax.ppermute(array, 'tensor', [(0, 1), (1, 0)])  0.52 us
  transfers between devices with their start and end apart: 10, of which 3 were waited for; matrix products, arithmetic and copies ran while one was open for 0% of the time, Pallas kernels for 14%

profile of v9, /device:TPU:0, one launch (start us, length us, event | category | flops | bytes accessed | tf_op | source)
XLA Modules:
  0.0 22.3 jit_solution(6698718248967470326)
XLA Ops:
  0.0 0.5 %collective-permute-start = (bf16[8,16,4096]{2,1,0:T(8,128)(2,1)}, bf16[8,16,4096]{2,1,0:T(8,128)(2,1)S(1)}, u32[]{:S(2)}, u32[]{:S(2)}) collective-permute-start(bf16[8,16,4096]{2,1,0:T(8,128)(2,1)} %up_hbm.1), channel_id=1, source_target_pairs={{0,1},{1,0},{2,3},{3,2},{4,5},{5,4},{6,7},{7,6},{8,9},{9,8},{10,11... | collective-permute-start | bytes 3145736 | tf_op jit(solution)/shard_map/ppermute | solution.py:213
  0.5 5.5 %collective-permute-start.3 = (bf16[2,8192]{1,0:T(2,128)(2,1)}, bf16[2,8192]{1,0:T(2,128)(2,1)S(1)}, u32[]{:S(2)}, u32[]{:S(2)}) collective-permute-start(bf16[2,8192]{1,0:T(2,128)(2,1)} %own_hbm.1), channel_id=1, source_target_pairs={{0,14},{1,13},{2,12},{3,15},{4,10},{5,9},{6,8},{7,11},{8,6},{9,5},... | collective-permute-start | bytes 98312 | tf_op jit(solution)/shard_map/ppermute | solution.py:210
  6.0 0.5 %collective-permute-start.4 = (bf16[2,8192]{1,0:T(2,128)(2,1)}, bf16[2,8192]{1,0:T(2,128)(2,1)S(1)}, u32[]{:S(2)}, u32[]{:S(2)}) collective-permute-start(bf16[2,8192]{1,0:T(2,128)(2,1)} %own_hbm.1), channel_id=1, source_target_pairs={{0,2},{1,7},{2,0},{3,5},{4,6},{5,3},{6,4},{7,1},{8,10},{9,15},{10,... | collective-permute-start | bytes 98312 | tf_op jit(solution)/shard_map/ppermute | solution.py:210
  6.5 0.0 collective-permute-start.1
  6.5 0.7 %collective-permute-start.2 = (bf16[2,8192]{1,0:T(2,128)(2,1)}, bf16[2,8192]{1,0:T(2,128)(2,1)S(1)}, u32[]{:S(2)}, u32[]{:S(2)}) collective-permute-start(bf16[2,8192]{1,0:T(2,128)(2,1)} %own_hbm.1), channel_id=1, source_target_pairs={{0,4},{1,5},{2,6},{3,7},{4,0},{5,1},{6,2},{7,3},{8,12},{9,13},{10,... | collective-permute-start | bytes 98312 | tf_op jit(solution)/shard_map/ppermute | solution.py:210
  7.2 2.2 %fetch.1 = (s32[16]{0:T(128)S(4)}, bf16[2,8192]{1,0:T(2,128)(2,1)S(1)}, bf16[8,16,8192]{2,1,0:T(8,128)(2,1)S(1)}, bf16[8,16,4096]{2,1,0:T(8,128)(2,1)S(1)}) custom-call(s32[16]{0:T(128)} %ids_hbm.1, bf16[2,8192]{1,0:T(2,128)(2,1)} %own_hbm.1, bf16[8,16,8192]{2,1,0:T(8,128)(2,1)} %down_hbm.1, bf16[8,16,4096]{2,1,0:T(8,128)(2,1)} %up_hbm.1), custom_call_target="tpu_custom_call" | custom-call | bytes 6357120 | tf_op jit(solution)/shard_map/fetch/pallas_call | solution.py:70
  9.4 0.0 collective-permute-done.3.refs_0_
  9.4 0.7 %collective-permute-done.4.refs_1_ = bf16[2,8192]{1,0:T(2,128)(2,1)S(1)} collective-permute-done((bf16[2,8192]{1,0:T(2,128)(2,1)}, bf16[2,8192]{1,0:T(2,128)(2,1)S(1)}, u32[]{:S(2)}, u32[]{:S(2)}) %collective-permute-start.4) | collective-permute-done | bytes 32800 | tf_op jit(solution)/shard_map/ppermute | solution.py:210
  10.1 0.0 collective-permute-done.other_ref
  10.1 0.3 %owner_far.1 = (bf16[2,2,32,128]{3,2,1,0:T(8,128)(2,1)S(1)}, bf16[2,2,32,128]{3,2,1,0:T(8,128)(2,1)S(1)}) custom-call(s32[16]{0:T(128)S(4)} %get-tuple-element.16.ids_ref, bf16[8,16,8192]{2,1,0:T(8,128)(2,1)S(1)} %get-tuple-element.17.down_ref, bf16[8,16,4096]{2,1,0:T(8,128)(2,1)S(1)} %get-tuple-element.18.mine_ref, ...), custom_call_target="tpu_custom_call" | custom-call | tf_op jit(solution)/shard_map/owner_far/pallas_call | solution.py:223
  10.5 4.0 %collective-permute-start.5 = (bf16[2,2,32,128]{3,2,1,0:T(8,128)(2,1)S(1)}, bf16[2,2,32,128]{3,2,1,0:T(8,128)(2,1)S(1)}, u32[]{:S(2)}, u32[]{:S(2)}) collective-permute-start(bf16[2,2,32,128]{3,2,1,0:T(8,128)(2,1)S(1)} %get-tuple-element.20.refs_3_), channel_id=1, source_target_pairs={{0,14},{1,13},{2,12},{3,15},{4,10},{5,9},{6,8},{7,11},{8,6},{9,5},... | collective-permute-start | bytes 98312 | tf_op jit(solution)/shard_map/ppermute | solution.py:210
  14.4 0.0 collective-permute-done.1.refs_0_
  14.5 0.0 collective-permute-done.2.refs_1_
  14.5 0.0 copy-start.3
  14.5 0.0 copy-start.2
  14.5 0.0 copy-start
  14.5 0.0 copy-start.1
  14.5 0.5 %owner_near.1 = (bf16[2,2,32,128]{3,2,1,0:T(8,128)(2,1)S(1)}, bf16[2,2,32,128]{3,2,1,0:T(8,128)(2,1)S(1)}, bf16[2,2,32,128]{3,2,1,0:T(8,128)(2,1)S(1)}) custom-call(s32[16]{0:T(128)S(4)} %get-tuple-element.16.ids_ref, bf16[8,16,8192]{2,1,0:T(8,128)(2,1)S(1)} %get-tuple-element.17.down_ref, bf16[8,16,4096]{2,1,0:T(8,128)(2,1)S(1)} %get-tuple-element.18.mine_ref, ...), custom_call_target="tpu_custom_call" | custom-call | tf_op jit(solution)/shard_map/owner_near/pallas_call | solution.py:223
  15.0 0.1 collective-permute-start.7
  15.1 0.4 %collective-permute-start.8 = (bf16[2,2,32,128]{3,2,1,0:T(8,128)(2,1)S(1)}, bf16[2,2,32,128]{3,2,1,0:T(8,128)(2,1)S(1)}, u32[]{:S(2)}, u32[]{:S(2)}) collective-permute-start(bf16[2,2,32,128]{3,2,1,0:T(8,128)(2,1)S(1)} %get-tuple-element.24), channel_id=1, source_target_pairs={{0,4},{1,5},{2,6},{3,7},{4,0},{5,1},{6,2},{7,3},{8,12},{9,13},{10,... | collective-permute-start | bytes 98312 | tf_op jit(solution)/shard_map/ppermute | solution.py:210
  15.5 1.5 %collective-permute-start.6 = (bf16[2,2,32,128]{3,2,1,0:T(8,128)(2,1)S(1)}, bf16[2,2,32,128]{3,2,1,0:T(8,128)(2,1)S(1)}, u32[]{:S(2)}, u32[]{:S(2)}) collective-permute-start(bf16[2,2,32,128]{3,2,1,0:T(8,128)(2,1)S(1)} %get-tuple-element.22), channel_id=1, source_target_pairs={{0,2},{1,7},{2,0},{3,5},{4,6},{5,3},{6,4},{7,1},{8,10},{9,15},{10,... | collective-permute-start | bytes 98312 | tf_op jit(solution)/shard_map/ppermute | solution.py:210
  17.0 2.9 %collective-permute-done.7.refs_2_ = bf16[2,2,32,128]{3,2,1,0:T(8,128)(2,1)S(1)} collective-permute-done((bf16[2,2,32,128]{3,2,1,0:T(8,128)(2,1)S(1)}, bf16[2,2,32,128]{3,2,1,0:T(8,128)(2,1)S(1)}, u32[]{:S(2)}, u32[]{:S(2)}) %collective-permute-start.7) | collective-permute-done | bytes 32800 | tf_op jit(solution)/shard_map/ppermute | solution.py:210
  19.9 0.0 collective-permute-done.8.refs_3_
  19.9 0.0 collective-permute-done.5.refs_0_
  19.9 0.0 collective-permute-done.6.refs_1_
  19.9 0.1 collective-permute-start.9
  20.0 0.0 copy-done.3
  20.0 0.1 compare_convert_fusion.live_ref
  20.1 0.0 copy-done.2
  20.1 1.1 %collective-permute-done.9.refs_1_ = bf16[2,32,128]{2,1,0:T(8,128)(2,1)S(1)} collective-permute-done((bf16[2,32,128]{2,1,0:T(8,128)(2,1)S(1)}, bf16[2,32,128]{2,1,0:T(8,128)(2,1)S(1)}, u32[]{:S(2)}, u32[]{:S(2)}) %collective-permute-start.9) | collective-permute-done | bytes 16416 | tf_op jit(solution)/shard_map/ppermute | solution.py:213
  21.2 0.0 copy-done
  21.2 0.0 copy-done.1
  21.2 1.2 %attend.1 = bf16[2,4096]{1,0:T(2,128)(2,1)} custom-call(f32[2,1,256]{2,1,0:T(1,128)S(1)} %compare_convert_fusion.live_ref, bf16[2,32,128]{2,1,0:T(8,128)(2,1)S(1)} %bitcast.4, bf16[2,32,128]{2,1,0:T(8,128)(2,1)S(1)} %get-tuple-element.25.refs_0_, bf16[2,32,128]{2,1,0:T(8,128)(2,1)S(1)} %collective-permute-done.9.refs_1_, ...), custom_call_target="tpu_custom_call" | custom-call | tf_op jit(solution)/shard_map/attend/pallas_call | solution.py:286
  (2 shorter events, 0.0 us)
Async XLA Ops:
  0.0 10.1 %collective-permute-start = (bf16[8,16,4096]{2,1,0:T(8,128)(2,1)}, bf16[8,16,4096]{2,1,0:T(8,128)(2,1)S(1)}, u32[]{:S(2)}, u32[]{:S(2)}) collective-permute-start(bf16[8,16,4096]{2,1,0:T(8,128)(2,1)} %up_hbm.1), channel_id=1, source_target_pairs={{0,1},{1,0},{2,3},{3,2},{4,5},{5,4},{6,7},{7,6},{8,9},{9,8},{10,11... | collective-permute-start | bytes 3145736 | tf_op jit(solution)/shard_map/ppermute | solution.py:213
  0.5 9.0 %collective-permute-start.3 = (bf16[2,8192]{1,0:T(2,128)(2,1)}, bf16[2,8192]{1,0:T(2,128)(2,1)S(1)}, u32[]{:S(2)}, u32[]{:S(2)}) collective-permute-start(bf16[2,8192]{1,0:T(2,128)(2,1)} %own_hbm.1), channel_id=1, source_target_pairs={{0,14},{1,13},{2,12},{3,15},{4,10},{5,9},{6,8},{7,11},{8,6},{9,5},... | collective-permute-start | bytes 98312 | tf_op jit(solution)/shard_map/ppermute | solution.py:210
  6.0 4.1 %collective-permute-start.4 = (bf16[2,8192]{1,0:T(2,128)(2,1)}, bf16[2,8192]{1,0:T(2,128)(2,1)S(1)}, u32[]{:S(2)}, u32[]{:S(2)}) collective-permute-start(bf16[2,8192]{1,0:T(2,128)(2,1)} %own_hbm.1), channel_id=1, source_target_pairs={{0,2},{1,7},{2,0},{3,5},{4,6},{5,3},{6,4},{7,1},{8,10},{9,15},{10,... | collective-permute-start | bytes 98312 | tf_op jit(solution)/shard_map/ppermute | solution.py:210
  6.5 7.9 %collective-permute-start.1 = (bf16[2,8192]{1,0:T(2,128)(2,1)}, bf16[2,8192]{1,0:T(2,128)(2,1)S(1)}, u32[]{:S(2)}, u32[]{:S(2)}) collective-permute-start(bf16[2,8192]{1,0:T(2,128)(2,1)} %own_hbm.1), channel_id=1, source_target_pairs={{0,8},{1,11},{2,10},{3,9},{4,12},{5,15},{6,14},{7,13},{8,0},{9,3},... | collective-permute-start | bytes 98312 | tf_op jit(solution)/shard_map/ppermute | solution.py:210
  6.5 7.9 %collective-permute-start.2 = (bf16[2,8192]{1,0:T(2,128)(2,1)}, bf16[2,8192]{1,0:T(2,128)(2,1)S(1)}, u32[]{:S(2)}, u32[]{:S(2)}) collective-permute-start(bf16[2,8192]{1,0:T(2,128)(2,1)} %own_hbm.1), channel_id=1, source_target_pairs={{0,4},{1,5},{2,6},{3,7},{4,0},{5,1},{6,2},{7,3},{8,12},{9,13},{10,... | collective-permute-start | bytes 98312 | tf_op jit(solution)/shard_map/ppermute | solution.py:210
  10.5 9.4 %collective-permute-start.5 = (bf16[2,2,32,128]{3,2,1,0:T(8,128)(2,1)S(1)}, bf16[2,2,32,128]{3,2,1,0:T(8,128)(2,1)S(1)}, u32[]{:S(2)}, u32[]{:S(2)}) collective-permute-start(bf16[2,2,32,128]{3,2,1,0:T(8,128)(2,1)S(1)} %get-tuple-element.20.refs_3_), channel_id=1, source_target_pairs={{0,14},{1,13},{2,12},{3,15},{4,10},{5,9},{6,8},{7,11},{8,6},{9,5},... | collective-permute-start | bytes 98312 | tf_op jit(solution)/shard_map/ppermute | solution.py:210
  14.5 5.5 %copy-start.3 = (s32[2]{0:T(128)S(1)}, s32[2]{0:T(128)}, u32[]{:S(2)}) copy-start(s32[2]{0:T(128)} %param.15) | copy-start | bytes 28
  14.5 5.6 %copy-start.2 = (bf16[2,4096]{1,0:T(2,128)(2,1)S(1)}, bf16[2,4096]{1,0:T(2,128)(2,1)}, u32[]{:S(2)}) copy-start(bf16[2,4096]{1,0:T(2,128)(2,1)} %param.9) | copy-start | bytes 49156
  14.5 6.7 %copy-start = (bf16[2,4,256,128]{3,2,1,0:T(8,128)(2,1)S(1)}, bf16[2,4,256,128]{3,2,1,0:T(8,128)(2,1)}, u32[]{:S(2)}) copy-start(bf16[2,4,256,128]{3,2,1,0:T(8,128)(2,1)} %refs_2_.1) | copy-start | bytes 1572868
  14.5 6.7 %copy-start.1 = (bf16[2,4,256,128]{3,2,1,0:T(8,128)(2,1)S(1)}, bf16[2,4,256,128]{3,2,1,0:T(8,128)(2,1)}, u32[]{:S(2)}) copy-start(bf16[2,4,256,128]{3,2,1,0:T(8,128)(2,1)} %refs_3_.1) | copy-start | bytes 1572868
  15.0 4.9 %collective-permute-start.7 = (bf16[2,2,32,128]{3,2,1,0:T(8,128)(2,1)S(1)}, bf16[2,2,32,128]{3,2,1,0:T(8,128)(2,1)S(1)}, u32[]{:S(2)}, u32[]{:S(2)}) collective-permute-start(bf16[2,2,32,128]{3,2,1,0:T(8,128)(2,1)S(1)} %get-tuple-element.23), channel_id=1, source_target_pairs={{0,8},{1,11},{2,10},{3,9},{4,12},{5,15},{6,14},{7,13},{8,0},{9,3},... | collective-permute-start | bytes 98312 | tf_op jit(solution)/shard_map/ppermute | solution.py:210
  15.1 4.8 %collective-permute-start.8 = (bf16[2,2,32,128]{3,2,1,0:T(8,128)(2,1)S(1)}, bf16[2,2,32,128]{3,2,1,0:T(8,128)(2,1)S(1)}, u32[]{:S(2)}, u32[]{:S(2)}) collective-permute-start(bf16[2,2,32,128]{3,2,1,0:T(8,128)(2,1)S(1)} %get-tuple-element.24), channel_id=1, source_target_pairs={{0,4},{1,5},{2,6},{3,7},{4,0},{5,1},{6,2},{7,3},{8,12},{9,13},{10,... | collective-permute-start | bytes 98312 | tf_op jit(solution)/shard_map/ppermute | solution.py:210
  15.5 4.4 %collective-permute-start.6 = (bf16[2,2,32,128]{3,2,1,0:T(8,128)(2,1)S(1)}, bf16[2,2,32,128]{3,2,1,0:T(8,128)(2,1)S(1)}, u32[]{:S(2)}, u32[]{:S(2)}) collective-permute-start(bf16[2,2,32,128]{3,2,1,0:T(8,128)(2,1)S(1)} %get-tuple-element.22), channel_id=1, source_target_pairs={{0,2},{1,7},{2,0},{3,5},{4,6},{5,3},{6,4},{7,1},{8,10},{9,15},{10,... | collective-permute-start | bytes 98312 | tf_op jit(solution)/shard_map/ppermute | solution.py:210
  19.9 1.2 %collective-permute-start.9 = (bf16[2,32,128]{2,1,0:T(8,128)(2,1)S(1)}, bf16[2,32,128]{2,1,0:T(8,128)(2,1)S(1)}, u32[]{:S(2)}, u32[]{:S(2)}) collective-permute-start(bf16[2,32,128]{2,1,0:T(8,128)(2,1)S(1)} %get-tuple-element.26), channel_id=1, source_target_pairs={{0,1},{1,0},{2,3},{3,2},{4,5},{5,4},{6,7},{7,6},{8,9},{9,8},{10,11... | collective-permute-start | bytes 49160 | tf_op jit(solution)/shard_map/ppermute | solution.py:213

commit v10 on v8

--- a/solution.py
+++ b/solution.py
@@ -21,31 +21,25 @@
 SHARED = [turn for turn in range(SENT + 1) if TURNS[0][turn] == TURNS[1][turn]][0]
 
 
-def fetch_kernel(*refs):
-    *pairs, arrived = refs
-    half = len(pairs) // 2
-    copies = [
-        pltpu.make_async_copy(source, target, arrived.at[i])
-        for i, (source, target) in enumerate(zip(pairs[:half], pairs[half:]))
-    ]
-    for copy in copies:
-        copy.start()
-    for copy in copies:
-        copy.wait()
-
-
-def fetch(name, *arrays):
-    size = sum(array.size * array.dtype.itemsize for array in arrays)
+def scalars_kernel(ids_hbm, *refs):
+    ids_ref, arrived = refs[-2:]
+    copy = pltpu.make_async_copy(ids_hbm, ids_ref, arrived)
+    copy.start()
+    copy.wait()
+
+
+def scalars(ids, *beside):
+    size = sum(array.size * array.dtype.itemsize for array in beside)
     return pl.pallas_call(
-        fetch_kernel,
-        out_shape=[pltpu.VMEM(array.shape, array.dtype) for array in arrays],
-        in_specs=[pl.BlockSpec(memory_space=pl.ANY)] * len(arrays),
-        out_specs=[VMEM] * len(arrays),
-        scratch_shapes=[pltpu.SemaphoreType.DMA((len(arrays),))],
+        scalars_kernel,
+        out_shape=pltpu.SMEM(ids.shape, ids.dtype),
+        in_specs=[pl.BlockSpec(memory_space=pl.ANY)] * (1 + len(beside)),
+        out_specs=SMEM,
+        scratch_shapes=[pltpu.SemaphoreType.DMA(())],
         compiler_params=PARAMS,
-        cost_estimate=pl.CostEstimate(flops=0, transcendentals=0, bytes_accessed=2 * size),
-        name=name,
-    )(*[pltpu.with_memory_space_constraint(array, pltpu.HBM) for array in arrays])
+        cost_estimate=pl.CostEstimate(flops=0, transcendentals=0, bytes_accessed=size),
+        name="scalars",
+    )(*[pltpu.with_memory_space_constraint(array, pltpu.HBM) for array in (ids,) + beside])
 
 
 def near(array):
@@ -179,8 +173,8 @@
 
     states = [visit(hidden, turn) for turn in range(SENT)]
     other = swap(adapter_up)
-    ids, own, down, up = fetch("fetch", adapter_ids, hidden, adapter_down, adapter_up)
-    other = near(other)
+    ids = scalars(adapter_ids, adapter_down, adapter_up)
+    down, up, other = near(adapter_down), near(adapter_up), near(other)
     wide = (rows, cores, heads, head_size)
 
     def work(name, after, *turns):
@@ -199,7 +193,7 @@
             name=name,
         )(ids, down, up, other, *[states[turn] for turn in turns], *after)
 
-    states.append(own)
+    states.append(near(hidden))
     deltas = work("owner_far", (), *range(FAR))
     deltas += work("owner_near", deltas[:1], *range(FAR, SENT + 1))
     came = [visit(delta, turn) for turn, delta in enumerate(deltas[:SENT])]

time: 23.2 us -> 22.2 us (0.957)
  Pallas kernels: 4.59 us -> 2.94 us
  waiting for transfers between devices: 5.07 us -> 5.86 us
    pallas_call x1, Pallas kernels: 1.92 us -> 0.67 us  [scalars(): pl.pallas_call(scalars_kernel, out_shape=pltpu.SMEM(ids.shape, ids.dtype)...]
    ppermute x8, waiting for transfers between devices: 3.99 us -> 4.78 us  [visit(): return lax.ppermute(array, ('store', 'tensor'), turn_pairs(turn))]
    pallas_call x2, Pallas kernels: 1.47 us -> 1.09 us  [work(): pl.pallas_call(functools.partial(owner_kernel, turns), out_shape=[jax.Sha...]
  transfers between devices with their start and end apart: 10 -> 10, of which waited for: 4 -> 5; matrix products, arithmetic and copies ran while one was open for 0% -> 0% of each run, Pallas kernels for 15% -> 8%
where the time goes in v10:
time: 22.2 us; the launch traced here: 22.1 us
  starting transfers between devices  13.1 us (59%)
  waiting for transfers between devices  5.86 us (26%)
  Pallas kernels  2.94 us (13%)
    ppermute x8, starting transfers between devices, visit(): return lax.ppermute(array, ('store', 'tensor'), turn_pairs(turn))  12.5 us
    ppermute x8, waiting for transfers between devices, visit(): return lax.ppermute(array, ('store', 'tensor'), turn_pairs(turn))  4.78 us
    pallas_call x1, Pallas kernels, per_device(): pl.pallas_call(functools.partial(attend_kernel, len(deltas)), out_shape=j...  1.16 us
    pallas_call x2, Pallas kernels, work(): pl.pallas_call(functools.partial(owner_kernel, turns), out_shape=[jax.Sha...  1.09 us
    ppermute x2, waiting for transfers between devices, swap(): return lax.ppermute(array, 'tensor', [(0, 1), (1, 0)])  1.08 us
    pallas_call x1, Pallas kernels, scalars(): pl.pallas_call(scalars_kernel, out_shape=pltpu.SMEM(ids.shape, ids.dtype)...  0.67 us
    ppermute x2, starting transfers between devices, swap(): return lax.ppermute(array, 'tensor', [(0, 1), (1, 0)])  0.52 us
  transfers between devices with their start and end apart: 10, of which 5 were waited for; matrix products, arithmetic and copies ran while one was open for 0% of the time, Pallas kernels for 8%

profile of v10, /device:TPU:0, one launch (start us, length us, event | category | flops | bytes accessed | tf_op | source)
XLA Modules:
  0.0 22.1 jit_solution(17758270935209770292)
XLA Ops:
  0.0 0.0 copy-start.1
  0.0 0.0 copy-start
  0.0 0.5 %collective-permute-start = (bf16[8,16,4096]{2,1,0:T(8,128)(2,1)}, bf16[8,16,4096]{2,1,0:T(8,128)(2,1)S(1)}, u32[]{:S(2)}, u32[]{:S(2)}) collective-permute-start(bf16[8,16,4096]{2,1,0:T(8,128)(2,1)} %mine_ref.3), channel_id=1, source_target_pairs={{0,1},{1,0},{2,3},{3,2},{4,5},{5,4},{6,7},{7,6},{8,9},{9,8},{10,11... | collective-permute-start | bytes 3145736 | tf_op jit(solution)/shard_map/ppermute | solution.py:172
  0.5 5.6 %collective-permute-start.3 = (bf16[2,8192]{1,0:T(2,128)(2,1)}, bf16[2,8192]{1,0:T(2,128)(2,1)S(1)}, u32[]{:S(2)}, u32[]{:S(2)}) collective-permute-start(bf16[2,8192]{1,0:T(2,128)(2,1)} %refs_2_.2), channel_id=1, source_target_pairs={{0,14},{1,13},{2,12},{3,15},{4,10},{5,9},{6,8},{7,11},{8,6},{9,5},... | collective-permute-start | bytes 98312 | tf_op jit(solution)/shard_map/ppermute | solution.py:169
  6.1 0.5 %collective-permute-start.4 = (bf16[2,8192]{1,0:T(2,128)(2,1)}, bf16[2,8192]{1,0:T(2,128)(2,1)S(1)}, u32[]{:S(2)}, u32[]{:S(2)}) collective-permute-start(bf16[2,8192]{1,0:T(2,128)(2,1)} %refs_2_.2), channel_id=1, source_target_pairs={{0,2},{1,7},{2,0},{3,5},{4,6},{5,3},{6,4},{7,1},{8,10},{9,15},{10,... | collective-permute-start | bytes 98312 | tf_op jit(solution)/shard_map/ppermute | solution.py:169
  6.6 0.0 collective-permute-start.1
  6.6 0.7 %collective-permute-start.2 = (bf16[2,8192]{1,0:T(2,128)(2,1)}, bf16[2,8192]{1,0:T(2,128)(2,1)S(1)}, u32[]{:S(2)}, u32[]{:S(2)}) collective-permute-start(bf16[2,8192]{1,0:T(2,128)(2,1)} %refs_2_.2), channel_id=1, source_target_pairs={{0,4},{1,5},{2,6},{3,7},{4,0},{5,1},{6,2},{7,3},{8,12},{9,13},{10,... | collective-permute-start | bytes 98312 | tf_op jit(solution)/shard_map/ppermute | solution.py:169
  7.3 0.7 %scalars.1.ids_ref = s32[16]{0:T(128)S(4)} custom-call(s32[16]{0:T(128)} %ids_hbm.1, bf16[8,16,8192]{2,1,0:T(8,128)(2,1)} %down_ref.3, bf16[8,16,4096]{2,1,0:T(8,128)(2,1)} %mine_ref.3), custom_call_target="tpu_custom_call" | custom-call | bytes 3145728 | tf_op jit(solution)/shard_map/scalars/pallas_call | solution.py:33
  7.9 0.0 copy-start.4
  8.0 0.6 %collective-permute-done.3.refs_0_ = bf16[2,8192]{1,0:T(2,128)(2,1)S(1)} collective-permute-done((bf16[2,8192]{1,0:T(2,128)(2,1)}, bf16[2,8192]{1,0:T(2,128)(2,1)S(1)}, u32[]{:S(2)}, u32[]{:S(2)}) %collective-permute-start.3) | collective-permute-done | bytes 32800 | tf_op jit(solution)/shard_map/ppermute | solution.py:169
  8.5 1.7 %collective-permute-done.4.refs_1_ = bf16[2,8192]{1,0:T(2,128)(2,1)S(1)} collective-permute-done((bf16[2,8192]{1,0:T(2,128)(2,1)}, bf16[2,8192]{1,0:T(2,128)(2,1)S(1)}, u32[]{:S(2)}, u32[]{:S(2)}) %collective-permute-start.4) | collective-permute-done | bytes 32800 | tf_op jit(solution)/shard_map/ppermute | solution.py:169
  10.2 0.0 collective-permute-done.other_ref
  10.2 0.0 copy-done.1
  10.2 0.0 copy-done
  10.2 0.4 %owner_far.1 = (bf16[2,2,32,128]{3,2,1,0:T(8,128)(2,1)S(1)}, bf16[2,2,32,128]{3,2,1,0:T(8,128)(2,1)S(1)}) custom-call(s32[16]{0:T(128)S(4)} %scalars.1.ids_ref, bf16[8,16,8192]{2,1,0:T(8,128)(2,1)S(1)} %copy-done, bf16[8,16,4096]{2,1,0:T(8,128)(2,1)S(1)} %copy-done.1, bf16[8,16,4096]{2,1,0:T(8,128)(2,1)S(1)} %collective-permute-done.other_ref, ...), custom_call_target="tpu_custom_call" | custom-call | tf_op jit(solution)/shard_map/owner_far/pallas_call | solution.py:182
  10.6 0.0 copy-start.6
  10.6 0.0 copy-start.5
  10.6 0.0 copy-start.2
  10.6 0.0 copy-start.3
  10.6 2.9 %collective-permute-start.5 = (bf16[2,2,32,128]{3,2,1,0:T(8,128)(2,1)S(1)}, bf16[2,2,32,128]{3,2,1,0:T(8,128)(2,1)S(1)}, u32[]{:S(2)}, u32[]{:S(2)}) collective-permute-start(bf16[2,2,32,128]{3,2,1,0:T(8,128)(2,1)S(1)} %get-tuple-element.12.refs_3_), channel_id=1, source_target_pairs={{0,14},{1,13},{2,12},{3,15},{4,10},{5,9},{6,8},{7,11},{8,6},{9,5},... | collective-permute-start | bytes 98312 | tf_op jit(solution)/shard_map/ppermute | solution.py:169
  13.5 0.0 collective-permute-done.1.refs_0_
  13.6 0.0 collective-permute-done.2.refs_1_
  13.6 0.0 copy-done.4
  13.6 0.7 %owner_near.1 = (bf16[2,2,32,128]{3,2,1,0:T(8,128)(2,1)S(1)}, bf16[2,2,32,128]{3,2,1,0:T(8,128)(2,1)S(1)}, bf16[2,2,32,128]{3,2,1,0:T(8,128)(2,1)S(1)}) custom-call(s32[16]{0:T(128)S(4)} %scalars.1.ids_ref, bf16[8,16,8192]{2,1,0:T(8,128)(2,1)S(1)} %copy-done, bf16[8,16,4096]{2,1,0:T(8,128)(2,1)S(1)} %copy-done.1, ...), custom_call_target="tpu_custom_call" | custom-call | tf_op jit(solution)/shard_map/owner_near/pallas_call | solution.py:182
  14.3 0.1 collective-permute-start.7
  14.4 1.4 %collective-permute-start.8 = (bf16[2,2,32,128]{3,2,1,0:T(8,128)(2,1)S(1)}, bf16[2,2,32,128]{3,2,1,0:T(8,128)(2,1)S(1)}, u32[]{:S(2)}, u32[]{:S(2)}) collective-permute-start(bf16[2,2,32,128]{3,2,1,0:T(8,128)(2,1)S(1)} %get-tuple-element.16), channel_id=1, source_target_pairs={{0,4},{1,5},{2,6},{3,7},{4,0},{5,1},{6,2},{7,3},{8,12},{9,13},{10,... | collective-permute-start | bytes 98312 | tf_op jit(solution)/shard_map/ppermute | solution.py:169
  15.7 1.4 %collective-permute-start.6 = (bf16[2,2,32,128]{3,2,1,0:T(8,128)(2,1)S(1)}, bf16[2,2,32,128]{3,2,1,0:T(8,128)(2,1)S(1)}, u32[]{:S(2)}, u32[]{:S(2)}) collective-permute-start(bf16[2,2,32,128]{3,2,1,0:T(8,128)(2,1)S(1)} %get-tuple-element.14), channel_id=1, source_target_pairs={{0,2},{1,7},{2,0},{3,5},{4,6},{5,3},{6,4},{7,1},{8,10},{9,15},{10,... | collective-permute-start | bytes 98312 | tf_op jit(solution)/shard_map/ppermute | solution.py:169
  17.1 2.0 %collective-permute-done.7.refs_2_ = bf16[2,2,32,128]{3,2,1,0:T(8,128)(2,1)S(1)} collective-permute-done((bf16[2,2,32,128]{3,2,1,0:T(8,128)(2,1)S(1)}, bf16[2,2,32,128]{3,2,1,0:T(8,128)(2,1)S(1)}, u32[]{:S(2)}, u32[]{:S(2)}) %collective-permute-start.7) | collective-permute-done | bytes 32800 | tf_op jit(solution)/shard_map/ppermute | solution.py:169
  19.2 0.0 collective-permute-done.8.refs_3_
  19.2 0.0 collective-permute-done.5.refs_0_
  19.2 0.5 %collective-permute-done.6.refs_1_ = bf16[2,2,32,128]{3,2,1,0:T(8,128)(2,1)S(1)} collective-permute-done((bf16[2,2,32,128]{3,2,1,0:T(8,128)(2,1)S(1)}, bf16[2,2,32,128]{3,2,1,0:T(8,128)(2,1)S(1)}, u32[]{:S(2)}, u32[]{:S(2)}) %collective-permute-start.6) | collective-permute-done | bytes 32800 | tf_op jit(solution)/shard_map/ppermute | solution.py:169
  19.7 0.1 collective-permute-start.9
  19.8 0.0 copy-done.6
  19.8 0.1 compare_convert_fusion.live_ref
  19.8 0.0 copy-done.5
  19.9 1.1 %collective-permute-done.9.refs_1_ = bf16[2,32,128]{2,1,0:T(8,128)(2,1)S(1)} collective-permute-done((bf16[2,32,128]{2,1,0:T(8,128)(2,1)S(1)}, bf16[2,32,128]{2,1,0:T(8,128)(2,1)S(1)}, u32[]{:S(2)}, u32[]{:S(2)}) %collective-permute-start.9) | collective-permute-done | bytes 16416 | tf_op jit(solution)/shard_map/ppermute | solution.py:172
  20.9 0.0 copy-done.2
  20.9 0.0 copy-done.3
  20.9 1.2 %attend.1 = bf16[2,4096]{1,0:T(2,128)(2,1)} custom-call(f32[2,1,256]{2,1,0:T(1,128)S(1)} %compare_convert_fusion.live_ref, bf16[2,32,128]{2,1,0:T(8,128)(2,1)S(1)} %bitcast.4, bf16[2,32,128]{2,1,0:T(8,128)(2,1)S(1)} %get-tuple-element.17.refs_0_, bf16[2,32,128]{2,1,0:T(8,128)(2,1)S(1)} %collective-permute-done.9.refs_1_, ...), custom_call_target="tpu_custom_call" | custom-call | tf_op jit(solution)/shard_map/attend/pallas_call | solution.py:245
  (2 shorter events, 0.0 us)
Async XLA Ops:
  0.0 10.2 %copy-start.1 = (bf16[8,16,4096]{2,1,0:T(8,128)(2,1)S(1)}, bf16[8,16,4096]{2,1,0:T(8,128)(2,1)}, u32[]{:S(2)}) copy-start(bf16[8,16,4096]{2,1,0:T(8,128)(2,1)} %mine_ref.3) | copy-start | bytes 3145732
  0.0 10.2 %copy-start = (bf16[8,16,8192]{2,1,0:T(8,128)(2,1)S(1)}, bf16[8,16,8192]{2,1,0:T(8,128)(2,1)}, u32[]{:S(2)}) copy-start(bf16[8,16,8192]{2,1,0:T(8,128)(2,1)} %down_ref.3) | copy-start | bytes 6291460
  0.0 10.2 %collective-permute-start = (bf16[8,16,4096]{2,1,0:T(8,128)(2,1)}, bf16[8,16,4096]{2,1,0:T(8,128)(2,1)S(1)}, u32[]{:S(2)}, u32[]{:S(2)}) collective-permute-start(bf16[8,16,4096]{2,1,0:T(8,128)(2,1)} %mine_ref.3), channel_id=1, source_target_pairs={{0,1},{1,0},{2,3},{3,2},{4,5},{5,4},{6,7},{7,6},{8,9},{9,8},{10,11... | collective-permute-start | bytes 3145736 | tf_op jit(solution)/shard_map/ppermute | solution.py:172
  0.5 8.0 %collective-permute-start.3 = (bf16[2,8192]{1,0:T(2,128)(2,1)}, bf16[2,8192]{1,0:T(2,128)(2,1)S(1)}, u32[]{:S(2)}, u32[]{:S(2)}) collective-permute-start(bf16[2,8192]{1,0:T(2,128)(2,1)} %refs_2_.2), channel_id=1, source_target_pairs={{0,14},{1,13},{2,12},{3,15},{4,10},{5,9},{6,8},{7,11},{8,6},{9,5},... | collective-permute-start | bytes 98312 | tf_op jit(solution)/shard_map/ppermute | solution.py:169
  6.1 4.1 %collective-permute-start.4 = (bf16[2,8192]{1,0:T(2,128)(2,1)}, bf16[2,8192]{1,0:T(2,128)(2,1)S(1)}, u32[]{:S(2)}, u32[]{:S(2)}) collective-permute-start(bf16[2,8192]{1,0:T(2,128)(2,1)} %refs_2_.2), channel_id=1, source_target_pairs={{0,2},{1,7},{2,0},{3,5},{4,6},{5,3},{6,4},{7,1},{8,10},{9,15},{10,... | collective-permute-start | bytes 98312 | tf_op jit(solution)/shard_map/ppermute | solution.py:169
  6.6 7.0 %collective-permute-start.1 = (bf16[2,8192]{1,0:T(2,128)(2,1)}, bf16[2,8192]{1,0:T(2,128)(2,1)S(1)}, u32[]{:S(2)}, u32[]{:S(2)}) collective-permute-start(bf16[2,8192]{1,0:T(2,128)(2,1)} %refs_2_.2), channel_id=1, source_target_pairs={{0,8},{1,11},{2,10},{3,9},{4,12},{5,15},{6,14},{7,13},{8,0},{9,3},... | collective-permute-start | bytes 98312 | tf_op jit(solution)/shard_map/ppermute | solution.py:169
  6.6 7.0 %collective-permute-start.2 = (bf16[2,8192]{1,0:T(2,128)(2,1)}, bf16[2,8192]{1,0:T(2,128)(2,1)S(1)}, u32[]{:S(2)}, u32[]{:S(2)}) collective-permute-start(bf16[2,8192]{1,0:T(2,128)(2,1)} %refs_2_.2), channel_id=1, source_target_pairs={{0,4},{1,5},{2,6},{3,7},{4,0},{5,1},{6,2},{7,3},{8,12},{9,13},{10,... | collective-permute-start | bytes 98312 | tf_op jit(solution)/shard_map/ppermute | solution.py:169
  7.9 5.6 %copy-start.4 = (bf16[2,8192]{1,0:T(2,128)(2,1)S(1)}, bf16[2,8192]{1,0:T(2,128)(2,1)}, u32[]{:S(2)}) copy-start(bf16[2,8192]{1,0:T(2,128)(2,1)} %refs_2_.2) | copy-start | bytes 98308
  10.6 9.2 %copy-start.6 = (s32[2]{0:T(128)S(1)}, s32[2]{0:T(128)}, u32[]{:S(2)}) copy-start(s32[2]{0:T(128)} %param.15) | copy-start | bytes 28
  10.6 9.2 %copy-start.5 = (bf16[2,4096]{1,0:T(2,128)(2,1)S(1)}, bf16[2,4096]{1,0:T(2,128)(2,1)}, u32[]{:S(2)}) copy-start(bf16[2,4096]{1,0:T(2,128)(2,1)} %param.9) | copy-start | bytes 49156
  10.6 10.3 %copy-start.2 = (bf16[2,4,256,128]{3,2,1,0:T(8,128)(2,1)S(1)}, bf16[2,4,256,128]{3,2,1,0:T(8,128)(2,1)}, u32[]{:S(2)}) copy-start(bf16[2,4,256,128]{3,2,1,0:T(8,128)(2,1)} %refs_2_.3) | copy-start | bytes 1572868
  10.6 10.3 %copy-start.3 = (bf16[2,4,256,128]{3,2,1,0:T(8,128)(2,1)S(1)}, bf16[2,4,256,128]{3,2,1,0:T(8,128)(2,1)}, u32[]{:S(2)}) copy-start(bf16[2,4,256,128]{3,2,1,0:T(8,128)(2,1)} %refs_3_.1) | copy-start | bytes 1572868
  10.6 8.5 %collective-permute-start.5 = (bf16[2,2,32,128]{3,2,1,0:T(8,128)(2,1)S(1)}, bf16[2,2,32,128]{3,2,1,0:T(8,128)(2,1)S(1)}, u32[]{:S(2)}, u32[]{:S(2)}) collective-permute-start(bf16[2,2,32,128]{3,2,1,0:T(8,128)(2,1)S(1)} %get-tuple-element.12.refs_3_), channel_id=1, source_target_pairs={{0,14},{1,13},{2,12},{3,15},{4,10},{5,9},{6,8},{7,11},{8,6},{9,5},... | collective-permute-start | bytes 98312 | tf_op jit(solution)/shard_map/ppermute | solution.py:169
  14.3 4.9 %collective-permute-start.7 = (bf16[2,2,32,128]{3,2,1,0:T(8,128)(2,1)S(1)}, bf16[2,2,32,128]{3,2,1,0:T(8,128)(2,1)S(1)}, u32[]{:S(2)}, u32[]{:S(2)}) collective-permute-start(bf16[2,2,32,128]{3,2,1,0:T(8,128)(2,1)S(1)} %get-tuple-element.15), channel_id=1, source_target_pairs={{0,8},{1,11},{2,10},{3,9},{4,12},{5,15},{6,14},{7,13},{8,0},{9,3},... | collective-permute-start | bytes 98312 | tf_op jit(solution)/shard_map/ppermute | solution.py:169
  14.4 4.8 %collective-permute-start.8 = (bf16[2,2,32,128]{3,2,1,0:T(8,128)(2,1)S(1)}, bf16[2,2,32,128]{3,2,1,0:T(8,128)(2,1)S(1)}, u32[]{:S(2)}, u32[]{:S(2)}) collective-permute-start(bf16[2,2,32,128]{3,2,1,0:T(8,128)(2,1)S(1)} %get-tuple-element.16), channel_id=1, source_target_pairs={{0,4},{1,5},{2,6},{3,7},{4,0},{5,1},{6,2},{7,3},{8,12},{9,13},{10,... | collective-permute-start | bytes 98312 | tf_op jit(solution)/shard_map/ppermute | solution.py:169
  15.7 3.9 %collective-permute-start.6 = (bf16[2,2,32,128]{3,2,1,0:T(8,128)(2,1)S(1)}, bf16[2,2,32,128]{3,2,1,0:T(8,128)(2,1)S(1)}, u32[]{:S(2)}, u32[]{:S(2)}) collective-permute-start(bf16[2,2,32,128]{3,2,1,0:T(8,128)(2,1)S(1)} %get-tuple-element.14), channel_id=1, source_target_pairs={{0,2},{1,7},{2,0},{3,5},{4,6},{5,3},{6,4},{7,1},{8,10},{9,15},{10,... | collective-permute-start | bytes 98312 | tf_op jit(solution)/shard_map/ppermute | solution.py:169
  19.7 1.2 %collective-permute-start.9 = (bf16[2,32,128]{2,1,0:T(8,128)(2,1)S(1)}, bf16[2,32,128]{2,1,0:T(8,128)(2,1)S(1)}, u32[]{:S(2)}, u32[]{:S(2)}) collective-permute-start(bf16[2,32,128]{2,1,0:T(8,128)(2,1)S(1)} %get-tuple-element.18), channel_id=1, source_target_pairs={{0,1},{1,0},{2,3},{3,2},{4,5},{5,4},{6,7},{7,6},{8,9},{9,8},{10,11... | collective-permute-start | bytes 49160 | tf_op jit(solution)/shard_map/ppermute | solution.py:172

commit v11 on v10

--- a/solution.py
+++ b/solution.py
@@ -15,10 +15,10 @@
 VMEM = pl.BlockSpec(memory_space=pltpu.VMEM)
 SMEM = pl.BlockSpec(memory_space=pltpu.SMEM)
 PARAMS = pltpu.CompilerParams(vmem_limit_bytes=VMEM_LIMIT)
-TURNS = ((7, 1, 4, 2, 0), (6, 3, 5, 2, 0))
+TURNS = ((4, 1, 6, 2, 0), (5, 1, 7, 3, 0))
 SENT = len(TURNS[0]) - 1
-FAR = 2
-SHARED = [turn for turn in range(SENT + 1) if TURNS[0][turn] == TURNS[1][turn]][0]
+EARLY = 2
+SHARED = [first == second for first, second in zip(*TURNS)]
 
 
 def scalars_kernel(ids_hbm, *refs):
@@ -64,7 +64,7 @@
     owned = {}
     for i, turn in enumerate(turns):
         for row in range(rows):
-            owned[i, row] = slot_of([steps[turn] for steps in TURNS], row, turn >= SHARED)[1]
+            owned[i, row] = slot_of([steps[turn] for steps in TURNS], row, SHARED[turn])[1]
 
             @pl.when(owned[i, row])
             def _():
@@ -73,12 +73,12 @@
         delta_refs[i][...] = jnp.zeros(delta_refs[i].shape, delta_refs[i].dtype)
 
     packed = [sum(steps[turn] << (4 * i) for i, turn in enumerate(turns)) for steps in TURNS]
-    late = sum((turn >= SHARED) << i for i, turn in enumerate(turns))
+    both = sum(SHARED[turn] << i for i, turn in enumerate(turns))
 
     def one_request(index, carry):
         i, row = lax.div(index, rows), lax.rem(index, rows)
         partners = [(jnp.int32(value) >> (4 * i)) & 15 for value in packed]
-        slot, here = slot_of(partners, row, ((jnp.int32(late) >> i) & 1) == 1)
+        slot, here = slot_of(partners, row, ((jnp.int32(both) >> i) & 1) == 1)
 
         @pl.when(here)
         def _():
@@ -194,8 +194,8 @@
         )(ids, down, up, other, *[states[turn] for turn in turns], *after)
 
     states.append(near(hidden))
-    deltas = work("owner_far", (), *range(FAR))
-    deltas += work("owner_near", deltas[:1], *range(FAR, SENT + 1))
+    deltas = work("owner_first", (), *range(EARLY))
+    deltas += work("owner_rest", deltas[:1], *range(EARLY, SENT + 1))
     came = [visit(delta, turn) for turn, delta in enumerate(deltas[:SENT])]
     kept, sent = pl.pallas_call(
         merge_kernel,

time: 22.2 us -> 21.4 us (0.964)
  starting transfers between devices: 13.1 us -> 12 us
  waiting for transfers between devices: 5.86 us -> 6.65 us
  Pallas kernels: 2.94 us -> 2.46 us
    ppermute x8, starting transfers between devices: 12.5 us -> 11.5 us  [visit(): return lax.ppermute(array, ('store', 'tensor'), turn_pairs(turn))]
    ppermute x8, waiting for transfers between devices: 4.78 us -> 5.57 us  [visit(): return lax.ppermute(array, ('store', 'tensor'), turn_pairs(turn))]
    pallas_call x2, Pallas kernels: 1.09 us -> 0.6 us  [work(): pl.pallas_call(functools.partial(owner_kernel, turns), out_shape=[jax.Sha...]
  transfers between devices with their start and end apart: 10 -> 10, of which waited for: 5 -> 6; matrix products, arithmetic and copies ran while one was open for 0% -> 0% of each run, Pallas kernels for 8% -> 6%
where the time goes in v11:
time: 21.4 us; the launch traced here: 21.3 us
  starting transfers between devices  12 us (56%)
  waiting for transfers between devices  6.65 us (31%)
  Pallas kernels  2.46 us (11%)
    ppermute x8, starting transfers between devices, visit(): return lax.ppermute(array, ('store', 'tensor'), turn_pairs(turn))  11.5 us
    ppermute x8, waiting for transfers between devices, visit(): return lax.ppermute(array, ('store', 'tensor'), turn_pairs(turn))  5.57 us
    pallas_call x1, Pallas kernels, per_device(): pl.pallas_call(functools.partial(attend_kernel, len(deltas)), out_shape=j...  1.16 us
    ppermute x2, waiting for transfers between devices, swap(): return lax.ppermute(array, 'tensor', [(0, 1), (1, 0)])  1.08 us
    pallas_call x1, Pallas kernels, scalars(): pl.pallas_call(scalars_kernel, out_shape=pltpu.SMEM(ids.shape, ids.dtype)...  0.67 us
    pallas_call x2, Pallas kernels, work(): pl.pallas_call(functools.partial(owner_kernel, turns), out_shape=[jax.Sha...  0.6 us
    ppermute x2, starting transfers between devices, swap(): return lax.ppermute(array, 'tensor', [(0, 1), (1, 0)])  0.52 us
  transfers between devices with their start and end apart: 10, of which 6 were waited for; matrix products, arithmetic and copies ran while one was open for 0% of the time, Pallas kernels for 6%

profile of v11, /device:TPU:0, one launch (start us, length us, event | category | flops | bytes accessed | tf_op | source)
XLA Modules:
  0.0 21.3 jit_solution(3211165817681810223)
XLA Ops:
  0.0 0.0 copy-start.1
  0.0 0.0 copy-start
  0.0 0.5 %collective-permute-start = (bf16[8,16,4096]{2,1,0:T(8,128)(2,1)}, bf16[8,16,4096]{2,1,0:T(8,128)(2,1)S(1)}, u32[]{:S(2)}, u32[]{:S(2)}) collective-permute-start(bf16[8,16,4096]{2,1,0:T(8,128)(2,1)} %mine_ref.3), channel_id=1, source_target_pairs={{0,1},{1,0},{2,3},{3,2},{4,5},{5,4},{6,7},{7,6},{8,9},{9,8},{10,11... | collective-permute-start | bytes 3145736 | tf_op jit(solution)/shard_map/ppermute | solution.py:172
  0.5 3.7 %collective-permute-start.3 = (bf16[2,8192]{1,0:T(2,128)(2,1)}, bf16[2,8192]{1,0:T(2,128)(2,1)S(1)}, u32[]{:S(2)}, u32[]{:S(2)}) collective-permute-start(bf16[2,8192]{1,0:T(2,128)(2,1)} %refs_2_.2), channel_id=1, source_target_pairs={{0,8},{1,11},{2,10},{3,9},{4,12},{5,15},{6,14},{7,13},{8,0},{9,3},... | collective-permute-start | bytes 98312 | tf_op jit(solution)/shard_map/ppermute | solution.py:169
  4.1 1.5 %collective-permute-start.4 = (bf16[2,8192]{1,0:T(2,128)(2,1)}, bf16[2,8192]{1,0:T(2,128)(2,1)S(1)}, u32[]{:S(2)}, u32[]{:S(2)}) collective-permute-start(bf16[2,8192]{1,0:T(2,128)(2,1)} %refs_2_.2), channel_id=1, source_target_pairs={{0,2},{1,3},{2,0},{3,1},{4,6},{5,7},{6,4},{7,5},{8,10},{9,11},{10,... | collective-permute-start | bytes 98312 | tf_op jit(solution)/shard_map/ppermute | solution.py:169
  5.6 1.3 %collective-permute-start.1 = (bf16[2,8192]{1,0:T(2,128)(2,1)}, bf16[2,8192]{1,0:T(2,128)(2,1)S(1)}, u32[]{:S(2)}, u32[]{:S(2)}) collective-permute-start(bf16[2,8192]{1,0:T(2,128)(2,1)} %refs_2_.2), channel_id=1, source_target_pairs={{0,12},{1,15},{2,14},{3,13},{4,8},{5,11},{6,10},{7,9},{8,4},{9,7},... | collective-permute-start | bytes 98312 | tf_op jit(solution)/shard_map/ppermute | solution.py:169
  7.0 0.2 %collective-permute-start.2 = (bf16[2,8192]{1,0:T(2,128)(2,1)}, bf16[2,8192]{1,0:T(2,128)(2,1)S(1)}, u32[]{:S(2)}, u32[]{:S(2)}) collective-permute-start(bf16[2,8192]{1,0:T(2,128)(2,1)} %refs_2_.2), channel_id=1, source_target_pairs={{0,4},{1,7},{2,6},{3,5},{4,0},{5,3},{6,2},{7,1},{8,12},{9,15},{10,... | collective-permute-start | bytes 98312 | tf_op jit(solution)/shard_map/ppermute | solution.py:169
  7.2 0.7 %scalars.1.ids_ref = s32[16]{0:T(128)S(4)} custom-call(s32[16]{0:T(128)} %ids_hbm.1, bf16[8,16,8192]{2,1,0:T(8,128)(2,1)} %down_ref.3, bf16[8,16,4096]{2,1,0:T(8,128)(2,1)} %mine_ref.3), custom_call_target="tpu_custom_call" | custom-call | bytes 3145728 | tf_op jit(solution)/shard_map/scalars/pallas_call | solution.py:33
  7.9 0.0 copy-start.4
  7.9 0.0 collective-permute-done.3.refs_0_
  7.9 0.6 %collective-permute-done.4.refs_1_ = bf16[2,8192]{1,0:T(2,128)(2,1)S(1)} collective-permute-done((bf16[2,8192]{1,0:T(2,128)(2,1)}, bf16[2,8192]{1,0:T(2,128)(2,1)S(1)}, u32[]{:S(2)}, u32[]{:S(2)}) %collective-permute-start.4) | collective-permute-done | bytes 32800 | tf_op jit(solution)/shard_map/ppermute | solution.py:169
  8.5 0.0 collective-permute-done.other_ref
  8.5 0.0 copy-done.1
  8.5 0.0 copy-done
  8.5 0.4 %owner_first.1 = (bf16[2,2,32,128]{3,2,1,0:T(8,128)(2,1)S(1)}, bf16[2,2,32,128]{3,2,1,0:T(8,128)(2,1)S(1)}) custom-call(s32[16]{0:T(128)S(4)} %scalars.1.ids_ref, bf16[8,16,8192]{2,1,0:T(8,128)(2,1)S(1)} %copy-done, bf16[8,16,4096]{2,1,0:T(8,128)(2,1)S(1)} %copy-done.1, bf16[8,16,4096]{2,1,0:T(8,128)(2,1)S(1)} %collective-permute-done.other_ref, ...), custom_call_target="tpu_custom_call" | custom-call | tf_op jit(solution)/shard_map/owner_first/pallas_call | solution.py:182
  8.9 0.0 copy-start.6
  8.9 0.0 copy-start.5
  8.9 0.0 copy-start.2
  8.9 0.0 copy-start.3
  8.9 2.3 %collective-permute-start.5 = (bf16[2,2,32,128]{3,2,1,0:T(8,128)(2,1)S(1)}, bf16[2,2,32,128]{3,2,1,0:T(8,128)(2,1)S(1)}, u32[]{:S(2)}, u32[]{:S(2)}) collective-permute-start(bf16[2,2,32,128]{3,2,1,0:T(8,128)(2,1)S(1)} %get-tuple-element.12.refs_3_), channel_id=1, source_target_pairs={{0,8},{1,11},{2,10},{3,9},{4,12},{5,15},{6,14},{7,13},{8,0},{9,3},... | collective-permute-start | bytes 98312 | tf_op jit(solution)/shard_map/ppermute | solution.py:169
  11.2 0.6 %collective-permute-done.1.refs_0_ = bf16[2,8192]{1,0:T(2,128)(2,1)S(1)} collective-permute-done((bf16[2,8192]{1,0:T(2,128)(2,1)}, bf16[2,8192]{1,0:T(2,128)(2,1)S(1)}, u32[]{:S(2)}, u32[]{:S(2)}) %collective-permute-start.1) | collective-permute-done | bytes 32800 | tf_op jit(solution)/shard_map/ppermute | solution.py:169
  11.9 0.0 collective-permute-done.2.refs_1_
  11.9 0.0 copy-done.4
  11.9 0.2 owner_rest.1
  12.1 2.4 %collective-permute-start.7 = (bf16[2,2,32,128]{3,2,1,0:T(8,128)(2,1)S(1)}, bf16[2,2,32,128]{3,2,1,0:T(8,128)(2,1)S(1)}, u32[]{:S(2)}, u32[]{:S(2)}) collective-permute-start(bf16[2,2,32,128]{3,2,1,0:T(8,128)(2,1)S(1)} %get-tuple-element.15), channel_id=1, source_target_pairs={{0,12},{1,15},{2,14},{3,13},{4,8},{5,11},{6,10},{7,9},{8,4},{9,7},... | collective-permute-start | bytes 98312 | tf_op jit(solution)/shard_map/ppermute | solution.py:169
  14.5 0.0 collective-permute-start.8
  14.5 0.0 collective-permute-start.6
  14.5 3.5 %collective-permute-done.7.refs_2_ = bf16[2,2,32,128]{3,2,1,0:T(8,128)(2,1)S(1)} collective-permute-done((bf16[2,2,32,128]{3,2,1,0:T(8,128)(2,1)S(1)}, bf16[2,2,32,128]{3,2,1,0:T(8,128)(2,1)S(1)}, u32[]{:S(2)}, u32[]{:S(2)}) %collective-permute-start.7) | collective-permute-done | bytes 32800 | tf_op jit(solution)/shard_map/ppermute | solution.py:169
  18.0 0.5 %collective-permute-done.8.refs_3_ = bf16[2,2,32,128]{3,2,1,0:T(8,128)(2,1)S(1)} collective-permute-done((bf16[2,2,32,128]{3,2,1,0:T(8,128)(2,1)S(1)}, bf16[2,2,32,128]{3,2,1,0:T(8,128)(2,1)S(1)}, u32[]{:S(2)}, u32[]{:S(2)}) %collective-permute-start.8) | collective-permute-done | bytes 32800 | tf_op jit(solution)/shard_map/ppermute | solution.py:169
  18.6 0.0 collective-permute-done.5.refs_0_
  18.6 0.3 %collective-permute-done.6.refs_1_ = bf16[2,2,32,128]{3,2,1,0:T(8,128)(2,1)S(1)} collective-permute-done((bf16[2,2,32,128]{3,2,1,0:T(8,128)(2,1)S(1)}, bf16[2,2,32,128]{3,2,1,0:T(8,128)(2,1)S(1)}, u32[]{:S(2)}, u32[]{:S(2)}) %collective-permute-start.6) | collective-permute-done | bytes 32800 | tf_op jit(solution)/shard_map/ppermute | solution.py:169
  18.9 0.1 collective-permute-start.9
  19.0 0.0 copy-done.6
  19.0 0.1 compare_convert_fusion.live_ref
  19.1 0.0 copy-done.5
  19.1 1.1 %collective-permute-done.9.refs_1_ = bf16[2,32,128]{2,1,0:T(8,128)(2,1)S(1)} collective-permute-done((bf16[2,32,128]{2,1,0:T(8,128)(2,1)S(1)}, bf16[2,32,128]{2,1,0:T(8,128)(2,1)S(1)}, u32[]{:S(2)}, u32[]{:S(2)}) %collective-permute-start.9) | collective-permute-done | bytes 16416 | tf_op jit(solution)/shard_map/ppermute | solution.py:172
  20.2 0.0 copy-done.2
  20.2 0.0 copy-done.3
  20.2 1.2 %attend.1 = bf16[2,4096]{1,0:T(2,128)(2,1)} custom-call(f32[2,1,256]{2,1,0:T(1,128)S(1)} %compare_convert_fusion.live_ref, bf16[2,32,128]{2,1,0:T(8,128)(2,1)S(1)} %bitcast.4, bf16[2,32,128]{2,1,0:T(8,128)(2,1)S(1)} %get-tuple-element.17.refs_0_, bf16[2,32,128]{2,1,0:T(8,128)(2,1)S(1)} %collective-permute-done.9.refs_1_, ...), custom_call_target="tpu_custom_call" | custom-call | tf_op jit(solution)/shard_map/attend/pallas_call | solution.py:245
  (2 shorter events, 0.0 us)
Async XLA Ops:
  0.0 8.5 %copy-start.1 = (bf16[8,16,4096]{2,1,0:T(8,128)(2,1)S(1)}, bf16[8,16,4096]{2,1,0:T(8,128)(2,1)}, u32[]{:S(2)}) copy-start(bf16[8,16,4096]{2,1,0:T(8,128)(2,1)} %mine_ref.3) | copy-start | bytes 3145732
  0.0 8.5 %copy-start = (bf16[8,16,8192]{2,1,0:T(8,128)(2,1)S(1)}, bf16[8,16,8192]{2,1,0:T(8,128)(2,1)}, u32[]{:S(2)}) copy-start(bf16[8,16,8192]{2,1,0:T(8,128)(2,1)} %down_ref.3) | copy-start | bytes 6291460
  0.0 8.5 %collective-permute-start = (bf16[8,16,4096]{2,1,0:T(8,128)(2,1)}, bf16[8,16,4096]{2,1,0:T(8,128)(2,1)S(1)}, u32[]{:S(2)}, u32[]{:S(2)}) collective-permute-start(bf16[8,16,4096]{2,1,0:T(8,128)(2,1)} %mine_ref.3), channel_id=1, source_target_pairs={{0,1},{1,0},{2,3},{3,2},{4,5},{5,4},{6,7},{7,6},{8,9},{9,8},{10,11... | collective-permute-start | bytes 3145736 | tf_op jit(solution)/shard_map/ppermute | solution.py:172
  0.5 7.4 %collective-permute-start.3 = (bf16[2,8192]{1,0:T(2,128)(2,1)}, bf16[2,8192]{1,0:T(2,128)(2,1)S(1)}, u32[]{:S(2)}, u32[]{:S(2)}) collective-permute-start(bf16[2,8192]{1,0:T(2,128)(2,1)} %refs_2_.2), channel_id=1, source_target_pairs={{0,8},{1,11},{2,10},{3,9},{4,12},{5,15},{6,14},{7,13},{8,0},{9,3},... | collective-permute-start | bytes 98312 | tf_op jit(solution)/shard_map/ppermute | solution.py:169
  4.1 4.4 %collective-permute-start.4 = (bf16[2,8192]{1,0:T(2,128)(2,1)}, bf16[2,8192]{1,0:T(2,128)(2,1)S(1)}, u32[]{:S(2)}, u32[]{:S(2)}) collective-permute-start(bf16[2,8192]{1,0:T(2,128)(2,1)} %refs_2_.2), channel_id=1, source_target_pairs={{0,2},{1,3},{2,0},{3,1},{4,6},{5,7},{6,4},{7,5},{8,10},{9,11},{10,... | collective-permute-start | bytes 98312 | tf_op jit(solution)/shard_map/ppermute | solution.py:169
  5.6 6.3 %collective-permute-start.1 = (bf16[2,8192]{1,0:T(2,128)(2,1)}, bf16[2,8192]{1,0:T(2,128)(2,1)S(1)}, u32[]{:S(2)}, u32[]{:S(2)}) collective-permute-start(bf16[2,8192]{1,0:T(2,128)(2,1)} %refs_2_.2), channel_id=1, source_target_pairs={{0,12},{1,15},{2,14},{3,13},{4,8},{5,11},{6,10},{7,9},{8,4},{9,7},... | collective-permute-start | bytes 98312 | tf_op jit(solution)/shard_map/ppermute | solution.py:169
  7.0 4.9 %collective-permute-start.2 = (bf16[2,8192]{1,0:T(2,128)(2,1)}, bf16[2,8192]{1,0:T(2,128)(2,1)S(1)}, u32[]{:S(2)}, u32[]{:S(2)}) collective-permute-start(bf16[2,8192]{1,0:T(2,128)(2,1)} %refs_2_.2), channel_id=1, source_target_pairs={{0,4},{1,7},{2,6},{3,5},{4,0},{5,3},{6,2},{7,1},{8,12},{9,15},{10,... | collective-permute-start | bytes 98312 | tf_op jit(solution)/shard_map/ppermute | solution.py:169
  7.9 4.0 %copy-start.4 = (bf16[2,8192]{1,0:T(2,128)(2,1)S(1)}, bf16[2,8192]{1,0:T(2,128)(2,1)}, u32[]{:S(2)}) copy-start(bf16[2,8192]{1,0:T(2,128)(2,1)} %refs_2_.2) | copy-start | bytes 98308
  8.9 10.1 %copy-start.6 = (s32[2]{0:T(128)S(1)}, s32[2]{0:T(128)}, u32[]{:S(2)}) copy-start(s32[2]{0:T(128)} %param.15) | copy-start | bytes 28
  8.9 10.2 %copy-start.5 = (bf16[2,4096]{1,0:T(2,128)(2,1)S(1)}, bf16[2,4096]{1,0:T(2,128)(2,1)}, u32[]{:S(2)}) copy-start(bf16[2,4096]{1,0:T(2,128)(2,1)} %param.9) | copy-start | bytes 49156
  8.9 11.3 %copy-start.2 = (bf16[2,4,256,128]{3,2,1,0:T(8,128)(2,1)S(1)}, bf16[2,4,256,128]{3,2,1,0:T(8,128)(2,1)}, u32[]{:S(2)}) copy-start(bf16[2,4,256,128]{3,2,1,0:T(8,128)(2,1)} %refs_2_.3) | copy-start | bytes 1572868
  8.9 11.2 %copy-start.3 = (bf16[2,4,256,128]{3,2,1,0:T(8,128)(2,1)S(1)}, bf16[2,4,256,128]{3,2,1,0:T(8,128)(2,1)}, u32[]{:S(2)}) copy-start(bf16[2,4,256,128]{3,2,1,0:T(8,128)(2,1)} %refs_3_.1) | copy-start | bytes 1572868
  8.9 9.7 %collective-permute-start.5 = (bf16[2,2,32,128]{3,2,1,0:T(8,128)(2,1)S(1)}, bf16[2,2,32,128]{3,2,1,0:T(8,128)(2,1)S(1)}, u32[]{:S(2)}, u32[]{:S(2)}) collective-permute-start(bf16[2,2,32,128]{3,2,1,0:T(8,128)(2,1)S(1)} %get-tuple-element.12.refs_3_), channel_id=1, source_target_pairs={{0,8},{1,11},{2,10},{3,9},{4,12},{5,15},{6,14},{7,13},{8,0},{9,3},... | collective-permute-start | bytes 98312 | tf_op jit(solution)/shard_map/ppermute | solution.py:169
  12.1 5.9 %collective-permute-start.7 = (bf16[2,2,32,128]{3,2,1,0:T(8,128)(2,1)S(1)}, bf16[2,2,32,128]{3,2,1,0:T(8,128)(2,1)S(1)}, u32[]{:S(2)}, u32[]{:S(2)}) collective-permute-start(bf16[2,2,32,128]{3,2,1,0:T(8,128)(2,1)S(1)} %get-tuple-element.15), channel_id=1, source_target_pairs={{0,12},{1,15},{2,14},{3,13},{4,8},{5,11},{6,10},{7,9},{8,4},{9,7},... | collective-permute-start | bytes 98312 | tf_op jit(solution)/shard_map/ppermute | solution.py:169
  14.5 4.1 %collective-permute-start.8 = (bf16[2,2,32,128]{3,2,1,0:T(8,128)(2,1)S(1)}, bf16[2,2,32,128]{3,2,1,0:T(8,128)(2,1)S(1)}, u32[]{:S(2)}, u32[]{:S(2)}) collective-permute-start(bf16[2,2,32,128]{3,2,1,0:T(8,128)(2,1)S(1)} %get-tuple-element.16), channel_id=1, source_target_pairs={{0,4},{1,7},{2,6},{3,5},{4,0},{5,3},{6,2},{7,1},{8,12},{9,15},{10,... | collective-permute-start | bytes 98312 | tf_op jit(solution)/shard_map/ppermute | solution.py:169
  14.5 4.4 %collective-permute-start.6 = (bf16[2,2,32,128]{3,2,1,0:T(8,128)(2,1)S(1)}, bf16[2,2,32,128]{3,2,1,0:T(8,128)(2,1)S(1)}, u32[]{:S(2)}, u32[]{:S(2)}) collective-permute-start(bf16[2,2,32,128]{3,2,1,0:T(8,128)(2,1)S(1)} %get-tuple-element.14), channel_id=1, source_target_pairs={{0,2},{1,3},{2,0},{3,1},{4,6},{5,7},{6,4},{7,5},{8,10},{9,11},{10,... | collective-permute-start | bytes 98312 | tf_op jit(solution)/shard_map/ppermute | solution.py:169
  18.9 1.2 %collective-permute-start.9 = (bf16[2,32,128]{2,1,0:T(8,128)(2,1)S(1)}, bf16[2,32,128]{2,1,0:T(8,128)(2,1)S(1)}, u32[]{:S(2)}, u32[]{:S(2)}) collective-permute-start(bf16[2,32,128]{2,1,0:T(8,128)(2,1)S(1)} %get-tuple-element.18), channel_id=1, source_target_pairs={{0,1},{1,0},{2,3},{3,2},{4,5},{5,4},{6,7},{7,6},{8,9},{9,8},{10,11... | collective-permute-start | bytes 49160 | tf_op jit(solution)/shard_map/ppermute | solution.py:172

commit v12 on v11

--- a/solution.py
+++ b/solution.py
@@ -15,7 +15,7 @@
 VMEM = pl.BlockSpec(memory_space=pltpu.VMEM)
 SMEM = pl.BlockSpec(memory_space=pltpu.SMEM)
 PARAMS = pltpu.CompilerParams(vmem_limit_bytes=VMEM_LIMIT)
-TURNS = ((4, 1, 6, 2, 0), (5, 1, 7, 3, 0))
+TURNS = ((3, 1, 4, 2, 0), (7, 1, 5, 6, 0))
 SENT = len(TURNS[0]) - 1
 EARLY = 2
 SHARED = [first == second for first, second in zip(*TURNS)]

time: 21.4 us -> 20.9 us (0.977)
  waiting for transfers between devices: 6.65 us -> 5.33 us
  starting transfers between devices: 12 us -> 12.4 us
  Pallas kernels: 2.46 us -> 2.69 us
    ppermute x8, waiting for transfers between devices: 5.57 us -> 4.25 us  [visit(): return lax.ppermute(array, ('store', 'tensor'), turn_pairs(turn))]
    ppermute x8, starting transfers between devices: 11.5 us -> 11.9 us  [visit(): return lax.ppermute(array, ('store', 'tensor'), turn_pairs(turn))]
    pallas_call x2, Pallas kernels: 0.6 us -> 0.83 us  [work(): pl.pallas_call(functools.partial(owner_kernel, turns), out_shape=[jax.Sha...]
  transfers between devices with their start and end apart: 10 -> 10, of which waited for: 6 -> 4; matrix products, arithmetic and copies ran while one was open for 0% -> 0% of each run, Pallas kernels for 6% -> 7%
where the time goes in v12:
time: 20.9 us; the launch traced here: 20.7 us
  starting transfers between devices  12.4 us (59%)
  waiting for transfers between devices  5.33 us (26%)
  Pallas kernels  2.69 us (13%)
    ppermute x8, starting transfers between devices, visit(): return lax.ppermute(array, ('store', 'tensor'), turn_pairs(turn))  11.9 us
    ppermute x8, waiting for transfers between devices, visit(): return lax.ppermute(array, ('store', 'tensor'), turn_pairs(turn))  4.25 us
    pallas_call x1, Pallas kernels, per_device(): pl.pallas_call(functools.partial(attend_kernel, len(deltas)), out_shape=j...  1.16 us
    ppermute x2, waiting for transfers between devices, swap(): return lax.ppermute(array, 'tensor', [(0, 1), (1, 0)])  1.08 us
    pallas_call x2, Pallas kernels, work(): pl.pallas_call(functools.partial(owner_kernel, turns), out_shape=[jax.Sha...  0.83 us
    pallas_call x1, Pallas kernels, scalars(): pl.pallas_call(scalars_kernel, out_shape=pltpu.SMEM(ids.shape, ids.dtype)...  0.67 us
    ppermute x2, starting transfers between devices, swap(): return lax.ppermute(array, 'tensor', [(0, 1), (1, 0)])  0.54 us
  transfers between devices with their start and end apart: 10, of which 4 were waited for; matrix products, arithmetic and copies ran while one was open for 0% of the time, Pallas kernels for 7%

profile of v12, /device:TPU:0, one launch (start us, length us, event | category | flops | bytes accessed | tf_op | source)
XLA Modules:
  0.0 20.7 jit_solution(11495972873521651844)
XLA Ops:
  0.0 0.0 copy-start.1
  0.0 0.0 copy-start
  0.0 0.5 %collective-permute-start = (bf16[8,16,4096]{2,1,0:T(8,128)(2,1)}, bf16[8,16,4096]{2,1,0:T(8,128)(2,1)S(1)}, u32[]{:S(2)}, u32[]{:S(2)}) collective-permute-start(bf16[8,16,4096]{2,1,0:T(8,128)(2,1)} %mine_ref.3), channel_id=1, source_target_pairs={{0,1},{1,0},{2,3},{3,2},{4,5},{5,4},{6,7},{7,6},{8,9},{9,8},{10,11... | collective-permute-start | bytes 3145736 | tf_op jit(solution)/shard_map/ppermute | solution.py:172
  0.5 3.6 %collective-permute-start.3 = (bf16[2,8192]{1,0:T(2,128)(2,1)}, bf16[2,8192]{1,0:T(2,128)(2,1)S(1)}, u32[]{:S(2)}, u32[]{:S(2)}) collective-permute-start(bf16[2,8192]{1,0:T(2,128)(2,1)} %refs_2_.2), channel_id=1, source_target_pairs={{0,6},{1,15},{2,4},{3,13},{4,2},{5,11},{6,0},{7,9},{8,14},{9,7},{1... | collective-permute-start | bytes 98312 | tf_op jit(solution)/shard_map/ppermute | solution.py:169
  4.0 0.5 %collective-permute-start.4 = (bf16[2,8192]{1,0:T(2,128)(2,1)}, bf16[2,8192]{1,0:T(2,128)(2,1)S(1)}, u32[]{:S(2)}, u32[]{:S(2)}) collective-permute-start(bf16[2,8192]{1,0:T(2,128)(2,1)} %refs_2_.2), channel_id=1, source_target_pairs={{0,2},{1,3},{2,0},{3,1},{4,6},{5,7},{6,4},{7,5},{8,10},{9,11},{10,... | collective-permute-start | bytes 98312 | tf_op jit(solution)/shard_map/ppermute | solution.py:169
  4.6 2.6 %collective-permute-start.1 = (bf16[2,8192]{1,0:T(2,128)(2,1)}, bf16[2,8192]{1,0:T(2,128)(2,1)S(1)}, u32[]{:S(2)}, u32[]{:S(2)}) collective-permute-start(bf16[2,8192]{1,0:T(2,128)(2,1)} %refs_2_.2), channel_id=1, source_target_pairs={{0,8},{1,11},{2,10},{3,9},{4,12},{5,15},{6,14},{7,13},{8,0},{9,3},... | collective-permute-start | bytes 98312 | tf_op jit(solution)/shard_map/ppermute | solution.py:169
  7.2 0.4 %collective-permute-start.2 = (bf16[2,8192]{1,0:T(2,128)(2,1)}, bf16[2,8192]{1,0:T(2,128)(2,1)S(1)}, u32[]{:S(2)}, u32[]{:S(2)}) collective-permute-start(bf16[2,8192]{1,0:T(2,128)(2,1)} %refs_2_.2), channel_id=1, source_target_pairs={{0,4},{1,13},{2,6},{3,15},{4,0},{5,9},{6,2},{7,11},{8,12},{9,5},{1... | collective-permute-start | bytes 98312 | tf_op jit(solution)/shard_map/ppermute | solution.py:169
  7.6 0.7 %scalars.1.ids_ref = s32[16]{0:T(128)S(4)} custom-call(s32[16]{0:T(128)} %ids_hbm.1, bf16[8,16,8192]{2,1,0:T(8,128)(2,1)} %down_ref.3, bf16[8,16,4096]{2,1,0:T(8,128)(2,1)} %mine_ref.3), custom_call_target="tpu_custom_call" | custom-call | bytes 3145728 | tf_op jit(solution)/shard_map/scalars/pallas_call | solution.py:33
  8.3 0.0 copy-start.4
  8.3 0.0 collective-permute-done.3.refs_0_
  8.3 0.0 collective-permute-done.4.refs_1_
  8.3 0.0 collective-permute-done.other_ref
  8.3 0.0 copy-done.1
  8.3 0.0 copy-done
  8.3 0.2 owner_first.1
  8.5 0.0 copy-start.6
  8.5 0.0 copy-start.5
  8.5 0.0 copy-start.2
  8.6 0.0 copy-start.3
  8.6 2.6 %collective-permute-start.5 = (bf16[2,2,32,128]{3,2,1,0:T(8,128)(2,1)S(1)}, bf16[2,2,32,128]{3,2,1,0:T(8,128)(2,1)S(1)}, u32[]{:S(2)}, u32[]{:S(2)}) collective-permute-start(bf16[2,2,32,128]{3,2,1,0:T(8,128)(2,1)S(1)} %get-tuple-element.12.refs_3_), channel_id=1, source_target_pairs={{0,6},{1,15},{2,4},{3,13},{4,2},{5,11},{6,0},{7,9},{8,14},{9,7},{1... | collective-permute-start | bytes 98312 | tf_op jit(solution)/shard_map/ppermute | solution.py:169
  11.1 0.0 collective-permute-done.1.refs_0_
  11.1 0.8 %collective-permute-done.2.refs_1_ = bf16[2,8192]{1,0:T(2,128)(2,1)S(1)} collective-permute-done((bf16[2,8192]{1,0:T(2,128)(2,1)}, bf16[2,8192]{1,0:T(2,128)(2,1)S(1)}, u32[]{:S(2)}, u32[]{:S(2)}) %collective-permute-start.2) | collective-permute-done | bytes 32800 | tf_op jit(solution)/shard_map/ppermute | solution.py:169
  12.0 0.0 copy-done.4
  12.0 0.7 %owner_rest.1 = (bf16[2,2,32,128]{3,2,1,0:T(8,128)(2,1)S(1)}, bf16[2,2,32,128]{3,2,1,0:T(8,128)(2,1)S(1)}, bf16[2,2,32,128]{3,2,1,0:T(8,128)(2,1)S(1)}) custom-call(s32[16]{0:T(128)S(4)} %scalars.1.ids_ref, bf16[8,16,8192]{2,1,0:T(8,128)(2,1)S(1)} %copy-done, bf16[8,16,4096]{2,1,0:T(8,128)(2,1)S(1)} %copy-done.1, ...), custom_call_target="tpu_custom_call" | custom-call | tf_op jit(solution)/shard_map/owner_rest/pallas_call | solution.py:182
  12.7 0.1 collective-permute-start.7
  12.7 1.1 %collective-permute-start.8 = (bf16[2,2,32,128]{3,2,1,0:T(8,128)(2,1)S(1)}, bf16[2,2,32,128]{3,2,1,0:T(8,128)(2,1)S(1)}, u32[]{:S(2)}, u32[]{:S(2)}) collective-permute-start(bf16[2,2,32,128]{3,2,1,0:T(8,128)(2,1)S(1)} %get-tuple-element.16), channel_id=1, source_target_pairs={{0,4},{1,13},{2,6},{3,15},{4,0},{5,9},{6,2},{7,11},{8,12},{9,5},{1... | collective-permute-start | bytes 98312 | tf_op jit(solution)/shard_map/ppermute | solution.py:169
  13.8 1.0 %collective-permute-start.6 = (bf16[2,2,32,128]{3,2,1,0:T(8,128)(2,1)S(1)}, bf16[2,2,32,128]{3,2,1,0:T(8,128)(2,1)S(1)}, u32[]{:S(2)}, u32[]{:S(2)}) collective-permute-start(bf16[2,2,32,128]{3,2,1,0:T(8,128)(2,1)S(1)} %get-tuple-element.14), channel_id=1, source_target_pairs={{0,2},{1,3},{2,0},{3,1},{4,6},{5,7},{6,4},{7,5},{8,10},{9,11},{10,... | collective-permute-start | bytes 98312 | tf_op jit(solution)/shard_map/ppermute | solution.py:169
  14.9 2.9 %collective-permute-done.7.refs_2_ = bf16[2,2,32,128]{3,2,1,0:T(8,128)(2,1)S(1)} collective-permute-done((bf16[2,2,32,128]{3,2,1,0:T(8,128)(2,1)S(1)}, bf16[2,2,32,128]{3,2,1,0:T(8,128)(2,1)S(1)}, u32[]{:S(2)}, u32[]{:S(2)}) %collective-permute-start.7) | collective-permute-done | bytes 32800 | tf_op jit(solution)/shard_map/ppermute | solution.py:169
  17.8 0.0 collective-permute-done.8.refs_3_
  17.8 0.0 collective-permute-done.5.refs_0_
  17.8 0.5 %collective-permute-done.6.refs_1_ = bf16[2,2,32,128]{3,2,1,0:T(8,128)(2,1)S(1)} collective-permute-done((bf16[2,2,32,128]{3,2,1,0:T(8,128)(2,1)S(1)}, bf16[2,2,32,128]{3,2,1,0:T(8,128)(2,1)S(1)}, u32[]{:S(2)}, u32[]{:S(2)}) %collective-permute-start.6) | collective-permute-done | bytes 32800 | tf_op jit(solution)/shard_map/ppermute | solution.py:169
  18.3 0.1 collective-permute-start.9
  18.4 0.0 copy-done.6
  18.4 0.1 compare_convert_fusion.live_ref
  18.4 0.0 copy-done.5
  18.5 1.1 %collective-permute-done.9.refs_1_ = bf16[2,32,128]{2,1,0:T(8,128)(2,1)S(1)} collective-permute-done((bf16[2,32,128]{2,1,0:T(8,128)(2,1)S(1)}, bf16[2,32,128]{2,1,0:T(8,128)(2,1)S(1)}, u32[]{:S(2)}, u32[]{:S(2)}) %collective-permute-start.9) | collective-permute-done | bytes 16416 | tf_op jit(solution)/shard_map/ppermute | solution.py:172
  19.5 0.0 copy-done.2
  19.5 0.0 copy-done.3
  19.5 1.2 %attend.1 = bf16[2,4096]{1,0:T(2,128)(2,1)} custom-call(f32[2,1,256]{2,1,0:T(1,128)S(1)} %compare_convert_fusion.live_ref, bf16[2,32,128]{2,1,0:T(8,128)(2,1)S(1)} %bitcast.4, bf16[2,32,128]{2,1,0:T(8,128)(2,1)S(1)} %get-tuple-element.17.refs_0_, bf16[2,32,128]{2,1,0:T(8,128)(2,1)S(1)} %collective-permute-done.9.refs_1_, ...), custom_call_target="tpu_custom_call" | custom-call | tf_op jit(solution)/shard_map/attend/pallas_call | solution.py:245
  (2 shorter events, 0.0 us)
Async XLA Ops:
  0.0 8.3 %copy-start.1 = (bf16[8,16,4096]{2,1,0:T(8,128)(2,1)S(1)}, bf16[8,16,4096]{2,1,0:T(8,128)(2,1)}, u32[]{:S(2)}) copy-start(bf16[8,16,4096]{2,1,0:T(8,128)(2,1)} %mine_ref.3) | copy-start | bytes 3145732
  0.0 8.3 %copy-start = (bf16[8,16,8192]{2,1,0:T(8,128)(2,1)S(1)}, bf16[8,16,8192]{2,1,0:T(8,128)(2,1)}, u32[]{:S(2)}) copy-start(bf16[8,16,8192]{2,1,0:T(8,128)(2,1)} %down_ref.3) | copy-start | bytes 6291460
  0.0 8.3 %collective-permute-start = (bf16[8,16,4096]{2,1,0:T(8,128)(2,1)}, bf16[8,16,4096]{2,1,0:T(8,128)(2,1)S(1)}, u32[]{:S(2)}, u32[]{:S(2)}) collective-permute-start(bf16[8,16,4096]{2,1,0:T(8,128)(2,1)} %mine_ref.3), channel_id=1, source_target_pairs={{0,1},{1,0},{2,3},{3,2},{4,5},{5,4},{6,7},{7,6},{8,9},{9,8},{10,11... | collective-permute-start | bytes 3145736 | tf_op jit(solution)/shard_map/ppermute | solution.py:172
  0.5 7.8 %collective-permute-start.3 = (bf16[2,8192]{1,0:T(2,128)(2,1)}, bf16[2,8192]{1,0:T(2,128)(2,1)S(1)}, u32[]{:S(2)}, u32[]{:S(2)}) collective-permute-start(bf16[2,8192]{1,0:T(2,128)(2,1)} %refs_2_.2), channel_id=1, source_target_pairs={{0,6},{1,15},{2,4},{3,13},{4,2},{5,11},{6,0},{7,9},{8,14},{9,7},{1... | collective-permute-start | bytes 98312 | tf_op jit(solution)/shard_map/ppermute | solution.py:169
  4.0 4.3 %collective-permute-start.4 = (bf16[2,8192]{1,0:T(2,128)(2,1)}, bf16[2,8192]{1,0:T(2,128)(2,1)S(1)}, u32[]{:S(2)}, u32[]{:S(2)}) collective-permute-start(bf16[2,8192]{1,0:T(2,128)(2,1)} %refs_2_.2), channel_id=1, source_target_pairs={{0,2},{1,3},{2,0},{3,1},{4,6},{5,7},{6,4},{7,5},{8,10},{9,11},{10,... | collective-permute-start | bytes 98312 | tf_op jit(solution)/shard_map/ppermute | solution.py:169
  4.6 6.6 %collective-permute-start.1 = (bf16[2,8192]{1,0:T(2,128)(2,1)}, bf16[2,8192]{1,0:T(2,128)(2,1)S(1)}, u32[]{:S(2)}, u32[]{:S(2)}) collective-permute-start(bf16[2,8192]{1,0:T(2,128)(2,1)} %refs_2_.2), channel_id=1, source_target_pairs={{0,8},{1,11},{2,10},{3,9},{4,12},{5,15},{6,14},{7,13},{8,0},{9,3},... | collective-permute-start | bytes 98312 | tf_op jit(solution)/shard_map/ppermute | solution.py:169
  7.2 4.8 %collective-permute-start.2 = (bf16[2,8192]{1,0:T(2,128)(2,1)}, bf16[2,8192]{1,0:T(2,128)(2,1)S(1)}, u32[]{:S(2)}, u32[]{:S(2)}) collective-permute-start(bf16[2,8192]{1,0:T(2,128)(2,1)} %refs_2_.2), channel_id=1, source_target_pairs={{0,4},{1,13},{2,6},{3,15},{4,0},{5,9},{6,2},{7,11},{8,12},{9,5},{1... | collective-permute-start | bytes 98312 | tf_op jit(solution)/shard_map/ppermute | solution.py:169
  8.3 3.7 %copy-start.4 = (bf16[2,8192]{1,0:T(2,128)(2,1)S(1)}, bf16[2,8192]{1,0:T(2,128)(2,1)}, u32[]{:S(2)}) copy-start(bf16[2,8192]{1,0:T(2,128)(2,1)} %refs_2_.2) | copy-start | bytes 98308
  8.5 9.9 %copy-start.6 = (s32[2]{0:T(128)S(1)}, s32[2]{0:T(128)}, u32[]{:S(2)}) copy-start(s32[2]{0:T(128)} %param.15) | copy-start | bytes 28
  8.5 9.9 %copy-start.5 = (bf16[2,4096]{1,0:T(2,128)(2,1)S(1)}, bf16[2,4096]{1,0:T(2,128)(2,1)}, u32[]{:S(2)}) copy-start(bf16[2,4096]{1,0:T(2,128)(2,1)} %param.9) | copy-start | bytes 49156
  8.5 11.0 %copy-start.2 = (bf16[2,4,256,128]{3,2,1,0:T(8,128)(2,1)S(1)}, bf16[2,4,256,128]{3,2,1,0:T(8,128)(2,1)}, u32[]{:S(2)}) copy-start(bf16[2,4,256,128]{3,2,1,0:T(8,128)(2,1)} %refs_2_.3) | copy-start | bytes 1572868
  8.6 11.0 %copy-start.3 = (bf16[2,4,256,128]{3,2,1,0:T(8,128)(2,1)S(1)}, bf16[2,4,256,128]{3,2,1,0:T(8,128)(2,1)}, u32[]{:S(2)}) copy-start(bf16[2,4,256,128]{3,2,1,0:T(8,128)(2,1)} %refs_3_.1) | copy-start | bytes 1572868
  8.6 9.2 %collective-permute-start.5 = (bf16[2,2,32,128]{3,2,1,0:T(8,128)(2,1)S(1)}, bf16[2,2,32,128]{3,2,1,0:T(8,128)(2,1)S(1)}, u32[]{:S(2)}, u32[]{:S(2)}) collective-permute-start(bf16[2,2,32,128]{3,2,1,0:T(8,128)(2,1)S(1)} %get-tuple-element.12.refs_3_), channel_id=1, source_target_pairs={{0,6},{1,15},{2,4},{3,13},{4,2},{5,11},{6,0},{7,9},{8,14},{9,7},{1... | collective-permute-start | bytes 98312 | tf_op jit(solution)/shard_map/ppermute | solution.py:169
  12.7 5.1 %collective-permute-start.7 = (bf16[2,2,32,128]{3,2,1,0:T(8,128)(2,1)S(1)}, bf16[2,2,32,128]{3,2,1,0:T(8,128)(2,1)S(1)}, u32[]{:S(2)}, u32[]{:S(2)}) collective-permute-start(bf16[2,2,32,128]{3,2,1,0:T(8,128)(2,1)S(1)} %get-tuple-element.15), channel_id=1, source_target_pairs={{0,8},{1,11},{2,10},{3,9},{4,12},{5,15},{6,14},{7,13},{8,0},{9,3},... | collective-permute-start | bytes 98312 | tf_op jit(solution)/shard_map/ppermute | solution.py:169
  12.7 5.0 %collective-permute-start.8 = (bf16[2,2,32,128]{3,2,1,0:T(8,128)(2,1)S(1)}, bf16[2,2,32,128]{3,2,1,0:T(8,128)(2,1)S(1)}, u32[]{:S(2)}, u32[]{:S(2)}) collective-permute-start(bf16[2,2,32,128]{3,2,1,0:T(8,128)(2,1)S(1)} %get-tuple-element.16), channel_id=1, source_target_pairs={{0,4},{1,13},{2,6},{3,15},{4,0},{5,9},{6,2},{7,11},{8,12},{9,5},{1... | collective-permute-start | bytes 98312 | tf_op jit(solution)/shard_map/ppermute | solution.py:169
  13.8 4.4 %collective-permute-start.6 = (bf16[2,2,32,128]{3,2,1,0:T(8,128)(2,1)S(1)}, bf16[2,2,32,128]{3,2,1,0:T(8,128)(2,1)S(1)}, u32[]{:S(2)}, u32[]{:S(2)}) collective-permute-start(bf16[2,2,32,128]{3,2,1,0:T(8,128)(2,1)S(1)} %get-tuple-element.14), channel_id=1, source_target_pairs={{0,2},{1,3},{2,0},{3,1},{4,6},{5,7},{6,4},{7,5},{8,10},{9,11},{10,... | collective-permute-start | bytes 98312 | tf_op jit(solution)/shard_map/ppermute | solution.py:169
  18.3 1.2 %collective-permute-start.9 = (bf16[2,32,128]{2,1,0:T(8,128)(2,1)S(1)}, bf16[2,32,128]{2,1,0:T(8,128)(2,1)S(1)}, u32[]{:S(2)}, u32[]{:S(2)}) collective-permute-start(bf16[2,32,128]{2,1,0:T(8,128)(2,1)S(1)} %get-tuple-element.18), channel_id=1, source_target_pairs={{0,1},{1,0},{2,3},{3,2},{4,5},{5,4},{6,7},{7,6},{8,9},{9,8},{10,11... | collective-permute-start | bytes 49160 | tf_op jit(solution)/shard_map/ppermute | solution.py:172

commit v13 on v12

--- a/solution.py
+++ b/solution.py
@@ -116,9 +116,15 @@
         out_ref[...] = total.astype(out_ref.dtype)
 
 
+def turn_kernel(key_ref, turned_ref):
+    for row in range(key_ref.shape[0]):
+        for kv in range(key_ref.shape[1]):
+            turned_ref[row, kv] = key_ref[row, kv].T
+
+
 def attend_kernel(parts, live_ref, base_ref, *refs):
     delta_refs, (key_ref, value_ref, out_ref, rows_ref) = refs[:parts], refs[parts:]
-    rows, kv_heads, slots, head_size = key_ref.shape
+    rows, kv_heads, slots, head_size = value_ref.shape
     heads = base_ref.shape[1]
     group = heads // kv_heads
     scale = 1.0 / (float(head_size) ** 0.5)
@@ -135,7 +141,7 @@
             score = lax.dot_general(
                 mine,
                 key_ref[row, kv],
-                (((1,), (1,)), ((), ())),
+                (((1,), (0,)), ((), ())),
                 preferred_element_type=jnp.float32,
             )
             scores.append(jnp.where(live, score * scale, jnp.float32(-1e30)))
@@ -241,6 +247,14 @@
     deltas = (shared_deltas if shared else exchanged_deltas)(
         hidden, adapter_down, adapter_up, adapter_ids, block
     )
+    turned = pl.pallas_call(
+        turn_kernel,
+        out_shape=jax.ShapeDtypeStruct((rows, kv_heads, head_size, slots), key_cache.dtype),
+        in_specs=[VMEM],
+        out_specs=VMEM,
+        compiler_params=PARAMS,
+        name="turn",
+    )(near(key_cache))
     live = jnp.arange(slots, dtype=jnp.int32)[None, None, :] < kv_lengths[:, None, None]
     return pl.pallas_call(
         functools.partial(attend_kernel, len(deltas)),
@@ -254,7 +268,7 @@
         near(live.astype(jnp.float32)),
         near(query_base.reshape(block)),
         *deltas,
-        near(key_cache),
+        near(turned),
         near(value_cache),
     )
 

time: 20.9 us -> 20.8 us (level)
  starting transfers between devices: 12.4 us -> 14.1 us
  waiting for transfers between devices: 5.33 us -> 4.1 us
  Pallas kernels: 2.69 us -> 2.38 us
    ppermute x8, starting transfers between devices: 11.9 us -> 13.1 us  [visit(): return lax.ppermute(array, ('store', 'tensor'), turn_pairs(turn))]
    ppermute x8, waiting for transfers between devices: 4.25 us -> 3.55 us  [visit(): return lax.ppermute(array, ('store', 'tensor'), turn_pairs(turn))]
    ppermute x2, waiting for transfers between devices: 1.08 us -> 0.55 us  [swap(): return lax.ppermute(array, 'tensor', [(0, 1), (1, 0)])]
    pallas_call x2, Pallas kernels: 0.83 us -> 0.37 us  [work(): pl.pallas_call(functools.partial(owner_kernel, turns), out_shape=[jax.Sha...]
    ppermute x2, starting transfers between devices: 0.54 us -> 1 us  [swap(): return lax.ppermute(array, 'tensor', [(0, 1), (1, 0)])]
  transfers between devices with their start and end apart: 10 -> 10, of which waited for: 4 -> 4; matrix products, arithmetic and copies ran while one was open for 0% -> 0% of each run, Pallas kernels for 7% -> 6%
where the time goes in v13:
time: 20.8 us
  starting transfers between devices  14.1 us (68%)
  waiting for transfers between devices  4.1 us (20%)
  Pallas kernels  2.38 us (11%)
    ppermute x8, starting transfers between devices, visit(): return lax.ppermute(array, ('store', 'tensor'), turn_pairs(turn))  13.1 us
    ppermute x8, waiting for transfers between devices, visit(): return lax.ppermute(array, ('store', 'tensor'), turn_pairs(turn))  3.55 us
    pallas_call x1, Pallas kernels, per_device(): pl.pallas_call(functools.partial(attend_kernel, len(deltas)), out_shape=j...  1.13 us
    ppermute x2, starting transfers between devices, swap(): return lax.ppermute(array, 'tensor', [(0, 1), (1, 0)])  1 us
    pallas_call x1, Pallas kernels, scalars(): pl.pallas_call(scalars_kernel, out_shape=pltpu.SMEM(ids.shape, ids.dtype)...  0.67 us
    ppermute x2, waiting for transfers between devices, swap(): return lax.ppermute(array, 'tensor', [(0, 1), (1, 0)])  0.55 us
  transfers between devices with their start and end apart: 10, of which 4 were waited for; matrix products, arithmetic and copies ran while one was open for 0% of the time, Pallas kernels for 6%

profile of v13, /device:TPU:0, one launch (start us, length us, event | category | flops | bytes accessed | tf_op | source)
XLA Modules:
  0.0 20.8 jit_solution(14908976500238779915)
XLA Ops:
  0.0 0.0 copy-start.1
  0.0 0.0 copy-start
  0.0 0.5 %collective-permute-start = (bf16[8,16,4096]{2,1,0:T(8,128)(2,1)}, bf16[8,16,4096]{2,1,0:T(8,128)(2,1)S(1)}, u32[]{:S(2)}, u32[]{:S(2)}) collective-permute-start(bf16[8,16,4096]{2,1,0:T(8,128)(2,1)} %mine_ref.3), channel_id=1, source_target_pairs={{0,1},{1,0},{2,3},{3,2},{4,5},{5,4},{6,7},{7,6},{8,9},{9,8},{10,11... | collective-permute-start | bytes 3145736 | tf_op jit(solution)/shard_map/ppermute | solution.py:178
  0.5 3.6 %collective-permute-start.3 = (bf16[2,8192]{1,0:T(2,128)(2,1)}, bf16[2,8192]{1,0:T(2,128)(2,1)S(1)}, u32[]{:S(2)}, u32[]{:S(2)}) collective-permute-start(bf16[2,8192]{1,0:T(2,128)(2,1)} %refs_2_.1), channel_id=1, source_target_pairs={{0,6},{1,15},{2,4},{3,13},{4,2},{5,11},{6,0},{7,9},{8,14},{9,7},{1... | collective-permute-start | bytes 98312 | tf_op jit(solution)/shard_map/ppermute | solution.py:175
  4.0 0.5 %collective-permute-start.4 = (bf16[2,8192]{1,0:T(2,128)(2,1)}, bf16[2,8192]{1,0:T(2,128)(2,1)S(1)}, u32[]{:S(2)}, u32[]{:S(2)}) collective-permute-start(bf16[2,8192]{1,0:T(2,128)(2,1)} %refs_2_.1), channel_id=1, source_target_pairs={{0,2},{1,3},{2,0},{3,1},{4,6},{5,7},{6,4},{7,5},{8,10},{9,11},{10,... | collective-permute-start | bytes 98312 | tf_op jit(solution)/shard_map/ppermute | solution.py:175
  4.6 2.6 %collective-permute-start.1 = (bf16[2,8192]{1,0:T(2,128)(2,1)}, bf16[2,8192]{1,0:T(2,128)(2,1)S(1)}, u32[]{:S(2)}, u32[]{:S(2)}) collective-permute-start(bf16[2,8192]{1,0:T(2,128)(2,1)} %refs_2_.1), channel_id=1, source_target_pairs={{0,8},{1,11},{2,10},{3,9},{4,12},{5,15},{6,14},{7,13},{8,0},{9,3},... | collective-permute-start | bytes 98312 | tf_op jit(solution)/shard_map/ppermute | solution.py:175
  7.2 0.4 %collective-permute-start.2 = (bf16[2,8192]{1,0:T(2,128)(2,1)}, bf16[2,8192]{1,0:T(2,128)(2,1)S(1)}, u32[]{:S(2)}, u32[]{:S(2)}) collective-permute-start(bf16[2,8192]{1,0:T(2,128)(2,1)} %refs_2_.1), channel_id=1, source_target_pairs={{0,4},{1,13},{2,6},{3,15},{4,0},{5,9},{6,2},{7,11},{8,12},{9,5},{1... | collective-permute-start | bytes 98312 | tf_op jit(solution)/shard_map/ppermute | solution.py:175
  7.6 0.7 %scalars.1.ids_ref = s32[16]{0:T(128)S(4)} custom-call(s32[16]{0:T(128)} %ids_hbm.1, bf16[8,16,8192]{2,1,0:T(8,128)(2,1)} %down_ref.3, bf16[8,16,4096]{2,1,0:T(8,128)(2,1)} %mine_ref.3), custom_call_target="tpu_custom_call" | custom-call | bytes 3145728 | tf_op jit(solution)/shard_map/scalars/pallas_call | solution.py:33
  8.3 0.0 copy-start.4
  8.3 0.0 collective-permute-done.3.refs_0_
  8.3 0.0 collective-permute-done.4.refs_1_
  8.3 0.0 collective-permute-done.other_ref
  8.3 0.0 copy-done.1
  8.3 0.0 copy-done
  8.3 0.2 owner_first.1
  8.5 0.0 copy-start.6
  8.5 0.0 copy-start.2
  8.5 0.0 copy-start.5
  8.6 0.0 copy-start.3
  8.6 2.8 %collective-permute-start.5 = (bf16[2,2,32,128]{3,2,1,0:T(8,128)(2,1)S(1)}, bf16[2,2,32,128]{3,2,1,0:T(8,128)(2,1)S(1)}, u32[]{:S(2)}, u32[]{:S(2)}) collective-permute-start(bf16[2,2,32,128]{3,2,1,0:T(8,128)(2,1)S(1)} %get-tuple-element.12.refs_3_), channel_id=1, source_target_pairs={{0,6},{1,15},{2,4},{3,13},{4,2},{5,11},{6,0},{7,9},{8,14},{9,7},{1... | collective-permute-start | bytes 98312 | tf_op jit(solution)/shard_map/ppermute | solution.py:175
  11.4 0.0 collective-permute-done.1.refs_0_
  11.4 0.6 %collective-permute-done.2.refs_1_ = bf16[2,8192]{1,0:T(2,128)(2,1)S(1)} collective-permute-done((bf16[2,8192]{1,0:T(2,128)(2,1)}, bf16[2,8192]{1,0:T(2,128)(2,1)S(1)}, u32[]{:S(2)}, u32[]{:S(2)}) %collective-permute-start.2) | collective-permute-done | bytes 32800 | tf_op jit(solution)/shard_map/ppermute | solution.py:175
  12.0 0.0 copy-done.4
  12.0 0.2 owner_rest.1
  12.2 0.3 %collective-permute-start.7 = (bf16[2,2,32,128]{3,2,1,0:T(8,128)(2,1)S(1)}, bf16[2,2,32,128]{3,2,1,0:T(8,128)(2,1)S(1)}, u32[]{:S(2)}, u32[]{:S(2)}) collective-permute-start(bf16[2,2,32,128]{3,2,1,0:T(8,128)(2,1)S(1)} %get-tuple-element.15), channel_id=1, source_target_pairs={{0,8},{1,11},{2,10},{3,9},{4,12},{5,15},{6,14},{7,13},{8,0},{9,3},... | collective-permute-start | bytes 98312 | tf_op jit(solution)/shard_map/ppermute | solution.py:175
  12.5 1.6 %collective-permute-start.8 = (bf16[2,2,32,128]{3,2,1,0:T(8,128)(2,1)S(1)}, bf16[2,2,32,128]{3,2,1,0:T(8,128)(2,1)S(1)}, u32[]{:S(2)}, u32[]{:S(2)}) collective-permute-start(bf16[2,2,32,128]{3,2,1,0:T(8,128)(2,1)S(1)} %get-tuple-element.16), channel_id=1, source_target_pairs={{0,4},{1,13},{2,6},{3,15},{4,0},{5,9},{6,2},{7,11},{8,12},{9,5},{1... | collective-permute-start | bytes 98312 | tf_op jit(solution)/shard_map/ppermute | solution.py:175
  14.1 1.3 %collective-permute-start.6 = (bf16[2,2,32,128]{3,2,1,0:T(8,128)(2,1)S(1)}, bf16[2,2,32,128]{3,2,1,0:T(8,128)(2,1)S(1)}, u32[]{:S(2)}, u32[]{:S(2)}) collective-permute-start(bf16[2,2,32,128]{3,2,1,0:T(8,128)(2,1)S(1)} %get-tuple-element.14), channel_id=1, source_target_pairs={{0,2},{1,3},{2,0},{3,1},{4,6},{5,7},{6,4},{7,5},{8,10},{9,11},{10,... | collective-permute-start | bytes 98312 | tf_op jit(solution)/shard_map/ppermute | solution.py:175
  15.3 2.0 %collective-permute-done.7.refs_2_ = bf16[2,2,32,128]{3,2,1,0:T(8,128)(2,1)S(1)} collective-permute-done((bf16[2,2,32,128]{3,2,1,0:T(8,128)(2,1)S(1)}, bf16[2,2,32,128]{3,2,1,0:T(8,128)(2,1)S(1)}, u32[]{:S(2)}, u32[]{:S(2)}) %collective-permute-start.7) | collective-permute-done | bytes 32800 | tf_op jit(solution)/shard_map/ppermute | solution.py:175
  17.3 0.0 collective-permute-done.8.refs_3_
  17.3 0.0 collective-permute-done.5.refs_0_
  17.3 0.9 %collective-permute-done.6.refs_1_ = bf16[2,2,32,128]{3,2,1,0:T(8,128)(2,1)S(1)} collective-permute-done((bf16[2,2,32,128]{3,2,1,0:T(8,128)(2,1)S(1)}, bf16[2,2,32,128]{3,2,1,0:T(8,128)(2,1)S(1)}, u32[]{:S(2)}, u32[]{:S(2)}) %collective-permute-start.6) | collective-permute-done | bytes 32800 | tf_op jit(solution)/shard_map/ppermute | solution.py:175
  18.3 0.5 %collective-permute-start.9 = (bf16[2,32,128]{2,1,0:T(8,128)(2,1)S(1)}, bf16[2,32,128]{2,1,0:T(8,128)(2,1)S(1)}, u32[]{:S(2)}, u32[]{:S(2)}) collective-permute-start(bf16[2,32,128]{2,1,0:T(8,128)(2,1)S(1)} %get-tuple-element.18), channel_id=1, source_target_pairs={{0,1},{1,0},{2,3},{3,2},{4,5},{5,4},{6,7},{7,6},{8,9},{9,8},{10,11... | collective-permute-start | bytes 49160 | tf_op jit(solution)/shard_map/ppermute | solution.py:178
  18.8 0.0 copy-done.6
  18.8 0.1 compare_convert_fusion.live_ref
  18.9 0.0 copy-done.2
  18.9 0.2 turn.1.refs_2_
  19.1 0.0 copy-done.5
  19.1 0.5 %collective-permute-done.9.refs_1_ = bf16[2,32,128]{2,1,0:T(8,128)(2,1)S(1)} collective-permute-done((bf16[2,32,128]{2,1,0:T(8,128)(2,1)S(1)}, bf16[2,32,128]{2,1,0:T(8,128)(2,1)S(1)}, u32[]{:S(2)}, u32[]{:S(2)}) %collective-permute-start.9) | collective-permute-done | bytes 16416 | tf_op jit(solution)/shard_map/ppermute | solution.py:178
  19.7 0.0 copy-done.3
  19.7 1.1 %attend.1 = bf16[2,4096]{1,0:T(2,128)(2,1)} custom-call(f32[2,1,256]{2,1,0:T(1,128)S(1)} %compare_convert_fusion.live_ref, bf16[2,32,128]{2,1,0:T(8,128)(2,1)S(1)} %bitcast.4, bf16[2,32,128]{2,1,0:T(8,128)(2,1)S(1)} %get-tuple-element.17.refs_0_, bf16[2,32,128]{2,1,0:T(8,128)(2,1)S(1)} %collective-permute-done.9.refs_1_, ...), custom_call_target="tpu_custom_call" | custom-call | tf_op jit(solution)/shard_map/attend/pallas_call | solution.py:259
  (2 shorter events, 0.0 us)
Async XLA Ops:
  0.0 8.3 %copy-start.1 = (bf16[8,16,4096]{2,1,0:T(8,128)(2,1)S(1)}, bf16[8,16,4096]{2,1,0:T(8,128)(2,1)}, u32[]{:S(2)}) copy-start(bf16[8,16,4096]{2,1,0:T(8,128)(2,1)} %mine_ref.3) | copy-start | bytes 3145732
  0.0 8.3 %copy-start = (bf16[8,16,8192]{2,1,0:T(8,128)(2,1)S(1)}, bf16[8,16,8192]{2,1,0:T(8,128)(2,1)}, u32[]{:S(2)}) copy-start(bf16[8,16,8192]{2,1,0:T(8,128)(2,1)} %down_ref.3) | copy-start | bytes 6291460
  0.0 8.3 %collective-permute-start = (bf16[8,16,4096]{2,1,0:T(8,128)(2,1)}, bf16[8,16,4096]{2,1,0:T(8,128)(2,1)S(1)}, u32[]{:S(2)}, u32[]{:S(2)}) collective-permute-start(bf16[8,16,4096]{2,1,0:T(8,128)(2,1)} %mine_ref.3), channel_id=1, source_target_pairs={{0,1},{1,0},{2,3},{3,2},{4,5},{5,4},{6,7},{7,6},{8,9},{9,8},{10,11... | collective-permute-start | bytes 3145736 | tf_op jit(solution)/shard_map/ppermute | solution.py:178
  0.5 7.8 %collective-permute-start.3 = (bf16[2,8192]{1,0:T(2,128)(2,1)}, bf16[2,8192]{1,0:T(2,128)(2,1)S(1)}, u32[]{:S(2)}, u32[]{:S(2)}) collective-permute-start(bf16[2,8192]{1,0:T(2,128)(2,1)} %refs_2_.1), channel_id=1, source_target_pairs={{0,6},{1,15},{2,4},{3,13},{4,2},{5,11},{6,0},{7,9},{8,14},{9,7},{1... | collective-permute-start | bytes 98312 | tf_op jit(solution)/shard_map/ppermute | solution.py:175
  4.0 4.3 %collective-permute-start.4 = (bf16[2,8192]{1,0:T(2,128)(2,1)}, bf16[2,8192]{1,0:T(2,128)(2,1)S(1)}, u32[]{:S(2)}, u32[]{:S(2)}) collective-permute-start(bf16[2,8192]{1,0:T(2,128)(2,1)} %refs_2_.1), channel_id=1, source_target_pairs={{0,2},{1,3},{2,0},{3,1},{4,6},{5,7},{6,4},{7,5},{8,10},{9,11},{10,... | collective-permute-start | bytes 98312 | tf_op jit(solution)/shard_map/ppermute | solution.py:175
  4.6 6.8 %collective-permute-start.1 = (bf16[2,8192]{1,0:T(2,128)(2,1)}, bf16[2,8192]{1,0:T(2,128)(2,1)S(1)}, u32[]{:S(2)}, u32[]{:S(2)}) collective-permute-start(bf16[2,8192]{1,0:T(2,128)(2,1)} %refs_2_.1), channel_id=1, source_target_pairs={{0,8},{1,11},{2,10},{3,9},{4,12},{5,15},{6,14},{7,13},{8,0},{9,3},... | collective-permute-start | bytes 98312 | tf_op jit(solution)/shard_map/ppermute | solution.py:175
  7.2 4.8 %collective-permute-start.2 = (bf16[2,8192]{1,0:T(2,128)(2,1)}, bf16[2,8192]{1,0:T(2,128)(2,1)S(1)}, u32[]{:S(2)}, u32[]{:S(2)}) collective-permute-start(bf16[2,8192]{1,0:T(2,128)(2,1)} %refs_2_.1), channel_id=1, source_target_pairs={{0,4},{1,13},{2,6},{3,15},{4,0},{5,9},{6,2},{7,11},{8,12},{9,5},{1... | collective-permute-start | bytes 98312 | tf_op jit(solution)/shard_map/ppermute | solution.py:175
  8.3 3.7 %copy-start.4 = (bf16[2,8192]{1,0:T(2,128)(2,1)S(1)}, bf16[2,8192]{1,0:T(2,128)(2,1)}, u32[]{:S(2)}) copy-start(bf16[2,8192]{1,0:T(2,128)(2,1)} %refs_2_.1) | copy-start | bytes 98308
  8.5 10.3 %copy-start.6 = (s32[2]{0:T(128)S(1)}, s32[2]{0:T(128)}, u32[]{:S(2)}) copy-start(s32[2]{0:T(128)} %param.15) | copy-start | bytes 28
  8.5 10.4 %copy-start.2 = (bf16[2,4,256,128]{3,2,1,0:T(8,128)(2,1)S(1)}, bf16[2,4,256,128]{3,2,1,0:T(8,128)(2,1)}, u32[]{:S(2)}) copy-start(bf16[2,4,256,128]{3,2,1,0:T(8,128)(2,1)} %key_ref.1) | copy-start | bytes 1572868
  8.5 10.5 %copy-start.5 = (bf16[2,4096]{1,0:T(2,128)(2,1)S(1)}, bf16[2,4096]{1,0:T(2,128)(2,1)}, u32[]{:S(2)}) copy-start(bf16[2,4096]{1,0:T(2,128)(2,1)} %param.9) | copy-start | bytes 49156
  8.6 11.1 %copy-start.3 = (bf16[2,4,256,128]{3,2,1,0:T(8,128)(2,1)S(1)}, bf16[2,4,256,128]{3,2,1,0:T(8,128)(2,1)}, u32[]{:S(2)}) copy-start(bf16[2,4,256,128]{3,2,1,0:T(8,128)(2,1)} %refs_3_.1) | copy-start | bytes 1572868
  8.6 8.8 %collective-permute-start.5 = (bf16[2,2,32,128]{3,2,1,0:T(8,128)(2,1)S(1)}, bf16[2,2,32,128]{3,2,1,0:T(8,128)(2,1)S(1)}, u32[]{:S(2)}, u32[]{:S(2)}) collective-permute-start(bf16[2,2,32,128]{3,2,1,0:T(8,128)(2,1)S(1)} %get-tuple-element.12.refs_3_), channel_id=1, source_target_pairs={{0,6},{1,15},{2,4},{3,13},{4,2},{5,11},{6,0},{7,9},{8,14},{9,7},{1... | collective-permute-start | bytes 98312 | tf_op jit(solution)/shard_map/ppermute | solution.py:175
  12.2 5.1 %collective-permute-start.7 = (bf16[2,2,32,128]{3,2,1,0:T(8,128)(2,1)S(1)}, bf16[2,2,32,128]{3,2,1,0:T(8,128)(2,1)S(1)}, u32[]{:S(2)}, u32[]{:S(2)}) collective-permute-start(bf16[2,2,32,128]{3,2,1,0:T(8,128)(2,1)S(1)} %get-tuple-element.15), channel_id=1, source_target_pairs={{0,8},{1,11},{2,10},{3,9},{4,12},{5,15},{6,14},{7,13},{8,0},{9,3},... | collective-permute-start | bytes 98312 | tf_op jit(solution)/shard_map/ppermute | solution.py:175
  12.5 4.9 %collective-permute-start.8 = (bf16[2,2,32,128]{3,2,1,0:T(8,128)(2,1)S(1)}, bf16[2,2,32,128]{3,2,1,0:T(8,128)(2,1)S(1)}, u32[]{:S(2)}, u32[]{:S(2)}) collective-permute-start(bf16[2,2,32,128]{3,2,1,0:T(8,128)(2,1)S(1)} %get-tuple-element.16), channel_id=1, source_target_pairs={{0,4},{1,13},{2,6},{3,15},{4,0},{5,9},{6,2},{7,11},{8,12},{9,5},{1... | collective-permute-start | bytes 98312 | tf_op jit(solution)/shard_map/ppermute | solution.py:175
  14.1 4.2 %collective-permute-start.6 = (bf16[2,2,32,128]{3,2,1,0:T(8,128)(2,1)S(1)}, bf16[2,2,32,128]{3,2,1,0:T(8,128)(2,1)S(1)}, u32[]{:S(2)}, u32[]{:S(2)}) collective-permute-start(bf16[2,2,32,128]{3,2,1,0:T(8,128)(2,1)S(1)} %get-tuple-element.14), channel_id=1, source_target_pairs={{0,2},{1,3},{2,0},{3,1},{4,6},{5,7},{6,4},{7,5},{8,10},{9,11},{10,... | collective-permute-start | bytes 98312 | tf_op jit(solution)/shard_map/ppermute | solution.py:175
  18.3 1.4 %collective-permute-start.9 = (bf16[2,32,128]{2,1,0:T(8,128)(2,1)S(1)}, bf16[2,32,128]{2,1,0:T(8,128)(2,1)S(1)}, u32[]{:S(2)}, u32[]{:S(2)}) collective-permute-start(bf16[2,32,128]{2,1,0:T(8,128)(2,1)S(1)} %get-tuple-element.18), channel_id=1, source_target_pairs={{0,1},{1,0},{2,3},{3,2},{4,5},{5,4},{6,7},{7,6},{8,9},{9,8},{10,11... | collective-permute-start | bytes 49160 | tf_op jit(solution)/shard_map/ppermute | solution.py:178

commit v14 on v12

--- a/solution.py
+++ b/solution.py
@@ -15,7 +15,7 @@
 VMEM = pl.BlockSpec(memory_space=pltpu.VMEM)
 SMEM = pl.BlockSpec(memory_space=pltpu.SMEM)
 PARAMS = pltpu.CompilerParams(vmem_limit_bytes=VMEM_LIMIT)
-TURNS = ((3, 1, 4, 2, 0), (7, 1, 5, 6, 0))
+TURNS = ((4, 1, 3, 2, 0), (7, 1, 5, 6, 0))
 SENT = len(TURNS[0]) - 1
 EARLY = 2
 SHARED = [first == second for first, second in zip(*TURNS)]

time: 20.9 us -> 21.5 us (1.029)
  waiting for transfers between devices: 5.33 us -> 6.63 us
  starting transfers between devices: 12.4 us -> 11.9 us
    ppermute x8, waiting for transfers between devices: 4.25 us -> 5.55 us  [visit(): return lax.ppermute(array, ('store', 'tensor'), turn_pairs(turn))]
    ppermute x8, starting transfers between devices: 11.9 us -> 11.4 us  [visit(): return lax.ppermute(array, ('store', 'tensor'), turn_pairs(turn))]
  transfers between devices with their start and end apart: 10 -> 10, of which waited for: 4 -> 6; matrix products, arithmetic and copies ran while one was open for 0% -> 0% of each run, Pallas kernels for 7% -> 7%
where the time goes in v14:
time: 21.5 us
  starting transfers between devices  11.9 us (55%)
  waiting for transfers between devices  6.63 us (31%)
  Pallas kernels  2.69 us (13%)
    ppermute x8, starting transfers between devices, visit(): return lax.ppermute(array, ('store', 'tensor'), turn_pairs(turn))  11.4 us
    ppermute x8, waiting for transfers between devices, visit(): return lax.ppermute(array, ('store', 'tensor'), turn_pairs(turn))  5.55 us
    pallas_call x1, Pallas kernels, per_device(): pl.pallas_call(functools.partial(attend_kernel, len(deltas)), out_shape=j...  1.16 us
    ppermute x2, waiting for transfers between devices, swap(): return lax.ppermute(array, 'tensor', [(0, 1), (1, 0)])  1.08 us
    pallas_call x2, Pallas kernels, work(): pl.pallas_call(functools.partial(owner_kernel, turns), out_shape=[jax.Sha...  0.83 us
    pallas_call x1, Pallas kernels, scalars(): pl.pallas_call(scalars_kernel, out_shape=pltpu.SMEM(ids.shape, ids.dtype)...  0.67 us
    ppermute x2, starting transfers between devices, swap(): return lax.ppermute(array, 'tensor', [(0, 1), (1, 0)])  0.52 us
  transfers between devices with their start and end apart: 10, of which 6 were waited for; matrix products, arithmetic and copies ran while one was open for 0% of the time, Pallas kernels for 7%

profile of v14, /device:TPU:0, one launch (start us, length us, event | category | flops | bytes accessed | tf_op | source)
XLA Modules:
  0.0 21.5 jit_solution(14997592380287202685)
XLA Ops:
  0.0 0.0 copy-start.1
  0.0 0.0 copy-start
  0.0 0.5 %collective-permute-start = (bf16[8,16,4096]{2,1,0:T(8,128)(2,1)}, bf16[8,16,4096]{2,1,0:T(8,128)(2,1)S(1)}, u32[]{:S(2)}, u32[]{:S(2)}) collective-permute-start(bf16[8,16,4096]{2,1,0:T(8,128)(2,1)} %mine_ref.3), channel_id=1, source_target_pairs={{0,1},{1,0},{2,3},{3,2},{4,5},{5,4},{6,7},{7,6},{8,9},{9,8},{10,11... | collective-permute-start | bytes 3145736 | tf_op jit(solution)/shard_map/ppermute | solution.py:172
  0.5 3.7 %collective-permute-start.3 = (bf16[2,8192]{1,0:T(2,128)(2,1)}, bf16[2,8192]{1,0:T(2,128)(2,1)S(1)}, u32[]{:S(2)}, u32[]{:S(2)}) collective-permute-start(bf16[2,8192]{1,0:T(2,128)(2,1)} %refs_2_.2), channel_id=1, source_target_pairs={{0,8},{1,15},{2,10},{3,13},{4,12},{5,11},{6,14},{7,9},{8,0},{9,7},... | collective-permute-start | bytes 98312 | tf_op jit(solution)/shard_map/ppermute | solution.py:169
  4.1 1.5 %collective-permute-start.4 = (bf16[2,8192]{1,0:T(2,128)(2,1)}, bf16[2,8192]{1,0:T(2,128)(2,1)S(1)}, u32[]{:S(2)}, u32[]{:S(2)}) collective-permute-start(bf16[2,8192]{1,0:T(2,128)(2,1)} %refs_2_.2), channel_id=1, source_target_pairs={{0,2},{1,3},{2,0},{3,1},{4,6},{5,7},{6,4},{7,5},{8,10},{9,11},{10,... | collective-permute-start | bytes 98312 | tf_op jit(solution)/shard_map/ppermute | solution.py:169
  5.6 1.5 %collective-permute-start.1 = (bf16[2,8192]{1,0:T(2,128)(2,1)}, bf16[2,8192]{1,0:T(2,128)(2,1)S(1)}, u32[]{:S(2)}, u32[]{:S(2)}) collective-permute-start(bf16[2,8192]{1,0:T(2,128)(2,1)} %refs_2_.2), channel_id=1, source_target_pairs={{0,6},{1,11},{2,4},{3,9},{4,2},{5,15},{6,0},{7,13},{8,14},{9,3},{1... | collective-permute-start | bytes 98312 | tf_op jit(solution)/shard_map/ppermute | solution.py:169
  7.2 0.4 %collective-permute-start.2 = (bf16[2,8192]{1,0:T(2,128)(2,1)}, bf16[2,8192]{1,0:T(2,128)(2,1)S(1)}, u32[]{:S(2)}, u32[]{:S(2)}) collective-permute-start(bf16[2,8192]{1,0:T(2,128)(2,1)} %refs_2_.2), channel_id=1, source_target_pairs={{0,4},{1,13},{2,6},{3,15},{4,0},{5,9},{6,2},{7,11},{8,12},{9,5},{1... | collective-permute-start | bytes 98312 | tf_op jit(solution)/shard_map/ppermute | solution.py:169
  7.6 0.7 %scalars.1.ids_ref = s32[16]{0:T(128)S(4)} custom-call(s32[16]{0:T(128)} %ids_hbm.1, bf16[8,16,8192]{2,1,0:T(8,128)(2,1)} %down_ref.3, bf16[8,16,4096]{2,1,0:T(8,128)(2,1)} %mine_ref.3), custom_call_target="tpu_custom_call" | custom-call | bytes 3145728 | tf_op jit(solution)/shard_map/scalars/pallas_call | solution.py:33
  8.3 0.0 copy-start.4
  8.3 0.0 collective-permute-done.3.refs_0_
  8.3 0.0 collective-permute-done.4.refs_1_
  8.3 0.0 collective-permute-done.other_ref
  8.3 0.0 copy-done.1
  8.3 0.0 copy-done
  8.3 0.4 %owner_first.1 = (bf16[2,2,32,128]{3,2,1,0:T(8,128)(2,1)S(1)}, bf16[2,2,32,128]{3,2,1,0:T(8,128)(2,1)S(1)}) custom-call(s32[16]{0:T(128)S(4)} %scalars.1.ids_ref, bf16[8,16,8192]{2,1,0:T(8,128)(2,1)S(1)} %copy-done, bf16[8,16,4096]{2,1,0:T(8,128)(2,1)S(1)} %copy-done.1, bf16[8,16,4096]{2,1,0:T(8,128)(2,1)S(1)} %collective-permute-done.other_ref, ...), custom_call_target="tpu_custom_call" | custom-call | tf_op jit(solution)/shard_map/owner_first/pallas_call | solution.py:182
  8.7 0.0 copy-start.6
  8.8 0.0 copy-start.5
  8.8 0.0 copy-start.2
  8.8 0.0 copy-start.3
  8.8 0.7 %collective-permute-start.5 = (bf16[2,2,32,128]{3,2,1,0:T(8,128)(2,1)S(1)}, bf16[2,2,32,128]{3,2,1,0:T(8,128)(2,1)S(1)}, u32[]{:S(2)}, u32[]{:S(2)}) collective-permute-start(bf16[2,2,32,128]{3,2,1,0:T(8,128)(2,1)S(1)} %get-tuple-element.12.refs_3_), channel_id=1, source_target_pairs={{0,8},{1,15},{2,10},{3,13},{4,12},{5,11},{6,14},{7,9},{8,0},{9,7},... | collective-permute-start | bytes 98312 | tf_op jit(solution)/shard_map/ppermute | solution.py:169
  9.5 1.2 %collective-permute-done.1.refs_0_ = bf16[2,8192]{1,0:T(2,128)(2,1)S(1)} collective-permute-done((bf16[2,8192]{1,0:T(2,128)(2,1)}, bf16[2,8192]{1,0:T(2,128)(2,1)S(1)}, u32[]{:S(2)}, u32[]{:S(2)}) %collective-permute-start.1) | collective-permute-done | bytes 32800 | tf_op jit(solution)/shard_map/ppermute | solution.py:169
  10.6 1.4 %collective-permute-done.2.refs_1_ = bf16[2,8192]{1,0:T(2,128)(2,1)S(1)} collective-permute-done((bf16[2,8192]{1,0:T(2,128)(2,1)}, bf16[2,8192]{1,0:T(2,128)(2,1)S(1)}, u32[]{:S(2)}, u32[]{:S(2)}) %collective-permute-start.2) | collective-permute-done | bytes 32800 | tf_op jit(solution)/shard_map/ppermute | solution.py:169
  12.0 0.0 copy-done.4
  12.0 0.4 %owner_rest.1 = (bf16[2,2,32,128]{3,2,1,0:T(8,128)(2,1)S(1)}, bf16[2,2,32,128]{3,2,1,0:T(8,128)(2,1)S(1)}, bf16[2,2,32,128]{3,2,1,0:T(8,128)(2,1)S(1)}) custom-call(s32[16]{0:T(128)S(4)} %scalars.1.ids_ref, bf16[8,16,8192]{2,1,0:T(8,128)(2,1)S(1)} %copy-done, bf16[8,16,4096]{2,1,0:T(8,128)(2,1)S(1)} %copy-done.1, ...), custom_call_target="tpu_custom_call" | custom-call | tf_op jit(solution)/shard_map/owner_rest/pallas_call | solution.py:182
  12.4 0.9 %collective-permute-start.7 = (bf16[2,2,32,128]{3,2,1,0:T(8,128)(2,1)S(1)}, bf16[2,2,32,128]{3,2,1,0:T(8,128)(2,1)S(1)}, u32[]{:S(2)}, u32[]{:S(2)}) collective-permute-start(bf16[2,2,32,128]{3,2,1,0:T(8,128)(2,1)S(1)} %get-tuple-element.15), channel_id=1, source_target_pairs={{0,6},{1,11},{2,4},{3,9},{4,2},{5,15},{6,0},{7,13},{8,14},{9,3},{1... | collective-permute-start | bytes 98312 | tf_op jit(solution)/shard_map/ppermute | solution.py:169
  13.4 1.7 %collective-permute-start.8 = (bf16[2,2,32,128]{3,2,1,0:T(8,128)(2,1)S(1)}, bf16[2,2,32,128]{3,2,1,0:T(8,128)(2,1)S(1)}, u32[]{:S(2)}, u32[]{:S(2)}) collective-permute-start(bf16[2,2,32,128]{3,2,1,0:T(8,128)(2,1)S(1)} %get-tuple-element.16), channel_id=1, source_target_pairs={{0,4},{1,13},{2,6},{3,15},{4,0},{5,9},{6,2},{7,11},{8,12},{9,5},{1... | collective-permute-start | bytes 98312 | tf_op jit(solution)/shard_map/ppermute | solution.py:169
  15.1 0.9 %collective-permute-start.6 = (bf16[2,2,32,128]{3,2,1,0:T(8,128)(2,1)S(1)}, bf16[2,2,32,128]{3,2,1,0:T(8,128)(2,1)S(1)}, u32[]{:S(2)}, u32[]{:S(2)}) collective-permute-start(bf16[2,2,32,128]{3,2,1,0:T(8,128)(2,1)S(1)} %get-tuple-element.14), channel_id=1, source_target_pairs={{0,2},{1,3},{2,0},{3,1},{4,6},{5,7},{6,4},{7,5},{8,10},{9,11},{10,... | collective-permute-start | bytes 98312 | tf_op jit(solution)/shard_map/ppermute | solution.py:169
  16.0 1.3 %collective-permute-done.7.refs_2_ = bf16[2,2,32,128]{3,2,1,0:T(8,128)(2,1)S(1)} collective-permute-done((bf16[2,2,32,128]{3,2,1,0:T(8,128)(2,1)S(1)}, bf16[2,2,32,128]{3,2,1,0:T(8,128)(2,1)S(1)}, u32[]{:S(2)}, u32[]{:S(2)}) %collective-permute-start.7) | collective-permute-done | bytes 32800 | tf_op jit(solution)/shard_map/ppermute | solution.py:169
  17.3 0.4 %collective-permute-done.8.refs_3_ = bf16[2,2,32,128]{3,2,1,0:T(8,128)(2,1)S(1)} collective-permute-done((bf16[2,2,32,128]{3,2,1,0:T(8,128)(2,1)S(1)}, bf16[2,2,32,128]{3,2,1,0:T(8,128)(2,1)S(1)}, u32[]{:S(2)}, u32[]{:S(2)}) %collective-permute-start.8) | collective-permute-done | bytes 32800 | tf_op jit(solution)/shard_map/ppermute | solution.py:169
  17.7 0.0 collective-permute-done.5.refs_0_
  17.7 1.3 %collective-permute-done.6.refs_1_ = bf16[2,2,32,128]{3,2,1,0:T(8,128)(2,1)S(1)} collective-permute-done((bf16[2,2,32,128]{3,2,1,0:T(8,128)(2,1)S(1)}, bf16[2,2,32,128]{3,2,1,0:T(8,128)(2,1)S(1)}, u32[]{:S(2)}, u32[]{:S(2)}) %collective-permute-start.6) | collective-permute-done | bytes 32800 | tf_op jit(solution)/shard_map/ppermute | solution.py:169
  19.0 0.1 collective-permute-start.9
  19.1 0.0 copy-done.6
  19.1 0.1 compare_convert_fusion.live_ref
  19.2 0.0 copy-done.5
  19.2 1.1 %collective-permute-done.9.refs_1_ = bf16[2,32,128]{2,1,0:T(8,128)(2,1)S(1)} collective-permute-done((bf16[2,32,128]{2,1,0:T(8,128)(2,1)S(1)}, bf16[2,32,128]{2,1,0:T(8,128)(2,1)S(1)}, u32[]{:S(2)}, u32[]{:S(2)}) %collective-permute-start.9) | collective-permute-done | bytes 16416 | tf_op jit(solution)/shard_map/ppermute | solution.py:172
  20.3 0.0 copy-done.2
  20.3 0.0 copy-done.3
  20.3 1.2 %attend.1 = bf16[2,4096]{1,0:T(2,128)(2,1)} custom-call(f32[2,1,256]{2,1,0:T(1,128)S(1)} %compare_convert_fusion.live_ref, bf16[2,32,128]{2,1,0:T(8,128)(2,1)S(1)} %bitcast.4, bf16[2,32,128]{2,1,0:T(8,128)(2,1)S(1)} %get-tuple-element.17.refs_0_, bf16[2,32,128]{2,1,0:T(8,128)(2,1)S(1)} %collective-permute-done.9.refs_1_, ...), custom_call_target="tpu_custom_call" | custom-call | tf_op jit(solution)/shard_map/attend/pallas_call | solution.py:245
  (2 shorter events, 0.0 us)
Async XLA Ops:
  0.0 8.3 %copy-start.1 = (bf16[8,16,4096]{2,1,0:T(8,128)(2,1)S(1)}, bf16[8,16,4096]{2,1,0:T(8,128)(2,1)}, u32[]{:S(2)}) copy-start(bf16[8,16,4096]{2,1,0:T(8,128)(2,1)} %mine_ref.3) | copy-start | bytes 3145732
  0.0 8.3 %copy-start = (bf16[8,16,8192]{2,1,0:T(8,128)(2,1)S(1)}, bf16[8,16,8192]{2,1,0:T(8,128)(2,1)}, u32[]{:S(2)}) copy-start(bf16[8,16,8192]{2,1,0:T(8,128)(2,1)} %down_ref.3) | copy-start | bytes 6291460
  0.0 8.3 %collective-permute-start = (bf16[8,16,4096]{2,1,0:T(8,128)(2,1)}, bf16[8,16,4096]{2,1,0:T(8,128)(2,1)S(1)}, u32[]{:S(2)}, u32[]{:S(2)}) collective-permute-start(bf16[8,16,4096]{2,1,0:T(8,128)(2,1)} %mine_ref.3), channel_id=1, source_target_pairs={{0,1},{1,0},{2,3},{3,2},{4,5},{5,4},{6,7},{7,6},{8,9},{9,8},{10,11... | collective-permute-start | bytes 3145736 | tf_op jit(solution)/shard_map/ppermute | solution.py:172
  0.5 7.8 %collective-permute-start.3 = (bf16[2,8192]{1,0:T(2,128)(2,1)}, bf16[2,8192]{1,0:T(2,128)(2,1)S(1)}, u32[]{:S(2)}, u32[]{:S(2)}) collective-permute-start(bf16[2,8192]{1,0:T(2,128)(2,1)} %refs_2_.2), channel_id=1, source_target_pairs={{0,8},{1,15},{2,10},{3,13},{4,12},{5,11},{6,14},{7,9},{8,0},{9,7},... | collective-permute-start | bytes 98312 | tf_op jit(solution)/shard_map/ppermute | solution.py:169
  4.1 4.2 %collective-permute-start.4 = (bf16[2,8192]{1,0:T(2,128)(2,1)}, bf16[2,8192]{1,0:T(2,128)(2,1)S(1)}, u32[]{:S(2)}, u32[]{:S(2)}) collective-permute-start(bf16[2,8192]{1,0:T(2,128)(2,1)} %refs_2_.2), channel_id=1, source_target_pairs={{0,2},{1,3},{2,0},{3,1},{4,6},{5,7},{6,4},{7,5},{8,10},{9,11},{10,... | collective-permute-start | bytes 98312 | tf_op jit(solution)/shard_map/ppermute | solution.py:169
  5.6 5.0 %collective-permute-start.1 = (bf16[2,8192]{1,0:T(2,128)(2,1)}, bf16[2,8192]{1,0:T(2,128)(2,1)S(1)}, u32[]{:S(2)}, u32[]{:S(2)}) collective-permute-start(bf16[2,8192]{1,0:T(2,128)(2,1)} %refs_2_.2), channel_id=1, source_target_pairs={{0,6},{1,11},{2,4},{3,9},{4,2},{5,15},{6,0},{7,13},{8,14},{9,3},{1... | collective-permute-start | bytes 98312 | tf_op jit(solution)/shard_map/ppermute | solution.py:169
  7.2 4.8 %collective-permute-start.2 = (bf16[2,8192]{1,0:T(2,128)(2,1)}, bf16[2,8192]{1,0:T(2,128)(2,1)S(1)}, u32[]{:S(2)}, u32[]{:S(2)}) collective-permute-start(bf16[2,8192]{1,0:T(2,128)(2,1)} %refs_2_.2), channel_id=1, source_target_pairs={{0,4},{1,13},{2,6},{3,15},{4,0},{5,9},{6,2},{7,11},{8,12},{9,5},{1... | collective-permute-start | bytes 98312 | tf_op jit(solution)/shard_map/ppermute | solution.py:169
  8.3 3.7 %copy-start.4 = (bf16[2,8192]{1,0:T(2,128)(2,1)S(1)}, bf16[2,8192]{1,0:T(2,128)(2,1)}, u32[]{:S(2)}) copy-start(bf16[2,8192]{1,0:T(2,128)(2,1)} %refs_2_.2) | copy-start | bytes 98308
  8.7 10.4 %copy-start.6 = (s32[2]{0:T(128)S(1)}, s32[2]{0:T(128)}, u32[]{:S(2)}) copy-start(s32[2]{0:T(128)} %param.15) | copy-start | bytes 28
  8.8 10.4 %copy-start.5 = (bf16[2,4096]{1,0:T(2,128)(2,1)S(1)}, bf16[2,4096]{1,0:T(2,128)(2,1)}, u32[]{:S(2)}) copy-start(bf16[2,4096]{1,0:T(2,128)(2,1)} %param.9) | copy-start | bytes 49156
  8.8 11.5 %copy-start.2 = (bf16[2,4,256,128]{3,2,1,0:T(8,128)(2,1)S(1)}, bf16[2,4,256,128]{3,2,1,0:T(8,128)(2,1)}, u32[]{:S(2)}) copy-start(bf16[2,4,256,128]{3,2,1,0:T(8,128)(2,1)} %refs_2_.3) | copy-start | bytes 1572868
  8.8 11.5 %copy-start.3 = (bf16[2,4,256,128]{3,2,1,0:T(8,128)(2,1)S(1)}, bf16[2,4,256,128]{3,2,1,0:T(8,128)(2,1)}, u32[]{:S(2)}) copy-start(bf16[2,4,256,128]{3,2,1,0:T(8,128)(2,1)} %refs_3_.1) | copy-start | bytes 1572868
  8.8 8.9 %collective-permute-start.5 = (bf16[2,2,32,128]{3,2,1,0:T(8,128)(2,1)S(1)}, bf16[2,2,32,128]{3,2,1,0:T(8,128)(2,1)S(1)}, u32[]{:S(2)}, u32[]{:S(2)}) collective-permute-start(bf16[2,2,32,128]{3,2,1,0:T(8,128)(2,1)S(1)} %get-tuple-element.12.refs_3_), channel_id=1, source_target_pairs={{0,8},{1,15},{2,10},{3,13},{4,12},{5,11},{6,14},{7,9},{8,0},{9,7},... | collective-permute-start | bytes 98312 | tf_op jit(solution)/shard_map/ppermute | solution.py:169
  12.4 4.9 %collective-permute-start.7 = (bf16[2,2,32,128]{3,2,1,0:T(8,128)(2,1)S(1)}, bf16[2,2,32,128]{3,2,1,0:T(8,128)(2,1)S(1)}, u32[]{:S(2)}, u32[]{:S(2)}) collective-permute-start(bf16[2,2,32,128]{3,2,1,0:T(8,128)(2,1)S(1)} %get-tuple-element.15), channel_id=1, source_target_pairs={{0,6},{1,11},{2,4},{3,9},{4,2},{5,15},{6,0},{7,13},{8,14},{9,3},{1... | collective-permute-start | bytes 98312 | tf_op jit(solution)/shard_map/ppermute | solution.py:169
  13.4 4.3 %collective-permute-start.8 = (bf16[2,2,32,128]{3,2,1,0:T(8,128)(2,1)S(1)}, bf16[2,2,32,128]{3,2,1,0:T(8,128)(2,1)S(1)}, u32[]{:S(2)}, u32[]{:S(2)}) collective-permute-start(bf16[2,2,32,128]{3,2,1,0:T(8,128)(2,1)S(1)} %get-tuple-element.16), channel_id=1, source_target_pairs={{0,4},{1,13},{2,6},{3,15},{4,0},{5,9},{6,2},{7,11},{8,12},{9,5},{1... | collective-permute-start | bytes 98312 | tf_op jit(solution)/shard_map/ppermute | solution.py:169
  15.1 3.9 %collective-permute-start.6 = (bf16[2,2,32,128]{3,2,1,0:T(8,128)(2,1)S(1)}, bf16[2,2,32,128]{3,2,1,0:T(8,128)(2,1)S(1)}, u32[]{:S(2)}, u32[]{:S(2)}) collective-permute-start(bf16[2,2,32,128]{3,2,1,0:T(8,128)(2,1)S(1)} %get-tuple-element.14), channel_id=1, source_target_pairs={{0,2},{1,3},{2,0},{3,1},{4,6},{5,7},{6,4},{7,5},{8,10},{9,11},{10,... | collective-permute-start | bytes 98312 | tf_op jit(solution)/shard_map/ppermute | solution.py:169
  19.0 1.2 %collective-permute-start.9 = (bf16[2,32,128]{2,1,0:T(8,128)(2,1)S(1)}, bf16[2,32,128]{2,1,0:T(8,128)(2,1)S(1)}, u32[]{:S(2)}, u32[]{:S(2)}) collective-permute-start(bf16[2,32,128]{2,1,0:T(8,128)(2,1)S(1)} %get-tuple-element.18), channel_id=1, source_target_pairs={{0,1},{1,0},{2,3},{3,2},{4,5},{5,4},{6,7},{7,6},{8,9},{9,8},{10,11... | collective-permute-start | bytes 49160 | tf_op jit(solution)/shard_map/ppermute | solution.py:172

commit v15 on v12

--- a/solution.py
+++ b/solution.py
@@ -55,16 +55,15 @@
     heads = row_ref.shape[0]
     me, core = lax.axis_index("store"), lax.axis_index("tensor")
 
-    def slot_of(partners, row, shared):
+    def slot_of(partners, row):
         source = me ^ jnp.where(core == 0, partners[0], partners[1])
         slot = ids_ref[source * rows + row] - me * count
-        mine = jnp.logical_not(shared) | (core == lax.rem(row, len(TURNS)))
-        return slot, mine & (slot >= 0) & (slot < count)
+        return slot, (slot >= 0) & (slot < count)
 
     owned = {}
     for i, turn in enumerate(turns):
         for row in range(rows):
-            owned[i, row] = slot_of([steps[turn] for steps in TURNS], row, SHARED[turn])[1]
+            owned[i, row] = slot_of([steps[turn] for steps in TURNS], row)[1]
 
             @pl.when(owned[i, row])
             def _():
@@ -78,7 +77,8 @@
     def one_request(index, carry):
         i, row = lax.div(index, rows), lax.rem(index, rows)
         partners = [(jnp.int32(value) >> (4 * i)) & 15 for value in packed]
-        slot, here = slot_of(partners, row, ((jnp.int32(both) >> i) & 1) == 1)
+        slot, here = slot_of(partners, row)
+        whole = ((jnp.int32(both) >> i) & 1) == 0
 
         @pl.when(here)
         def _():
@@ -88,7 +88,8 @@
                 total = total + down * state_ref[i, pl.ds(row, 1), start : start + CHUNK]
             low = jnp.sum(total, axis=1, keepdims=True)
             low = low.astype(jnp.bfloat16).astype(jnp.float32)
-            for half, up_ref in ((core, mine_ref), (1 - core, other_ref)):
+
+            def spread(half, up_ref):
                 for head in range(heads):
                     up = up_ref[slot, :, head * LANES : (head + 1) * LANES]
                     row_ref[head : head + 1, :] = jnp.sum(
@@ -96,6 +97,9 @@
                     )
                 sum_ref[i, row, half] = row_ref[...].astype(sum_ref.dtype)
 
+            spread(core, mine_ref)
+            pl.when(whole)(lambda: spread(1 - core, other_ref))
+
         return carry
 
     lax.fori_loop(0, amount * rows, one_request, 0)
@@ -103,15 +107,16 @@
 
         @pl.when(here)
         def _():
-            delta_refs[i][row] = sum_ref[i, row]
-
-
-def merge_kernel(own_ref, *refs):
+            part = sum_ref.at[i, row]
+            delta_refs[i][row] = part[core] if SHARED[turns[i]] else part[...]
+
+
+def merge_kernel(*refs):
     came_refs, (kept_ref, sent_ref) = refs[:-2], refs[-2:]
     core = lax.axis_index("tensor")
     for half, out_ref in ((core, kept_ref), (1 - core, sent_ref)):
-        total = own_ref[:, half].astype(jnp.float32)
-        for came_ref in came_refs:
+        total = came_refs[0][:, half].astype(jnp.float32)
+        for came_ref in came_refs[1:]:
             total = total + came_ref[:, half].astype(jnp.float32)
         out_ref[...] = total.astype(out_ref.dtype)
 
@@ -181,7 +186,10 @@
         amount = len(turns)
         return pl.pallas_call(
             functools.partial(owner_kernel, turns),
-            out_shape=[jax.ShapeDtypeStruct(wide, jnp.bfloat16)] * amount,
+            out_shape=[
+                jax.ShapeDtypeStruct(block if SHARED[turn] else wide, jnp.bfloat16)
+                for turn in turns
+            ],
             in_specs=[SMEM] + [VMEM] * (amount + 3) + [pl.BlockSpec(memory_space=pl.ANY)] * len(after),
             out_specs=[VMEM] * amount,
             scratch_shapes=[
@@ -197,15 +205,17 @@
     deltas = work("owner_first", (), *range(EARLY))
     deltas += work("owner_rest", deltas[:1], *range(EARLY, SENT + 1))
     came = [visit(delta, turn) for turn, delta in enumerate(deltas[:SENT])]
+    halves = [came[turn] for turn in range(SENT) if SHARED[turn]]
+    wholes = [came[turn] for turn in range(SENT) if not SHARED[turn]]
     kept, sent = pl.pallas_call(
         merge_kernel,
         out_shape=[jax.ShapeDtypeStruct(block, jnp.bfloat16)] * 2,
-        in_specs=[VMEM] * (SENT + 1),
+        in_specs=[VMEM] * len(wholes),
         out_specs=[VMEM] * 2,
         compiler_params=PARAMS,
         name="merge",
-    )(deltas[-1], *came)
-    return [kept, swap(sent)]
+    )(*wholes)
+    return [kept, deltas[-1], *halves, swap(sent)]
 
 
 def exchanged_deltas(hidden, adapter_down, adapter_up, adapter_ids, block):

time: 20.9 us -> 22.4 us (1.072)
  waiting for transfers between devices: 5.33 us -> 6.54 us
  starting transfers between devices: 12.4 us -> 13 us
  Pallas kernels: 2.69 us -> 2.46 us
    ppermute x2, starting transfers between devices: 0.54 us -> 2.1 us  [swap(): return lax.ppermute(array, 'tensor', [(0, 1), (1, 0)])]
    ppermute x8, waiting for transfers between devices: 4.25 us -> 5.8 us  [visit(): return lax.ppermute(array, ('store', 'tensor'), turn_pairs(turn))]
    ppermute x8, starting transfers between devices: 11.9 us -> 10.9 us  [visit(): return lax.ppermute(array, ('store', 'tensor'), turn_pairs(turn))]
    ppermute x2, waiting for transfers between devices: 1.08 us -> 0.74 us  [swap(): return lax.ppermute(array, 'tensor', [(0, 1), (1, 0)])]
  transfers between devices with their start and end apart: 10 -> 10, of which waited for: 4 -> 5; matrix products, arithmetic and copies ran while one was open for 0% -> 0% of each run, Pallas kernels for 7% -> 4%
where the time goes in v15:
time: 22.4 us; the launch traced here: 22.2 us
  starting transfers between devices  13 us (58%)
  waiting for transfers between devices  6.54 us (29%)
  Pallas kernels  2.46 us (11%)
    ppermute x8, starting transfers between devices, visit(): return lax.ppermute(array, ('store', 'tensor'), turn_pairs(turn))  10.9 us
    ppermute x8, waiting for transfers between devices, visit(): return lax.ppermute(array, ('store', 'tensor'), turn_pairs(turn))  5.8 us
    ppermute x2, starting transfers between devices, swap(): return lax.ppermute(array, 'tensor', [(0, 1), (1, 0)])  2.1 us
    pallas_call x1, Pallas kernels, per_device(): pl.pallas_call(functools.partial(attend_kernel, len(deltas)), out_shape=j...  1.16 us
    ppermute x2, waiting for transfers between devices, swap(): return lax.ppermute(array, 'tensor', [(0, 1), (1, 0)])  0.74 us
    pallas_call x1, Pallas kernels, scalars(): pl.pallas_call(scalars_kernel, out_shape=pltpu.SMEM(ids.shape, ids.dtype)...  0.67 us
    pallas_call x2, Pallas kernels, work(): pl.pallas_call(functools.partial(owner_kernel, turns), out_shape=[jax.Sha...  0.61 us
  transfers between devices with their start and end apart: 10, of which 5 were waited for; matrix products, arithmetic and copies ran while one was open for 0% of the time, Pallas kernels for 4%

profile of v15, /device:TPU:0, one launch (start us, length us, event | category | flops | bytes accessed | tf_op | source)
XLA Modules:
  0.0 22.2 jit_solution(10257236890838249688)
XLA Ops:
  0.0 0.0 copy-start.1
  0.0 0.0 copy-start
  0.0 0.5 %collective-permute-start = (bf16[8,16,4096]{2,1,0:T(8,128)(2,1)}, bf16[8,16,4096]{2,1,0:T(8,128)(2,1)S(1)}, u32[]{:S(2)}, u32[]{:S(2)}) collective-permute-start(bf16[8,16,4096]{2,1,0:T(8,128)(2,1)} %mine_ref.3), channel_id=1, source_target_pairs={{0,1},{1,0},{2,3},{3,2},{4,5},{5,4},{6,7},{7,6},{8,9},{9,8},{10,11... | collective-permute-start | bytes 3145736 | tf_op jit(solution)/shard_map/ppermute | solution.py:177
  0.5 3.6 %collective-permute-start.1 = (bf16[2,8192]{1,0:T(2,128)(2,1)}, bf16[2,8192]{1,0:T(2,128)(2,1)S(1)}, u32[]{:S(2)}, u32[]{:S(2)}) collective-permute-start(bf16[2,8192]{1,0:T(2,128)(2,1)} %refs_2_.1), channel_id=1, source_target_pairs={{0,6},{1,15},{2,4},{3,13},{4,2},{5,11},{6,0},{7,9},{8,14},{9,7},{1... | collective-permute-start | bytes 98312 | tf_op jit(solution)/shard_map/ppermute | solution.py:174
  4.0 0.5 %collective-permute-start.2 = (bf16[2,8192]{1,0:T(2,128)(2,1)}, bf16[2,8192]{1,0:T(2,128)(2,1)S(1)}, u32[]{:S(2)}, u32[]{:S(2)}) collective-permute-start(bf16[2,8192]{1,0:T(2,128)(2,1)} %refs_2_.1), channel_id=1, source_target_pairs={{0,2},{1,3},{2,0},{3,1},{4,6},{5,7},{6,4},{7,5},{8,10},{9,11},{10,... | collective-permute-start | bytes 98312 | tf_op jit(solution)/shard_map/ppermute | solution.py:174
  4.6 2.6 %collective-permute-start.4 = (bf16[2,8192]{1,0:T(2,128)(2,1)}, bf16[2,8192]{1,0:T(2,128)(2,1)S(1)}, u32[]{:S(2)}, u32[]{:S(2)}) collective-permute-start(bf16[2,8192]{1,0:T(2,128)(2,1)} %refs_2_.1), channel_id=1, source_target_pairs={{0,8},{1,11},{2,10},{3,9},{4,12},{5,15},{6,14},{7,13},{8,0},{9,3},... | collective-permute-start | bytes 98312 | tf_op jit(solution)/shard_map/ppermute | solution.py:174
  7.2 0.4 %collective-permute-start.5 = (bf16[2,8192]{1,0:T(2,128)(2,1)}, bf16[2,8192]{1,0:T(2,128)(2,1)S(1)}, u32[]{:S(2)}, u32[]{:S(2)}) collective-permute-start(bf16[2,8192]{1,0:T(2,128)(2,1)} %refs_2_.1), channel_id=1, source_target_pairs={{0,4},{1,13},{2,6},{3,15},{4,0},{5,9},{6,2},{7,11},{8,12},{9,5},{1... | collective-permute-start | bytes 98312 | tf_op jit(solution)/shard_map/ppermute | solution.py:174
  7.6 0.7 %scalars.1.ids_ref = s32[16]{0:T(128)S(4)} custom-call(s32[16]{0:T(128)} %ids_hbm.1, bf16[8,16,8192]{2,1,0:T(8,128)(2,1)} %down_ref.3, bf16[8,16,4096]{2,1,0:T(8,128)(2,1)} %mine_ref.3), custom_call_target="tpu_custom_call" | custom-call | bytes 3145728 | tf_op jit(solution)/shard_map/scalars/pallas_call | solution.py:33
  8.3 0.0 copy-start.4
  8.3 0.0 collective-permute-done.1.refs_0_
  8.3 0.0 collective-permute-done.2.refs_1_
  8.3 0.0 collective-permute-done.other_ref
  8.3 0.0 copy-done.1
  8.3 0.0 copy-done
  8.3 0.2 owner_first.1
  8.5 1.1 %collective-permute-done.4.refs_0_ = bf16[2,8192]{1,0:T(2,128)(2,1)S(1)} collective-permute-done((bf16[2,8192]{1,0:T(2,128)(2,1)}, bf16[2,8192]{1,0:T(2,128)(2,1)S(1)}, u32[]{:S(2)}, u32[]{:S(2)}) %collective-permute-start.4) | collective-permute-done | bytes 32800 | tf_op jit(solution)/shard_map/ppermute | solution.py:174
  9.6 2.4 %collective-permute-done.5.refs_1_ = bf16[2,8192]{1,0:T(2,128)(2,1)S(1)} collective-permute-done((bf16[2,8192]{1,0:T(2,128)(2,1)}, bf16[2,8192]{1,0:T(2,128)(2,1)S(1)}, u32[]{:S(2)}, u32[]{:S(2)}) %collective-permute-start.5) | collective-permute-done | bytes 32800 | tf_op jit(solution)/shard_map/ppermute | solution.py:174
  12.0 0.0 copy-done.4
  12.0 0.0 copy-start.6
  12.0 0.0 copy-start.5
  12.0 0.0 copy-start.2
  12.0 0.0 copy-start.3
  12.0 0.5 %owner_rest.1 = (bf16[2,2,32,128]{3,2,1,0:T(8,128)(2,1)S(1)}, bf16[2,2,32,128]{3,2,1,0:T(8,128)(2,1)S(1)}, bf16[2,32,128]{2,1,0:T(8,128)(2,1)S(1)}) custom-call(s32[16]{0:T(128)S(4)} %scalars.1.ids_ref, bf16[8,16,8192]{2,1,0:T(8,128)(2,1)S(1)} %copy-done, bf16[8,16,4096]{2,1,0:T(8,128)(2,1)S(1)} %copy-done.1, ...), custom_call_target="tpu_custom_call" | custom-call | tf_op jit(solution)/shard_map/owner_rest/pallas_call | solution.py:187
  12.5 0.3 %collective-permute-start.6 = (bf16[2,2,32,128]{3,2,1,0:T(8,128)(2,1)S(1)}, bf16[2,2,32,128]{3,2,1,0:T(8,128)(2,1)S(1)}, u32[]{:S(2)}, u32[]{:S(2)}) collective-permute-start(bf16[2,2,32,128]{3,2,1,0:T(8,128)(2,1)S(1)} %get-tuple-element.13), channel_id=1, source_target_pairs={{0,8},{1,11},{2,10},{3,9},{4,12},{5,15},{6,14},{7,13},{8,0},{9,3},... | collective-permute-start | bytes 98312 | tf_op jit(solution)/shard_map/ppermute | solution.py:174
  12.8 0.7 %collective-permute-start.7 = (bf16[2,2,32,128]{3,2,1,0:T(8,128)(2,1)S(1)}, bf16[2,2,32,128]{3,2,1,0:T(8,128)(2,1)S(1)}, u32[]{:S(2)}, u32[]{:S(2)}) collective-permute-start(bf16[2,2,32,128]{3,2,1,0:T(8,128)(2,1)S(1)} %get-tuple-element.14), channel_id=1, source_target_pairs={{0,4},{1,13},{2,6},{3,15},{4,0},{5,9},{6,2},{7,11},{8,12},{9,5},{1... | collective-permute-start | bytes 98312 | tf_op jit(solution)/shard_map/ppermute | solution.py:174
  13.4 2.4 %collective-permute-start.3 = (bf16[2,2,32,128]{3,2,1,0:T(8,128)(2,1)S(1)}, bf16[2,2,32,128]{3,2,1,0:T(8,128)(2,1)S(1)}, u32[]{:S(2)}, u32[]{:S(2)}) collective-permute-start(bf16[2,2,32,128]{3,2,1,0:T(8,128)(2,1)S(1)} %get-tuple-element.12.refs_3_), channel_id=1, source_target_pairs={{0,6},{1,15},{2,4},{3,13},{4,2},{5,11},{6,0},{7,9},{8,14},{9,7},{1... | collective-permute-start | bytes 98312 | tf_op jit(solution)/shard_map/ppermute | solution.py:174
  15.8 0.4 %collective-permute-start.8 = (bf16[2,32,128]{2,1,0:T(8,128)(2,1)S(1)}, bf16[2,32,128]{2,1,0:T(8,128)(2,1)S(1)}, u32[]{:S(2)}, u32[]{:S(2)}) collective-permute-start(bf16[2,32,128]{2,1,0:T(8,128)(2,1)S(1)} %get-tuple-element.17), channel_id=1, source_target_pairs={{0,2},{1,3},{2,0},{3,1},{4,6},{5,7},{6,4},{7,5},{8,10},{9,11},{10,... | collective-permute-start | bytes 49160 | tf_op jit(solution)/shard_map/ppermute | solution.py:174
  16.2 1.5 %collective-permute-done.6.refs_1_ = bf16[2,2,32,128]{3,2,1,0:T(8,128)(2,1)S(1)} collective-permute-done((bf16[2,2,32,128]{3,2,1,0:T(8,128)(2,1)S(1)}, bf16[2,2,32,128]{3,2,1,0:T(8,128)(2,1)S(1)}, u32[]{:S(2)}, u32[]{:S(2)}) %collective-permute-start.6) | collective-permute-done | bytes 32800 | tf_op jit(solution)/shard_map/ppermute | solution.py:174
  17.7 0.0 collective-permute-done.7.refs_2_
  17.7 0.9 %collective-permute-done.3.refs_0_ = bf16[2,2,32,128]{3,2,1,0:T(8,128)(2,1)S(1)} collective-permute-done((bf16[2,2,32,128]{3,2,1,0:T(8,128)(2,1)S(1)}, bf16[2,2,32,128]{3,2,1,0:T(8,128)(2,1)S(1)}, u32[]{:S(2)}, u32[]{:S(2)}) %collective-permute-start.3) | collective-permute-done | bytes 32800 | tf_op jit(solution)/shard_map/ppermute | solution.py:174
  18.6 1.6 %collective-permute-start.9 = (bf16[2,32,128]{2,1,0:T(8,128)(2,1)S(1)}, bf16[2,32,128]{2,1,0:T(8,128)(2,1)S(1)}, u32[]{:S(2)}, u32[]{:S(2)}) collective-permute-start(bf16[2,32,128]{2,1,0:T(8,128)(2,1)S(1)} %get-tuple-element.18), channel_id=1, source_target_pairs={{0,1},{1,0},{2,3},{3,2},{4,5},{5,4},{6,7},{7,6},{8,9},{9,8},{10,11... | collective-permute-start | bytes 49160 | tf_op jit(solution)/shard_map/ppermute | solution.py:177
  20.2 0.0 copy-done.6
  20.2 0.1 compare_convert_fusion.live_ref
  20.3 0.0 copy-done.5
  20.3 0.0 collective-permute-done.8.refs_2_
  20.3 0.7 %collective-permute-done.9.refs_3_ = bf16[2,32,128]{2,1,0:T(8,128)(2,1)S(1)} collective-permute-done((bf16[2,32,128]{2,1,0:T(8,128)(2,1)S(1)}, bf16[2,32,128]{2,1,0:T(8,128)(2,1)S(1)}, u32[]{:S(2)}, u32[]{:S(2)}) %collective-permute-start.9) | collective-permute-done | bytes 16416 | tf_op jit(solution)/shard_map/ppermute | solution.py:177
  21.1 0.0 copy-done.2
  21.1 0.0 copy-done.3
  21.1 1.2 %attend.1 = bf16[2,4096]{1,0:T(2,128)(2,1)} custom-call(f32[2,1,256]{2,1,0:T(1,128)S(1)} %compare_convert_fusion.live_ref, bf16[2,32,128]{2,1,0:T(8,128)(2,1)S(1)} %bitcast.4, bf16[2,32,128]{2,1,0:T(8,128)(2,1)S(1)} %get-tuple-element.15.refs_0_, bf16[2,32,128]{2,1,0:T(8,128)(2,1)S(1)} %get-tuple-element.16.refs_1_, ...), custom_call_target="tpu_custom_call" | custom-call | tf_op jit(solution)/shard_map/attend/pallas_call | solution.py:255
  (2 shorter events, 0.0 us)
Async XLA Ops:
  0.0 8.3 %copy-start.1 = (bf16[8,16,4096]{2,1,0:T(8,128)(2,1)S(1)}, bf16[8,16,4096]{2,1,0:T(8,128)(2,1)}, u32[]{:S(2)}) copy-start(bf16[8,16,4096]{2,1,0:T(8,128)(2,1)} %mine_ref.3) | copy-start | bytes 3145732
  0.0 8.3 %copy-start = (bf16[8,16,8192]{2,1,0:T(8,128)(2,1)S(1)}, bf16[8,16,8192]{2,1,0:T(8,128)(2,1)}, u32[]{:S(2)}) copy-start(bf16[8,16,8192]{2,1,0:T(8,128)(2,1)} %down_ref.3) | copy-start | bytes 6291460
  0.0 8.3 %collective-permute-start = (bf16[8,16,4096]{2,1,0:T(8,128)(2,1)}, bf16[8,16,4096]{2,1,0:T(8,128)(2,1)S(1)}, u32[]{:S(2)}, u32[]{:S(2)}) collective-permute-start(bf16[8,16,4096]{2,1,0:T(8,128)(2,1)} %mine_ref.3), channel_id=1, source_target_pairs={{0,1},{1,0},{2,3},{3,2},{4,5},{5,4},{6,7},{7,6},{8,9},{9,8},{10,11... | collective-permute-start | bytes 3145736 | tf_op jit(solution)/shard_map/ppermute | solution.py:177
  0.5 7.8 %collective-permute-start.1 = (bf16[2,8192]{1,0:T(2,128)(2,1)}, bf16[2,8192]{1,0:T(2,128)(2,1)S(1)}, u32[]{:S(2)}, u32[]{:S(2)}) collective-permute-start(bf16[2,8192]{1,0:T(2,128)(2,1)} %refs_2_.1), channel_id=1, source_target_pairs={{0,6},{1,15},{2,4},{3,13},{4,2},{5,11},{6,0},{7,9},{8,14},{9,7},{1... | collective-permute-start | bytes 98312 | tf_op jit(solution)/shard_map/ppermute | solution.py:174
  4.0 4.3 %collective-permute-start.2 = (bf16[2,8192]{1,0:T(2,128)(2,1)}, bf16[2,8192]{1,0:T(2,128)(2,1)S(1)}, u32[]{:S(2)}, u32[]{:S(2)}) collective-permute-start(bf16[2,8192]{1,0:T(2,128)(2,1)} %refs_2_.1), channel_id=1, source_target_pairs={{0,2},{1,3},{2,0},{3,1},{4,6},{5,7},{6,4},{7,5},{8,10},{9,11},{10,... | collective-permute-start | bytes 98312 | tf_op jit(solution)/shard_map/ppermute | solution.py:174
  4.6 5.0 %collective-permute-start.4 = (bf16[2,8192]{1,0:T(2,128)(2,1)}, bf16[2,8192]{1,0:T(2,128)(2,1)S(1)}, u32[]{:S(2)}, u32[]{:S(2)}) collective-permute-start(bf16[2,8192]{1,0:T(2,128)(2,1)} %refs_2_.1), channel_id=1, source_target_pairs={{0,8},{1,11},{2,10},{3,9},{4,12},{5,15},{6,14},{7,13},{8,0},{9,3},... | collective-permute-start | bytes 98312 | tf_op jit(solution)/shard_map/ppermute | solution.py:174
  7.2 4.8 %collective-permute-start.5 = (bf16[2,8192]{1,0:T(2,128)(2,1)}, bf16[2,8192]{1,0:T(2,128)(2,1)S(1)}, u32[]{:S(2)}, u32[]{:S(2)}) collective-permute-start(bf16[2,8192]{1,0:T(2,128)(2,1)} %refs_2_.1), channel_id=1, source_target_pairs={{0,4},{1,13},{2,6},{3,15},{4,0},{5,9},{6,2},{7,11},{8,12},{9,5},{1... | collective-permute-start | bytes 98312 | tf_op jit(solution)/shard_map/ppermute | solution.py:174
  8.3 3.7 %copy-start.4 = (bf16[2,8192]{1,0:T(2,128)(2,1)S(1)}, bf16[2,8192]{1,0:T(2,128)(2,1)}, u32[]{:S(2)}) copy-start(bf16[2,8192]{1,0:T(2,128)(2,1)} %refs_2_.1) | copy-start | bytes 98308
  12.0 8.2 %copy-start.6 = (s32[2]{0:T(128)S(1)}, s32[2]{0:T(128)}, u32[]{:S(2)}) copy-start(s32[2]{0:T(128)} %param.15) | copy-start | bytes 28
  12.0 8.3 %copy-start.5 = (bf16[2,4096]{1,0:T(2,128)(2,1)S(1)}, bf16[2,4096]{1,0:T(2,128)(2,1)}, u32[]{:S(2)}) copy-start(bf16[2,4096]{1,0:T(2,128)(2,1)} %param.9) | copy-start | bytes 49156
  12.0 9.1 %copy-start.2 = (bf16[2,4,256,128]{3,2,1,0:T(8,128)(2,1)S(1)}, bf16[2,4,256,128]{3,2,1,0:T(8,128)(2,1)}, u32[]{:S(2)}) copy-start(bf16[2,4,256,128]{3,2,1,0:T(8,128)(2,1)} %refs_4_.1) | copy-start | bytes 1572868
  12.0 9.1 %copy-start.3 = (bf16[2,4,256,128]{3,2,1,0:T(8,128)(2,1)S(1)}, bf16[2,4,256,128]{3,2,1,0:T(8,128)(2,1)}, u32[]{:S(2)}) copy-start(bf16[2,4,256,128]{3,2,1,0:T(8,128)(2,1)} %refs_5_.1) | copy-start | bytes 1572868
  12.5 5.2 %collective-permute-start.6 = (bf16[2,2,32,128]{3,2,1,0:T(8,128)(2,1)S(1)}, bf16[2,2,32,128]{3,2,1,0:T(8,128)(2,1)S(1)}, u32[]{:S(2)}, u32[]{:S(2)}) collective-permute-start(bf16[2,2,32,128]{3,2,1,0:T(8,128)(2,1)S(1)} %get-tuple-element.13), channel_id=1, source_target_pairs={{0,8},{1,11},{2,10},{3,9},{4,12},{5,15},{6,14},{7,13},{8,0},{9,3},... | collective-permute-start | bytes 98312 | tf_op jit(solution)/shard_map/ppermute | solution.py:174
  12.8 4.9 %collective-permute-start.7 = (bf16[2,2,32,128]{3,2,1,0:T(8,128)(2,1)S(1)}, bf16[2,2,32,128]{3,2,1,0:T(8,128)(2,1)S(1)}, u32[]{:S(2)}, u32[]{:S(2)}) collective-permute-start(bf16[2,2,32,128]{3,2,1,0:T(8,128)(2,1)S(1)} %get-tuple-element.14), channel_id=1, source_target_pairs={{0,4},{1,13},{2,6},{3,15},{4,0},{5,9},{6,2},{7,11},{8,12},{9,5},{1... | collective-permute-start | bytes 98312 | tf_op jit(solution)/shard_map/ppermute | solution.py:174
  13.4 5.2 %collective-permute-start.3 = (bf16[2,2,32,128]{3,2,1,0:T(8,128)(2,1)S(1)}, bf16[2,2,32,128]{3,2,1,0:T(8,128)(2,1)S(1)}, u32[]{:S(2)}, u32[]{:S(2)}) collective-permute-start(bf16[2,2,32,128]{3,2,1,0:T(8,128)(2,1)S(1)} %get-tuple-element.12.refs_3_), channel_id=1, source_target_pairs={{0,6},{1,15},{2,4},{3,13},{4,2},{5,11},{6,0},{7,9},{8,14},{9,7},{1... | collective-permute-start | bytes 98312 | tf_op jit(solution)/shard_map/ppermute | solution.py:174
  15.8 4.5 %collective-permute-start.8 = (bf16[2,32,128]{2,1,0:T(8,128)(2,1)S(1)}, bf16[2,32,128]{2,1,0:T(8,128)(2,1)S(1)}, u32[]{:S(2)}, u32[]{:S(2)}) collective-permute-start(bf16[2,32,128]{2,1,0:T(8,128)(2,1)S(1)} %get-tuple-element.17), channel_id=1, source_target_pairs={{0,2},{1,3},{2,0},{3,1},{4,6},{5,7},{6,4},{7,5},{8,10},{9,11},{10,... | collective-permute-start | bytes 49160 | tf_op jit(solution)/shard_map/ppermute | solution.py:174
  18.6 2.5 %collective-permute-start.9 = (bf16[2,32,128]{2,1,0:T(8,128)(2,1)S(1)}, bf16[2,32,128]{2,1,0:T(8,128)(2,1)S(1)}, u32[]{:S(2)}, u32[]{:S(2)}) collective-permute-start(bf16[2,32,128]{2,1,0:T(8,128)(2,1)S(1)} %get-tuple-element.18), channel_id=1, source_target_pairs={{0,1},{1,0},{2,3},{3,2},{4,5},{5,4},{6,7},{7,6},{8,9},{9,8},{10,11... | collective-permute-start | bytes 49160 | tf_op jit(solution)/shard_map/ppermute | solution.py:177

commit v16 on v12

--- a/solution.py
+++ b/solution.py
@@ -17,7 +17,7 @@
 PARAMS = pltpu.CompilerParams(vmem_limit_bytes=VMEM_LIMIT)
 TURNS = ((3, 1, 4, 2, 0), (7, 1, 5, 6, 0))
 SENT = len(TURNS[0]) - 1
-EARLY = 2
+GROUPS = ((0, 1), (2, 3), (4,))
 SHARED = [first == second for first, second in zip(*TURNS)]
 
 
@@ -194,8 +194,10 @@
         )(ids, down, up, other, *[states[turn] for turn in turns], *after)
 
     states.append(near(hidden))
-    deltas = work("owner_first", (), *range(EARLY))
-    deltas += work("owner_rest", deltas[:1], *range(EARLY, SENT + 1))
+    deltas = []
+    for group in GROUPS:
+        after = [deltas[others[0]] for others in GROUPS if others[0] < group[0]][-1:]
+        deltas += work("owner%d" % group[0], after, *group)
     came = [visit(delta, turn) for turn, delta in enumerate(deltas[:SENT])]
     kept, sent = pl.pallas_call(
         merge_kernel,

time: 20.9 us -> 20.5 us (0.981)
  waiting for transfers between devices: 5.33 us -> 4.1 us
  starting transfers between devices: 12.4 us -> 13.5 us
  Pallas kernels: 2.69 us -> 2.36 us
    ppermute x8, waiting for transfers between devices: 4.25 us -> 3.35 us  [visit(): return lax.ppermute(array, ('store', 'tensor'), turn_pairs(turn))]
    ppermute x8, starting transfers between devices: 11.9 us -> 12.6 us  [visit(): return lax.ppermute(array, ('store', 'tensor'), turn_pairs(turn))]
    ppermute x2, starting transfers between devices: 0.54 us -> 0.87 us  [swap(): return lax.ppermute(array, 'tensor', [(0, 1), (1, 0)])]
    pallas_call x2 -> x3, Pallas kernels: 0.83 us -> 0.5 us  [work(): pl.pallas_call(functools.partial(owner_kernel, turns), out_shape=[jax.Sha...]
    ppermute x2, waiting for transfers between devices: 1.08 us -> 0.75 us  [swap(): return lax.ppermute(array, 'tensor', [(0, 1), (1, 0)])]
  transfers between devices with their start and end apart: 10 -> 10, of which waited for: 4 -> 4; matrix products, arithmetic and copies ran while one was open for 0% -> 0% of each run, Pallas kernels for 7% -> 6%
where the time goes in v16:
time: 20.5 us; the launch traced here: 20.2 us
  starting transfers between devices  13.5 us (66%)
  waiting for transfers between devices  4.1 us (20%)
  Pallas kernels  2.36 us (12%)
    ppermute x8, starting transfers between devices, visit(): return lax.ppermute(array, ('store', 'tensor'), turn_pairs(turn))  12.6 us
    ppermute x8, waiting for transfers between devices, visit(): return lax.ppermute(array, ('store', 'tensor'), turn_pairs(turn))  3.35 us
    pallas_call x1, Pallas kernels, per_device(): pl.pallas_call(functools.partial(attend_kernel, len(deltas)), out_shape=j...  1.16 us
    ppermute x2, starting transfers between devices, swap(): return lax.ppermute(array, 'tensor', [(0, 1), (1, 0)])  0.87 us
    ppermute x2, waiting for transfers between devices, swap(): return lax.ppermute(array, 'tensor', [(0, 1), (1, 0)])  0.75 us
    pallas_call x1, Pallas kernels, scalars(): pl.pallas_call(scalars_kernel, out_shape=pltpu.SMEM(ids.shape, ids.dtype)...  0.67 us
    pallas_call x3, Pallas kernels, work(): pl.pallas_call(functools.partial(owner_kernel, turns), out_shape=[jax.Sha...  0.5 us
  transfers between devices with their start and end apart: 10, of which 4 were waited for; matrix products, arithmetic and copies ran while one was open for 0% of the time, Pallas kernels for 6%

profile of v16, /device:TPU:0, one launch (start us, length us, event | category | flops | bytes accessed | tf_op | source)
XLA Modules:
  0.0 20.2 jit_solution(6663121793245370901)
XLA Ops:
  0.0 0.0 copy-start.1
  0.0 0.0 copy-start
  0.0 0.5 %collective-permute-start = (bf16[8,16,4096]{2,1,0:T(8,128)(2,1)}, bf16[8,16,4096]{2,1,0:T(8,128)(2,1)S(1)}, u32[]{:S(2)}, u32[]{:S(2)}) collective-permute-start(bf16[8,16,4096]{2,1,0:T(8,128)(2,1)} %mine_ref.5), channel_id=1, source_target_pairs={{0,1},{1,0},{2,3},{3,2},{4,5},{5,4},{6,7},{7,6},{8,9},{9,8},{10,11... | collective-permute-start | bytes 3145736 | tf_op jit(solution)/shard_map/ppermute | solution.py:172
  0.5 3.6 %collective-permute-start.3 = (bf16[2,8192]{1,0:T(2,128)(2,1)}, bf16[2,8192]{1,0:T(2,128)(2,1)S(1)}, u32[]{:S(2)}, u32[]{:S(2)}) collective-permute-start(bf16[2,8192]{1,0:T(2,128)(2,1)} %refs_0_.3), channel_id=1, source_target_pairs={{0,6},{1,15},{2,4},{3,13},{4,2},{5,11},{6,0},{7,9},{8,14},{9,7},{1... | collective-permute-start | bytes 98312 | tf_op jit(solution)/shard_map/ppermute | solution.py:169
  4.0 0.5 %collective-permute-start.4 = (bf16[2,8192]{1,0:T(2,128)(2,1)}, bf16[2,8192]{1,0:T(2,128)(2,1)S(1)}, u32[]{:S(2)}, u32[]{:S(2)}) collective-permute-start(bf16[2,8192]{1,0:T(2,128)(2,1)} %refs_0_.3), channel_id=1, source_target_pairs={{0,2},{1,3},{2,0},{3,1},{4,6},{5,7},{6,4},{7,5},{8,10},{9,11},{10,... | collective-permute-start | bytes 98312 | tf_op jit(solution)/shard_map/ppermute | solution.py:169
  4.6 2.6 %collective-permute-start.1 = (bf16[2,8192]{1,0:T(2,128)(2,1)}, bf16[2,8192]{1,0:T(2,128)(2,1)S(1)}, u32[]{:S(2)}, u32[]{:S(2)}) collective-permute-start(bf16[2,8192]{1,0:T(2,128)(2,1)} %refs_0_.3), channel_id=1, source_target_pairs={{0,8},{1,11},{2,10},{3,9},{4,12},{5,15},{6,14},{7,13},{8,0},{9,3},... | collective-permute-start | bytes 98312 | tf_op jit(solution)/shard_map/ppermute | solution.py:169
  7.2 0.4 %collective-permute-start.2 = (bf16[2,8192]{1,0:T(2,128)(2,1)}, bf16[2,8192]{1,0:T(2,128)(2,1)S(1)}, u32[]{:S(2)}, u32[]{:S(2)}) collective-permute-start(bf16[2,8192]{1,0:T(2,128)(2,1)} %refs_0_.3), channel_id=1, source_target_pairs={{0,4},{1,13},{2,6},{3,15},{4,0},{5,9},{6,2},{7,11},{8,12},{9,5},{1... | collective-permute-start | bytes 98312 | tf_op jit(solution)/shard_map/ppermute | solution.py:169
  7.6 0.7 %scalars.1.ids_ref = s32[16]{0:T(128)S(4)} custom-call(s32[16]{0:T(128)} %ids_hbm.1, bf16[8,16,8192]{2,1,0:T(8,128)(2,1)} %down_ref.5, bf16[8,16,4096]{2,1,0:T(8,128)(2,1)} %mine_ref.5), custom_call_target="tpu_custom_call" | custom-call | bytes 3145728 | tf_op jit(solution)/shard_map/scalars/pallas_call | solution.py:33
  8.3 0.0 collective-permute-done.3.refs_0_
  8.3 0.0 collective-permute-done.4.refs_1_
  8.3 0.0 collective-permute-done.other_ref
  8.3 0.0 copy-done.1
  8.3 0.0 copy-done
  8.3 0.2 owner0.1
  8.5 0.0 copy-start.4
  8.5 2.6 %collective-permute-start.5 = (bf16[2,2,32,128]{3,2,1,0:T(8,128)(2,1)S(1)}, bf16[2,2,32,128]{3,2,1,0:T(8,128)(2,1)S(1)}, u32[]{:S(2)}, u32[]{:S(2)}) collective-permute-start(bf16[2,2,32,128]{3,2,1,0:T(8,128)(2,1)S(1)} %get-tuple-element.11.refs_2_), channel_id=1, source_target_pairs={{0,6},{1,15},{2,4},{3,13},{4,2},{5,11},{6,0},{7,9},{8,14},{9,7},{1... | collective-permute-start | bytes 98312 | tf_op jit(solution)/shard_map/ppermute | solution.py:169
  11.1 0.0 collective-permute-done.1.refs_0_
  11.1 0.9 %collective-permute-done.2.refs_1_ = bf16[2,8192]{1,0:T(2,128)(2,1)S(1)} collective-permute-done((bf16[2,8192]{1,0:T(2,128)(2,1)}, bf16[2,8192]{1,0:T(2,128)(2,1)S(1)}, u32[]{:S(2)}, u32[]{:S(2)}) %collective-permute-start.2) | collective-permute-done | bytes 32800 | tf_op jit(solution)/shard_map/ppermute | solution.py:169
  12.0 0.3 %owner2.1 = (bf16[2,2,32,128]{3,2,1,0:T(8,128)(2,1)S(1)}, bf16[2,2,32,128]{3,2,1,0:T(8,128)(2,1)S(1)}) custom-call(s32[16]{0:T(128)S(4)} %scalars.1.ids_ref, bf16[8,16,8192]{2,1,0:T(8,128)(2,1)S(1)} %copy-done, bf16[8,16,4096]{2,1,0:T(8,128)(2,1)S(1)} %copy-done.1, bf16[8,16,4096]{2,1,0:T(8,128)(2,1)S(1)} %collective-permute-done.other_ref, ...), custom_call_target="tpu_custom_call" | custom-call | tf_op jit(solution)/shard_map/owner2/pallas_call | solution.py:182
  12.3 0.1 collective-permute-start.7
  12.4 1.1 %collective-permute-start.8 = (bf16[2,2,32,128]{3,2,1,0:T(8,128)(2,1)S(1)}, bf16[2,2,32,128]{3,2,1,0:T(8,128)(2,1)S(1)}, u32[]{:S(2)}, u32[]{:S(2)}) collective-permute-start(bf16[2,2,32,128]{3,2,1,0:T(8,128)(2,1)S(1)} %get-tuple-element.14), channel_id=1, source_target_pairs={{0,4},{1,13},{2,6},{3,15},{4,0},{5,9},{6,2},{7,11},{8,12},{9,5},{1... | collective-permute-start | bytes 98312 | tf_op jit(solution)/shard_map/ppermute | solution.py:169
  13.5 0.0 copy-start.6
  13.5 0.0 copy-start.5
  13.5 0.0 copy-start.2
  13.5 0.0 copy-start.3
  13.5 1.7 %collective-permute-start.6 = (bf16[2,2,32,128]{3,2,1,0:T(8,128)(2,1)S(1)}, bf16[2,2,32,128]{3,2,1,0:T(8,128)(2,1)S(1)}, u32[]{:S(2)}, u32[]{:S(2)}) collective-permute-start(bf16[2,2,32,128]{3,2,1,0:T(8,128)(2,1)S(1)} %get-tuple-element.13), channel_id=1, source_target_pairs={{0,2},{1,3},{2,0},{3,1},{4,6},{5,7},{6,4},{7,5},{8,10},{9,11},{10,... | collective-permute-start | bytes 98312 | tf_op jit(solution)/shard_map/ppermute | solution.py:169
  15.2 0.0 copy-done.4
  15.2 2.2 %collective-permute-done.7.refs_2_ = bf16[2,2,32,128]{3,2,1,0:T(8,128)(2,1)S(1)} collective-permute-done((bf16[2,2,32,128]{3,2,1,0:T(8,128)(2,1)S(1)}, bf16[2,2,32,128]{3,2,1,0:T(8,128)(2,1)S(1)}, u32[]{:S(2)}, u32[]{:S(2)}) %collective-permute-start.7) | collective-permute-done | bytes 32800 | tf_op jit(solution)/shard_map/ppermute | solution.py:169
  17.5 0.0 collective-permute-done.8.refs_3_
  17.5 0.0 collective-permute-done.5.refs_0_
  17.5 0.2 %collective-permute-done.6.refs_1_ = bf16[2,2,32,128]{3,2,1,0:T(8,128)(2,1)S(1)} collective-permute-done((bf16[2,2,32,128]{3,2,1,0:T(8,128)(2,1)S(1)}, bf16[2,2,32,128]{3,2,1,0:T(8,128)(2,1)S(1)}, u32[]{:S(2)}, u32[]{:S(2)}) %collective-permute-start.6) | collective-permute-done | bytes 32800 | tf_op jit(solution)/shard_map/ppermute | solution.py:169
  17.7 0.4 %collective-permute-start.9 = (bf16[2,32,128]{2,1,0:T(8,128)(2,1)S(1)}, bf16[2,32,128]{2,1,0:T(8,128)(2,1)S(1)}, u32[]{:S(2)}, u32[]{:S(2)}) collective-permute-start(bf16[2,32,128]{2,1,0:T(8,128)(2,1)S(1)} %get-tuple-element.16), channel_id=1, source_target_pairs={{0,1},{1,0},{2,3},{3,2},{4,5},{5,4},{6,7},{7,6},{8,9},{9,8},{10,11... | collective-permute-start | bytes 49160 | tf_op jit(solution)/shard_map/ppermute | solution.py:172
  18.1 0.0 copy-done.6
  18.1 0.1 compare_convert_fusion.live_ref
  18.2 0.0 copy-done.5
  18.2 0.8 %collective-permute-done.9.refs_1_ = bf16[2,32,128]{2,1,0:T(8,128)(2,1)S(1)} collective-permute-done((bf16[2,32,128]{2,1,0:T(8,128)(2,1)S(1)}, bf16[2,32,128]{2,1,0:T(8,128)(2,1)S(1)}, u32[]{:S(2)}, u32[]{:S(2)}) %collective-permute-start.9) | collective-permute-done | bytes 16416 | tf_op jit(solution)/shard_map/ppermute | solution.py:172
  19.0 0.0 copy-done.2
  19.0 0.0 copy-done.3
  19.0 1.2 %attend.1 = bf16[2,4096]{1,0:T(2,128)(2,1)} custom-call(f32[2,1,256]{2,1,0:T(1,128)S(1)} %compare_convert_fusion.live_ref, bf16[2,32,128]{2,1,0:T(8,128)(2,1)S(1)} %bitcast.4, bf16[2,32,128]{2,1,0:T(8,128)(2,1)S(1)} %get-tuple-element.15.refs_0_, bf16[2,32,128]{2,1,0:T(8,128)(2,1)S(1)} %collective-permute-done.9.refs_1_, ...), custom_call_target="tpu_custom_call" | custom-call | tf_op jit(solution)/shard_map/attend/pallas_call | solution.py:247
  (3 shorter events, 0.0 us)
Async XLA Ops:
  0.0 8.3 %copy-start.1 = (bf16[8,16,4096]{2,1,0:T(8,128)(2,1)S(1)}, bf16[8,16,4096]{2,1,0:T(8,128)(2,1)}, u32[]{:S(2)}) copy-start(bf16[8,16,4096]{2,1,0:T(8,128)(2,1)} %mine_ref.5) | copy-start | bytes 3145732
  0.0 8.3 %copy-start = (bf16[8,16,8192]{2,1,0:T(8,128)(2,1)S(1)}, bf16[8,16,8192]{2,1,0:T(8,128)(2,1)}, u32[]{:S(2)}) copy-start(bf16[8,16,8192]{2,1,0:T(8,128)(2,1)} %down_ref.5) | copy-start | bytes 6291460
  0.0 8.3 %collective-permute-start = (bf16[8,16,4096]{2,1,0:T(8,128)(2,1)}, bf16[8,16,4096]{2,1,0:T(8,128)(2,1)S(1)}, u32[]{:S(2)}, u32[]{:S(2)}) collective-permute-start(bf16[8,16,4096]{2,1,0:T(8,128)(2,1)} %mine_ref.5), channel_id=1, source_target_pairs={{0,1},{1,0},{2,3},{3,2},{4,5},{5,4},{6,7},{7,6},{8,9},{9,8},{10,11... | collective-permute-start | bytes 3145736 | tf_op jit(solution)/shard_map/ppermute | solution.py:172
  0.5 7.8 %collective-permute-start.3 = (bf16[2,8192]{1,0:T(2,128)(2,1)}, bf16[2,8192]{1,0:T(2,128)(2,1)S(1)}, u32[]{:S(2)}, u32[]{:S(2)}) collective-permute-start(bf16[2,8192]{1,0:T(2,128)(2,1)} %refs_0_.3), channel_id=1, source_target_pairs={{0,6},{1,15},{2,4},{3,13},{4,2},{5,11},{6,0},{7,9},{8,14},{9,7},{1... | collective-permute-start | bytes 98312 | tf_op jit(solution)/shard_map/ppermute | solution.py:169
  4.0 4.3 %collective-permute-start.4 = (bf16[2,8192]{1,0:T(2,128)(2,1)}, bf16[2,8192]{1,0:T(2,128)(2,1)S(1)}, u32[]{:S(2)}, u32[]{:S(2)}) collective-permute-start(bf16[2,8192]{1,0:T(2,128)(2,1)} %refs_0_.3), channel_id=1, source_target_pairs={{0,2},{1,3},{2,0},{3,1},{4,6},{5,7},{6,4},{7,5},{8,10},{9,11},{10,... | collective-permute-start | bytes 98312 | tf_op jit(solution)/shard_map/ppermute | solution.py:169
  4.6 6.5 %collective-permute-start.1 = (bf16[2,8192]{1,0:T(2,128)(2,1)}, bf16[2,8192]{1,0:T(2,128)(2,1)S(1)}, u32[]{:S(2)}, u32[]{:S(2)}) collective-permute-start(bf16[2,8192]{1,0:T(2,128)(2,1)} %refs_0_.3), channel_id=1, source_target_pairs={{0,8},{1,11},{2,10},{3,9},{4,12},{5,15},{6,14},{7,13},{8,0},{9,3},... | collective-permute-start | bytes 98312 | tf_op jit(solution)/shard_map/ppermute | solution.py:169
  7.2 4.8 %collective-permute-start.2 = (bf16[2,8192]{1,0:T(2,128)(2,1)}, bf16[2,8192]{1,0:T(2,128)(2,1)S(1)}, u32[]{:S(2)}, u32[]{:S(2)}) collective-permute-start(bf16[2,8192]{1,0:T(2,128)(2,1)} %refs_0_.3), channel_id=1, source_target_pairs={{0,4},{1,13},{2,6},{3,15},{4,0},{5,9},{6,2},{7,11},{8,12},{9,5},{1... | collective-permute-start | bytes 98312 | tf_op jit(solution)/shard_map/ppermute | solution.py:169
  8.5 6.7 %copy-start.4 = (bf16[2,8192]{1,0:T(2,128)(2,1)S(1)}, bf16[2,8192]{1,0:T(2,128)(2,1)}, u32[]{:S(2)}) copy-start(bf16[2,8192]{1,0:T(2,128)(2,1)} %refs_0_.3) | copy-start | bytes 98308
  8.5 9.0 %collective-permute-start.5 = (bf16[2,2,32,128]{3,2,1,0:T(8,128)(2,1)S(1)}, bf16[2,2,32,128]{3,2,1,0:T(8,128)(2,1)S(1)}, u32[]{:S(2)}, u32[]{:S(2)}) collective-permute-start(bf16[2,2,32,128]{3,2,1,0:T(8,128)(2,1)S(1)} %get-tuple-element.11.refs_2_), channel_id=1, source_target_pairs={{0,6},{1,15},{2,4},{3,13},{4,2},{5,11},{6,0},{7,9},{8,14},{9,7},{1... | collective-permute-start | bytes 98312 | tf_op jit(solution)/shard_map/ppermute | solution.py:169
  12.3 5.2 %collective-permute-start.7 = (bf16[2,2,32,128]{3,2,1,0:T(8,128)(2,1)S(1)}, bf16[2,2,32,128]{3,2,1,0:T(8,128)(2,1)S(1)}, u32[]{:S(2)}, u32[]{:S(2)}) collective-permute-start(bf16[2,2,32,128]{3,2,1,0:T(8,128)(2,1)S(1)} %get-tuple-element.12.refs_1_), channel_id=1, source_target_pairs={{0,8},{1,11},{2,10},{3,9},{4,12},{5,15},{6,14},{7,13},{8,0},{9,3},... | collective-permute-start | bytes 98312 | tf_op jit(solution)/shard_map/ppermute | solution.py:169
  12.4 5.1 %collective-permute-start.8 = (bf16[2,2,32,128]{3,2,1,0:T(8,128)(2,1)S(1)}, bf16[2,2,32,128]{3,2,1,0:T(8,128)(2,1)S(1)}, u32[]{:S(2)}, u32[]{:S(2)}) collective-permute-start(bf16[2,2,32,128]{3,2,1,0:T(8,128)(2,1)S(1)} %get-tuple-element.14), channel_id=1, source_target_pairs={{0,4},{1,13},{2,6},{3,15},{4,0},{5,9},{6,2},{7,11},{8,12},{9,5},{1... | collective-permute-start | bytes 98312 | tf_op jit(solution)/shard_map/ppermute | solution.py:169
  13.5 4.7 %copy-start.6 = (s32[2]{0:T(128)S(1)}, s32[2]{0:T(128)}, u32[]{:S(2)}) copy-start(s32[2]{0:T(128)} %param.15) | copy-start | bytes 28
  13.5 4.7 %copy-start.5 = (bf16[2,4096]{1,0:T(2,128)(2,1)S(1)}, bf16[2,4096]{1,0:T(2,128)(2,1)}, u32[]{:S(2)}) copy-start(bf16[2,4096]{1,0:T(2,128)(2,1)} %param.9) | copy-start | bytes 49156
  13.5 5.5 %copy-start.2 = (bf16[2,4,256,128]{3,2,1,0:T(8,128)(2,1)S(1)}, bf16[2,4,256,128]{3,2,1,0:T(8,128)(2,1)}, u32[]{:S(2)}) copy-start(bf16[2,4,256,128]{3,2,1,0:T(8,128)(2,1)} %refs_2_.1) | copy-start | bytes 1572868
  13.5 5.5 %copy-start.3 = (bf16[2,4,256,128]{3,2,1,0:T(8,128)(2,1)S(1)}, bf16[2,4,256,128]{3,2,1,0:T(8,128)(2,1)}, u32[]{:S(2)}) copy-start(bf16[2,4,256,128]{3,2,1,0:T(8,128)(2,1)} %refs_3_.1) | copy-start | bytes 1572868
  13.5 4.2 %collective-permute-start.6 = (bf16[2,2,32,128]{3,2,1,0:T(8,128)(2,1)S(1)}, bf16[2,2,32,128]{3,2,1,0:T(8,128)(2,1)S(1)}, u32[]{:S(2)}, u32[]{:S(2)}) collective-permute-start(bf16[2,2,32,128]{3,2,1,0:T(8,128)(2,1)S(1)} %get-tuple-element.13), channel_id=1, source_target_pairs={{0,2},{1,3},{2,0},{3,1},{4,6},{5,7},{6,4},{7,5},{8,10},{9,11},{10,... | collective-permute-start | bytes 98312 | tf_op jit(solution)/shard_map/ppermute | solution.py:169
  17.7 1.3 %collective-permute-start.9 = (bf16[2,32,128]{2,1,0:T(8,128)(2,1)S(1)}, bf16[2,32,128]{2,1,0:T(8,128)(2,1)S(1)}, u32[]{:S(2)}, u32[]{:S(2)}) collective-permute-start(bf16[2,32,128]{2,1,0:T(8,128)(2,1)S(1)} %get-tuple-element.16), channel_id=1, source_target_pairs={{0,1},{1,0},{2,3},{3,2},{4,5},{5,4},{6,7},{7,6},{8,9},{9,8},{10,11... | collective-permute-start | bytes 49160 | tf_op jit(solution)/shard_map/ppermute | solution.py:172

commit v17 on v16

--- a/solution.py
+++ b/solution.py
@@ -10,7 +10,7 @@
 HEADS = 64
 KVH = 8
 LANES = 128
-CHUNK = 1024
+CHUNK = 512
 VMEM_LIMIT = 32 * 1024 * 1024
 VMEM = pl.BlockSpec(memory_space=pltpu.VMEM)
 SMEM = pl.BlockSpec(memory_space=pltpu.SMEM)

time: 20.5 us -> 20.6 us (level); the launches traced: 20.2 us -> 20.7 us
  waiting for transfers between devices: 4.1 us -> 4.51 us
  starting transfers between devices: 13.5 us -> 13.9 us
  Pallas kernels: 2.36 us -> 2.13 us
    ppermute x8, waiting for transfers between devices: 3.35 us -> 3.76 us  [visit(): return lax.ppermute(array, ('store', 'tensor'), turn_pairs(turn))]
    pallas_call x3, Pallas kernels: 0.5 us -> 0.27 us  [work(): pl.pallas_call(functools.partial(owner_kernel, turns), out_shape=[jax.Sha...]
    ppermute x8, starting transfers between devices: 12.6 us -> 12.8 us  [visit(): return lax.ppermute(array, ('store', 'tensor'), turn_pairs(turn))]
  transfers between devices with their start and end apart: 10 -> 10, of which waited for: 4 -> 5; matrix products, arithmetic and copies ran while one was open for 0% -> 0% of each run, Pallas kernels for 6% -> 5%
where the time goes in v17:
time: 20.6 us; the launch traced here: 20.7 us
  starting transfers between devices  13.9 us (67%)
  waiting for transfers between devices  4.51 us (22%)
  Pallas kernels  2.13 us (10%)
    ppermute x8, starting transfers between devices, visit(): return lax.ppermute(array, ('store', 'tensor'), turn_pairs(turn))  12.8 us
    ppermute x8, waiting for transfers between devices, visit(): return lax.ppermute(array, ('store', 'tensor'), turn_pairs(turn))  3.76 us
    pallas_call x1, Pallas kernels, per_device(): pl.pallas_call(functools.partial(attend_kernel, len(deltas)), out_shape=j...  1.16 us
    ppermute x2, starting transfers between devices, swap(): return lax.ppermute(array, 'tensor', [(0, 1), (1, 0)])  1.04 us
    ppermute x2, waiting for transfers between devices, swap(): return lax.ppermute(array, 'tensor', [(0, 1), (1, 0)])  0.75 us
    pallas_call x1, Pallas kernels, scalars(): pl.pallas_call(scalars_kernel, out_shape=pltpu.SMEM(ids.shape, ids.dtype)...  0.67 us
  transfers between devices with their start and end apart: 10, of which 5 were waited for; matrix products, arithmetic and copies ran while one was open for 0% of the time, Pallas kernels for 5%

profile of v17, /device:TPU:0, one launch (start us, length us, event | category | flops | bytes accessed | tf_op | source)
XLA Modules:
  0.0 20.7 jit_solution(4551686530052518132)
XLA Ops:
  0.0 0.0 copy-start.1
  0.0 0.0 copy-start
  0.0 0.5 %collective-permute-start = (bf16[8,16,4096]{2,1,0:T(8,128)(2,1)}, bf16[8,16,4096]{2,1,0:T(8,128)(2,1)S(1)}, u32[]{:S(2)}, u32[]{:S(2)}) collective-permute-start(bf16[8,16,4096]{2,1,0:T(8,128)(2,1)} %mine_ref.5), channel_id=1, source_target_pairs={{0,1},{1,0},{2,3},{3,2},{4,5},{5,4},{6,7},{7,6},{8,9},{9,8},{10,11... | collective-permute-start | bytes 3145736 | tf_op jit(solution)/shard_map/ppermute | solution.py:172
  0.5 3.6 %collective-permute-start.3 = (bf16[2,8192]{1,0:T(2,128)(2,1)}, bf16[2,8192]{1,0:T(2,128)(2,1)S(1)}, u32[]{:S(2)}, u32[]{:S(2)}) collective-permute-start(bf16[2,8192]{1,0:T(2,128)(2,1)} %refs_0_.3), channel_id=1, source_target_pairs={{0,6},{1,15},{2,4},{3,13},{4,2},{5,11},{6,0},{7,9},{8,14},{9,7},{1... | collective-permute-start | bytes 98312 | tf_op jit(solution)/shard_map/ppermute | solution.py:169
  4.0 0.5 %collective-permute-start.4 = (bf16[2,8192]{1,0:T(2,128)(2,1)}, bf16[2,8192]{1,0:T(2,128)(2,1)S(1)}, u32[]{:S(2)}, u32[]{:S(2)}) collective-permute-start(bf16[2,8192]{1,0:T(2,128)(2,1)} %refs_0_.3), channel_id=1, source_target_pairs={{0,2},{1,3},{2,0},{3,1},{4,6},{5,7},{6,4},{7,5},{8,10},{9,11},{10,... | collective-permute-start | bytes 98312 | tf_op jit(solution)/shard_map/ppermute | solution.py:169
  4.6 2.6 %collective-permute-start.1 = (bf16[2,8192]{1,0:T(2,128)(2,1)}, bf16[2,8192]{1,0:T(2,128)(2,1)S(1)}, u32[]{:S(2)}, u32[]{:S(2)}) collective-permute-start(bf16[2,8192]{1,0:T(2,128)(2,1)} %refs_0_.3), channel_id=1, source_target_pairs={{0,8},{1,11},{2,10},{3,9},{4,12},{5,15},{6,14},{7,13},{8,0},{9,3},... | collective-permute-start | bytes 98312 | tf_op jit(solution)/shard_map/ppermute | solution.py:169
  7.2 0.4 %collective-permute-start.2 = (bf16[2,8192]{1,0:T(2,128)(2,1)}, bf16[2,8192]{1,0:T(2,128)(2,1)S(1)}, u32[]{:S(2)}, u32[]{:S(2)}) collective-permute-start(bf16[2,8192]{1,0:T(2,128)(2,1)} %refs_0_.3), channel_id=1, source_target_pairs={{0,4},{1,13},{2,6},{3,15},{4,0},{5,9},{6,2},{7,11},{8,12},{9,5},{1... | collective-permute-start | bytes 98312 | tf_op jit(solution)/shard_map/ppermute | solution.py:169
  7.6 0.7 %scalars.1.ids_ref = s32[16]{0:T(128)S(4)} custom-call(s32[16]{0:T(128)} %ids_hbm.1, bf16[8,16,8192]{2,1,0:T(8,128)(2,1)} %down_ref.5, bf16[8,16,4096]{2,1,0:T(8,128)(2,1)} %mine_ref.5), custom_call_target="tpu_custom_call" | custom-call | bytes 3145728 | tf_op jit(solution)/shard_map/scalars/pallas_call | solution.py:33
  8.3 0.0 collective-permute-done.3.refs_0_
  8.3 0.0 collective-permute-done.4.refs_1_
  8.3 0.0 collective-permute-done.other_ref
  8.3 0.0 copy-done.1
  8.3 0.0 copy-done
  8.3 0.2 owner0.1
  8.5 0.0 copy-start.4
  8.5 2.6 %collective-permute-start.5 = (bf16[2,2,32,128]{3,2,1,0:T(8,128)(2,1)S(1)}, bf16[2,2,32,128]{3,2,1,0:T(8,128)(2,1)S(1)}, u32[]{:S(2)}, u32[]{:S(2)}) collective-permute-start(bf16[2,2,32,128]{3,2,1,0:T(8,128)(2,1)S(1)} %get-tuple-element.11.refs_2_), channel_id=1, source_target_pairs={{0,6},{1,15},{2,4},{3,13},{4,2},{5,11},{6,0},{7,9},{8,14},{9,7},{1... | collective-permute-start | bytes 98312 | tf_op jit(solution)/shard_map/ppermute | solution.py:169
  11.1 0.0 collective-permute-done.1.refs_0_
  11.1 0.9 %collective-permute-done.2.refs_1_ = bf16[2,8192]{1,0:T(2,128)(2,1)S(1)} collective-permute-done((bf16[2,8192]{1,0:T(2,128)(2,1)}, bf16[2,8192]{1,0:T(2,128)(2,1)S(1)}, u32[]{:S(2)}, u32[]{:S(2)}) %collective-permute-start.2) | collective-permute-done | bytes 32800 | tf_op jit(solution)/shard_map/ppermute | solution.py:169
  12.0 0.1 owner2.1
  12.1 0.5 %collective-permute-start.7 = (bf16[2,2,32,128]{3,2,1,0:T(8,128)(2,1)S(1)}, bf16[2,2,32,128]{3,2,1,0:T(8,128)(2,1)S(1)}, u32[]{:S(2)}, u32[]{:S(2)}) collective-permute-start(bf16[2,2,32,128]{3,2,1,0:T(8,128)(2,1)S(1)} %get-tuple-element.12.refs_1_), channel_id=1, source_target_pairs={{0,8},{1,11},{2,10},{3,9},{4,12},{5,15},{6,14},{7,13},{8,0},{9,3},... | collective-permute-start | bytes 98312 | tf_op jit(solution)/shard_map/ppermute | solution.py:169
  12.6 0.8 %collective-permute-start.8 = (bf16[2,2,32,128]{3,2,1,0:T(8,128)(2,1)S(1)}, bf16[2,2,32,128]{3,2,1,0:T(8,128)(2,1)S(1)}, u32[]{:S(2)}, u32[]{:S(2)}) collective-permute-start(bf16[2,2,32,128]{3,2,1,0:T(8,128)(2,1)S(1)} %get-tuple-element.14), channel_id=1, source_target_pairs={{0,4},{1,13},{2,6},{3,15},{4,0},{5,9},{6,2},{7,11},{8,12},{9,5},{1... | collective-permute-start | bytes 98312 | tf_op jit(solution)/shard_map/ppermute | solution.py:169
  13.4 0.0 copy-start.6
  13.4 0.0 copy-start.5
  13.4 0.0 copy-start.2
  13.4 0.0 copy-start.3
  13.4 1.8 %collective-permute-start.6 = (bf16[2,2,32,128]{3,2,1,0:T(8,128)(2,1)S(1)}, bf16[2,2,32,128]{3,2,1,0:T(8,128)(2,1)S(1)}, u32[]{:S(2)}, u32[]{:S(2)}) collective-permute-start(bf16[2,2,32,128]{3,2,1,0:T(8,128)(2,1)S(1)} %get-tuple-element.13), channel_id=1, source_target_pairs={{0,2},{1,3},{2,0},{3,1},{4,6},{5,7},{6,4},{7,5},{8,10},{9,11},{10,... | collective-permute-start | bytes 98312 | tf_op jit(solution)/shard_map/ppermute | solution.py:169
  15.2 0.0 copy-done.4
  15.2 1.9 %collective-permute-done.7.refs_2_ = bf16[2,2,32,128]{3,2,1,0:T(8,128)(2,1)S(1)} collective-permute-done((bf16[2,2,32,128]{3,2,1,0:T(8,128)(2,1)S(1)}, bf16[2,2,32,128]{3,2,1,0:T(8,128)(2,1)S(1)}, u32[]{:S(2)}, u32[]{:S(2)}) %collective-permute-start.7) | collective-permute-done | bytes 32800 | tf_op jit(solution)/shard_map/ppermute | solution.py:169
  17.1 0.1 collective-permute-done.8.refs_3_
  17.2 0.0 collective-permute-done.5.refs_0_
  17.2 0.9 %collective-permute-done.6.refs_1_ = bf16[2,2,32,128]{3,2,1,0:T(8,128)(2,1)S(1)} collective-permute-done((bf16[2,2,32,128]{3,2,1,0:T(8,128)(2,1)S(1)}, bf16[2,2,32,128]{3,2,1,0:T(8,128)(2,1)S(1)}, u32[]{:S(2)}, u32[]{:S(2)}) %collective-permute-start.6) | collective-permute-done | bytes 32800 | tf_op jit(solution)/shard_map/ppermute | solution.py:169
  18.1 0.6 %collective-permute-start.9 = (bf16[2,32,128]{2,1,0:T(8,128)(2,1)S(1)}, bf16[2,32,128]{2,1,0:T(8,128)(2,1)S(1)}, u32[]{:S(2)}, u32[]{:S(2)}) collective-permute-start(bf16[2,32,128]{2,1,0:T(8,128)(2,1)S(1)} %get-tuple-element.16), channel_id=1, source_target_pairs={{0,1},{1,0},{2,3},{3,2},{4,5},{5,4},{6,7},{7,6},{8,9},{9,8},{10,11... | collective-permute-start | bytes 49160 | tf_op jit(solution)/shard_map/ppermute | solution.py:172
  18.7 0.0 copy-done.6
  18.7 0.1 compare_convert_fusion.live_ref
  18.8 0.0 copy-done.5
  18.8 0.8 %collective-permute-done.9.refs_1_ = bf16[2,32,128]{2,1,0:T(8,128)(2,1)S(1)} collective-permute-done((bf16[2,32,128]{2,1,0:T(8,128)(2,1)S(1)}, bf16[2,32,128]{2,1,0:T(8,128)(2,1)S(1)}, u32[]{:S(2)}, u32[]{:S(2)}) %collective-permute-start.9) | collective-permute-done | bytes 16416 | tf_op jit(solution)/shard_map/ppermute | solution.py:172
  19.5 0.0 copy-done.2
  19.5 0.0 copy-done.3
  19.6 1.2 %attend.1 = bf16[2,4096]{1,0:T(2,128)(2,1)} custom-call(f32[2,1,256]{2,1,0:T(1,128)S(1)} %compare_convert_fusion.live_ref, bf16[2,32,128]{2,1,0:T(8,128)(2,1)S(1)} %bitcast.4, bf16[2,32,128]{2,1,0:T(8,128)(2,1)S(1)} %get-tuple-element.15.refs_0_, bf16[2,32,128]{2,1,0:T(8,128)(2,1)S(1)} %collective-permute-done.9.refs_1_, ...), custom_call_target="tpu_custom_call" | custom-call | tf_op jit(solution)/shard_map/attend/pallas_call | solution.py:247
  (3 shorter events, 0.0 us)
Async XLA Ops:
  0.0 8.3 %copy-start.1 = (bf16[8,16,4096]{2,1,0:T(8,128)(2,1)S(1)}, bf16[8,16,4096]{2,1,0:T(8,128)(2,1)}, u32[]{:S(2)}) copy-start(bf16[8,16,4096]{2,1,0:T(8,128)(2,1)} %mine_ref.5) | copy-start | bytes 3145732
  0.0 8.3 %copy-start = (bf16[8,16,8192]{2,1,0:T(8,128)(2,1)S(1)}, bf16[8,16,8192]{2,1,0:T(8,128)(2,1)}, u32[]{:S(2)}) copy-start(bf16[8,16,8192]{2,1,0:T(8,128)(2,1)} %down_ref.5) | copy-start | bytes 6291460
  0.0 8.3 %collective-permute-start = (bf16[8,16,4096]{2,1,0:T(8,128)(2,1)}, bf16[8,16,4096]{2,1,0:T(8,128)(2,1)S(1)}, u32[]{:S(2)}, u32[]{:S(2)}) collective-permute-start(bf16[8,16,4096]{2,1,0:T(8,128)(2,1)} %mine_ref.5), channel_id=1, source_target_pairs={{0,1},{1,0},{2,3},{3,2},{4,5},{5,4},{6,7},{7,6},{8,9},{9,8},{10,11... | collective-permute-start | bytes 3145736 | tf_op jit(solution)/shard_map/ppermute | solution.py:172
  0.5 7.8 %collective-permute-start.3 = (bf16[2,8192]{1,0:T(2,128)(2,1)}, bf16[2,8192]{1,0:T(2,128)(2,1)S(1)}, u32[]{:S(2)}, u32[]{:S(2)}) collective-permute-start(bf16[2,8192]{1,0:T(2,128)(2,1)} %refs_0_.3), channel_id=1, source_target_pairs={{0,6},{1,15},{2,4},{3,13},{4,2},{5,11},{6,0},{7,9},{8,14},{9,7},{1... | collective-permute-start | bytes 98312 | tf_op jit(solution)/shard_map/ppermute | solution.py:169
  4.0 4.3 %collective-permute-start.4 = (bf16[2,8192]{1,0:T(2,128)(2,1)}, bf16[2,8192]{1,0:T(2,128)(2,1)S(1)}, u32[]{:S(2)}, u32[]{:S(2)}) collective-permute-start(bf16[2,8192]{1,0:T(2,128)(2,1)} %refs_0_.3), channel_id=1, source_target_pairs={{0,2},{1,3},{2,0},{3,1},{4,6},{5,7},{6,4},{7,5},{8,10},{9,11},{10,... | collective-permute-start | bytes 98312 | tf_op jit(solution)/shard_map/ppermute | solution.py:169
  4.6 6.5 %collective-permute-start.1 = (bf16[2,8192]{1,0:T(2,128)(2,1)}, bf16[2,8192]{1,0:T(2,128)(2,1)S(1)}, u32[]{:S(2)}, u32[]{:S(2)}) collective-permute-start(bf16[2,8192]{1,0:T(2,128)(2,1)} %refs_0_.3), channel_id=1, source_target_pairs={{0,8},{1,11},{2,10},{3,9},{4,12},{5,15},{6,14},{7,13},{8,0},{9,3},... | collective-permute-start | bytes 98312 | tf_op jit(solution)/shard_map/ppermute | solution.py:169
  7.2 4.8 %collective-permute-start.2 = (bf16[2,8192]{1,0:T(2,128)(2,1)}, bf16[2,8192]{1,0:T(2,128)(2,1)S(1)}, u32[]{:S(2)}, u32[]{:S(2)}) collective-permute-start(bf16[2,8192]{1,0:T(2,128)(2,1)} %refs_0_.3), channel_id=1, source_target_pairs={{0,4},{1,13},{2,6},{3,15},{4,0},{5,9},{6,2},{7,11},{8,12},{9,5},{1... | collective-permute-start | bytes 98312 | tf_op jit(solution)/shard_map/ppermute | solution.py:169
  8.5 6.7 %copy-start.4 = (bf16[2,8192]{1,0:T(2,128)(2,1)S(1)}, bf16[2,8192]{1,0:T(2,128)(2,1)}, u32[]{:S(2)}) copy-start(bf16[2,8192]{1,0:T(2,128)(2,1)} %refs_0_.3) | copy-start | bytes 98308
  8.5 8.7 %collective-permute-start.5 = (bf16[2,2,32,128]{3,2,1,0:T(8,128)(2,1)S(1)}, bf16[2,2,32,128]{3,2,1,0:T(8,128)(2,1)S(1)}, u32[]{:S(2)}, u32[]{:S(2)}) collective-permute-start(bf16[2,2,32,128]{3,2,1,0:T(8,128)(2,1)S(1)} %get-tuple-element.11.refs_2_), channel_id=1, source_target_pairs={{0,6},{1,15},{2,4},{3,13},{4,2},{5,11},{6,0},{7,9},{8,14},{9,7},{1... | collective-permute-start | bytes 98312 | tf_op jit(solution)/shard_map/ppermute | solution.py:169
  12.1 5.0 %collective-permute-start.7 = (bf16[2,2,32,128]{3,2,1,0:T(8,128)(2,1)S(1)}, bf16[2,2,32,128]{3,2,1,0:T(8,128)(2,1)S(1)}, u32[]{:S(2)}, u32[]{:S(2)}) collective-permute-start(bf16[2,2,32,128]{3,2,1,0:T(8,128)(2,1)S(1)} %get-tuple-element.12.refs_1_), channel_id=1, source_target_pairs={{0,8},{1,11},{2,10},{3,9},{4,12},{5,15},{6,14},{7,13},{8,0},{9,3},... | collective-permute-start | bytes 98312 | tf_op jit(solution)/shard_map/ppermute | solution.py:169
  12.6 4.6 %collective-permute-start.8 = (bf16[2,2,32,128]{3,2,1,0:T(8,128)(2,1)S(1)}, bf16[2,2,32,128]{3,2,1,0:T(8,128)(2,1)S(1)}, u32[]{:S(2)}, u32[]{:S(2)}) collective-permute-start(bf16[2,2,32,128]{3,2,1,0:T(8,128)(2,1)S(1)} %get-tuple-element.14), channel_id=1, source_target_pairs={{0,4},{1,13},{2,6},{3,15},{4,0},{5,9},{6,2},{7,11},{8,12},{9,5},{1... | collective-permute-start | bytes 98312 | tf_op jit(solution)/shard_map/ppermute | solution.py:169
  13.4 5.3 %copy-start.6 = (s32[2]{0:T(128)S(1)}, s32[2]{0:T(128)}, u32[]{:S(2)}) copy-start(s32[2]{0:T(128)} %param.15) | copy-start | bytes 28
  13.4 5.4 %copy-start.5 = (bf16[2,4096]{1,0:T(2,128)(2,1)S(1)}, bf16[2,4096]{1,0:T(2,128)(2,1)}, u32[]{:S(2)}) copy-start(bf16[2,4096]{1,0:T(2,128)(2,1)} %param.9) | copy-start | bytes 49156
  13.4 6.1 %copy-start.2 = (bf16[2,4,256,128]{3,2,1,0:T(8,128)(2,1)S(1)}, bf16[2,4,256,128]{3,2,1,0:T(8,128)(2,1)}, u32[]{:S(2)}) copy-start(bf16[2,4,256,128]{3,2,1,0:T(8,128)(2,1)} %refs_2_.1) | copy-start | bytes 1572868
  13.4 6.1 %copy-start.3 = (bf16[2,4,256,128]{3,2,1,0:T(8,128)(2,1)S(1)}, bf16[2,4,256,128]{3,2,1,0:T(8,128)(2,1)}, u32[]{:S(2)}) copy-start(bf16[2,4,256,128]{3,2,1,0:T(8,128)(2,1)} %refs_3_.1) | copy-start | bytes 1572868
  13.4 4.6 %collective-permute-start.6 = (bf16[2,2,32,128]{3,2,1,0:T(8,128)(2,1)S(1)}, bf16[2,2,32,128]{3,2,1,0:T(8,128)(2,1)S(1)}, u32[]{:S(2)}, u32[]{:S(2)}) collective-permute-start(bf16[2,2,32,128]{3,2,1,0:T(8,128)(2,1)S(1)} %get-tuple-element.13), channel_id=1, source_target_pairs={{0,2},{1,3},{2,0},{3,1},{4,6},{5,7},{6,4},{7,5},{8,10},{9,11},{10,... | collective-permute-start | bytes 98312 | tf_op jit(solution)/shard_map/ppermute | solution.py:169
  18.1 1.4 %collective-permute-start.9 = (bf16[2,32,128]{2,1,0:T(8,128)(2,1)S(1)}, bf16[2,32,128]{2,1,0:T(8,128)(2,1)S(1)}, u32[]{:S(2)}, u32[]{:S(2)}) collective-permute-start(bf16[2,32,128]{2,1,0:T(8,128)(2,1)S(1)} %get-tuple-element.16), channel_id=1, source_target_pairs={{0,1},{1,0},{2,3},{3,2},{4,5},{5,4},{6,7},{7,6},{8,9},{9,8},{10,11... | collective-permute-start | bytes 49160 | tf_op jit(solution)/shard_map/ppermute | solution.py:172

commit v18 on v16

--- a/solution.py
+++ b/solution.py
@@ -141,7 +141,7 @@
             scores.append(jnp.where(live, score * scale, jnp.float32(-1e30)))
     scores = jnp.concatenate(scores, axis=0)
     grown = jnp.exp(scores - jnp.max(scores, axis=1, keepdims=True))
-    weights = grown / jnp.sum(grown, axis=1, keepdims=True)
+    weights = grown * (1.0 / jnp.sum(grown, axis=1, keepdims=True))
     for row in range(rows):
         for kv in range(kv_heads):
             at = (row * kv_heads + kv) * group

time: 20.5 us -> 20.4 us (level)
    ppermute x2, starting transfers between devices: 0.87 us -> 1.15 us  [swap(): return lax.ppermute(array, 'tensor', [(0, 1), (1, 0)])]
    ppermute x8, starting transfers between devices: 12.6 us -> 12.3 us  [visit(): return lax.ppermute(array, ('store', 'tensor'), turn_pairs(turn))]
  transfers between devices with their start and end apart: 10 -> 10, of which waited for: 4 -> 3; matrix products, arithmetic and copies ran while one was open for 0% -> 0% of each run, Pallas kernels for 6% -> 6%
where the time goes in v18:
time: 20.4 us; the launch traced here: 20.2 us
  starting transfers between devices  13.5 us (66%)
  waiting for transfers between devices  4.11 us (20%)
  Pallas kernels  2.39 us (12%)
    ppermute x8, starting transfers between devices, visit(): return lax.ppermute(array, ('store', 'tensor'), turn_pairs(turn))  12.3 us
    ppermute x8, waiting for transfers between devices, visit(): return lax.ppermute(array, ('store', 'tensor'), turn_pairs(turn))  3.35 us
    pallas_call x1, Pallas kernels, per_device(): pl.pallas_call(functools.partial(attend_kernel, len(deltas)), out_shape=j...  1.16 us
    ppermute x2, starting transfers between devices, swap(): return lax.ppermute(array, 'tensor', [(0, 1), (1, 0)])  1.15 us
    ppermute x2, waiting for transfers between devices, swap(): return lax.ppermute(array, 'tensor', [(0, 1), (1, 0)])  0.75 us
    pallas_call x1, Pallas kernels, scalars(): pl.pallas_call(scalars_kernel, out_shape=pltpu.SMEM(ids.shape, ids.dtype)...  0.67 us
    pallas_call x3, Pallas kernels, work(): pl.pallas_call(functools.partial(owner_kernel, turns), out_shape=[jax.Sha...  0.52 us
  transfers between devices with their start and end apart: 10, of which 3 were waited for; matrix products, arithmetic and copies ran while one was open for 0% of the time, Pallas kernels for 6%

profile of v18, /device:TPU:0, one launch (start us, length us, event | category | flops | bytes accessed | tf_op | source)
XLA Modules:
  0.0 20.2 jit_solution(6663121793245370901)
XLA Ops:
  0.0 0.0 copy-start.1
  0.0 0.0 copy-start
  0.0 0.5 %collective-permute-start = (bf16[8,16,4096]{2,1,0:T(8,128)(2,1)}, bf16[8,16,4096]{2,1,0:T(8,128)(2,1)S(1)}, u32[]{:S(2)}, u32[]{:S(2)}) collective-permute-start(bf16[8,16,4096]{2,1,0:T(8,128)(2,1)} %mine_ref.5), channel_id=1, source_target_pairs={{0,1},{1,0},{2,3},{3,2},{4,5},{5,4},{6,7},{7,6},{8,9},{9,8},{10,11... | collective-permute-start | bytes 3145736 | tf_op jit(solution)/shard_map/ppermute | solution.py:172
  0.5 3.6 %collective-permute-start.3 = (bf16[2,8192]{1,0:T(2,128)(2,1)}, bf16[2,8192]{1,0:T(2,128)(2,1)S(1)}, u32[]{:S(2)}, u32[]{:S(2)}) collective-permute-start(bf16[2,8192]{1,0:T(2,128)(2,1)} %refs_0_.3), channel_id=1, source_target_pairs={{0,6},{1,15},{2,4},{3,13},{4,2},{5,11},{6,0},{7,9},{8,14},{9,7},{1... | collective-permute-start | bytes 98312 | tf_op jit(solution)/shard_map/ppermute | solution.py:169
  4.0 0.5 %collective-permute-start.4 = (bf16[2,8192]{1,0:T(2,128)(2,1)}, bf16[2,8192]{1,0:T(2,128)(2,1)S(1)}, u32[]{:S(2)}, u32[]{:S(2)}) collective-permute-start(bf16[2,8192]{1,0:T(2,128)(2,1)} %refs_0_.3), channel_id=1, source_target_pairs={{0,2},{1,3},{2,0},{3,1},{4,6},{5,7},{6,4},{7,5},{8,10},{9,11},{10,... | collective-permute-start | bytes 98312 | tf_op jit(solution)/shard_map/ppermute | solution.py:169
  4.6 2.6 %collective-permute-start.1 = (bf16[2,8192]{1,0:T(2,128)(2,1)}, bf16[2,8192]{1,0:T(2,128)(2,1)S(1)}, u32[]{:S(2)}, u32[]{:S(2)}) collective-permute-start(bf16[2,8192]{1,0:T(2,128)(2,1)} %refs_0_.3), channel_id=1, source_target_pairs={{0,8},{1,11},{2,10},{3,9},{4,12},{5,15},{6,14},{7,13},{8,0},{9,3},... | collective-permute-start | bytes 98312 | tf_op jit(solution)/shard_map/ppermute | solution.py:169
  7.2 0.4 %collective-permute-start.2 = (bf16[2,8192]{1,0:T(2,128)(2,1)}, bf16[2,8192]{1,0:T(2,128)(2,1)S(1)}, u32[]{:S(2)}, u32[]{:S(2)}) collective-permute-start(bf16[2,8192]{1,0:T(2,128)(2,1)} %refs_0_.3), channel_id=1, source_target_pairs={{0,4},{1,13},{2,6},{3,15},{4,0},{5,9},{6,2},{7,11},{8,12},{9,5},{1... | collective-permute-start | bytes 98312 | tf_op jit(solution)/shard_map/ppermute | solution.py:169
  7.6 0.7 %scalars.1.ids_ref = s32[16]{0:T(128)S(4)} custom-call(s32[16]{0:T(128)} %ids_hbm.1, bf16[8,16,8192]{2,1,0:T(8,128)(2,1)} %down_ref.5, bf16[8,16,4096]{2,1,0:T(8,128)(2,1)} %mine_ref.5), custom_call_target="tpu_custom_call" | custom-call | bytes 3145728 | tf_op jit(solution)/shard_map/scalars/pallas_call | solution.py:33
  8.3 0.0 collective-permute-done.3.refs_0_
  8.3 0.0 collective-permute-done.4.refs_1_
  8.3 0.0 collective-permute-done.other_ref
  8.3 0.0 copy-done.1
  8.3 0.0 copy-done
  8.3 0.2 owner0.1
  8.5 0.0 copy-start.4
  8.5 2.6 %collective-permute-start.5 = (bf16[2,2,32,128]{3,2,1,0:T(8,128)(2,1)S(1)}, bf16[2,2,32,128]{3,2,1,0:T(8,128)(2,1)S(1)}, u32[]{:S(2)}, u32[]{:S(2)}) collective-permute-start(bf16[2,2,32,128]{3,2,1,0:T(8,128)(2,1)S(1)} %get-tuple-element.11.refs_2_), channel_id=1, source_target_pairs={{0,6},{1,15},{2,4},{3,13},{4,2},{5,11},{6,0},{7,9},{8,14},{9,7},{1... | collective-permute-start | bytes 98312 | tf_op jit(solution)/shard_map/ppermute | solution.py:169
  11.1 0.0 collective-permute-done.1.refs_0_
  11.1 0.9 %collective-permute-done.2.refs_1_ = bf16[2,8192]{1,0:T(2,128)(2,1)S(1)} collective-permute-done((bf16[2,8192]{1,0:T(2,128)(2,1)}, bf16[2,8192]{1,0:T(2,128)(2,1)S(1)}, u32[]{:S(2)}, u32[]{:S(2)}) %collective-permute-start.2) | collective-permute-done | bytes 32800 | tf_op jit(solution)/shard_map/ppermute | solution.py:169
  12.0 0.4 %owner2.1 = (bf16[2,2,32,128]{3,2,1,0:T(8,128)(2,1)S(1)}, bf16[2,2,32,128]{3,2,1,0:T(8,128)(2,1)S(1)}) custom-call(s32[16]{0:T(128)S(4)} %scalars.1.ids_ref, bf16[8,16,8192]{2,1,0:T(8,128)(2,1)S(1)} %copy-done, bf16[8,16,4096]{2,1,0:T(8,128)(2,1)S(1)} %copy-done.1, bf16[8,16,4096]{2,1,0:T(8,128)(2,1)S(1)} %collective-permute-done.other_ref, ...), custom_call_target="tpu_custom_call" | custom-call | tf_op jit(solution)/shard_map/owner2/pallas_call | solution.py:182
  12.3 0.2 %collective-permute-start.7 = (bf16[2,2,32,128]{3,2,1,0:T(8,128)(2,1)S(1)}, bf16[2,2,32,128]{3,2,1,0:T(8,128)(2,1)S(1)}, u32[]{:S(2)}, u32[]{:S(2)}) collective-permute-start(bf16[2,2,32,128]{3,2,1,0:T(8,128)(2,1)S(1)} %get-tuple-element.12.refs_1_), channel_id=1, source_target_pairs={{0,8},{1,11},{2,10},{3,9},{4,12},{5,15},{6,14},{7,13},{8,0},{9,3},... | collective-permute-start | bytes 98312 | tf_op jit(solution)/shard_map/ppermute | solution.py:169
  12.6 0.7 %collective-permute-start.8 = (bf16[2,2,32,128]{3,2,1,0:T(8,128)(2,1)S(1)}, bf16[2,2,32,128]{3,2,1,0:T(8,128)(2,1)S(1)}, u32[]{:S(2)}, u32[]{:S(2)}) collective-permute-start(bf16[2,2,32,128]{3,2,1,0:T(8,128)(2,1)S(1)} %get-tuple-element.14), channel_id=1, source_target_pairs={{0,4},{1,13},{2,6},{3,15},{4,0},{5,9},{6,2},{7,11},{8,12},{9,5},{1... | collective-permute-start | bytes 98312 | tf_op jit(solution)/shard_map/ppermute | solution.py:169
  13.3 0.0 copy-start.6
  13.3 0.0 copy-start.5
  13.3 0.0 copy-start.2
  13.3 0.0 copy-start.3
  13.3 1.7 %collective-permute-start.6 = (bf16[2,2,32,128]{3,2,1,0:T(8,128)(2,1)S(1)}, bf16[2,2,32,128]{3,2,1,0:T(8,128)(2,1)S(1)}, u32[]{:S(2)}, u32[]{:S(2)}) collective-permute-start(bf16[2,2,32,128]{3,2,1,0:T(8,128)(2,1)S(1)} %get-tuple-element.13), channel_id=1, source_target_pairs={{0,2},{1,3},{2,0},{3,1},{4,6},{5,7},{6,4},{7,5},{8,10},{9,11},{10,... | collective-permute-start | bytes 98312 | tf_op jit(solution)/shard_map/ppermute | solution.py:169
  15.0 0.0 copy-done.4
  15.0 2.4 %collective-permute-done.7.refs_2_ = bf16[2,2,32,128]{3,2,1,0:T(8,128)(2,1)S(1)} collective-permute-done((bf16[2,2,32,128]{3,2,1,0:T(8,128)(2,1)S(1)}, bf16[2,2,32,128]{3,2,1,0:T(8,128)(2,1)S(1)}, u32[]{:S(2)}, u32[]{:S(2)}) %collective-permute-start.7) | collective-permute-done | bytes 32800 | tf_op jit(solution)/shard_map/ppermute | solution.py:169
  17.4 0.0 collective-permute-done.8.refs_3_
  17.5 0.0 collective-permute-done.5.refs_0_
  17.5 0.0 collective-permute-done.6.refs_1_
  17.5 0.7 %collective-permute-start.9 = (bf16[2,32,128]{2,1,0:T(8,128)(2,1)S(1)}, bf16[2,32,128]{2,1,0:T(8,128)(2,1)S(1)}, u32[]{:S(2)}, u32[]{:S(2)}) collective-permute-start(bf16[2,32,128]{2,1,0:T(8,128)(2,1)S(1)} %get-tuple-element.16), channel_id=1, source_target_pairs={{0,1},{1,0},{2,3},{3,2},{4,5},{5,4},{6,7},{7,6},{8,9},{9,8},{10,11... | collective-permute-start | bytes 49160 | tf_op jit(solution)/shard_map/ppermute | solution.py:172
  18.2 0.0 copy-done.6
  18.2 0.1 compare_convert_fusion.live_ref
  18.3 0.0 copy-done.5
  18.3 0.8 %collective-permute-done.9.refs_1_ = bf16[2,32,128]{2,1,0:T(8,128)(2,1)S(1)} collective-permute-done((bf16[2,32,128]{2,1,0:T(8,128)(2,1)S(1)}, bf16[2,32,128]{2,1,0:T(8,128)(2,1)S(1)}, u32[]{:S(2)}, u32[]{:S(2)}) %collective-permute-start.9) | collective-permute-done | bytes 16416 | tf_op jit(solution)/shard_map/ppermute | solution.py:172
  19.0 0.0 copy-done.2
  19.0 0.0 copy-done.3
  19.0 1.2 %attend.1 = bf16[2,4096]{1,0:T(2,128)(2,1)} custom-call(f32[2,1,256]{2,1,0:T(1,128)S(1)} %compare_convert_fusion.live_ref, bf16[2,32,128]{2,1,0:T(8,128)(2,1)S(1)} %bitcast.4, bf16[2,32,128]{2,1,0:T(8,128)(2,1)S(1)} %get-tuple-element.15.refs_0_, bf16[2,32,128]{2,1,0:T(8,128)(2,1)S(1)} %collective-permute-done.9.refs_1_, ...), custom_call_target="tpu_custom_call" | custom-call | tf_op jit(solution)/shard_map/attend/pallas_call | solution.py:247
  (3 shorter events, 0.0 us)
Async XLA Ops:
  0.0 8.3 %copy-start.1 = (bf16[8,16,4096]{2,1,0:T(8,128)(2,1)S(1)}, bf16[8,16,4096]{2,1,0:T(8,128)(2,1)}, u32[]{:S(2)}) copy-start(bf16[8,16,4096]{2,1,0:T(8,128)(2,1)} %mine_ref.5) | copy-start | bytes 3145732
  0.0 8.3 %copy-start = (bf16[8,16,8192]{2,1,0:T(8,128)(2,1)S(1)}, bf16[8,16,8192]{2,1,0:T(8,128)(2,1)}, u32[]{:S(2)}) copy-start(bf16[8,16,8192]{2,1,0:T(8,128)(2,1)} %down_ref.5) | copy-start | bytes 6291460
  0.0 8.3 %collective-permute-start = (bf16[8,16,4096]{2,1,0:T(8,128)(2,1)}, bf16[8,16,4096]{2,1,0:T(8,128)(2,1)S(1)}, u32[]{:S(2)}, u32[]{:S(2)}) collective-permute-start(bf16[8,16,4096]{2,1,0:T(8,128)(2,1)} %mine_ref.5), channel_id=1, source_target_pairs={{0,1},{1,0},{2,3},{3,2},{4,5},{5,4},{6,7},{7,6},{8,9},{9,8},{10,11... | collective-permute-start | bytes 3145736 | tf_op jit(solution)/shard_map/ppermute | solution.py:172
  0.5 7.8 %collective-permute-start.3 = (bf16[2,8192]{1,0:T(2,128)(2,1)}, bf16[2,8192]{1,0:T(2,128)(2,1)S(1)}, u32[]{:S(2)}, u32[]{:S(2)}) collective-permute-start(bf16[2,8192]{1,0:T(2,128)(2,1)} %refs_0_.3), channel_id=1, source_target_pairs={{0,6},{1,15},{2,4},{3,13},{4,2},{5,11},{6,0},{7,9},{8,14},{9,7},{1... | collective-permute-start | bytes 98312 | tf_op jit(solution)/shard_map/ppermute | solution.py:169
  4.0 4.3 %collective-permute-start.4 = (bf16[2,8192]{1,0:T(2,128)(2,1)}, bf16[2,8192]{1,0:T(2,128)(2,1)S(1)}, u32[]{:S(2)}, u32[]{:S(2)}) collective-permute-start(bf16[2,8192]{1,0:T(2,128)(2,1)} %refs_0_.3), channel_id=1, source_target_pairs={{0,2},{1,3},{2,0},{3,1},{4,6},{5,7},{6,4},{7,5},{8,10},{9,11},{10,... | collective-permute-start | bytes 98312 | tf_op jit(solution)/shard_map/ppermute | solution.py:169
  4.6 6.5 %collective-permute-start.1 = (bf16[2,8192]{1,0:T(2,128)(2,1)}, bf16[2,8192]{1,0:T(2,128)(2,1)S(1)}, u32[]{:S(2)}, u32[]{:S(2)}) collective-permute-start(bf16[2,8192]{1,0:T(2,128)(2,1)} %refs_0_.3), channel_id=1, source_target_pairs={{0,8},{1,11},{2,10},{3,9},{4,12},{5,15},{6,14},{7,13},{8,0},{9,3},... | collective-permute-start | bytes 98312 | tf_op jit(solution)/shard_map/ppermute | solution.py:169
  7.2 4.8 %collective-permute-start.2 = (bf16[2,8192]{1,0:T(2,128)(2,1)}, bf16[2,8192]{1,0:T(2,128)(2,1)S(1)}, u32[]{:S(2)}, u32[]{:S(2)}) collective-permute-start(bf16[2,8192]{1,0:T(2,128)(2,1)} %refs_0_.3), channel_id=1, source_target_pairs={{0,4},{1,13},{2,6},{3,15},{4,0},{5,9},{6,2},{7,11},{8,12},{9,5},{1... | collective-permute-start | bytes 98312 | tf_op jit(solution)/shard_map/ppermute | solution.py:169
  8.5 6.5 %copy-start.4 = (bf16[2,8192]{1,0:T(2,128)(2,1)S(1)}, bf16[2,8192]{1,0:T(2,128)(2,1)}, u32[]{:S(2)}) copy-start(bf16[2,8192]{1,0:T(2,128)(2,1)} %refs_0_.3) | copy-start | bytes 98308
  8.5 8.9 %collective-permute-start.5 = (bf16[2,2,32,128]{3,2,1,0:T(8,128)(2,1)S(1)}, bf16[2,2,32,128]{3,2,1,0:T(8,128)(2,1)S(1)}, u32[]{:S(2)}, u32[]{:S(2)}) collective-permute-start(bf16[2,2,32,128]{3,2,1,0:T(8,128)(2,1)S(1)} %get-tuple-element.11.refs_2_), channel_id=1, source_target_pairs={{0,6},{1,15},{2,4},{3,13},{4,2},{5,11},{6,0},{7,9},{8,14},{9,7},{1... | collective-permute-start | bytes 98312 | tf_op jit(solution)/shard_map/ppermute | solution.py:169
  12.3 5.1 %collective-permute-start.7 = (bf16[2,2,32,128]{3,2,1,0:T(8,128)(2,1)S(1)}, bf16[2,2,32,128]{3,2,1,0:T(8,128)(2,1)S(1)}, u32[]{:S(2)}, u32[]{:S(2)}) collective-permute-start(bf16[2,2,32,128]{3,2,1,0:T(8,128)(2,1)S(1)} %get-tuple-element.12.refs_1_), channel_id=1, source_target_pairs={{0,8},{1,11},{2,10},{3,9},{4,12},{5,15},{6,14},{7,13},{8,0},{9,3},... | collective-permute-start | bytes 98312 | tf_op jit(solution)/shard_map/ppermute | solution.py:169
  12.6 4.9 %collective-permute-start.8 = (bf16[2,2,32,128]{3,2,1,0:T(8,128)(2,1)S(1)}, bf16[2,2,32,128]{3,2,1,0:T(8,128)(2,1)S(1)}, u32[]{:S(2)}, u32[]{:S(2)}) collective-permute-start(bf16[2,2,32,128]{3,2,1,0:T(8,128)(2,1)S(1)} %get-tuple-element.14), channel_id=1, source_target_pairs={{0,4},{1,13},{2,6},{3,15},{4,0},{5,9},{6,2},{7,11},{8,12},{9,5},{1... | collective-permute-start | bytes 98312 | tf_op jit(solution)/shard_map/ppermute | solution.py:169
  13.3 5.0 %copy-start.6 = (s32[2]{0:T(128)S(1)}, s32[2]{0:T(128)}, u32[]{:S(2)}) copy-start(s32[2]{0:T(128)} %param.15) | copy-start | bytes 28
  13.3 5.0 %copy-start.5 = (bf16[2,4096]{1,0:T(2,128)(2,1)S(1)}, bf16[2,4096]{1,0:T(2,128)(2,1)}, u32[]{:S(2)}) copy-start(bf16[2,4096]{1,0:T(2,128)(2,1)} %param.9) | copy-start | bytes 49156
  13.3 5.8 %copy-start.2 = (bf16[2,4,256,128]{3,2,1,0:T(8,128)(2,1)S(1)}, bf16[2,4,256,128]{3,2,1,0:T(8,128)(2,1)}, u32[]{:S(2)}) copy-start(bf16[2,4,256,128]{3,2,1,0:T(8,128)(2,1)} %refs_2_.1) | copy-start | bytes 1572868
  13.3 5.8 %copy-start.3 = (bf16[2,4,256,128]{3,2,1,0:T(8,128)(2,1)S(1)}, bf16[2,4,256,128]{3,2,1,0:T(8,128)(2,1)}, u32[]{:S(2)}) copy-start(bf16[2,4,256,128]{3,2,1,0:T(8,128)(2,1)} %refs_3_.1) | copy-start | bytes 1572868
  13.3 4.2 %collective-permute-start.6 = (bf16[2,2,32,128]{3,2,1,0:T(8,128)(2,1)S(1)}, bf16[2,2,32,128]{3,2,1,0:T(8,128)(2,1)S(1)}, u32[]{:S(2)}, u32[]{:S(2)}) collective-permute-start(bf16[2,2,32,128]{3,2,1,0:T(8,128)(2,1)S(1)} %get-tuple-element.13), channel_id=1, source_target_pairs={{0,2},{1,3},{2,0},{3,1},{4,6},{5,7},{6,4},{7,5},{8,10},{9,11},{10,... | collective-permute-start | bytes 98312 | tf_op jit(solution)/shard_map/ppermute | solution.py:169
  17.5 1.5 %collective-permute-start.9 = (bf16[2,32,128]{2,1,0:T(8,128)(2,1)S(1)}, bf16[2,32,128]{2,1,0:T(8,128)(2,1)S(1)}, u32[]{:S(2)}, u32[]{:S(2)}) collective-permute-start(bf16[2,32,128]{2,1,0:T(8,128)(2,1)S(1)} %get-tuple-element.16), channel_id=1, source_target_pairs={{0,1},{1,0},{2,3},{3,2},{4,5},{5,4},{6,7},{7,6},{8,9},{9,8},{10,11... | collective-permute-start | bytes 49160 | tf_op jit(solution)/shard_map/ppermute | solution.py:172

commit v19 on v13

--- a/solution.py
+++ b/solution.py
@@ -17,7 +17,7 @@
 PARAMS = pltpu.CompilerParams(vmem_limit_bytes=VMEM_LIMIT)
 TURNS = ((3, 1, 4, 2, 0), (7, 1, 5, 6, 0))
 SENT = len(TURNS[0]) - 1
-EARLY = 2
+GROUPS = ((0, 1), (2, 3), (4,))
 SHARED = [first == second for first, second in zip(*TURNS)]
 
 
@@ -147,7 +147,7 @@
             scores.append(jnp.where(live, score * scale, jnp.float32(-1e30)))
     scores = jnp.concatenate(scores, axis=0)
     grown = jnp.exp(scores - jnp.max(scores, axis=1, keepdims=True))
-    weights = grown / jnp.sum(grown, axis=1, keepdims=True)
+    weights = grown * (1.0 / jnp.sum(grown, axis=1, keepdims=True))
     for row in range(rows):
         for kv in range(kv_heads):
             at = (row * kv_heads + kv) * group
@@ -200,8 +200,10 @@
         )(ids, down, up, other, *[states[turn] for turn in turns], *after)
 
     states.append(near(hidden))
-    deltas = work("owner_first", (), *range(EARLY))
-    deltas += work("owner_rest", deltas[:1], *range(EARLY, SENT + 1))
+    deltas = []
+    for group in GROUPS:
+        after = [deltas[others[0]] for others in GROUPS if others[0] < group[0]][-1:]
+        deltas += work("owner%d" % group[0], after, *group)
     came = [visit(delta, turn) for turn, delta in enumerate(deltas[:SENT])]
     kept, sent = pl.pallas_call(
         merge_kernel,

time: 20.8 us -> 20.7 us (level)
  starting transfers between devices: 14.1 us -> 13 us
  waiting for transfers between devices: 4.1 us -> 4.8 us
    ppermute x8, starting transfers between devices: 13.1 us -> 12.1 us  [visit(): return lax.ppermute(array, ('store', 'tensor'), turn_pairs(turn))]
    ppermute x8, waiting for transfers between devices: 3.55 us -> 4.22 us  [visit(): return lax.ppermute(array, ('store', 'tensor'), turn_pairs(turn))]
    pallas_call x2 -> x3, Pallas kernels: 0.37 us -> 0.52 us  [work(): pl.pallas_call(functools.partial(owner_kernel, turns), out_shape=[jax.Sha...]
  transfers between devices with their start and end apart: 10 -> 10, of which waited for: 4 -> 4; matrix products, arithmetic and copies ran while one was open for 0% -> 0% of each run, Pallas kernels for 6% -> 7%
where the time goes in v19:
time: 20.7 us; the launch traced here: 20.5 us
  starting transfers between devices  13 us (63%)
  waiting for transfers between devices  4.8 us (23%)
  Pallas kernels  2.53 us (12%)
    ppermute x8, starting transfers between devices, visit(): return lax.ppermute(array, ('store', 'tensor'), turn_pairs(turn))  12.1 us
    ppermute x8, waiting for transfers between devices, visit(): return lax.ppermute(array, ('store', 'tensor'), turn_pairs(turn))  4.22 us
    pallas_call x1, Pallas kernels, per_device(): pl.pallas_call(functools.partial(attend_kernel, len(deltas)), out_shape=j...  1.13 us
    ppermute x2, starting transfers between devices, swap(): return lax.ppermute(array, 'tensor', [(0, 1), (1, 0)])  0.83 us
    pallas_call x1, Pallas kernels, scalars(): pl.pallas_call(scalars_kernel, out_shape=pltpu.SMEM(ids.shape, ids.dtype)...  0.67 us
    ppermute x2, waiting for transfers between devices, swap(): return lax.ppermute(array, 'tensor', [(0, 1), (1, 0)])  0.58 us
    pallas_call x3, Pallas kernels, work(): pl.pallas_call(functools.partial(owner_kernel, turns), out_shape=[jax.Sha...  0.52 us
  transfers between devices with their start and end apart: 10, of which 4 were waited for; matrix products, arithmetic and copies ran while one was open for 0% of the time, Pallas kernels for 7%

profile of v19, /device:TPU:0, one launch (start us, length us, event | category | flops | bytes accessed | tf_op | source)
XLA Modules:
  0.0 20.5 jit_solution(13078848014778416691)
XLA Ops:
  0.0 0.0 copy-start.1
  0.0 0.0 copy-start
  0.0 0.5 %collective-permute-start = (bf16[8,16,4096]{2,1,0:T(8,128)(2,1)}, bf16[8,16,4096]{2,1,0:T(8,128)(2,1)S(1)}, u32[]{:S(2)}, u32[]{:S(2)}) collective-permute-start(bf16[8,16,4096]{2,1,0:T(8,128)(2,1)} %mine_ref.5), channel_id=1, source_target_pairs={{0,1},{1,0},{2,3},{3,2},{4,5},{5,4},{6,7},{7,6},{8,9},{9,8},{10,11... | collective-permute-start | bytes 3145736 | tf_op jit(solution)/shard_map/ppermute | solution.py:178
  0.5 3.6 %collective-permute-start.3 = (bf16[2,8192]{1,0:T(2,128)(2,1)}, bf16[2,8192]{1,0:T(2,128)(2,1)S(1)}, u32[]{:S(2)}, u32[]{:S(2)}) collective-permute-start(bf16[2,8192]{1,0:T(2,128)(2,1)} %refs_0_.3), channel_id=1, source_target_pairs={{0,6},{1,15},{2,4},{3,13},{4,2},{5,11},{6,0},{7,9},{8,14},{9,7},{1... | collective-permute-start | bytes 98312 | tf_op jit(solution)/shard_map/ppermute | solution.py:175
  4.0 0.5 %collective-permute-start.4 = (bf16[2,8192]{1,0:T(2,128)(2,1)}, bf16[2,8192]{1,0:T(2,128)(2,1)S(1)}, u32[]{:S(2)}, u32[]{:S(2)}) collective-permute-start(bf16[2,8192]{1,0:T(2,128)(2,1)} %refs_0_.3), channel_id=1, source_target_pairs={{0,2},{1,3},{2,0},{3,1},{4,6},{5,7},{6,4},{7,5},{8,10},{9,11},{10,... | collective-permute-start | bytes 98312 | tf_op jit(solution)/shard_map/ppermute | solution.py:175
  4.6 2.6 %collective-permute-start.1 = (bf16[2,8192]{1,0:T(2,128)(2,1)}, bf16[2,8192]{1,0:T(2,128)(2,1)S(1)}, u32[]{:S(2)}, u32[]{:S(2)}) collective-permute-start(bf16[2,8192]{1,0:T(2,128)(2,1)} %refs_0_.3), channel_id=1, source_target_pairs={{0,8},{1,11},{2,10},{3,9},{4,12},{5,15},{6,14},{7,13},{8,0},{9,3},... | collective-permute-start | bytes 98312 | tf_op jit(solution)/shard_map/ppermute | solution.py:175
  7.2 0.4 %collective-permute-start.2 = (bf16[2,8192]{1,0:T(2,128)(2,1)}, bf16[2,8192]{1,0:T(2,128)(2,1)S(1)}, u32[]{:S(2)}, u32[]{:S(2)}) collective-permute-start(bf16[2,8192]{1,0:T(2,128)(2,1)} %refs_0_.3), channel_id=1, source_target_pairs={{0,4},{1,13},{2,6},{3,15},{4,0},{5,9},{6,2},{7,11},{8,12},{9,5},{1... | collective-permute-start | bytes 98312 | tf_op jit(solution)/shard_map/ppermute | solution.py:175
  7.6 0.7 %scalars.1.ids_ref = s32[16]{0:T(128)S(4)} custom-call(s32[16]{0:T(128)} %ids_hbm.1, bf16[8,16,8192]{2,1,0:T(8,128)(2,1)} %down_ref.5, bf16[8,16,4096]{2,1,0:T(8,128)(2,1)} %mine_ref.5), custom_call_target="tpu_custom_call" | custom-call | bytes 3145728 | tf_op jit(solution)/shard_map/scalars/pallas_call | solution.py:33
  8.3 0.0 collective-permute-done.3.refs_0_
  8.3 0.0 collective-permute-done.4.refs_1_
  8.3 0.0 collective-permute-done.other_ref
  8.3 0.0 copy-done.1
  8.3 0.0 copy-done
  8.3 0.2 owner0.1
  8.5 0.0 copy-start.4
  8.5 2.6 %collective-permute-start.5 = (bf16[2,2,32,128]{3,2,1,0:T(8,128)(2,1)S(1)}, bf16[2,2,32,128]{3,2,1,0:T(8,128)(2,1)S(1)}, u32[]{:S(2)}, u32[]{:S(2)}) collective-permute-start(bf16[2,2,32,128]{3,2,1,0:T(8,128)(2,1)S(1)} %get-tuple-element.11.refs_2_), channel_id=1, source_target_pairs={{0,6},{1,15},{2,4},{3,13},{4,2},{5,11},{6,0},{7,9},{8,14},{9,7},{1... | collective-permute-start | bytes 98312 | tf_op jit(solution)/shard_map/ppermute | solution.py:175
  11.1 0.0 collective-permute-done.1.refs_0_
  11.1 0.9 %collective-permute-done.2.refs_1_ = bf16[2,8192]{1,0:T(2,128)(2,1)S(1)} collective-permute-done((bf16[2,8192]{1,0:T(2,128)(2,1)}, bf16[2,8192]{1,0:T(2,128)(2,1)S(1)}, u32[]{:S(2)}, u32[]{:S(2)}) %collective-permute-start.2) | collective-permute-done | bytes 32800 | tf_op jit(solution)/shard_map/ppermute | solution.py:175
  12.0 0.3 %owner2.1 = (bf16[2,2,32,128]{3,2,1,0:T(8,128)(2,1)S(1)}, bf16[2,2,32,128]{3,2,1,0:T(8,128)(2,1)S(1)}) custom-call(s32[16]{0:T(128)S(4)} %scalars.1.ids_ref, bf16[8,16,8192]{2,1,0:T(8,128)(2,1)S(1)} %copy-done, bf16[8,16,4096]{2,1,0:T(8,128)(2,1)S(1)} %copy-done.1, bf16[8,16,4096]{2,1,0:T(8,128)(2,1)S(1)} %collective-permute-done.other_ref, ...), custom_call_target="tpu_custom_call" | custom-call | tf_op jit(solution)/shard_map/owner2/pallas_call | solution.py:188
  12.3 0.3 %collective-permute-start.7 = (bf16[2,2,32,128]{3,2,1,0:T(8,128)(2,1)S(1)}, bf16[2,2,32,128]{3,2,1,0:T(8,128)(2,1)S(1)}, u32[]{:S(2)}, u32[]{:S(2)}) collective-permute-start(bf16[2,2,32,128]{3,2,1,0:T(8,128)(2,1)S(1)} %get-tuple-element.12.refs_1_), channel_id=1, source_target_pairs={{0,8},{1,11},{2,10},{3,9},{4,12},{5,15},{6,14},{7,13},{8,0},{9,3},... | collective-permute-start | bytes 98312 | tf_op jit(solution)/shard_map/ppermute | solution.py:175
  12.6 1.1 %collective-permute-start.8 = (bf16[2,2,32,128]{3,2,1,0:T(8,128)(2,1)S(1)}, bf16[2,2,32,128]{3,2,1,0:T(8,128)(2,1)S(1)}, u32[]{:S(2)}, u32[]{:S(2)}) collective-permute-start(bf16[2,2,32,128]{3,2,1,0:T(8,128)(2,1)S(1)} %get-tuple-element.14), channel_id=1, source_target_pairs={{0,4},{1,13},{2,6},{3,15},{4,0},{5,9},{6,2},{7,11},{8,12},{9,5},{1... | collective-permute-start | bytes 98312 | tf_op jit(solution)/shard_map/ppermute | solution.py:175
  13.7 0.0 copy-start.6
  13.7 0.0 copy-start.2
  13.7 0.0 copy-start.5
  13.7 0.0 copy-start.3
  13.7 1.1 %collective-permute-start.6 = (bf16[2,2,32,128]{3,2,1,0:T(8,128)(2,1)S(1)}, bf16[2,2,32,128]{3,2,1,0:T(8,128)(2,1)S(1)}, u32[]{:S(2)}, u32[]{:S(2)}) collective-permute-start(bf16[2,2,32,128]{3,2,1,0:T(8,128)(2,1)S(1)} %get-tuple-element.13), channel_id=1, source_target_pairs={{0,2},{1,3},{2,0},{3,1},{4,6},{5,7},{6,4},{7,5},{8,10},{9,11},{10,... | collective-permute-start | bytes 98312 | tf_op jit(solution)/shard_map/ppermute | solution.py:175
  14.8 0.0 copy-done.4
  14.8 2.7 %collective-permute-done.7.refs_2_ = bf16[2,2,32,128]{3,2,1,0:T(8,128)(2,1)S(1)} collective-permute-done((bf16[2,2,32,128]{3,2,1,0:T(8,128)(2,1)S(1)}, bf16[2,2,32,128]{3,2,1,0:T(8,128)(2,1)S(1)}, u32[]{:S(2)}, u32[]{:S(2)}) %collective-permute-start.7) | collective-permute-done | bytes 32800 | tf_op jit(solution)/shard_map/ppermute | solution.py:175
  17.5 0.0 collective-permute-done.8.refs_3_
  17.5 0.0 collective-permute-done.5.refs_0_
  17.5 0.6 %collective-permute-done.6.refs_1_ = bf16[2,2,32,128]{3,2,1,0:T(8,128)(2,1)S(1)} collective-permute-done((bf16[2,2,32,128]{3,2,1,0:T(8,128)(2,1)S(1)}, bf16[2,2,32,128]{3,2,1,0:T(8,128)(2,1)S(1)}, u32[]{:S(2)}, u32[]{:S(2)}) %collective-permute-start.6) | collective-permute-done | bytes 32800 | tf_op jit(solution)/shard_map/ppermute | solution.py:175
  18.1 0.4 %collective-permute-start.9 = (bf16[2,32,128]{2,1,0:T(8,128)(2,1)S(1)}, bf16[2,32,128]{2,1,0:T(8,128)(2,1)S(1)}, u32[]{:S(2)}, u32[]{:S(2)}) collective-permute-start(bf16[2,32,128]{2,1,0:T(8,128)(2,1)S(1)} %get-tuple-element.16), channel_id=1, source_target_pairs={{0,1},{1,0},{2,3},{3,2},{4,5},{5,4},{6,7},{7,6},{8,9},{9,8},{10,11... | collective-permute-start | bytes 49160 | tf_op jit(solution)/shard_map/ppermute | solution.py:178
  18.5 0.0 copy-done.6
  18.5 0.1 compare_convert_fusion.live_ref
  18.6 0.0 copy-done.2
  18.6 0.2 turn.1.refs_2_
  18.8 0.0 copy-done.5
  18.8 0.6 %collective-permute-done.9.refs_1_ = bf16[2,32,128]{2,1,0:T(8,128)(2,1)S(1)} collective-permute-done((bf16[2,32,128]{2,1,0:T(8,128)(2,1)S(1)}, bf16[2,32,128]{2,1,0:T(8,128)(2,1)S(1)}, u32[]{:S(2)}, u32[]{:S(2)}) %collective-permute-start.9) | collective-permute-done | bytes 16416 | tf_op jit(solution)/shard_map/ppermute | solution.py:178
  19.4 0.0 copy-done.3
  19.4 1.1 %attend.1 = bf16[2,4096]{1,0:T(2,128)(2,1)} custom-call(f32[2,1,256]{2,1,0:T(1,128)S(1)} %compare_convert_fusion.live_ref, bf16[2,32,128]{2,1,0:T(8,128)(2,1)S(1)} %bitcast.4, bf16[2,32,128]{2,1,0:T(8,128)(2,1)S(1)} %get-tuple-element.15.refs_0_, bf16[2,32,128]{2,1,0:T(8,128)(2,1)S(1)} %collective-permute-done.9.refs_1_, ...), custom_call_target="tpu_custom_call" | custom-call | tf_op jit(solution)/shard_map/attend/pallas_call | solution.py:261
  (3 shorter events, 0.0 us)
Async XLA Ops:
  0.0 8.3 %copy-start.1 = (bf16[8,16,4096]{2,1,0:T(8,128)(2,1)S(1)}, bf16[8,16,4096]{2,1,0:T(8,128)(2,1)}, u32[]{:S(2)}) copy-start(bf16[8,16,4096]{2,1,0:T(8,128)(2,1)} %mine_ref.5) | copy-start | bytes 3145732
  0.0 8.3 %copy-start = (bf16[8,16,8192]{2,1,0:T(8,128)(2,1)S(1)}, bf16[8,16,8192]{2,1,0:T(8,128)(2,1)}, u32[]{:S(2)}) copy-start(bf16[8,16,8192]{2,1,0:T(8,128)(2,1)} %down_ref.5) | copy-start | bytes 6291460
  0.0 8.3 %collective-permute-start = (bf16[8,16,4096]{2,1,0:T(8,128)(2,1)}, bf16[8,16,4096]{2,1,0:T(8,128)(2,1)S(1)}, u32[]{:S(2)}, u32[]{:S(2)}) collective-permute-start(bf16[8,16,4096]{2,1,0:T(8,128)(2,1)} %mine_ref.5), channel_id=1, source_target_pairs={{0,1},{1,0},{2,3},{3,2},{4,5},{5,4},{6,7},{7,6},{8,9},{9,8},{10,11... | collective-permute-start | bytes 3145736 | tf_op jit(solution)/shard_map/ppermute | solution.py:178
  0.5 7.8 %collective-permute-start.3 = (bf16[2,8192]{1,0:T(2,128)(2,1)}, bf16[2,8192]{1,0:T(2,128)(2,1)S(1)}, u32[]{:S(2)}, u32[]{:S(2)}) collective-permute-start(bf16[2,8192]{1,0:T(2,128)(2,1)} %refs_0_.3), channel_id=1, source_target_pairs={{0,6},{1,15},{2,4},{3,13},{4,2},{5,11},{6,0},{7,9},{8,14},{9,7},{1... | collective-permute-start | bytes 98312 | tf_op jit(solution)/shard_map/ppermute | solution.py:175
  4.0 4.3 %collective-permute-start.4 = (bf16[2,8192]{1,0:T(2,128)(2,1)}, bf16[2,8192]{1,0:T(2,128)(2,1)S(1)}, u32[]{:S(2)}, u32[]{:S(2)}) collective-permute-start(bf16[2,8192]{1,0:T(2,128)(2,1)} %refs_0_.3), channel_id=1, source_target_pairs={{0,2},{1,3},{2,0},{3,1},{4,6},{5,7},{6,4},{7,5},{8,10},{9,11},{10,... | collective-permute-start | bytes 98312 | tf_op jit(solution)/shard_map/ppermute | solution.py:175
  4.6 6.5 %collective-permute-start.1 = (bf16[2,8192]{1,0:T(2,128)(2,1)}, bf16[2,8192]{1,0:T(2,128)(2,1)S(1)}, u32[]{:S(2)}, u32[]{:S(2)}) collective-permute-start(bf16[2,8192]{1,0:T(2,128)(2,1)} %refs_0_.3), channel_id=1, source_target_pairs={{0,8},{1,11},{2,10},{3,9},{4,12},{5,15},{6,14},{7,13},{8,0},{9,3},... | collective-permute-start | bytes 98312 | tf_op jit(solution)/shard_map/ppermute | solution.py:175
  7.2 4.8 %collective-permute-start.2 = (bf16[2,8192]{1,0:T(2,128)(2,1)}, bf16[2,8192]{1,0:T(2,128)(2,1)S(1)}, u32[]{:S(2)}, u32[]{:S(2)}) collective-permute-start(bf16[2,8192]{1,0:T(2,128)(2,1)} %refs_0_.3), channel_id=1, source_target_pairs={{0,4},{1,13},{2,6},{3,15},{4,0},{5,9},{6,2},{7,11},{8,12},{9,5},{1... | collective-permute-start | bytes 98312 | tf_op jit(solution)/shard_map/ppermute | solution.py:175
  8.5 6.3 %copy-start.4 = (bf16[2,8192]{1,0:T(2,128)(2,1)S(1)}, bf16[2,8192]{1,0:T(2,128)(2,1)}, u32[]{:S(2)}) copy-start(bf16[2,8192]{1,0:T(2,128)(2,1)} %refs_0_.3) | copy-start | bytes 98308
  8.5 9.0 %collective-permute-start.5 = (bf16[2,2,32,128]{3,2,1,0:T(8,128)(2,1)S(1)}, bf16[2,2,32,128]{3,2,1,0:T(8,128)(2,1)S(1)}, u32[]{:S(2)}, u32[]{:S(2)}) collective-permute-start(bf16[2,2,32,128]{3,2,1,0:T(8,128)(2,1)S(1)} %get-tuple-element.11.refs_2_), channel_id=1, source_target_pairs={{0,6},{1,15},{2,4},{3,13},{4,2},{5,11},{6,0},{7,9},{8,14},{9,7},{1... | collective-permute-start | bytes 98312 | tf_op jit(solution)/shard_map/ppermute | solution.py:175
  12.3 5.2 %collective-permute-start.7 = (bf16[2,2,32,128]{3,2,1,0:T(8,128)(2,1)S(1)}, bf16[2,2,32,128]{3,2,1,0:T(8,128)(2,1)S(1)}, u32[]{:S(2)}, u32[]{:S(2)}) collective-permute-start(bf16[2,2,32,128]{3,2,1,0:T(8,128)(2,1)S(1)} %get-tuple-element.12.refs_1_), channel_id=1, source_target_pairs={{0,8},{1,11},{2,10},{3,9},{4,12},{5,15},{6,14},{7,13},{8,0},{9,3},... | collective-permute-start | bytes 98312 | tf_op jit(solution)/shard_map/ppermute | solution.py:175
  12.6 4.9 %collective-permute-start.8 = (bf16[2,2,32,128]{3,2,1,0:T(8,128)(2,1)S(1)}, bf16[2,2,32,128]{3,2,1,0:T(8,128)(2,1)S(1)}, u32[]{:S(2)}, u32[]{:S(2)}) collective-permute-start(bf16[2,2,32,128]{3,2,1,0:T(8,128)(2,1)S(1)} %get-tuple-element.14), channel_id=1, source_target_pairs={{0,4},{1,13},{2,6},{3,15},{4,0},{5,9},{6,2},{7,11},{8,12},{9,5},{1... | collective-permute-start | bytes 98312 | tf_op jit(solution)/shard_map/ppermute | solution.py:175
  13.7 4.8 %copy-start.6 = (s32[2]{0:T(128)S(1)}, s32[2]{0:T(128)}, u32[]{:S(2)}) copy-start(s32[2]{0:T(128)} %param.15) | copy-start | bytes 28
  13.7 4.9 %copy-start.2 = (bf16[2,4,256,128]{3,2,1,0:T(8,128)(2,1)S(1)}, bf16[2,4,256,128]{3,2,1,0:T(8,128)(2,1)}, u32[]{:S(2)}) copy-start(bf16[2,4,256,128]{3,2,1,0:T(8,128)(2,1)} %key_ref.1) | copy-start | bytes 1572868
  13.7 5.1 %copy-start.5 = (bf16[2,4096]{1,0:T(2,128)(2,1)S(1)}, bf16[2,4096]{1,0:T(2,128)(2,1)}, u32[]{:S(2)}) copy-start(bf16[2,4096]{1,0:T(2,128)(2,1)} %param.9) | copy-start | bytes 49156
  13.7 5.7 %copy-start.3 = (bf16[2,4,256,128]{3,2,1,0:T(8,128)(2,1)S(1)}, bf16[2,4,256,128]{3,2,1,0:T(8,128)(2,1)}, u32[]{:S(2)}) copy-start(bf16[2,4,256,128]{3,2,1,0:T(8,128)(2,1)} %refs_3_.1) | copy-start | bytes 1572868
  13.7 4.4 %collective-permute-start.6 = (bf16[2,2,32,128]{3,2,1,0:T(8,128)(2,1)S(1)}, bf16[2,2,32,128]{3,2,1,0:T(8,128)(2,1)S(1)}, u32[]{:S(2)}, u32[]{:S(2)}) collective-permute-start(bf16[2,2,32,128]{3,2,1,0:T(8,128)(2,1)S(1)} %get-tuple-element.13), channel_id=1, source_target_pairs={{0,2},{1,3},{2,0},{3,1},{4,6},{5,7},{6,4},{7,5},{8,10},{9,11},{10,... | collective-permute-start | bytes 98312 | tf_op jit(solution)/shard_map/ppermute | solution.py:175
  18.1 1.2 %collective-permute-start.9 = (bf16[2,32,128]{2,1,0:T(8,128)(2,1)S(1)}, bf16[2,32,128]{2,1,0:T(8,128)(2,1)S(1)}, u32[]{:S(2)}, u32[]{:S(2)}) collective-permute-start(bf16[2,32,128]{2,1,0:T(8,128)(2,1)S(1)} %get-tuple-element.16), channel_id=1, source_target_pairs={{0,1},{1,0},{2,3},{3,2},{4,5},{5,4},{6,7},{7,6},{8,9},{9,8},{10,11... | collective-permute-start | bytes 49160 | tf_op jit(solution)/shard_map/ppermute | solution.py:178
